TPU v7x, 32 devices: a whole 2x2x4 slice. The times are simulated.
32 devices in a mesh: groups: 2 (over y), tp: 16 (over z, x, core).
Axes of the slice: x: 2, y: 2, z: 4, core: 2. Of those that a mesh axis runs over, the one named last changes fastest.
Arguments:
- queries: bfloat16 [16, 256, 128], P('tp', 'groups'), parts along dimension 1, may hold values from -32 to 32
- cache_keys: bfloat16 [16, 16384, 128], P('tp', 'groups'), parts along dimension 1, may hold values from -6 to 6
- cache_values: bfloat16 [16, 16384, 128], P('tp', 'groups'), parts along dimension 1, may hold values from -6 to 6
- query_positions: int32 [256], P('groups'), parts along dimension 0, may hold values from 0 to 8191, as said below
- out_weight: bfloat16 [2048, 16384], P('tp'), may hold values from -0.75 to 0.75
- residual: bfloat16 [256, 16384], P('groups', 'tp'), parts along dimension 0, may hold values from -80 to 80
- scale_table: int32 [2, 128], replicated, may hold values from 2 to 127
- norm_gain: bfloat16 [16384], replicated, may hold values from 0.099609375 to 1.8984375
- next_query_weight: bfloat16 [16384, 2048], P(None, 'tp'), may hold values from -0.046875 to 0.046875
Outputs:
- hidden_out: bfloat16 [256, 16384], P('groups', 'tp'), parts along dimension 0
- query_next: bfloat16 [256, 2048], P('groups', 'tp'), parts along dimension 0
There are 2 independent parts, one for each index of `groups`. A program takes and returns all parts, laid end to end along the dimension named above; an argument that names none is the same for every part. Nothing has to cross between parts.
Inputs may be any that keep to these rules, and one draw needn't show every extreme that they name: `query_positions`: strictly increasing along the span; the last entry is 8191.
All inputs are finite; a program needn't handle non-finite values.
Results may differ from a plain program's by a relative error of at most 0.0065.
Values may be sent and summed in bfloat16 or wider, within the bound.
No kernel may reach another device: no remote copies, remote signals or barrier semaphores. Data moves between devices by JAX's collectives and lax.ppermute only.
A program may use at most 128 MiB of HBM per device.

v0:
```python
import math

import jax
import jax.numpy as jnp
from jax import lax
from jax.sharding import PartitionSpec as P

HD = 128
ROT = 128


def sylvester(length):
    row_ids = lax.broadcasted_iota(jnp.int32, (length, length), 0)
    col_ids = lax.broadcasted_iota(jnp.int32, (length, length), 1)
    common_bits = jnp.bitwise_and(row_ids, col_ids)
    parity = jnp.zeros((length, length), jnp.int32)
    for bit_index in range(length.bit_length()):
        parity = parity + jnp.bitwise_and(jnp.right_shift(common_bits, bit_index), 1)
    sign_table = 1 - 2 * jnp.bitwise_and(parity, 1)
    return sign_table.astype(jnp.float32) / math.sqrt(length)


def rotate(values_in, rotation):
    leading = values_in.shape[:-1]
    blocks = values_in.reshape(leading + (values_in.shape[-1] // ROT, ROT))
    turned = jnp.einsum("...bi,ij->...bj", blocks, rotation, precision=lax.Precision.HIGHEST)
    return turned.reshape(values_in.shape)


def blockwise(values_in, block_scale):
    leading = values_in.shape[:-1]
    blocks = values_in.reshape(leading + (block_scale.shape[0], ROT))
    return (blocks * block_scale[:, None]).reshape(values_in.shape)


def to_grid(values_in, block_scale):
    leading = values_in.shape[:-1]
    blocks = values_in.reshape(leading + (block_scale.shape[0], ROT))
    clipped = jnp.clip(blocks / block_scale[:, None], -127.0, 127.0)
    return clipped.reshape(values_in.shape).astype(jnp.bfloat16)


def body(
    queries,
    cache_keys,
    cache_values,
    query_positions,
    out_weight,
    residual,
    scale_table,
    norm_gain,
    next_query_weight,
):
    rotation = sylvester(ROT)
    shard_cols = residual.shape[1]
    block_count = shard_cols // ROT
    first_block = lax.axis_index("tp") * block_count
    scores = jnp.einsum(
        "qd,kd->qk", queries[0], cache_keys[0], preferred_element_type=jnp.float32
    ) / math.sqrt(HD)
    slot_ids = lax.broadcasted_iota(jnp.int32, (1, cache_keys.shape[1]), 1)
    scores = jnp.where(slot_ids <= query_positions[:, None], scores, -jnp.inf)
    largest = jnp.max(scores, axis=-1, keepdims=True)
    raised = jnp.exp(scores - largest)
    soft_weights = (raised / jnp.sum(raised, axis=-1, keepdims=True)).astype(jnp.bfloat16)
    context = jnp.dot(soft_weights, cache_values[0], preferred_element_type=jnp.float32).astype(
        jnp.bfloat16
    )
    low_table = scale_table[0].astype(jnp.float32) / 65536.0
    high_table = scale_table[1].astype(jnp.float32) / 256.0
    low_local = lax.dynamic_slice_in_dim(low_table, first_block, block_count)
    high_local = lax.dynamic_slice_in_dim(high_table, first_block, block_count)
    partial_value = jnp.dot(context, out_weight, preferred_element_type=jnp.float32)
    on_grid = to_grid(rotate(partial_value, rotation), low_table)
    summed = lax.psum_scatter(on_grid.astype(jnp.float32), "tp", scatter_dimension=1, tiled=True)
    stream = residual.astype(jnp.float32) + rotate(blockwise(summed, low_local), rotation)
    hidden_out = stream.astype(jnp.bfloat16)
    regrid = to_grid(rotate(stream, rotation), high_local)
    gathered = lax.all_gather(regrid, "tp", axis=1, tiled=True)
    restored = rotate(blockwise(gathered.astype(jnp.float32), high_table), rotation)
    mean_square = jnp.mean(restored * restored, axis=-1, keepdims=True)
    normed = (restored * lax.rsqrt(mean_square + 1e-05) * norm_gain.astype(jnp.float32)).astype(
        jnp.bfloat16
    )
    query_next = jnp.dot(normed, next_query_weight, preferred_element_type=jnp.float32).astype(
        jnp.bfloat16
    )
    return (hidden_out, query_next)


def solution(mesh):
    placed = (
        P("tp", "groups", None),
        P("tp", "groups", None),
        P("tp", "groups", None),
        P("groups"),
        P("tp", None),
        P("groups", "tp"),
        P(),
        P(),
        P(None, "tp"),
    )
    return jax.shard_map(
        body,
        mesh=mesh,
        in_specs=placed,
        out_specs=(P("groups", "tp"), P("groups", "tp")),
        check_vma=False,
    )
```

profile of v0, /device:TPU:0, one launch (start us, length us, event | category | flops | bytes accessed | tf_op | source)
XLA Modules:
  0.0 236.3 jit_solution(5988568385219968743)
XLA Ops:
  7.2 0.0 copy-start
  7.2 0.0 reduce-scatter.2.cloned.1.call-start
  7.2 0.8 fusion.74
  8.1 2.5 %fusion.75 = (f32[128]{0:T(128)S(1)}, f32[128,8192]{1,0:T(8,128)S(1)}) fusion(bf16[1,8192,128]{2,1,0:T(8,128)(2,1)} %param.10, bf16[1,128,128]{2,1,0:T(8,128)(2,1)} %param.9, s32[128]{0:T(128)} %param.12), kind=kOutput, calls=%fused_computation.84 | convolution fusion | flops 272629632 | bytes 6325248 | tf_op jit(solution)/shard_map/qd,kd->qk/dot_general | solution.py:58
  10.6 0.0 copy-start.2
  10.6 1.9 copy-done.2
  12.6 0.8 fusion.11
  13.3 0.0 copy-done
  13.3 8.9 %convolution_bitcast_fusion = f32[16,8,128,128]{3,1,2,0:T(8,128)} fusion(bf16[128,16384]{1,0:T(8,128)(2,1)} %param.13, bf16[1,8192,128]{2,1,0:T(8,128)(2,1)S(1)} %copy-done, f32[128,8192]{1,0:T(8,128)} %copy-done.2, f32[128]{0:T(128)S(1)} %fusion.11, f32[128]{0:T(128)S(1)} %get-tuple-element.8), kind=kOutput, calls=%fused_computation.18 | convolution fusion | flops 808468480 | bytes 18875392 | tf_op jit(solution)/shard_map/dot_general | solution.py:73
  22.2 4.8 %copy.31 = f32[16,8,128,128]{3,2,1,0:T(8,128)S(1)} copy(f32[16,8,128,128]{3,1,2,0:T(8,128)} %convolution_bitcast_fusion) | data formatting | bytes 16777216
  27.0 9.0 %fusion.5 = f32[128,128,128]{2,1,0:T(8,128)} fusion(f32[128]{0:T(128)S(1)} %get-tuple-element.5, f32[128,128,128]{2,1,0:T(8,128)S(1)} %bitcast.67), kind=kOutput, calls=%fused_computation.9 | convolution fusion | flops 3230089216 | bytes 16777728 | tf_op jit(solution)/shard_map/...bi,ij->...bj/dot_general | solution.py:26
  36.0 9.3 %copy.26 = f32[128,128,128]{0,2,1:T(8,128)} copy(f32[128,128,128]{2,1,0:T(8,128)} %fusion.5) | data formatting | bytes 16777216 | tf_op jit(solution)/shard_map/convert_element_type | solution.py:75
  45.4 0.0 copy-start.4
  45.4 0.0 reduce-scatter.2.cloned.1.call-update
  45.4 0.0 copy-start.5
  45.4 0.2 all-gather.2.cloned.1.call-start
  45.6 0.1 dynamic-slice_bitcast_fusion.1
  45.7 0.1 dynamic-slice_bitcast_fusion
  45.8 107.1 %reduce-scatter.2.cloned.1.call-done = f32[128,1024]{0,1:T(8,128)} async-done(((f32[128,16384]{0,1:T(8,128)}), f32[128,1024]{0,1:T(8,128)}) %reduce-scatter.2.cloned.1.call-update) | async-done | bytes 524304 | tf_op jit(solution)/shard_map/reduce_scatter | solution.py:75
  152.8 1.7 fusion.27
  154.6 0.2 copy.19
  154.8 0.0 copy-done.4
  154.8 0.8 fusion.29
  155.6 1.4 fusion.16
  157.0 0.0 all-gather.2.cloned.1.call-update
  157.0 0.0 copy-done.5
  157.0 50.5 %all-gather.2.cloned.1.call-done = bf16[128,16384]{0,1:T(8,128)(2,1)} async-done(((bf16[128,1024]{0,1:T(8,128)(2,1)}), bf16[128,16384]{0,1:T(8,128)(2,1)}) %all-gather.2.cloned.1.call-update) | async-done | bytes 4194320 | tf_op jit(solution)/shard_map/all_gather | solution.py:79
  207.5 7.0 %copy.29 = f32[128,128,128]{2,1,0:T(8,128)} copy(bf16[128,128,128]{0,2,1:T(8,128)(2,1)} %bitcast.68) | data formatting | bytes 12582912 | tf_op jit(solution)/shard_map/reshape | solution.py:32
  214.4 9.5 %multiply_reduce_fusion = (f32[128]{0:T(128)S(1)}, f32[128,128,128]{2,1,0:T(8,128)S(1)}) fusion(f32[128,128,128]{2,1,0:T(8,128)} %copy.29, f32[128]{0:T(128)S(1)} %get-tuple-element.4), kind=kOutput, calls=%fused_computation.5 | convolution fusion | flops 3227992064 | bytes 16778240 | tf_op jit(solution)/shard_map/...bi,ij->...bj/dot_general | solution.py:26
  223.9 0.0 copy-done.3
  223.9 5.6 %fusion.20 = bf16[128,128]{1,0:T(8,128)(2,1)} fusion(bf16[16384,128]{1,0:T(8,128)(2,1)S(1)} %copy-done.3, f32[16,8,128,128]{3,2,1,0:T(8,128)S(1)} %bitcast.66, f32[16384]{0:T(1024)S(1)} %convert_element_type.75, f32[128]{0:T(128)S(1)} %add_rsqrt_fusion), kind=kOutput, calls=%fused_computation.26 | convolution fusion | flops 543178752 | bytes 12681728 | tf_op jit(solution)/shard_map/dot_general | solution.py:85
  229.5 0.0 copy-done.1
  (4 shorter events, 0.0 us)
Async XLA Ops:
  7.2 6.1 %copy-start = (bf16[1,8192,128]{2,1,0:T(8,128)(2,1)S(1)}, bf16[1,8192,128]{2,1,0:T(8,128)(2,1)}, u32[]{:S(2)}) copy-start(bf16[1,8192,128]{2,1,0:T(8,128)(2,1)} %param.11) | copy-start | bytes 6291460
  7.2 145.7 %reduce-scatter.2.cloned.1.call-start = ((), (), s32[]{:S(2)}) async-start(), calls=%async_computation.1 | async-start | bytes 8912896 | tf_op jit(solution)/shard_map/reduce_scatter | solution.py:75
  10.6 1.9 copy-start.2
  45.4 109.4 %copy-start.4 = (bf16[128,1024]{1,0:T(8,128)(2,1)S(1)}, bf16[128,1024]{1,0:T(8,128)(2,1)}, u32[]{:S(2)}) copy-start(bf16[128,1024]{1,0:T(8,128)(2,1)} %param.14) | copy-start | bytes 786436
  45.4 111.6 %copy-start.5 = (bf16[16384]{0:T(1024)(128)(2,1)S(1)}, bf16[16384]{0:T(1024)(128)(2,1)}, u32[]{:S(2)}) copy-start(bf16[16384]{0:T(1024)(128)(2,1)} %param.16) | copy-start | bytes 98308
  45.4 162.1 %all-gather.2.cloned.1.call-start = ((), (), s32[]{:S(2)}) async-start(), calls=%async_computation.2 | async-start | bytes 4456448 | tf_op jit(solution)/shard_map/all_gather | solution.py:79
  214.4 9.5 %copy-start.3 = (bf16[16384,128]{1,0:T(8,128)(2,1)S(1)}, bf16[16384,128]{1,0:T(8,128)(2,1)}, u32[]{:S(2)}) copy-start(bf16[16384,128]{1,0:T(8,128)(2,1)} %param.17) | copy-start | bytes 12582916
  223.9 5.6 %copy-start.1 = (bf16[1,8192,128]{2,1,0:T(8,128)(2,1)S(1)}, bf16[1,8192,128]{2,1,0:T(8,128)(2,1)}, u32[]{:S(2)}) copy-start(bf16[1,8192,128]{2,1,0:T(8,128)(2,1)} %param.11) | copy-start | bytes 6291460
Sparse Core Ops, SparseCore 0:
  45.5 107.2 reduce-scatter.1
  157.1 50.3 all-gather.1
where the time goes:
time: 237 us; the launch traced here: 236 us
  waiting for transfers between devices  158 us (67%)
  matrix products  38.6 us (16%)
  local copies, waits for them, and re-layouts  23.4 us (10%)
  between operations  14.1 us (6%)
  other arithmetic  2.4 us (1%)
    reduce_scatter x1, waiting for transfers between devices, body(): lax.psum_scatter(on_grid.astype(jnp.float32), 'tp', scatter_dimension=1,...  107 us
    all_gather x1, waiting for transfers between devices, body(): gathered = lax.all_gather(regrid, 'tp', axis=1, tiled=True)  50.5 us
    dot_general x4, matrix products, rotate(): jnp.einsum('...bi,ij->...bj', blocks, rotation, precision=lax.Precision.H...  21.6 us
    convert_element_type x1, local copies, waits for them, and re-layouts, body(): on_grid.astype(jnp.float32)  9.33 us
    dot_general x1, matrix products, body(): jnp.dot(context, out_weight, preferred_element_type=jnp.float32)  8.85 us
    reshape x1, local copies, waits for them, and re-layouts, blockwise(): blocks = values_in.reshape(leading + (block_scale.shape[0], ROT))  6.96 us
    unnamed x13, local copies, waits for them, and re-layouts  6.81 us
    dot_general x1, matrix products, body(): jnp.dot(normed, next_query_weight, preferred_element_type=jnp.float32)  5.6 us
  transfers between devices with their start and end apart: 2, of which 2 were waited for; matrix products, arithmetic and copies ran while one was open for 0% of the time, Pallas kernels for 0%

commit v1 on v0

v1 whole, which is shorter than its diff:
```python
import functools
import math

import jax
import jax.numpy as jnp
import numpy as np
from jax import lax
from jax.experimental import pallas as pl
from jax.experimental.pallas import tpu as pltpu
from jax.sharding import PartitionSpec as P

HD = 128
ROT = 128
OUTER = 4
SUM_ORDER = np.array([[3, 2, 1, 0], [3, 2, 0, 1], [0, 1, 3, 2], [0, 1, 2, 3]], np.int32)
GATHER_ORDER = np.array([[0, 1, 2, 3], [1, 0, 2, 3], [2, 3, 1, 0], [3, 2, 1, 0]], np.int32)

F32 = jnp.float32
BF16 = jnp.bfloat16
MIB = 1024 * 1024


def hadamard(length):
    rows = np.arange(length)
    common = rows[:, None] & rows[None, :]
    parity = np.zeros((length, length), np.int64)
    for bit in range(length.bit_length()):
        parity += (common >> bit) & 1
    return (1 - 2 * (parity & 1)).astype(np.float32)


def params(limit=24):
    return pltpu.CompilerParams(vmem_limit_bytes=limit * MIB)


def cost(flops, nbytes, exps=0):
    return pl.CostEstimate(flops=int(flops), bytes_accessed=int(nbytes), transcendentals=int(exps))


def vmem():
    return pl.BlockSpec(memory_space=pltpu.VMEM)


def smem():
    return pl.BlockSpec(memory_space=pltpu.SMEM)


def select_cols_kernel(blocks, cols, info, w_ref, out_ref, sem):
    other = 1 - info[10]
    copies = []
    for j in range(blocks):
        start = pl.multiple_of((2 * j + other) * cols, 128)
        copies.append(
            pltpu.make_async_copy(w_ref.at[:, pl.ds(start, cols)], out_ref.at[j], sem.at[j])
        )
    for copy in copies:
        copy.start()
    for copy in copies:
        copy.wait()


def select_cols(info, weight, blocks, cols):
    rows = weight.shape[0]
    return pl.pallas_call(
        functools.partial(select_cols_kernel, blocks, cols),
        out_shape=jax.ShapeDtypeStruct((blocks, rows, cols), weight.dtype),
        in_specs=[smem(), pl.BlockSpec(memory_space=pl.ANY)],
        out_specs=pl.BlockSpec(memory_space=pl.ANY),
        scratch_shapes=[pltpu.SemaphoreType.DMA((blocks,))],
        cost_estimate=cost(0, 4 * blocks * rows * cols),
        compiler_params=params(4),
        name="select_cols",
    )(info, weight)


def select_rows_kernel(blocks, cols, info, w_ref, out_ref, sem):
    other = 1 - info[10]
    copies = []
    for j in range(blocks):
        start = pl.multiple_of((2 * j + other) * cols, 128)
        copies.append(
            pltpu.make_async_copy(w_ref.at[pl.ds(start, cols)], out_ref.at[j], sem.at[j])
        )
    for copy in copies:
        copy.start()
    for copy in copies:
        copy.wait()


def select_rows(info, weight, blocks, cols):
    return pl.pallas_call(
        functools.partial(select_rows_kernel, blocks, cols),
        out_shape=jax.ShapeDtypeStruct((blocks, cols, weight.shape[1]), weight.dtype),
        in_specs=[smem(), pl.BlockSpec(memory_space=pl.ANY)],
        out_specs=pl.BlockSpec(memory_space=pl.ANY),
        scratch_shapes=[pltpu.SemaphoreType.DMA((blocks,))],
        cost_estimate=cost(0, 4 * blocks * cols * weight.shape[1]),
        compiler_params=params(4),
        name="select_rows",
    )(info, weight)


def attend_kernel(steps, chunk, q_ref, k_ref, v_ref, pos_ref, out_ref, m_ref, l_ref, acc_ref):
    step = pl.program_id(0)
    tok = q_ref.shape[0]

    @pl.when(step == 0)
    def _():
        m_ref[...] = jnp.full_like(m_ref, -jnp.inf)
        l_ref[...] = jnp.zeros_like(l_ref)
        acc_ref[...] = jnp.zeros_like(acc_ref)

    positions = jnp.broadcast_to(pos_ref[...].astype(F32), (tok, tok)).T[:, :1]
    scores = lax.dot_general(
        q_ref[...], k_ref[...], (((1,), (1,)), ((), ())), preferred_element_type=F32
    )
    slots = lax.broadcasted_iota(jnp.int32, (tok, chunk), 1) + step * chunk
    scores = jnp.where(slots <= positions.astype(jnp.int32), scores, -jnp.inf)
    before = m_ref[:, :1]
    largest = jnp.maximum(before, jnp.max(scores, axis=1, keepdims=True))
    factor = math.log2(math.e) / math.sqrt(HD)
    raised = jnp.exp2((scores - largest) * factor)
    shrink = jnp.exp2((before - largest) * factor)
    total = l_ref[:, :1] * shrink + jnp.sum(raised, axis=1, keepdims=True)
    acc = acc_ref[...] * shrink + jnp.dot(
        raised.astype(BF16), v_ref[...], preferred_element_type=F32
    )
    m_ref[...] = jnp.broadcast_to(largest, m_ref.shape)
    l_ref[...] = jnp.broadcast_to(total, l_ref.shape)
    acc_ref[...] = acc

    @pl.when(step == steps - 1)
    def _():
        out_ref[...] = (acc / total).astype(BF16)


def attend(queries, keys, values, positions):
    tok = queries.shape[0]
    slots = keys.shape[0]
    chunk = min(2048, slots)
    steps = slots // chunk
    return pl.pallas_call(
        functools.partial(attend_kernel, steps, chunk),
        out_shape=jax.ShapeDtypeStruct((tok, HD), BF16),
        grid=(steps,),
        in_specs=[
            pl.BlockSpec((tok, HD), lambda i: (0, 0)),
            pl.BlockSpec((chunk, HD), lambda i: (i, 0)),
            pl.BlockSpec((chunk, HD), lambda i: (i, 0)),
            pl.BlockSpec((1, tok), lambda i: (0, 0)),
        ],
        out_specs=pl.BlockSpec((tok, HD), lambda i: (0, 0)),
        scratch_shapes=[pltpu.VMEM((tok, HD), F32)] * 3,
        cost_estimate=cost(4 * tok * slots * HD, 4 * slots * HD, tok * slots),
        compiler_params=params(),
        name="attend",
    )(queries, keys, values, positions[None, :])


def turn_out_kernel(inner, cols, info, scales, own_ref, other_ref, h_ref, out_ref):
    shard = pl.program_id(0) * 2 + info[10]
    for i in range(cols // ROT):
        scale = scales[0, shard * (cols // ROT) + i].astype(F32)
        factor = (65536.0 / math.sqrt(ROT)) / jnp.full((1, ROT), scale, F32)
        part = slice(i * ROT, (i + 1) * ROT)
        for head, ref in enumerate((own_ref, other_ref.at[0])):
            turned = jnp.dot(ref[:, part], h_ref[...], preferred_element_type=F32)
            out_ref[0, head, :, part] = (turned * factor).astype(BF16)


def turn_out(info, scales, weight, other, had):
    blocks, rows, cols = other.shape
    return pl.pallas_call(
        functools.partial(turn_out_kernel, blocks // OUTER, cols),
        out_shape=jax.ShapeDtypeStruct((blocks, 2, rows, cols), BF16),
        grid_spec=pltpu.PrefetchScalarGridSpec(
            num_scalar_prefetch=2,
            grid=(blocks,),
            in_specs=[
                pl.BlockSpec((rows, cols), lambda j, info, scales: (0, 2 * j + info[10])),
                pl.BlockSpec((1, rows, cols), lambda j, info, scales: (j, 0, 0)),
                pl.BlockSpec((ROT, ROT), lambda j, info, scales: (0, 0)),
            ],
            out_specs=pl.BlockSpec((1, 2, rows, cols), lambda j, info, scales: (j, 0, 0, 0)),
        ),
        cost_estimate=cost(4 * blocks * rows * cols * ROT, 8 * blocks * rows * cols),
        compiler_params=params(),
        name="turn_out",
    )(info, scales, weight, other, had)


def partial_kernel(inner, info, own_ref, other_ref, w_ref, keep_ref, *send_refs):
    cols = keep_ref.shape[1]
    step = min(cols, 256)
    for shift in range(inner):
        dest = lax.rem(info[9] + shift, inner)
        for start in range(0, cols, step):
            part = slice(start, start + step)
            total = None
            for head, ctx_ref in enumerate((own_ref, other_ref)):
                value = jnp.dot(ctx_ref[...], w_ref[dest, head, :, part], preferred_element_type=F32)
                value = jnp.clip(value, -127.0, 127.0)
                total = value if total is None else total + value
            if shift == 0:
                keep_ref[:, part] = total
            else:
                send_refs[shift - 1][:, part] = total.astype(BF16)


def partials(phase, info, own, other, weight):
    blocks, _, rows, cols = weight.shape
    inner = blocks // OUTER
    tok = own.shape[0]
    return pl.pallas_call(
        functools.partial(partial_kernel, inner),
        out_shape=[jax.ShapeDtypeStruct((tok, cols), F32)]
        + [jax.ShapeDtypeStruct((tok, cols), BF16)] * (inner - 1),
        grid_spec=pltpu.PrefetchScalarGridSpec(
            num_scalar_prefetch=1,
            grid=(1,),
            in_specs=[
                pl.BlockSpec((tok, rows), lambda j, info: (0, 0)),
                pl.BlockSpec((tok, rows), lambda j, info: (0, 0)),
                pl.BlockSpec((inner, 2, rows, cols), lambda j, info: (info[phase], 0, 0, 0)),
            ],
            out_specs=[pl.BlockSpec((tok, cols), lambda j, info: (0, 0))] * inner,
        ),
        cost_estimate=cost(4 * tok * inner * rows * cols, 4 * inner * rows * cols + 4 * tok * cols * inner),
        compiler_params=params(),
        name="partials",
    )(info, own, other, weight)


def add_kernel(*refs):
    *ins, out_ref = refs
    total = ins[0][...].astype(F32)
    for ref in ins[1:]:
        total = total + ref[...].astype(F32)
    out_ref[...] = total.astype(out_ref.dtype)


def add_up(arrays, dtype=BF16):
    return pl.pallas_call(
        add_kernel,
        out_shape=jax.ShapeDtypeStruct(arrays[0].shape, dtype),
        in_specs=[vmem()] * len(arrays),
        out_specs=vmem(),
        cost_estimate=cost(arrays[0].size * len(arrays), 3 * arrays[0].size * len(arrays)),
        compiler_params=params(),
        name="add_up",
    )(*arrays)


def turn_residual_kernel(res_ref, h_ref, out_ref):
    for i in range(res_ref.shape[1] // ROT):
        part = slice(i * ROT, (i + 1) * ROT)
        turned = jnp.dot(res_ref[:, part], h_ref[...], preferred_element_type=F32)
        out_ref[:, part] = turned * (1.0 / math.sqrt(ROT))


def turn_residual(residual, had):
    return pl.pallas_call(
        turn_residual_kernel,
        out_shape=jax.ShapeDtypeStruct(residual.shape, F32),
        in_specs=[vmem()] * 2,
        out_specs=vmem(),
        cost_estimate=cost(2 * residual.size * ROT, 6 * residual.size),
        compiler_params=params(),
        name="turn_residual",
    )(residual, had)


def regrid_kernel(count, *refs):
    info, scales, turned_ref = refs[:3]
    ins = refs[3 : 3 + count]
    grid_ref, low_ref = refs[3 + count :]
    cols = turned_ref.shape[1]
    for i in range(cols // ROT):
        block = info[11] * (cols // ROT) + i
        low = jnp.full((1, ROT), scales[0, block].astype(F32), F32) * (1.0 / 65536.0)
        high = 256.0 / jnp.full((1, ROT), scales[1, block].astype(F32), F32)
        part = slice(i * ROT, (i + 1) * ROT)
        total = ins[0][:, part].astype(F32)
        for ref in ins[1:]:
            total = total + ref[:, part].astype(F32)
        total = total * low
        low_ref[:, part] = total
        value = (turned_ref[:, part] + total) * high
        grid_ref[:, part] = jnp.clip(value, -127.0, 127.0).astype(BF16)


def regrid(info, scales, turned, arrays):
    return pl.pallas_call(
        functools.partial(regrid_kernel, len(arrays)),
        out_shape=[
            jax.ShapeDtypeStruct(turned.shape, BF16),
            jax.ShapeDtypeStruct(turned.shape, F32),
        ],
        in_specs=[smem(), smem()] + [vmem()] * (1 + len(arrays)),
        out_specs=[vmem(), vmem()],
        cost_estimate=cost(8 * turned.size, 16 * turned.size),
        compiler_params=params(),
        name="regrid",
    )(info, scales, turned, *arrays)


def hidden_kernel(res_ref, low_ref, h_ref, out_ref):
    for i in range(res_ref.shape[1] // ROT):
        part = slice(i * ROT, (i + 1) * ROT)
        value = low_ref[:, part]
        upper = value.astype(BF16)
        lower = (value - upper.astype(F32)).astype(BF16)
        turned = jnp.dot(upper, h_ref[...], preferred_element_type=F32)
        turned = turned + jnp.dot(lower, h_ref[...], preferred_element_type=F32)
        stream = res_ref[:, part].astype(F32) + turned * (1.0 / math.sqrt(ROT))
        out_ref[:, part] = stream.astype(BF16)


def hidden(residual, low, had):
    return pl.pallas_call(
        hidden_kernel,
        out_shape=jax.ShapeDtypeStruct(residual.shape, BF16),
        in_specs=[vmem()] * 3,
        out_specs=vmem(),
        cost_estimate=cost(4 * residual.size * ROT, 8 * residual.size),
        compiler_params=params(),
        name="hidden",
    )(residual, low, had)


def turn_next_kernel(cols, info, scales, own_ref, other_ref, gain_ref, h_ref, out_ref):
    shard = pl.program_id(0) * 2 + info[10]
    for i in range(cols // ROT):
        block = shard * (cols // ROT) + i
        scale = jnp.full((1, HD), scales[1, block].astype(F32), F32)
        factor = scale * (1.0 / (256.0 * math.sqrt(ROT)))
        rotation = (h_ref[...].astype(F32) * gain_ref[pl.ds(block, 1), :]).astype(BF16)
        part = slice(i * ROT, (i + 1) * ROT)
        for half, ref in enumerate((own_ref, other_ref.at[0])):
            turned = jnp.dot(rotation, ref[part, :], preferred_element_type=F32)
            out_ref[0, part, half * HD : (half + 1) * HD] = (turned * factor).astype(BF16)


def turn_next(info, scales, weight, other, gain, had):
    blocks, cols, width = other.shape
    return pl.pallas_call(
        functools.partial(turn_next_kernel, cols),
        out_shape=jax.ShapeDtypeStruct((blocks, cols, 2 * width), BF16),
        grid_spec=pltpu.PrefetchScalarGridSpec(
            num_scalar_prefetch=2,
            grid=(blocks,),
            in_specs=[
                pl.BlockSpec((cols, width), lambda j, info, scales: (2 * j + info[10], 0)),
                pl.BlockSpec((1, cols, width), lambda j, info, scales: (j, 0, 0)),
                pl.BlockSpec(gain.shape, lambda j, info, scales: (0, 0)),
                pl.BlockSpec((ROT, ROT), lambda j, info, scales: (0, 0)),
            ],
            out_specs=pl.BlockSpec((1, cols, 2 * width), lambda j, info, scales: (j, 0, 0)),
        ),
        cost_estimate=cost(4 * blocks * cols * width * ROT, 8 * blocks * cols * width),
        compiler_params=params(),
        name="turn_next",
    )(info, scales, weight, other, gain, had)


def project_kernel(inner, groups, has_acc, *refs):
    info, scales = refs[:2]
    refs = refs[2:]
    weights = refs[: len(groups)]
    refs = refs[len(groups) :]
    acc_in = refs[0] if has_acc else None
    refs = refs[1:] if has_acc else refs
    out_ref = refs[-1]
    refs = refs[:-1]
    cols = weights[0].shape[1]
    width = weights[0].shape[2]
    acc = acc_in[:, :width] if has_acc else 0.0
    squares = acc_in[:, width:] if has_acc else 0.0
    at = 0
    for w_ref, (phase, shift, count) in zip(weights, groups):
        values = refs[at][...]
        for ref in refs[at + 1 : at + count]:
            values = values + ref[...]
        at += count
        acc = acc + jnp.dot(values, w_ref[0], preferred_element_type=F32)
        source = lax.rem(info[9] + inner - shift, inner)
        shard = (info[4 + phase] * inner + source) * 2 + info[10]
        for i in range(cols // ROT):
            scale = scales[1, shard * (cols // ROT) + i].astype(F32)
            high = jnp.full((1, ROT), scale, F32) * (1.0 / 256.0)
            value = values[:, i * ROT : (i + 1) * ROT].astype(F32) * high
            squares = squares + value * value
    out_ref[:, :width] = acc
    out_ref[:, width:] = squares


def project(info, scales, weight, acc, pieces):
    blocks, cols, width = weight.shape
    inner = blocks // OUTER
    tok = pieces[0][2][0].shape[0]
    groups = tuple((phase, shift, len(arrays)) for phase, shift, arrays in pieces)

    def at(phase, shift):
        def index(j, info, scales):
            return (info[4 + phase] * inner + lax.rem(info[9] + inner - shift, inner), 0, 0)

        return index

    arrays = [array for _, _, group in pieces for array in group]
    accs = [] if acc is None else [acc]
    return pl.pallas_call(
        functools.partial(project_kernel, inner, groups, acc is not None),
        out_shape=jax.ShapeDtypeStruct((tok, width + ROT), F32),
        grid_spec=pltpu.PrefetchScalarGridSpec(
            num_scalar_prefetch=2,
            grid=(1,),
            in_specs=[pl.BlockSpec((1, cols, width), at(phase, shift)) for phase, shift, _ in groups]
            + [pl.BlockSpec((tok, width + ROT), lambda j, info, scales: (0, 0))] * len(accs)
            + [pl.BlockSpec((tok, cols), lambda j, info, scales: (0, 0))] * len(arrays),
            out_specs=pl.BlockSpec((tok, width + ROT), lambda j, info, scales: (0, 0)),
        ),
        cost_estimate=cost(2 * len(groups) * tok * cols * width, len(groups) * cols * (width + tok) * 2),
        compiler_params=params(),
        name="project",
    )(info, scales, *([weight] * len(groups)), *accs, *arrays)


def finish_kernel(features, acc_ref, other_ref, out_ref):
    squares = acc_ref[:, 2 * HD :] + other_ref[:, HD:]
    mean = jnp.sum(squares, axis=1, keepdims=True) * (1.0 / features)
    value = (acc_ref[:, :HD] + other_ref[:, :HD]) * lax.rsqrt(mean + 1e-05)
    out_ref[...] = value.astype(BF16)


def finish(acc, other, features):
    tok = acc.shape[0]
    return pl.pallas_call(
        functools.partial(finish_kernel, features),
        out_shape=jax.ShapeDtypeStruct((tok, HD), BF16),
        in_specs=[vmem()] * 2,
        out_specs=vmem(),
        cost_estimate=cost(4 * tok * HD, 4 * acc.size * 2),
        compiler_params=params(),
        name="finish",
    )(acc, other)


def body(
    size,
    queries,
    cache_keys,
    cache_values,
    query_positions,
    out_weight,
    residual,
    scale_table,
    norm_gain,
    next_query_weight,
):
    inner = size // (2 * OUTER)
    blocks = OUTER * inner
    cols = residual.shape[1]
    index = lax.axis_index("tp").astype(jnp.int32)
    core = lax.rem(index, 2)
    mid = lax.rem(index // 2, inner)
    outer = index // (2 * inner)
    info = jnp.concatenate(
        [
            lax.dynamic_index_in_dim(jnp.asarray(SUM_ORDER), outer, 0, False),
            lax.dynamic_index_in_dim(jnp.asarray(GATHER_ORDER), outer, 0, False),
            jnp.stack([outer, mid, core, index]),
        ]
    )
    had = jnp.asarray(hadamard(ROT), BF16)

    def number(a, b, c):
        return (a * inner + b) * 2 + c

    def permute(value, moves):
        return lax.ppermute(value, "tp", moves)

    def swap_core(value):
        return permute(value, [(i, i ^ 1) for i in range(size)])

    def shift_mid(value, shift, outers=range(OUTER)):
        return permute(
            value,
            [
                (number(a, b, c), number(a, (b + shift) % inner, c))
                for a in outers
                for b in range(inner)
                for c in range(2)
            ],
        )

    def along(value, hops):
        return permute(
            value,
            [(number(f, b, c), number(t, b, c)) for f, t in hops for b in range(inner) for c in range(2)],
        )

    inward = [(0, 1), (3, 2)]
    outward = [(1, 0), (2, 3)]
    middle = [(1, 2), (2, 1)]

    out_other = swap_core(select_cols(info, out_weight, blocks, cols))
    context = attend(queries[0], cache_keys[0], cache_values[0], query_positions)
    context_other = swap_core(context)
    turned_out = turn_out(info, scale_table, out_weight, out_other, had)

    keeps, arrived = [], []
    for phase in range(OUTER):
        keep, *sends = partials(phase, info, context, context_other, turned_out)
        keeps.append(keep)
        arrived.append([shift_mid(send, s + 1) for s, send in enumerate(sends)])
    first = add_up([keeps[0], *arrived[0]])
    end1 = along(first, inward)
    second = add_up([keeps[1], *arrived[1]])
    end2 = along(second, inward)
    mid2 = along(add_up([keeps[0], *arrived[0], end1]), middle)
    mid3 = along(add_up([keeps[1], *arrived[1], end2]), middle)
    swap3 = along(add_up([keeps[2], *arrived[2], mid2]), inward + outward)

    turned_residual = turn_residual(residual, had)
    grid, low = regrid(
        info, scale_table, turned_residual, [keeps[3], *arrived[3], swap3, mid3]
    )

    next_other = swap_core(select_rows(info, next_query_weight, blocks, cols))
    gain = norm_gain.astype(F32).reshape(-1, ROT)
    turned_next = turn_next(info, scale_table, next_query_weight, next_other, gain, had)

    shifts = range(1, inner)
    ends, inners = (0, 3), (1, 2)
    x1 = [shift_mid(grid, s) for s in shifts]
    near = along(grid, inward + outward)
    mid1 = along(grid, middle)
    x2 = [shift_mid(near, s) for s in shifts]
    end2 = along(mid1, outward)
    mid2 = along(near, middle)
    x3 = [(shift_mid(end2, s, ends), shift_mid(mid1, s, inners)) for s in shifts]
    end3 = along(mid2, outward)
    x4 = [(shift_mid(end3, s, ends), shift_mid(mid2, s, inners)) for s in shifts]

    hidden_out = hidden(residual, low, had)
    acc = project(
        info,
        scale_table,
        turned_next,
        None,
        [(0, 0, [grid]), (1, 0, [near])] + [(0, s, [x1[s - 1]]) for s in shifts],
    )
    acc = project(
        info,
        scale_table,
        turned_next,
        acc,
        [(2, 0, [end2, mid1])] + [(1, s, [x2[s - 1]]) for s in shifts],
    )
    acc = project(
        info,
        scale_table,
        turned_next,
        acc,
        [(3, 0, [end3, mid2])] + [(2, s, list(x3[s - 1])) for s in shifts],
    )
    acc = project(info, scale_table, turned_next, acc, [(3, s, list(x4[s - 1])) for s in shifts])
    other = swap_core(acc[:, HD:])
    query_next = finish(acc, other, norm_gain.shape[0])
    return (hidden_out, query_next)


def solution(mesh):
    placed = (
        P("tp", "groups", None),
        P("tp", "groups", None),
        P("tp", "groups", None),
        P("groups"),
        P("tp", None),
        P("groups", "tp"),
        P(),
        P(),
        P(None, "tp"),
    )
    return jax.shard_map(
        functools.partial(body, mesh.shape["tp"]),
        mesh=mesh,
        in_specs=placed,
        out_specs=(P("groups", "tp"), P("groups", "tp")),
        check_vma=False,
    )
```

time: 237 us -> 89.2 us (0.38)
  waiting for transfers between devices: 158 us -> 29.7 us
  matrix products: 38.6 us -> 0 us
  starting transfers between devices: 0.26 us -> 32 us
  Pallas kernels: 0 us -> 21.9 us
  local copies, waits for them, and re-layouts: 23.4 us -> 4.04 us
  between operations: 14.1 us -> 1.05 us
  other arithmetic: 2.4 us -> 0.01 us
    reduce_scatter x1 -> x0, waiting for transfers between devices: 107 us -> none  [body(): lax.psum_scatter(on_grid.astype(jnp.float32), 'tp', scatter_dimension=1,...]
    all_gather x1 -> x0, waiting for transfers between devices: 50.5 us -> none  [body(): gathered = lax.all_gather(regrid, 'tp', axis=1, tiled=True)]
    dot_general x7 -> x0, matrix products: 38.6 us -> none  [the longest x4 21.6 us: rotate(): jnp.einsum('...bi,ij->...bj', blocks, rotation, precision=lax.Precision.H...]
    ppermute x0 -> x24, starting transfers between devices: none -> 32 us  [permute(): return lax.ppermute(value, 'tp', moves)]
    ppermute x0 -> x24, waiting for transfers between devices: none -> 29.7 us  [permute(): return lax.ppermute(value, 'tp', moves)]
    pallas_call x0 -> x22, Pallas kernels: none -> 21.9 us  [the longest x4 3.89 us: partials(): pl.pallas_call(functools.partial(partial_kernel, inner), out_shape=[jax.S...]
    convert_element_type x1 -> x0, local copies, waits for them, and re-layouts: 9.33 us -> none  [body(): on_grid.astype(jnp.float32)]
    reshape x2 -> x0, local copies, waits for them, and re-layouts: 7.16 us -> none  [the longest x1 6.96 us: blockwise(): blocks = values_in.reshape(leading + (block_scale.shape[0], ROT))]
  transfers between devices with their start and end apart: 2 -> 24, of which waited for: 2 -> 12; matrix products, arithmetic and copies ran while one was open for 0% -> 0% of each run, Pallas kernels for 0% -> 22%
where the time goes in v1:
time: 89.2 us; the launch traced here: 88.7 us
  starting transfers between devices  32 us (36%)
  waiting for transfers between devices  29.7 us (33%)
  Pallas kernels  21.9 us (25%)
  local copies, waits for them, and re-layouts  4.04 us (5%)
  between operations  1.05 us (1%)
    ppermute x24, starting transfers between devices, permute(): return lax.ppermute(value, 'tp', moves)  32 us
    ppermute x24, waiting for transfers between devices, permute(): return lax.ppermute(value, 'tp', moves)  29.7 us
    pallas_call x4, Pallas kernels, partials(): pl.pallas_call(functools.partial(partial_kernel, inner), out_shape=[jax.S...  3.89 us
    pallas_call x4, Pallas kernels, project(): pl.pallas_call(functools.partial(project_kernel, inner, groups, acc is no...  3.65 us
    pallas_call x1, Pallas kernels, turn_out(): pl.pallas_call(functools.partial(turn_out_kernel, blocks // OUTER, cols),...  3.41 us
    pallas_call x1, Pallas kernels, attend(): pl.pallas_call(functools.partial(attend_kernel, steps, chunk), out_shape=...  3.31 us
    unnamed x22, local copies, waits for them, and re-layouts  3.24 us
    pallas_call x1, Pallas kernels, turn_next(): pl.pallas_call(functools.partial(turn_next_kernel, cols), out_shape=jax.S...  3 us
  transfers between devices with their start and end apart: 24, of which 12 were waited for; matrix products, arithmetic and copies ran while one was open for 0% of the time, Pallas kernels for 22%

profile of v1, /device:TPU:0, one launch (start us, length us, event | category | flops | bytes accessed | tf_op | source)
XLA Modules:
  0.0 88.7 jit_solution(2567921816587966737)
XLA Ops:
  1.5 2.2 %copy-done = bf16[128,16384]{1,0:T(8,128)(2,1)S(1)} copy-done((bf16[128,16384]{1,0:T(8,128)(2,1)S(1)}, bf16[128,16384]{1,0:T(8,128)(2,1)}, u32[]{:S(2)}) %copy-start) | copy-done | bytes 4194328
  7.4 3.3 %attend.1.own_ref = bf16[128,128]{1,0:T(8,128)(2,1)S(1)} custom-call(bf16[128,128]{1,0:T(8,128)(2,1)S(1)} %bitcast.17, bf16[8192,128]{1,0:T(8,128)(2,1)S(1)} %bitcast.15, bf16[8192,128]{1,0:T(8,128)(2,1)S(1)} %bitcast.16, s32[1,128]{1,0:T(1,128)S(1)} %bitcast.18), custom_call_target="tpu_custom_call" | custom-call | flops 536870912 | bytes 4194304 | tf_op jit(solution)/shard_map/attend/pallas_call | solution.py:142
  11.2 3.4 %turn_out.1.w_ref = bf16[8,2,128,1024]{3,2,1,0:T(8,128)(2,1)S(1)} custom-call(s32[12]{0:T(128)S(1)} %concatenate.3.info.refs_0_, s32[2,128]{1,0:T(2,128)S(1)} %copy-done.7, bf16[128,16384]{1,0:T(8,128)(2,1)S(1)} %copy-done.1, bf16[8,128,1024]{2,1,0:T(8,128)(2,1)S(1)} %collective-permute-done.1.other_ref, bf16[128,128]{1,0:T(8,128)(2,1)S(1)} %copy-done.6), custom_call_target="tpu_custom_call" | custom-call | flops 536870912 | bytes 8388608 | tf_op jit(solution)/shard_map/turn_out/pallas_call | solution.py:173
  14.6 1.0 %partials.6 = (f32[128,1024]{1,0:T(8,128)S(1)}, bf16[128,1024]{1,0:T(8,128)(2,1)S(1)}) custom-call(s32[12]{0:T(128)S(1)} %concatenate.3.info.refs_0_, bf16[128,128]{1,0:T(8,128)(2,1)S(1)} %attend.1.own_ref, bf16[128,128]{1,0:T(8,128)(2,1)S(1)} %collective-permute-done.other_ref, bf16[8,2,128,1024]{3,2,1,0:T(8,128)(2,1)S(1)} %turn_out.1.w_ref), custom_call_target="tpu_custom_call" | custom-call | flops 134217728 | bytes 2097152 | tf_op jit(solution)/shard_map/partials/pallas_call | solution.py:214
  15.6 2.6 %collective-permute-start.4 = (bf16[128,1024]{1,0:T(8,128)(2,1)S(1)}, bf16[128,1024]{1,0:T(8,128)(2,1)S(1)}, u32[]{:S(2)}, u32[]{:S(2)}) collective-permute-start(bf16[128,1024]{1,0:T(8,128)(2,1)S(1)} %get-tuple-element.17), channel_id=1, source_target_pairs={{0,2},{1,3},{2,0},{3,1},{4,6},{5,7},{6,4},{7,5},{8,10},{9,11},{10,... | collective-permute-start | bytes 786440 | tf_op jit(solution)/shard_map/ppermute | solution.py:480
  18.2 1.0 %partials.7 = (f32[128,1024]{1,0:T(8,128)S(1)}, bf16[128,1024]{1,0:T(8,128)(2,1)S(1)}) custom-call(s32[12]{0:T(128)S(1)} %concatenate.3.info.refs_0_, bf16[128,128]{1,0:T(8,128)(2,1)S(1)} %attend.1.own_ref, bf16[128,128]{1,0:T(8,128)(2,1)S(1)} %collective-permute-done.other_ref, bf16[8,2,128,1024]{3,2,1,0:T(8,128)(2,1)S(1)} %turn_out.1.w_ref), custom_call_target="tpu_custom_call" | custom-call | flops 134217728 | bytes 2097152 | tf_op jit(solution)/shard_map/partials/pallas_call | solution.py:214
  19.3 6.1 %collective-permute-done.4.refs_1_ = bf16[128,1024]{1,0:T(8,128)(2,1)S(1)} collective-permute-done((bf16[128,1024]{1,0:T(8,128)(2,1)S(1)}, bf16[128,1024]{1,0:T(8,128)(2,1)S(1)}, u32[]{:S(2)}, u32[]{:S(2)}) %collective-permute-start.4) | collective-permute-done | bytes 262176 | tf_op jit(solution)/shard_map/ppermute | solution.py:480
  25.4 3.9 %collective-permute-start.5 = (bf16[128,1024]{1,0:T(8,128)(2,1)S(1)}, bf16[128,1024]{1,0:T(8,128)(2,1)S(1)}, u32[]{:S(2)}, u32[]{:S(2)}) collective-permute-start(bf16[128,1024]{1,0:T(8,128)(2,1)S(1)} %add_up.5), channel_id=1, source_target_pairs={{0,4},{1,5},{2,6},{3,7},{12,8},{13,9},{14,10},{15,11},{16,20},{17,... | collective-permute-start | bytes 786440 | tf_op jit(solution)/shard_map/ppermute | solution.py:480
  29.4 1.0 %partials.5 = (f32[128,1024]{1,0:T(8,128)S(1)}, bf16[128,1024]{1,0:T(8,128)(2,1)S(1)}) custom-call(s32[12]{0:T(128)S(1)} %concatenate.3.info.refs_0_, bf16[128,128]{1,0:T(8,128)(2,1)S(1)} %attend.1.own_ref, bf16[128,128]{1,0:T(8,128)(2,1)S(1)} %collective-permute-done.other_ref, bf16[8,2,128,1024]{3,2,1,0:T(8,128)(2,1)S(1)} %turn_out.1.w_ref), custom_call_target="tpu_custom_call" | custom-call | flops 134217728 | bytes 2097152 | tf_op jit(solution)/shard_map/partials/pallas_call | solution.py:214
  30.8 3.7 %collective-permute-start.9 = (bf16[128,1024]{1,0:T(8,128)(2,1)S(1)}, bf16[128,1024]{1,0:T(8,128)(2,1)S(1)}, u32[]{:S(2)}, u32[]{:S(2)}) collective-permute-start(bf16[128,1024]{1,0:T(8,128)(2,1)S(1)} %add_up.8), channel_id=1, source_target_pairs={{0,4},{1,5},{2,6},{3,7},{12,8},{13,9},{14,10},{15,11},{16,20},{17,... | collective-permute-start | bytes 786440 | tf_op jit(solution)/shard_map/ppermute | solution.py:480
  34.6 1.6 %collective-permute-start.3 = (bf16[128,1024]{1,0:T(8,128)(2,1)S(1)}, bf16[128,1024]{1,0:T(8,128)(2,1)S(1)}, u32[]{:S(2)}, u32[]{:S(2)}) collective-permute-start(bf16[128,1024]{1,0:T(8,128)(2,1)S(1)} %get-tuple-element.15), channel_id=1, source_target_pairs={{0,2},{1,3},{2,0},{3,1},{4,6},{5,7},{6,4},{7,5},{8,10},{9,11},{10,... | collective-permute-start | bytes 786440 | tf_op jit(solution)/shard_map/ppermute | solution.py:480
  36.9 1.0 %partials.4 = (f32[128,1024]{1,0:T(8,128)S(1)}, bf16[128,1024]{1,0:T(8,128)(2,1)S(1)}) custom-call(s32[12]{0:T(128)S(1)} %concatenate.3.info.refs_0_, bf16[128,128]{1,0:T(8,128)(2,1)S(1)} %attend.1.own_ref, bf16[128,128]{1,0:T(8,128)(2,1)S(1)} %collective-permute-done.other_ref, bf16[8,2,128,1024]{3,2,1,0:T(8,128)(2,1)S(1)} %turn_out.1.w_ref), custom_call_target="tpu_custom_call" | custom-call | flops 134217728 | bytes 2097152 | tf_op jit(solution)/shard_map/partials/pallas_call | solution.py:214
  38.5 1.5 %collective-permute-done.9.refs_2_ = bf16[128,1024]{1,0:T(8,128)(2,1)S(1)} collective-permute-done((bf16[128,1024]{1,0:T(8,128)(2,1)S(1)}, bf16[128,1024]{1,0:T(8,128)(2,1)S(1)}, u32[]{:S(2)}, u32[]{:S(2)}) %collective-permute-start.9) | collective-permute-done | bytes 262176 | tf_op jit(solution)/shard_map/ppermute | solution.py:480
  40.8 3.1 %collective-permute-done.3.refs_1_ = bf16[128,1024]{1,0:T(8,128)(2,1)S(1)} collective-permute-done((bf16[128,1024]{1,0:T(8,128)(2,1)S(1)}, bf16[128,1024]{1,0:T(8,128)(2,1)S(1)}, u32[]{:S(2)}, u32[]{:S(2)}) %collective-permute-start.3) | collective-permute-done | bytes 262176 | tf_op jit(solution)/shard_map/ppermute | solution.py:480
  44.0 2.3 %collective-permute-start.7 = (bf16[128,1024]{1,0:T(8,128)(2,1)S(1)}, bf16[128,1024]{1,0:T(8,128)(2,1)S(1)}, u32[]{:S(2)}, u32[]{:S(2)}) collective-permute-start(bf16[128,1024]{1,0:T(8,128)(2,1)S(1)} %add_up.7), channel_id=1, source_target_pairs={{0,4},{1,5},{2,6},{3,7},{12,8},{13,9},{14,10},{15,11},{4,0},{5,1},... | collective-permute-start | bytes 786440 | tf_op jit(solution)/shard_map/ppermute | solution.py:480
  46.4 1.4 %collective-permute-done.2.refs_4_ = bf16[128,1024]{1,0:T(8,128)(2,1)S(1)} collective-permute-done((bf16[128,1024]{1,0:T(8,128)(2,1)S(1)}, bf16[128,1024]{1,0:T(8,128)(2,1)S(1)}, u32[]{:S(2)}, u32[]{:S(2)}) %collective-permute-start.2) | collective-permute-done | bytes 262176 | tf_op jit(solution)/shard_map/ppermute | solution.py:480
  47.9 3.3 %collective-permute-done.7.refs_5_ = bf16[128,1024]{1,0:T(8,128)(2,1)S(1)} collective-permute-done((bf16[128,1024]{1,0:T(8,128)(2,1)S(1)}, bf16[128,1024]{1,0:T(8,128)(2,1)S(1)}, u32[]{:S(2)}, u32[]{:S(2)}) %collective-permute-start.7) | collective-permute-done | bytes 262176 | tf_op jit(solution)/shard_map/ppermute | solution.py:480
  52.0 1.8 %collective-permute-start.12 = (bf16[128,1024]{1,0:T(8,128)(2,1)S(1)}, bf16[128,1024]{1,0:T(8,128)(2,1)S(1)}, u32[]{:S(2)}, u32[]{:S(2)}) collective-permute-start(bf16[128,1024]{1,0:T(8,128)(2,1)S(1)} %get-tuple-element.21.refs_5_), channel_id=1, source_target_pairs={{0,4},{1,5},{2,6},{3,7},{12,8},{13,9},{14,10},{15,11},{4,0},{5,1},... | collective-permute-start | bytes 786440 | tf_op jit(solution)/shard_map/ppermute | solution.py:480
  54.5 4.0 %collective-permute-done.12.refs_6_ = bf16[128,1024]{1,0:T(8,128)(2,1)S(1)} collective-permute-done((bf16[128,1024]{1,0:T(8,128)(2,1)S(1)}, bf16[128,1024]{1,0:T(8,128)(2,1)S(1)}, u32[]{:S(2)}, u32[]{:S(2)}) %collective-permute-start.12) | collective-permute-done | bytes 262176 | tf_op jit(solution)/shard_map/ppermute | solution.py:480
  59.2 1.6 %collective-permute-start.13 = (bf16[128,1024]{1,0:T(8,128)(2,1)S(1)}, bf16[128,1024]{1,0:T(8,128)(2,1)S(1)}, u32[]{:S(2)}, u32[]{:S(2)}) collective-permute-start(bf16[128,1024]{1,0:T(8,128)(2,1)S(1)} %get-tuple-element.21.refs_5_), channel_id=1, source_target_pairs={{0,2},{1,3},{2,0},{3,1},{4,6},{5,7},{6,4},{7,5},{8,10},{9,11},{10,... | collective-permute-start | bytes 786440 | tf_op jit(solution)/shard_map/ppermute | solution.py:480
  60.7 1.3 %collective-permute-start.15 = (bf16[128,1024]{1,0:T(8,128)(2,1)S(1)}, bf16[128,1024]{1,0:T(8,128)(2,1)S(1)}, u32[]{:S(2)}, u32[]{:S(2)}) collective-permute-start(bf16[128,1024]{1,0:T(8,128)(2,1)S(1)} %collective-permute-done.14.refs_6_), channel_id=1, source_target_pairs={{4,0},{5,1},{6,2},{7,3},{8,12},{9,13},{10,14},{11,15},{20,16},{21,... | collective-permute-start | bytes 786440 | tf_op jit(solution)/shard_map/ppermute | solution.py:480
  62.0 1.3 %collective-permute-start.18 = (bf16[128,1024]{1,0:T(8,128)(2,1)S(1)}, bf16[128,1024]{1,0:T(8,128)(2,1)S(1)}, u32[]{:S(2)}, u32[]{:S(2)}) collective-permute-start(bf16[128,1024]{1,0:T(8,128)(2,1)S(1)} %collective-permute-done.17.refs_6_), channel_id=1, source_target_pairs={{4,0},{5,1},{6,2},{7,3},{8,12},{9,13},{10,14},{11,15},{20,16},{21,... | collective-permute-start | bytes 786440 | tf_op jit(solution)/shard_map/ppermute | solution.py:480
  64.6 3.5 %collective-permute-done.13.refs_7_ = bf16[128,1024]{1,0:T(8,128)(2,1)S(1)} collective-permute-done((bf16[128,1024]{1,0:T(8,128)(2,1)S(1)}, bf16[128,1024]{1,0:T(8,128)(2,1)S(1)}, u32[]{:S(2)}, u32[]{:S(2)}) %collective-permute-start.13) | collective-permute-done | bytes 262176 | tf_op jit(solution)/shard_map/ppermute | solution.py:480
  68.7 3.8 %collective-permute-done.15.refs_5_ = bf16[128,1024]{1,0:T(8,128)(2,1)S(1)} collective-permute-done((bf16[128,1024]{1,0:T(8,128)(2,1)S(1)}, bf16[128,1024]{1,0:T(8,128)(2,1)S(1)}, u32[]{:S(2)}, u32[]{:S(2)}) %collective-permute-start.15) | collective-permute-done | bytes 262176 | tf_op jit(solution)/shard_map/ppermute | solution.py:480
  72.5 2.1 %collective-permute-start.19 = (bf16[128,1024]{1,0:T(8,128)(2,1)S(1)}, bf16[128,1024]{1,0:T(8,128)(2,1)S(1)}, u32[]{:S(2)}, u32[]{:S(2)}) collective-permute-start(bf16[128,1024]{1,0:T(8,128)(2,1)S(1)} %collective-permute-done.15.refs_5_), channel_id=1, source_target_pairs={{0,2},{1,3},{2,0},{3,1},{12,14},{13,15},{14,12},{15,13},{16,18},{1... | collective-permute-start | bytes 786440 | tf_op jit(solution)/shard_map/ppermute | solution.py:480
  75.5 2.9 %collective-permute-start.21 = (bf16[128,1024]{1,0:T(8,128)(2,1)S(1)}, bf16[128,1024]{1,0:T(8,128)(2,1)S(1)}, u32[]{:S(2)}, u32[]{:S(2)}) collective-permute-start(bf16[128,1024]{1,0:T(8,128)(2,1)S(1)} %collective-permute-done.18.refs_5_), channel_id=1, source_target_pairs={{0,2},{1,3},{2,0},{3,1},{12,14},{13,15},{14,12},{15,13},{16,18},{1... | collective-permute-start | bytes 786440 | tf_op jit(solution)/shard_map/ppermute | solution.py:480
  78.4 3.0 %turn_next.1.refs_2_.refs_3_.refs_4_ = bf16[8,1024,256]{2,1,0:T(8,128)(2,1)S(1)} custom-call(s32[12]{0:T(128)S(1)} %concatenate.3.info.refs_0_, s32[2,128]{1,0:T(2,128)S(1)} %copy-done.7, bf16[16384,128]{1,0:T(8,128)(2,1)S(1)} %copy-done.2, bf16[8,1024,128]{2,1,0:T(8,128)(2,1)S(1)} %collective-permute-done.11.other_ref, ...), custom_call_target="tpu_custom_call" | custom-call | flops 536870912 | bytes 8388608 | tf_op jit(solution)/shard_map/turn_next/pallas_call | solution.py:346
  81.4 1.0 %project.4.refs_4_ = f32[128,384]{1,0:T(8,128)S(1)} custom-call(s32[12]{0:T(128)S(1)} %concatenate.3.info.refs_0_, s32[2,128]{1,0:T(2,128)S(1)} %copy-done.7, bf16[8,1024,256]{2,1,0:T(8,128)(2,1)S(1)} %turn_next.1.refs_2_.refs_3_.refs_4_, bf16[8,1024,256]{2,1,0:T(8,128)(2,1)S(1)} %turn_next.1.refs_2_.refs_3_.refs_4_, ...), custom_call_target="tpu_custom_call" | custom-call | flops 201326592 | bytes 2359296 | tf_op jit(solution)/shard_map/project/pallas_call | solution.py:411
  82.5 0.9 %project.5.refs_4_ = f32[128,384]{1,0:T(8,128)S(1)} custom-call(s32[12]{0:T(128)S(1)} %concatenate.3.info.refs_0_, s32[2,128]{1,0:T(2,128)S(1)} %copy-done.7, bf16[8,1024,256]{2,1,0:T(8,128)(2,1)S(1)} %turn_next.1.refs_2_.refs_3_.refs_4_, bf16[8,1024,256]{2,1,0:T(8,128)(2,1)S(1)} %turn_next.1.refs_2_.refs_3_.refs_4_, f32[128,384]{1,0:T(8,128)S(1)} %project.4.refs_4_, ...), custom_call_target="tpu_custom_call" | custom-call | flops 134217728 | bytes 1572864 | tf_op jit(solution)/shard_map/project/pallas_call | solution.py:411
  83.4 0.9 %project.6.refs_3_ = f32[128,384]{1,0:T(8,128)S(1)} custom-call(s32[12]{0:T(128)S(1)} %concatenate.3.info.refs_0_, s32[2,128]{1,0:T(2,128)S(1)} %copy-done.7, bf16[8,1024,256]{2,1,0:T(8,128)(2,1)S(1)} %turn_next.1.refs_2_.refs_3_.refs_4_, bf16[8,1024,256]{2,1,0:T(8,128)(2,1)S(1)} %turn_next.1.refs_2_.refs_3_.refs_4_, f32[128,384]{1,0:T(8,128)S(1)} %project.5.refs_4_, ...), custom_call_target="tpu_custom_call" | custom-call | flops 134217728 | bytes 1572864 | tf_op jit(solution)/shard_map/project/pallas_call | solution.py:411
  84.3 1.5 %collective-permute-done.21.refs_4_ = bf16[128,1024]{1,0:T(8,128)(2,1)S(1)} collective-permute-done((bf16[128,1024]{1,0:T(8,128)(2,1)S(1)}, bf16[128,1024]{1,0:T(8,128)(2,1)S(1)}, u32[]{:S(2)}, u32[]{:S(2)}) %collective-permute-start.21) | collective-permute-done | bytes 262176 | tf_op jit(solution)/shard_map/ppermute | solution.py:480
  86.7 1.0 %hidden.1 = bf16[128,1024]{1,0:T(8,128)(2,1)} custom-call(bf16[128,1024]{1,0:T(8,128)(2,1)S(1)} %copy-done.5, f32[128,1024]{1,0:T(8,128)S(1)} %get-tuple-element.20.low_ref, bf16[128,128]{1,0:T(8,128)(2,1)S(1)} %copy-done.6), custom_call_target="tpu_custom_call" | custom-call | flops 67108864 | bytes 1048576 | tf_op jit(solution)/shard_map/hidden/pallas_call | solution.py:320
  (64 shorter events, 14.9 us)
Async XLA Ops:
  4.5 2.9 %copy-start.4 = (bf16[1,8192,128]{2,1,0:T(8,128)(2,1)S(1)}, bf16[1,8192,128]{2,1,0:T(8,128)(2,1)}, u32[]{:S(2)}) copy-start(bf16[1,8192,128]{2,1,0:T(8,128)(2,1)} %param.14) | copy-start | bytes 6291460
  4.5 2.9 %copy-start.8 = (bf16[1,128,128]{2,1,0:T(8,128)(2,1)S(1)}, bf16[1,128,128]{2,1,0:T(8,128)(2,1)}, u32[]{:S(2)}) copy-start(bf16[1,128,128]{2,1,0:T(8,128)(2,1)} %param.12) | copy-start | bytes 98308
  4.5 2.8 %copy-start.9 = (s32[128]{0:T(128)S(1)}, s32[128]{0:T(128)}, u32[]{:S(2)}) copy-start(s32[128]{0:T(128)} %param.15) | copy-start | bytes 1540
  4.5 6.7 %collective-permute-start.1 = (bf16[8,128,1024]{2,1,0:T(8,128)(2,1)S(1)}, bf16[8,128,1024]{2,1,0:T(8,128)(2,1)S(1)}, u32[]{:S(2)}, u32[]{:S(2)}) collective-permute-start(bf16[8,128,1024]{2,1,0:T(8,128)(2,1)S(1)} %select_cols.1), channel_id=1, source_target_pairs={{0,1},{1,0},{2,3},{3,2},{4,5},{5,4},{6,7},{7,6},{8,9},{9,8},{10,11... | collective-permute-start | bytes 6291464 | tf_op jit(solution)/shard_map/ppermute | solution.py:480
  6.6 57.3 %collective-permute-start.11 = (bf16[8,1024,128]{2,1,0:T(8,128)(2,1)S(1)}, bf16[8,1024,128]{2,1,0:T(8,128)(2,1)S(1)}, u32[]{:S(2)}, u32[]{:S(2)}) collective-permute-start(bf16[8,1024,128]{2,1,0:T(8,128)(2,1)S(1)} %select_rows.1), channel_id=1, source_target_pairs={{0,1},{1,0},{2,3},{3,2},{4,5},{5,4},{6,7},{7,6},{8,9},{9,8},{10,11... | collective-permute-start | bytes 6291464 | tf_op jit(solution)/shard_map/ppermute | solution.py:480
  7.3 3.9 %copy-start.1 = (bf16[128,16384]{1,0:T(8,128)(2,1)S(1)}, bf16[128,16384]{1,0:T(8,128)(2,1)}, u32[]{:S(2)}) copy-start(bf16[128,16384]{1,0:T(8,128)(2,1)} %own_ref.2) | copy-start | bytes 12582916
  7.3 3.9 %copy-start.6 = (bf16[128,128]{1,0:T(8,128)(2,1)S(1)}, bf16[128,128]{1,0:T(8,128)(2,1)}, u32[]{:S(2)}) copy-start(bf16[128,128]{1,0:T(8,128)(2,1)} %constant.46.clone.h_ref) | copy-start | bytes 98308
  7.3 3.9 %copy-start.7 = (s32[2,128]{1,0:T(2,128)S(1)}, s32[2,128]{1,0:T(2,128)}, u32[]{:S(2)}) copy-start(s32[2,128]{1,0:T(2,128)} %refs_1_.9) | copy-start | bytes 3076
  10.7 4.0 %collective-permute-start = (bf16[128,128]{1,0:T(8,128)(2,1)S(1)}, bf16[128,128]{1,0:T(8,128)(2,1)S(1)}, u32[]{:S(2)}, u32[]{:S(2)}) collective-permute-start(bf16[128,128]{1,0:T(8,128)(2,1)S(1)} %attend.1.own_ref), channel_id=1, source_target_pairs={{0,1},{1,0},{2,3},{3,2},{4,5},{5,4},{6,7},{7,6},{8,9},{9,8},{10,11... | collective-permute-start | bytes 98312 | tf_op jit(solution)/shard_map/ppermute | solution.py:480
  15.6 9.7 %collective-permute-start.4 = (bf16[128,1024]{1,0:T(8,128)(2,1)S(1)}, bf16[128,1024]{1,0:T(8,128)(2,1)S(1)}, u32[]{:S(2)}, u32[]{:S(2)}) collective-permute-start(bf16[128,1024]{1,0:T(8,128)(2,1)S(1)} %get-tuple-element.17), channel_id=1, source_target_pairs={{0,2},{1,3},{2,0},{3,1},{4,6},{5,7},{6,4},{7,5},{8,10},{9,11},{10,... | collective-permute-start | bytes 786440 | tf_op jit(solution)/shard_map/ppermute | solution.py:480
  19.2 11.6 %collective-permute-start.8 = (bf16[128,1024]{1,0:T(8,128)(2,1)S(1)}, bf16[128,1024]{1,0:T(8,128)(2,1)S(1)}, u32[]{:S(2)}, u32[]{:S(2)}) collective-permute-start(bf16[128,1024]{1,0:T(8,128)(2,1)S(1)} %get-tuple-element.19), channel_id=1, source_target_pairs={{0,2},{1,3},{2,0},{3,1},{4,6},{5,7},{6,4},{7,5},{8,10},{9,11},{10,... | collective-permute-start | bytes 786440 | tf_op jit(solution)/shard_map/ppermute | solution.py:480
  25.4 10.7 %collective-permute-start.5 = (bf16[128,1024]{1,0:T(8,128)(2,1)S(1)}, bf16[128,1024]{1,0:T(8,128)(2,1)S(1)}, u32[]{:S(2)}, u32[]{:S(2)}) collective-permute-start(bf16[128,1024]{1,0:T(8,128)(2,1)S(1)} %add_up.5), channel_id=1, source_target_pairs={{0,4},{1,5},{2,6},{3,7},{12,8},{13,9},{14,10},{15,11},{16,20},{17,... | collective-permute-start | bytes 786440 | tf_op jit(solution)/shard_map/ppermute | solution.py:480
  30.8 9.1 %collective-permute-start.9 = (bf16[128,1024]{1,0:T(8,128)(2,1)S(1)}, bf16[128,1024]{1,0:T(8,128)(2,1)S(1)}, u32[]{:S(2)}, u32[]{:S(2)}) collective-permute-start(bf16[128,1024]{1,0:T(8,128)(2,1)S(1)} %add_up.8), channel_id=1, source_target_pairs={{0,4},{1,5},{2,6},{3,7},{12,8},{13,9},{14,10},{15,11},{16,20},{17,... | collective-permute-start | bytes 786440 | tf_op jit(solution)/shard_map/ppermute | solution.py:480
  34.6 9.3 %collective-permute-start.3 = (bf16[128,1024]{1,0:T(8,128)(2,1)S(1)}, bf16[128,1024]{1,0:T(8,128)(2,1)S(1)}, u32[]{:S(2)}, u32[]{:S(2)}) collective-permute-start(bf16[128,1024]{1,0:T(8,128)(2,1)S(1)} %get-tuple-element.15), channel_id=1, source_target_pairs={{0,2},{1,3},{2,0},{3,1},{4,6},{5,7},{6,4},{7,5},{8,10},{9,11},{10,... | collective-permute-start | bytes 786440 | tf_op jit(solution)/shard_map/ppermute | solution.py:480
  36.2 7.7 %collective-permute-start.6 = (bf16[128,1024]{1,0:T(8,128)(2,1)S(1)}, bf16[128,1024]{1,0:T(8,128)(2,1)S(1)}, u32[]{:S(2)}, u32[]{:S(2)}) collective-permute-start(bf16[128,1024]{1,0:T(8,128)(2,1)S(1)} %add_up.6), channel_id=1, source_target_pairs={{4,8},{5,9},{6,10},{7,11},{8,4},{9,5},{10,6},{11,7},{20,24},{21,25... | collective-permute-start | bytes 786440 | tf_op jit(solution)/shard_map/ppermute | solution.py:480
  37.9 8.3 %copy-start.5 = (bf16[128,1024]{1,0:T(8,128)(2,1)S(1)}, bf16[128,1024]{1,0:T(8,128)(2,1)}, u32[]{:S(2)}) copy-start(bf16[128,1024]{1,0:T(8,128)(2,1)} %res_ref.3) | copy-start | bytes 786436
  37.9 10.0 %collective-permute-start.2 = (bf16[128,1024]{1,0:T(8,128)(2,1)S(1)}, bf16[128,1024]{1,0:T(8,128)(2,1)S(1)}, u32[]{:S(2)}, u32[]{:S(2)}) collective-permute-start(bf16[128,1024]{1,0:T(8,128)(2,1)S(1)} %get-tuple-element.13), channel_id=1, source_target_pairs={{0,2},{1,3},{2,0},{3,1},{4,6},{5,7},{6,4},{7,5},{8,10},{9,11},{10,... | collective-permute-start | bytes 786440 | tf_op jit(solution)/shard_map/ppermute | solution.py:480
  40.1 38.3 %copy-start.10 = (bf16[16384]{0:T(1024)(128)(2,1)S(1)}, bf16[16384]{0:T(1024)(128)(2,1)}, u32[]{:S(2)}) copy-start(bf16[16384]{0:T(1024)(128)(2,1)} %param.19) | copy-start | bytes 98308
  40.1 7.8 %collective-permute-start.10 = (bf16[128,1024]{1,0:T(8,128)(2,1)S(1)}, bf16[128,1024]{1,0:T(8,128)(2,1)S(1)}, u32[]{:S(2)}, u32[]{:S(2)}) collective-permute-start(bf16[128,1024]{1,0:T(8,128)(2,1)S(1)} %add_up.9), channel_id=1, source_target_pairs={{4,8},{5,9},{6,10},{7,11},{8,4},{9,5},{10,6},{11,7},{20,24},{21,25... | collective-permute-start | bytes 786440 | tf_op jit(solution)/shard_map/ppermute | solution.py:480
  44.0 7.3 %collective-permute-start.7 = (bf16[128,1024]{1,0:T(8,128)(2,1)S(1)}, bf16[128,1024]{1,0:T(8,128)(2,1)S(1)}, u32[]{:S(2)}, u32[]{:S(2)}) collective-permute-start(bf16[128,1024]{1,0:T(8,128)(2,1)S(1)} %add_up.7), channel_id=1, source_target_pairs={{0,4},{1,5},{2,6},{3,7},{12,8},{13,9},{14,10},{15,11},{4,0},{5,1},... | collective-permute-start | bytes 786440 | tf_op jit(solution)/shard_map/ppermute | solution.py:480
  52.0 6.4 %collective-permute-start.12 = (bf16[128,1024]{1,0:T(8,128)(2,1)S(1)}, bf16[128,1024]{1,0:T(8,128)(2,1)S(1)}, u32[]{:S(2)}, u32[]{:S(2)}) collective-permute-start(bf16[128,1024]{1,0:T(8,128)(2,1)S(1)} %get-tuple-element.21.refs_5_), channel_id=1, source_target_pairs={{0,4},{1,5},{2,6},{3,7},{12,8},{13,9},{14,10},{15,11},{4,0},{5,1},... | collective-permute-start | bytes 786440 | tf_op jit(solution)/shard_map/ppermute | solution.py:480
  53.9 6.9 %collective-permute-start.14 = (bf16[128,1024]{1,0:T(8,128)(2,1)S(1)}, bf16[128,1024]{1,0:T(8,128)(2,1)S(1)}, u32[]{:S(2)}, u32[]{:S(2)}) collective-permute-start(bf16[128,1024]{1,0:T(8,128)(2,1)S(1)} %get-tuple-element.21.refs_5_), channel_id=1, source_target_pairs={{4,8},{5,9},{6,10},{7,11},{8,4},{9,5},{10,6},{11,7},{20,24},{21,25... | collective-permute-start | bytes 786440 | tf_op jit(solution)/shard_map/ppermute | solution.py:480
  58.5 3.5 %collective-permute-start.17 = (bf16[128,1024]{1,0:T(8,128)(2,1)S(1)}, bf16[128,1024]{1,0:T(8,128)(2,1)S(1)}, u32[]{:S(2)}, u32[]{:S(2)}) collective-permute-start(bf16[128,1024]{1,0:T(8,128)(2,1)S(1)} %collective-permute-done.12.refs_6_), channel_id=1, source_target_pairs={{4,8},{5,9},{6,10},{7,11},{8,4},{9,5},{10,6},{11,7},{20,24},{21,25... | collective-permute-start | bytes 786440 | tf_op jit(solution)/shard_map/ppermute | solution.py:480
  59.2 8.9 %collective-permute-start.13 = (bf16[128,1024]{1,0:T(8,128)(2,1)S(1)}, bf16[128,1024]{1,0:T(8,128)(2,1)S(1)}, u32[]{:S(2)}, u32[]{:S(2)}) collective-permute-start(bf16[128,1024]{1,0:T(8,128)(2,1)S(1)} %get-tuple-element.21.refs_5_), channel_id=1, source_target_pairs={{0,2},{1,3},{2,0},{3,1},{4,6},{5,7},{6,4},{7,5},{8,10},{9,11},{10,... | collective-permute-start | bytes 786440 | tf_op jit(solution)/shard_map/ppermute | solution.py:480
  60.7 11.8 %collective-permute-start.15 = (bf16[128,1024]{1,0:T(8,128)(2,1)S(1)}, bf16[128,1024]{1,0:T(8,128)(2,1)S(1)}, u32[]{:S(2)}, u32[]{:S(2)}) collective-permute-start(bf16[128,1024]{1,0:T(8,128)(2,1)S(1)} %collective-permute-done.14.refs_6_), channel_id=1, source_target_pairs={{4,0},{5,1},{6,2},{7,3},{8,12},{9,13},{10,14},{11,15},{20,16},{21,... | collective-permute-start | bytes 786440 | tf_op jit(solution)/shard_map/ppermute | solution.py:480
  62.0 13.4 %collective-permute-start.18 = (bf16[128,1024]{1,0:T(8,128)(2,1)S(1)}, bf16[128,1024]{1,0:T(8,128)(2,1)S(1)}, u32[]{:S(2)}, u32[]{:S(2)}) collective-permute-start(bf16[128,1024]{1,0:T(8,128)(2,1)S(1)} %collective-permute-done.17.refs_6_), channel_id=1, source_target_pairs={{4,0},{5,1},{6,2},{7,3},{8,12},{9,13},{10,14},{11,15},{20,16},{21,... | collective-permute-start | bytes 786440 | tf_op jit(solution)/shard_map/ppermute | solution.py:480
  63.3 19.1 %collective-permute-start.16 = (bf16[128,1024]{1,0:T(8,128)(2,1)S(1)}, bf16[128,1024]{1,0:T(8,128)(2,1)S(1)}, u32[]{:S(2)}, u32[]{:S(2)}) collective-permute-start(bf16[128,1024]{1,0:T(8,128)(2,1)S(1)} %collective-permute-done.12.refs_6_), channel_id=1, source_target_pairs={{0,2},{1,3},{2,0},{3,1},{4,6},{5,7},{6,4},{7,5},{8,10},{9,11},{10,... | collective-permute-start | bytes 786440 | tf_op jit(solution)/shard_map/ppermute | solution.py:480
  63.9 19.4 %collective-permute-start.20 = (bf16[128,1024]{1,0:T(8,128)(2,1)S(1)}, bf16[128,1024]{1,0:T(8,128)(2,1)S(1)}, u32[]{:S(2)}, u32[]{:S(2)}) collective-permute-start(bf16[128,1024]{1,0:T(8,128)(2,1)S(1)} %collective-permute-done.14.refs_6_), channel_id=1, source_target_pairs={{4,6},{5,7},{6,4},{7,5},{8,10},{9,11},{10,8},{11,9},{20,22},{21,23... | collective-permute-start | bytes 786440 | tf_op jit(solution)/shard_map/ppermute | solution.py:480
  68.1 16.3 %collective-permute-start.22 = (bf16[128,1024]{1,0:T(8,128)(2,1)S(1)}, bf16[128,1024]{1,0:T(8,128)(2,1)S(1)}, u32[]{:S(2)}, u32[]{:S(2)}) collective-permute-start(bf16[128,1024]{1,0:T(8,128)(2,1)S(1)} %collective-permute-done.17.refs_6_), channel_id=1, source_target_pairs={{4,6},{5,7},{6,4},{7,5},{8,10},{9,11},{10,8},{11,9},{20,22},{21,23... | collective-permute-start | bytes 786440 | tf_op jit(solution)/shard_map/ppermute | solution.py:480
  72.5 10.9 %collective-permute-start.19 = (bf16[128,1024]{1,0:T(8,128)(2,1)S(1)}, bf16[128,1024]{1,0:T(8,128)(2,1)S(1)}, u32[]{:S(2)}, u32[]{:S(2)}) collective-permute-start(bf16[128,1024]{1,0:T(8,128)(2,1)S(1)} %collective-permute-done.15.refs_5_), channel_id=1, source_target_pairs={{0,2},{1,3},{2,0},{3,1},{12,14},{13,15},{14,12},{15,13},{16,18},{1... | collective-permute-start | bytes 786440 | tf_op jit(solution)/shard_map/ppermute | solution.py:480
  75.5 10.3 %collective-permute-start.21 = (bf16[128,1024]{1,0:T(8,128)(2,1)S(1)}, bf16[128,1024]{1,0:T(8,128)(2,1)S(1)}, u32[]{:S(2)}, u32[]{:S(2)}) collective-permute-start(bf16[128,1024]{1,0:T(8,128)(2,1)S(1)} %collective-permute-done.18.refs_5_), channel_id=1, source_target_pairs={{0,2},{1,3},{2,0},{3,1},{12,14},{13,15},{14,12},{15,13},{16,18},{1... | collective-permute-start | bytes 786440 | tf_op jit(solution)/shard_map/ppermute | solution.py:480
  86.6 1.4 %collective-permute-start.23 = (f32[128,256]{1,0:T(8,128)S(1)}, f32[128,256]{1,0:T(8,128)S(1)}, u32[]{:S(2)}, u32[]{:S(2)}) collective-permute-start(f32[128,256]{1,0:T(8,128)S(1)} %slice.4), channel_id=1, source_target_pairs={{0,1},{1,0},{2,3},{3,2},{4,5},{5,4},{6,7},{7,6},{8,9},{9,8},{10,11... | collective-permute-start | bytes 393224 | tf_op jit(solution)/shard_map/ppermute | solution.py:480
  (3 other events, 7.1 us)

commit v2 on v0

v2 whole, which is shorter than its diff:
```python
import functools
import math

import jax
import jax.numpy as jnp
import numpy as np
from jax import lax
from jax.experimental import pallas as pl
from jax.experimental.pallas import tpu as pltpu
from jax.sharding import PartitionSpec as P

HD = 128
ROT = 128
OUTER = 4

F32 = jnp.float32
BF16 = jnp.bfloat16
MIB = 1024 * 1024


def hadamard(length):
    rows = np.arange(length)
    common = rows[:, None] & rows[None, :]
    parity = np.zeros((length, length), np.int64)
    for bit in range(length.bit_length()):
        parity += (common >> bit) & 1
    return (1 - 2 * (parity & 1)).astype(np.float32)


def vmem():
    return pl.BlockSpec(memory_space=pltpu.VMEM)


def anywhere():
    return pl.BlockSpec(memory_space=pl.ANY)


def place(inner):
    index = lax.axis_index("tp")
    return lax.div(index, 2 * inner), lax.rem(lax.div(index, 2), inner), lax.rem(index, 2)


def targets(outer):
    low = outer < 2
    near = outer + 1 - 2 * lax.rem(outer, 2)
    return jnp.where(low, 3, 0), jnp.where(low, 2, 1), near, outer


def is_inner(outer):
    return jnp.logical_or(outer == 1, outer == 2)


def kernel_call(kernel, out_shape, arrays, specs, after=(), scratch=(), flops=0, nbytes=0, exps=0, limit=24, name=None):
    count, extra = len(arrays), len(after)

    def ordered(*refs):
        kernel(*refs[:count], *refs[count + extra :])

    return pl.pallas_call(
        ordered,
        out_shape=out_shape,
        in_specs=list(specs) + [anywhere()] * extra,
        out_specs=jax.tree.map(lambda _: vmem(), out_shape),
        scratch_shapes=list(scratch),
        cost_estimate=pl.CostEstimate(
            flops=int(flops), bytes_accessed=int(nbytes), transcendentals=int(exps)
        ),
        compiler_params=pltpu.CompilerParams(vmem_limit_bytes=limit * MIB),
        name=name,
    )(*arrays, *after)


def gridded(context, h_ref, weight, scale_row, store):
    cols = weight.shape[1]
    count = cols // ROT
    value = jnp.dot(context, weight, preferred_element_type=F32).astype(BF16)
    stacked = jnp.concatenate([value[:, i * ROT : (i + 1) * ROT] for i in range(count)], axis=0)
    turned = jnp.dot(stacked, h_ref[...], preferred_element_type=F32)
    tok = value.shape[0]
    for i in range(count):
        part = turned[i * tok : (i + 1) * tok] * scale_row(i)
        store(i, jnp.clip(part, -127.0, 127.0).astype(BF16))


def attend_kernel(
    inner, cols, chunk, q_hbm, k_hbm, v_hbm, w_hbm, pos_ref, table_ref, h_ref,
    ctx_ref, rows_ref, send_ref, k_ref, v_ref, w_ref, s_ref, q_ref, sems,
):
    tok = q_ref.shape[0]
    slots = k_ref.shape[0]
    steps = slots // chunk
    outer, mid, core = place(inner)
    dest = targets(outer)[0]

    def copy_k(j):
        part = pl.ds(j * chunk, chunk)
        return pltpu.make_async_copy(k_hbm.at[0, part], k_ref.at[part], sems.at[1 + j])

    def copy_v(j):
        part = pl.ds(j * chunk, chunk)
        return pltpu.make_async_copy(v_hbm.at[0, part], v_ref.at[part], sems.at[1 + steps + j])

    def shard_of(shift):
        return (dest * inner + lax.rem(mid + shift, inner)) * 2 + 1 - core

    def copy_w(shift):
        start = pl.multiple_of(shard_of(shift) * cols, 128)
        return pltpu.make_async_copy(
            w_hbm.at[:, pl.ds(start, cols)], w_ref.at[shift - 1], sems.at[2 * steps + shift]
        )

    copy_q = pltpu.make_async_copy(q_hbm.at[0], q_ref, sems.at[0])
    copy_q.start()
    for j in range(steps):
        copy_k(j).start()
    for j in range(steps):
        copy_v(j).start()
    for shift in range(1, inner):
        copy_w(shift).start()

    table = table_ref[...].astype(F32)
    count = table.shape[1]
    for i in range(2):
        rows_ref[i] = jnp.broadcast_to(table[i : i + 1], (ROT, count)).T
    positions = jnp.broadcast_to(pos_ref[...].astype(F32), (ROT, tok)).T
    ahead = positions.astype(jnp.int32) - lax.broadcasted_iota(jnp.int32, (tok, ROT), 1)

    copy_q.wait()
    queries = q_ref[...]
    peak = jnp.full((tok, ROT), -jnp.inf, F32)
    for j in range(steps):
        copy_k(j).wait()
        scores = lax.dot_general(
            queries, k_ref[j * chunk : (j + 1) * chunk], (((1,), (1,)), ((), ())),
            preferred_element_type=F32,
        )
        for i in range(chunk // ROT):
            base = j * chunk + i * ROT
            part = jnp.where(ahead >= base, scores[:, i * ROT : (i + 1) * ROT], -jnp.inf)
            s_ref[:, base : base + ROT] = part
            peak = jnp.maximum(peak, part)
    largest = jnp.max(peak, axis=1, keepdims=True)
    factor = math.log2(math.e) / math.sqrt(HD)
    total = jnp.zeros((tok, ROT), F32)
    acc = jnp.zeros((tok, HD), F32)
    for j in range(steps):
        copy_v(j).wait()
        pieces = []
        for i in range(chunk // ROT):
            base = j * chunk + i * ROT
            raised = jnp.exp2((s_ref[:, base : base + ROT] - largest) * factor)
            total = total + raised
            pieces.append(raised.astype(BF16))
        acc = acc + jnp.dot(
            jnp.concatenate(pieces, axis=1), v_ref[j * chunk : (j + 1) * chunk],
            preferred_element_type=F32,
        )
    context = (acc / jnp.sum(total, axis=1, keepdims=True)).astype(BF16)
    ctx_ref[...] = context

    per = cols // ROT
    for shift in range(1, inner):
        copy_w(shift).wait()
        first = shard_of(shift) * per

        def scale_row(i):
            return (65536.0 / math.sqrt(ROT)) / rows_ref[0, pl.ds(first + i, 1), :]

        def store(i, value):
            send_ref[shift - 1, :, i * ROT : (i + 1) * ROT] = value

        gridded(context, h_ref, w_ref[shift - 1], scale_row, store)


def attend(inner, cols, queries, keys, values, weight, positions, table, had):
    tok, slots = queries.shape[1], keys.shape[1]
    chunk = min(1024, slots)
    steps = slots // chunk
    blocks = table.shape[1]
    return kernel_call(
        functools.partial(attend_kernel, inner, cols, chunk),
        [
            jax.ShapeDtypeStruct((tok, HD), BF16),
            jax.ShapeDtypeStruct((2, blocks, ROT), F32),
            jax.ShapeDtypeStruct((inner - 1, tok, cols), BF16),
        ],
        [queries, keys, values, weight, positions[None, :], table, had],
        [pl.BlockSpec(memory_space=pltpu.HBM)] * 4 + [vmem()] * 3,
        scratch=[
            pltpu.VMEM((slots, HD), BF16),
            pltpu.VMEM((slots, HD), BF16),
            pltpu.VMEM((inner - 1, weight.shape[0], cols), BF16),
            pltpu.VMEM((tok, slots), F32),
            pltpu.VMEM((tok, HD), BF16),
            pltpu.SemaphoreType.DMA((2 * steps + inner,)),
        ],
        flops=4 * tok * slots * HD,
        nbytes=4 * slots * HD,
        exps=tok * slots,
        limit=28,
        name="attend",
    )


def partial_kernel(inner, work, ctx_ref, w_ref, rows_ref, h_ref, *out_refs):
    cols = out_refs[0].shape[2]
    per = cols // ROT
    outer, mid, core = place(inner)
    dests = targets(outer)
    context = ctx_ref[...]
    for out_ref, (mine, blocks) in zip(out_refs, work):
        for at, (phase, shift) in enumerate(blocks):
            shard = (dests[phase] * inner + lax.rem(mid + shift, inner)) * 2
            shard = shard + (core if mine else 1 - core)

            def scale_row(i):
                return (65536.0 / math.sqrt(ROT)) / rows_ref[0, pl.ds(shard * per + i, 1), :]

            def store(i, value):
                out_ref[at, :, i * ROT : (i + 1) * ROT] = value

            start = pl.multiple_of(shard * cols, 128)
            gridded(context, h_ref, w_ref[:, pl.ds(start, cols)], scale_row, store)


def partials(inner, cols, work, context, weight, rows, had, after=()):
    tok = context.shape[0]
    count = sum(len(blocks) for _, blocks in work)
    return kernel_call(
        functools.partial(partial_kernel, inner, work),
        [jax.ShapeDtypeStruct((len(blocks), tok, cols), BF16) for _, blocks in work],
        [context, weight, rows, had],
        [vmem()] * 4,
        after=after,
        flops=4 * count * tok * HD * cols,
        nbytes=2 * count * (tok + HD) * cols,
        name="partials",
    )


def add_kernel(inner, inputs, outputs, *refs):
    ins, outs = refs[:inputs], refs[inputs:]
    outer = place(inner)[0]
    for out_ref, items in zip(outs, outputs):
        total = None
        for which, at, inner_only in items:
            value = (ins[which][...] if at is None else ins[which][at]).astype(F32)
            if inner_only:
                value = jnp.where(is_inner(outer), value, 0.0)
            total = value if total is None else total + value
        out_ref[...] = total.astype(BF16)


def add_up(inner, arrays, outputs, after=()):
    shape = arrays[0].shape[-2:]
    terms = sum(len(items) for items in outputs)
    return kernel_call(
        functools.partial(add_kernel, inner, len(arrays), outputs),
        [jax.ShapeDtypeStruct(shape, BF16)] * len(outputs),
        arrays,
        [vmem()] * len(arrays),
        after=after,
        flops=terms * shape[0] * shape[1],
        nbytes=2 * (terms + len(outputs)) * shape[0] * shape[1],
        name="add_up",
    )


def turn_residual_kernel(inner, res_ref, rows_ref, h_ref, out_ref, factor_ref):
    per = res_ref.shape[1] // ROT
    first = lax.axis_index("tp") * per
    for i in range(per):
        part = slice(i * ROT, (i + 1) * ROT)
        high = 256.0 / rows_ref[1, pl.ds(first + i, 1), :]
        low = rows_ref[0, pl.ds(first + i, 1), :] * (1.0 / 65536.0)
        turned = jnp.dot(res_ref[:, part], h_ref[...], preferred_element_type=F32)
        out_ref[:, part] = turned * (high * (1.0 / math.sqrt(ROT)))
        factor_ref[0:1, part] = low * high
        factor_ref[1:2, part] = low


def turn_residual(inner, residual, rows, had, after=()):
    return kernel_call(
        functools.partial(turn_residual_kernel, inner),
        [
            jax.ShapeDtypeStruct(residual.shape, F32),
            jax.ShapeDtypeStruct((2, residual.shape[1]), F32),
        ],
        [residual, rows, had],
        [vmem()] * 3,
        after=after,
        flops=2 * residual.size * ROT,
        nbytes=6 * residual.size,
        name="turn_residual",
    )


def summed_at(inner, items, ins, part):
    outer = place(inner)[0]
    total = None
    for (at, inner_only), ref in zip(items, ins):
        value = (ref[:, part] if at is None else ref[at, :, part]).astype(F32)
        if inner_only:
            value = jnp.where(is_inner(outer), value, 0.0)
        total = value if total is None else total + value
    return total


def regrid_kernel(inner, items, turned_ref, factor_ref, *refs):
    *ins, grid_ref = refs
    for i in range(turned_ref.shape[1] // ROT):
        part = slice(i * ROT, (i + 1) * ROT)
        value = turned_ref[:, part] + summed_at(inner, items, ins, part) * factor_ref[0:1, part]
        grid_ref[:, part] = jnp.clip(value, -127.0, 127.0).astype(BF16)


def regrid(inner, items, turned, factors, arrays, after=()):
    return kernel_call(
        functools.partial(regrid_kernel, inner, items),
        jax.ShapeDtypeStruct(turned.shape, BF16),
        [turned, factors, *arrays],
        [vmem()] * (2 + len(arrays)),
        after=after,
        flops=8 * turned.size,
        nbytes=16 * turned.size,
        name="regrid",
    )


def hidden_kernel(inner, items, res_ref, factor_ref, h_ref, *refs):
    *ins, out_ref = refs
    for i in range(res_ref.shape[1] // ROT):
        part = slice(i * ROT, (i + 1) * ROT)
        value = summed_at(inner, items, ins, part) * factor_ref[1:2, part]
        upper = value.astype(BF16)
        lower = (value - upper.astype(F32)).astype(BF16)
        turned = jnp.dot(upper, h_ref[...], preferred_element_type=F32)
        turned = turned + jnp.dot(lower, h_ref[...], preferred_element_type=F32)
        stream = res_ref[:, part].astype(F32) + turned * (1.0 / math.sqrt(ROT))
        out_ref[:, part] = stream.astype(BF16)


def hidden(inner, items, residual, factors, had, arrays, after=()):
    return kernel_call(
        functools.partial(hidden_kernel, inner, items),
        jax.ShapeDtypeStruct(residual.shape, BF16),
        [residual, factors, had, *arrays],
        [vmem()] * (3 + len(arrays)),
        after=after,
        flops=4 * residual.size * ROT,
        nbytes=12 * residual.size,
        name="hidden",
    )


def choose_kernel(inner, inner_ref, end_ref, out_ref):
    inside = is_inner(place(inner)[0])

    @pl.when(inside)
    def _():
        out_ref[...] = inner_ref[...]

    @pl.when(jnp.logical_not(inside))
    def _():
        out_ref[...] = end_ref[...]


def choose(inner, at_inner, at_end, after=()):
    return kernel_call(
        functools.partial(choose_kernel, inner),
        jax.ShapeDtypeStruct(at_inner.shape, at_inner.dtype),
        [at_inner, at_end],
        [vmem()] * 2,
        after=after,
        nbytes=4 * at_inner.size,
        name="choose",
    )


def select_rows_kernel(inner, cols, w_ref, out_ref):
    other = 1 - place(inner)[2]
    for j in range(out_ref.shape[0]):
        start = pl.multiple_of((2 * j + other) * cols, 128)
        out_ref[j] = w_ref[pl.ds(start, cols), :]


def select_rows(inner, weight, cols, after=()):
    blocks = OUTER * inner
    return kernel_call(
        functools.partial(select_rows_kernel, inner, cols),
        jax.ShapeDtypeStruct((blocks, cols, weight.shape[1]), weight.dtype),
        [weight],
        [vmem()],
        after=after,
        nbytes=4 * blocks * cols * weight.shape[1],
        name="select_rows",
    )


def turn_next_kernel(inner, cols, own_ref, other_ref, gain_ref, rows_ref, h_ref, out_ref):
    core = place(inner)[2]
    for j in range(out_ref.shape[0]):
        shard = j * 2 + core
        for i in range(cols // ROT):
            block = shard * (cols // ROT) + i
            factor = rows_ref[1, pl.ds(block, 1), :] * (1.0 / (256.0 * math.sqrt(ROT)))
            rotation = (h_ref[...].astype(F32) * gain_ref[pl.ds(block, 1), :]).astype(BF16)
            part = slice(i * ROT, (i + 1) * ROT)
            own = own_ref[pl.ds(pl.multiple_of(block * ROT, ROT), ROT), :]
            for half, value in enumerate((own, other_ref[j, part, :])):
                turned = jnp.dot(rotation, value, preferred_element_type=F32)
                out_ref[j, part, half * HD : (half + 1) * HD] = (turned * factor).astype(BF16)


def turn_next(inner, weight, other, gain, rows, had, after=()):
    count, cols, width = other.shape
    return kernel_call(
        functools.partial(turn_next_kernel, inner, cols),
        jax.ShapeDtypeStruct((count, cols, 2 * width), BF16),
        [weight, other, gain, rows, had],
        [vmem()] * 5,
        after=after,
        flops=4 * count * cols * width * ROT,
        nbytes=8 * count * cols * width,
        name="turn_next",
    )


def project_kernel(inner, places, has_acc, split, w_ref, rows_ref, *refs):
    outer, mid, core = place(inner)
    far, third, near, own = targets(outer)
    order = (own, near, third, far)
    acc_in = refs[0] if has_acc else None
    refs = refs[1:] if has_acc else refs
    values_in = refs[: len(places)]
    outs = refs[len(places) :]
    cols, width = w_ref.shape[1:]
    acc = acc_in[:, :width] if has_acc else 0.0
    squares = acc_in[:, width:] if has_acc else 0.0
    for ref, (phase, shift) in zip(values_in, places):
        block = order[phase] * inner + lax.rem(mid + inner - shift, inner)
        values = ref[...]
        acc = acc + jnp.dot(values, w_ref[block], preferred_element_type=F32)
        for i in range(cols // ROT):
            row = (block * 2 + core) * (cols // ROT) + i
            high = rows_ref[1, pl.ds(row, 1), :] * (1.0 / 256.0)
            value = values[:, i * ROT : (i + 1) * ROT].astype(F32) * high
            squares = squares + value * value
    if split:
        own_ref, other_ref = outs
        own_ref[:, :HD] = acc[:, :HD]
        own_ref[:, HD:] = squares
        other_ref[:, :HD] = acc[:, HD:]
        other_ref[:, HD:] = squares
    else:
        outs[0][:, :width] = acc
        outs[0][:, width:] = squares


def project(inner, weight, rows, acc, pieces, split=False, after=()):
    _, cols, width = weight.shape
    arrays = [array for _, _, array in pieces]
    tok = arrays[0].shape[0]
    places = tuple((phase, shift) for phase, shift, _ in pieces)
    accs = [] if acc is None else [acc]
    if split:
        out = [jax.ShapeDtypeStruct((tok, HD + ROT), F32)] * 2
    else:
        out = jax.ShapeDtypeStruct((tok, width + ROT), F32)
    return kernel_call(
        functools.partial(project_kernel, inner, places, acc is not None, split),
        out,
        [weight, rows, *accs, *arrays],
        [vmem()] * (2 + len(accs) + len(arrays)),
        after=after,
        flops=2 * len(places) * tok * cols * width,
        nbytes=2 * len(places) * cols * (width + tok),
        name="project",
    )


def finish_kernel(features, own_ref, other_ref, out_ref):
    squares = own_ref[:, HD:] + other_ref[:, HD:]
    mean = jnp.sum(squares, axis=1, keepdims=True) * (1.0 / features)
    value = (own_ref[:, :HD] + other_ref[:, :HD]) * lax.rsqrt(mean + 1e-05)
    out_ref[...] = value.astype(BF16)


def finish(own, other, features):
    tok = own.shape[0]
    return kernel_call(
        functools.partial(finish_kernel, features),
        jax.ShapeDtypeStruct((tok, HD), BF16),
        [own, other],
        [vmem()] * 2,
        flops=4 * tok * HD,
        nbytes=16 * tok * HD,
        name="finish",
    )


def body(
    size,
    queries,
    cache_keys,
    cache_values,
    query_positions,
    out_weight,
    residual,
    scale_table,
    norm_gain,
    next_query_weight,
):
    inner = size // (2 * OUTER)
    cols = residual.shape[1]
    had = jnp.asarray(hadamard(ROT), BF16)
    shifts = range(1, inner)

    def permute(value, move):
        moves = []
        for i in range(size):
            spot = move(i // (2 * inner), (i // 2) % inner, i % 2)
            moves.append((i, (spot[0] * inner + spot[1]) * 2 + spot[2]))
        return lax.ppermute(value, "tp", moves)

    def swap_core(value):
        return permute(value, lambda a, b, c: (a, b, 1 - c))

    def shift_mid(value, shift):
        return permute(value, lambda a, b, c: (a, (b + shift) % inner, c))

    def swap_pairs(value):
        return permute(value, lambda a, b, c: (a ^ 1, b, c))

    def swap_middle(value):
        return permute(value, lambda a, b, c: ((0, 2, 1, 3)[a], b, c))

    everything = range(inner)
    context, rows, send1 = attend(
        inner, cols, queries, cache_keys, cache_values, out_weight, query_positions, scale_table, had
    )
    other1 = swap_core(send1)
    away1 = tuple((0, s) for s in shifts)
    (keep1,) = partials(inner, cols, ((True, away1),), context, out_weight, rows, had)
    pay1 = add_up(inner, [keep1, other1], [((0, s - 1, False), (1, s - 1, False)) for s in shifts])
    come1 = [shift_mid(pay, s) for s, pay in zip(shifts, pay1)]

    def both(blocks, after):
        work = ((False, blocks), (True, blocks))
        return partials(inner, cols, work, context, out_weight, rows, had, after=after)

    def phase_blocks(phase):
        return tuple((phase, s) for s in everything)

    send2, keep2 = both(((0, 0),) + phase_blocks(1), pay1[:1])
    other2 = swap_core(send2)
    send3, keep3 = both(phase_blocks(2), [keep2])
    other3 = swap_core(send3)

    def pay_out(keep, other, first, after):
        items = [((0, first + s, False), (1, first + s, False)) for s in shifts]
        return add_up(inner, [keep, other], items, after=after)

    pay2 = pay_out(keep2, other2, 1, [keep3])
    come2 = [shift_mid(pay, s) for s, pay in zip(shifts, pay2)]

    n = len(come1)
    sum1 = [(0, 0, False), (1, 0, False)] + [(2 + i, None, False) for i in range(n)]
    sum2 = [(0, 1, False), (1, 1, False)] + [(2 + i, None, False) for i in range(n)]
    relay = [(2 + n, None, True)]
    (end1,) = add_up(inner, [keep2, other2, *come1], [sum1], after=pay2[:1])
    from_end1 = swap_pairs(end1)
    send4, keep4 = both(phase_blocks(3), [end1])
    other4 = swap_core(send4)
    pay3 = pay_out(keep3, other3, 0, [keep4])
    come3 = [shift_mid(pay, s) for s, pay in zip(shifts, pay3)]
    picked = select_rows(inner, next_query_weight, cols, after=pay3[:1])
    next_other = swap_core(picked)
    (end2,) = add_up(inner, [keep2, other2, *come2], [sum2], after=[picked])
    from_end2 = swap_pairs(end2)
    (mid2,) = add_up(inner, [keep2, other2, *come1, from_end1], [sum1 + relay], after=[end2])
    from_mid2 = swap_middle(mid2)
    pay4 = pay_out(keep4, other4, 0, [mid2])
    come4 = [shift_mid(pay, s) for s, pay in zip(shifts, pay4)]
    turned_residual, factors = turn_residual(inner, residual, rows, had, after=pay4[:1])
    gain = norm_gain.astype(F32).reshape(-1, ROT)
    (mid3,) = add_up(
        inner, [keep2, other2, *come2, from_end2], [sum2 + relay], after=[turned_residual]
    )
    from_mid3 = swap_middle(mid3)
    (near3,) = add_up(inner, [keep3, other3, *come3, from_mid2], [sum1 + relay], after=[mid3])
    from_near3 = swap_pairs(near3)
    turned_next = turn_next(inner, next_query_weight, next_other, gain, rows, had, after=[near3])

    last = [keep4, other4, *come4, from_near3, from_mid3]
    items = [(0, False)] * 2 + [(None, False)] * (n + 1) + [(None, True)]
    grid = regrid(inner, items, turned_residual, factors, last, after=[turned_next])

    x1 = [shift_mid(grid, s) for s in shifts]
    near = swap_pairs(grid)
    mid1 = swap_middle(grid)
    x2 = [shift_mid(near, s) for s in shifts]
    ends2 = swap_pairs(mid1)
    mids2 = swap_middle(near)
    acc = project(inner, turned_next, rows, None, [(0, 0, grid)])
    hidden_out = hidden(inner, items, residual, factors, had, last, after=[acc])
    third = choose(inner, mid1, ends2, after=[hidden_out])
    x3 = [shift_mid(third, s) for s in shifts]
    ends3 = swap_pairs(mids2)
    acc = project(
        inner, turned_next, rows, acc, [(1, 0, near)] + [(0, s, x1[s - 1]) for s in shifts], after=[third]
    )
    fourth = choose(inner, mids2, ends3, after=[acc])
    x4 = [shift_mid(fourth, s) for s in shifts]
    acc = project(
        inner, turned_next, rows, acc, [(2, 0, third)] + [(1, s, x2[s - 1]) for s in shifts], after=[fourth]
    )
    acc = project(
        inner, turned_next, rows, acc, [(3, 0, fourth)] + [(2, s, x3[s - 1]) for s in shifts]
    )
    own, other = project(
        inner, turned_next, rows, acc, [(3, s, x4[s - 1]) for s in shifts], split=True
    )
    query_next = finish(own, swap_core(other), norm_gain.shape[0])
    return (hidden_out, query_next)


def solution(mesh):
    placed = (
        P("tp", "groups", None),
        P("tp", "groups", None),
        P("tp", "groups", None),
        P("groups"),
        P("tp", None),
        P("groups", "tp"),
        P(),
        P(),
        P(None, "tp"),
    )
    return jax.shard_map(
        functools.partial(body, mesh.shape["tp"]),
        mesh=mesh,
        in_specs=placed,
        out_specs=(P("groups", "tp"), P("groups", "tp")),
        check_vma=False,
    )
```

time: 237 us -> 97.7 us (0.41)
  waiting for transfers between devices: 158 us -> 38.7 us
  matrix products: 38.6 us -> 0 us
  starting transfers between devices: 0.26 us -> 32.7 us
  Pallas kernels: 0 us -> 14.5 us
  between operations: 14.1 us -> 0.94 us
  local copies, waits for them, and re-layouts: 23.4 us -> 10.3 us
  other arithmetic: 2.4 us -> 0.01 us
    reduce_scatter x1 -> x0, waiting for transfers between devices: 107 us -> none  [body(): lax.psum_scatter(on_grid.astype(jnp.float32), 'tp', scatter_dimension=1,...]
    all_gather x1 -> x0, waiting for transfers between devices: 50.5 us -> none  [body(): gathered = lax.all_gather(regrid, 'tp', axis=1, tiled=True)]
    ppermute x0 -> x24, waiting for transfers between devices: none -> 38.7 us  [permute(): return lax.ppermute(value, 'tp', moves)]
    dot_general x7 -> x0, matrix products: 38.6 us -> none  [the longest x4 21.6 us: rotate(): jnp.einsum('...bi,ij->...bj', blocks, rotation, precision=lax.Precision.H...]
    ppermute x0 -> x24, starting transfers between devices: none -> 32.7 us  [permute(): return lax.ppermute(value, 'tp', moves)]
    pallas_call x0 -> x27, Pallas kernels: none -> 14.5 us  [kernel_call(): pl.pallas_call(ordered, out_shape=out_shape, in_specs=list(specs) + [anyw...]
    convert_element_type x1 -> x0, local copies, waits for them, and re-layouts: 9.33 us -> none  [body(): on_grid.astype(jnp.float32)]
    reshape x2 -> x0, local copies, waits for them, and re-layouts: 7.16 us -> none  [the longest x1 6.96 us: blockwise(): blocks = values_in.reshape(leading + (block_scale.shape[0], ROT))]
  transfers between devices with their start and end apart: 2 -> 24, of which waited for: 2 -> 13; matrix products, arithmetic and copies ran while one was open for 0% -> 0% of each run, Pallas kernels for 0% -> 7%
where the time goes in v2:
time: 97.7 us; the launch traced here: 97.2 us
  waiting for transfers between devices  38.7 us (40%)
  starting transfers between devices  32.7 us (33%)
  Pallas kernels  14.5 us (15%)
  local copies, waits for them, and re-layouts  10.3 us (11%)
    ppermute x24, waiting for transfers between devices, permute(): return lax.ppermute(value, 'tp', moves)  38.7 us
    ppermute x24, starting transfers between devices, permute(): return lax.ppermute(value, 'tp', moves)  32.7 us
    pallas_call x27, Pallas kernels, kernel_call(): pl.pallas_call(ordered, out_shape=out_shape, in_specs=list(specs) + [anyw...  14.5 us
    unnamed x24, local copies, waits for them, and re-layouts  10.3 us
  transfers between devices with their start and end apart: 24, of which 13 were waited for; matrix products, arithmetic and copies ran while one was open for 0% of the time, Pallas kernels for 7%

profile of v2, /device:TPU:0, one launch (start us, length us, event | category | flops | bytes accessed | tf_op | source)
XLA Modules:
  0.0 97.2 jit_solution(12728581109663258197)
XLA Ops:
  0.6 2.2 %copy-done = bf16[128,16384]{1,0:T(8,128)(2,1)S(1)} copy-done((bf16[128,16384]{1,0:T(8,128)(2,1)S(1)}, bf16[128,16384]{1,0:T(8,128)(2,1)}, u32[]{:S(2)}) %copy-start) | copy-done | bytes 4194328
  3.6 1.6 %copy-done.4 = bf16[1,8192,128]{2,1,0:T(8,128)(2,1)S(1)} copy-done((bf16[1,8192,128]{2,1,0:T(8,128)(2,1)S(1)}, bf16[1,8192,128]{2,1,0:T(8,128)(2,1)}, u32[]{:S(2)}) %copy-start.4) | copy-done | bytes 2097176
  5.2 1.6 %copy-done.5 = bf16[1,8192,128]{2,1,0:T(8,128)(2,1)S(1)} copy-done((bf16[1,8192,128]{2,1,0:T(8,128)(2,1)S(1)}, bf16[1,8192,128]{2,1,0:T(8,128)(2,1)}, u32[]{:S(2)}) %copy-start.5) | copy-done | bytes 2097176
  8.9 4.7 %attend.1 = (bf16[128,128]{1,0:T(8,128)(2,1)S(1)}, f32[2,128,128]{2,1,0:T(8,128)S(1)}, bf16[1,128,1024]{2,1,0:T(8,128)(2,1)S(1)}) custom-call(bf16[1,128,128]{2,1,0:T(8,128)(2,1)S(1)} %copy-done.8, bf16[1,8192,128]{2,1,0:T(8,128)(2,1)S(1)} %copy-done.4, bf16[1,8192,128]{2,1,0:T(8,128)(2,1)S(1)} %copy-done.5, bf16[128,16384]{1,0:T(8,128)(2,1)S(1)} %copy-done, ...), custom_call_target="tpu_custom_call" | custom-call | flops 536870912 | bytes 4194304 | tf_op jit(solution)/shard_map/attend/pallas_call | solution.py:59
  15.4 1.2 %partials.5 = (bf16[3,128,1024]{2,1,0:T(8,128)(2,1)S(1)}, bf16[3,128,1024]{2,1,0:T(8,128)(2,1)S(1)}) custom-call(bf16[128,128]{1,0:T(8,128)(2,1)S(1)} %get-tuple-element.16.refs_0_, bf16[128,16384]{1,0:T(8,128)(2,1)S(1)} %copy-done, f32[2,128,128]{2,1,0:T(8,128)S(1)} %get-tuple-element.15.refs_2_.refs_1_.refs_3_, bf16[128,128]{1,0:T(8,128)(2,1)S(1)} %copy-done.2, ...), custom_call_target="tpu_custom_call" | custom-call | flops 402653184 | bytes 3145728 | tf_op jit(solution)/shard_map/partials/pallas_call | solution.py:59
  17.0 0.9 partials.6
  18.2 2.9 %collective-permute-start.2 = (bf16[128,1024]{1,0:T(8,128)(2,1)S(1)}, bf16[128,1024]{1,0:T(8,128)(2,1)S(1)}, u32[]{:S(2)}, u32[]{:S(2)}) collective-permute-start(bf16[128,1024]{1,0:T(8,128)(2,1)S(1)} %add_up.9.refs_4_), channel_id=1, source_target_pairs={{0,2},{1,3},{2,0},{3,1},{4,6},{5,7},{6,4},{7,5},{8,10},{9,11},{10,... | collective-permute-start | bytes 786440 | tf_op jit(solution)/shard_map/ppermute | solution.py:524
  21.1 6.5 %collective-permute-done.2.refs_2_ = bf16[128,1024]{1,0:T(8,128)(2,1)S(1)} collective-permute-done((bf16[128,1024]{1,0:T(8,128)(2,1)S(1)}, bf16[128,1024]{1,0:T(8,128)(2,1)S(1)}, u32[]{:S(2)}, u32[]{:S(2)}) %collective-permute-start.2) | collective-permute-done | bytes 262176 | tf_op jit(solution)/shard_map/ppermute | solution.py:524
  27.8 1.0 partials.7
  28.8 1.1 %copy-done.1 = bf16[16384,128]{1,0:T(8,128)(2,1)S(1)} copy-done((bf16[16384,128]{1,0:T(8,128)(2,1)S(1)}, bf16[16384,128]{1,0:T(8,128)(2,1)}, u32[]{:S(2)}) %copy-start.1) | copy-done | bytes 4194328
  30.7 1.7 %collective-permute-start.5 = (bf16[128,1024]{1,0:T(8,128)(2,1)S(1)}, bf16[128,1024]{1,0:T(8,128)(2,1)S(1)}, u32[]{:S(2)}, u32[]{:S(2)}) collective-permute-start(bf16[128,1024]{1,0:T(8,128)(2,1)S(1)} %add_up.10.refs_3_), channel_id=1, source_target_pairs={{0,2},{1,3},{2,0},{3,1},{4,6},{5,7},{6,4},{7,5},{8,10},{9,11},{10,... | collective-permute-start | bytes 786440 | tf_op jit(solution)/shard_map/ppermute | solution.py:524
  32.4 1.6 %collective-permute-start.4 = (bf16[128,1024]{1,0:T(8,128)(2,1)S(1)}, bf16[128,1024]{1,0:T(8,128)(2,1)S(1)}, u32[]{:S(2)}, u32[]{:S(2)}) collective-permute-start(bf16[128,1024]{1,0:T(8,128)(2,1)S(1)} %add_up.11.refs_4_), channel_id=1, source_target_pairs={{0,4},{1,5},{2,6},{3,7},{4,0},{5,1},{6,2},{7,3},{8,12},{9,13},{10,... | collective-permute-start | bytes 786440 | tf_op jit(solution)/shard_map/ppermute | solution.py:524
  34.0 5.0 %collective-permute-done.5.refs_2_ = bf16[128,1024]{1,0:T(8,128)(2,1)S(1)} collective-permute-done((bf16[128,1024]{1,0:T(8,128)(2,1)S(1)}, bf16[128,1024]{1,0:T(8,128)(2,1)S(1)}, u32[]{:S(2)}, u32[]{:S(2)}) %collective-permute-start.5) | collective-permute-done | bytes 262176 | tf_op jit(solution)/shard_map/ppermute | solution.py:524
  39.1 1.9 %collective-permute-start.10 = (bf16[128,1024]{1,0:T(8,128)(2,1)S(1)}, bf16[128,1024]{1,0:T(8,128)(2,1)S(1)}, u32[]{:S(2)}, u32[]{:S(2)}) collective-permute-start(bf16[128,1024]{1,0:T(8,128)(2,1)S(1)} %add_up.13.refs_4_), channel_id=1, source_target_pairs={{0,4},{1,5},{2,6},{3,7},{4,0},{5,1},{6,2},{7,3},{8,12},{9,13},{10,... | collective-permute-start | bytes 786440 | tf_op jit(solution)/shard_map/ppermute | solution.py:524
  41.0 1.5 %collective-permute-start.8 = (bf16[128,1024]{1,0:T(8,128)(2,1)S(1)}, bf16[128,1024]{1,0:T(8,128)(2,1)S(1)}, u32[]{:S(2)}, u32[]{:S(2)}) collective-permute-start(bf16[128,1024]{1,0:T(8,128)(2,1)S(1)} %add_up.12.refs_1_), channel_id=1, source_target_pairs={{0,2},{1,3},{2,0},{3,1},{4,6},{5,7},{6,4},{7,5},{8,10},{9,11},{10,... | collective-permute-start | bytes 786440 | tf_op jit(solution)/shard_map/ppermute | solution.py:524
  44.2 2.5 %collective-permute-done.10.refs_3_ = bf16[128,1024]{1,0:T(8,128)(2,1)S(1)} collective-permute-done((bf16[128,1024]{1,0:T(8,128)(2,1)S(1)}, bf16[128,1024]{1,0:T(8,128)(2,1)S(1)}, u32[]{:S(2)}, u32[]{:S(2)}) %collective-permute-start.10) | collective-permute-done | bytes 262176 | tf_op jit(solution)/shard_map/ppermute | solution.py:524
  47.5 2.7 %collective-permute-done.8.refs_2_ = bf16[128,1024]{1,0:T(8,128)(2,1)S(1)} collective-permute-done((bf16[128,1024]{1,0:T(8,128)(2,1)S(1)}, bf16[128,1024]{1,0:T(8,128)(2,1)S(1)}, u32[]{:S(2)}, u32[]{:S(2)}) %collective-permute-start.8) | collective-permute-done | bytes 262176 | tf_op jit(solution)/shard_map/ppermute | solution.py:524
  50.4 4.0 %collective-permute-start.11 = (bf16[128,1024]{1,0:T(8,128)(2,1)S(1)}, bf16[128,1024]{1,0:T(8,128)(2,1)S(1)}, u32[]{:S(2)}, u32[]{:S(2)}) collective-permute-start(bf16[128,1024]{1,0:T(8,128)(2,1)S(1)} %add_up.17.refs_5_), channel_id=1, source_target_pairs={{0,4},{1,5},{2,6},{3,7},{4,0},{5,1},{6,2},{7,3},{8,12},{9,13},{10,... | collective-permute-start | bytes 786440 | tf_op jit(solution)/shard_map/ppermute | solution.py:524
  54.4 1.3 %turn_next.1.refs_7_.refs_0_ = bf16[8,1024,256]{2,1,0:T(8,128)(2,1)S(1)} custom-call(bf16[16384,128]{1,0:T(8,128)(2,1)S(1)} %copy-done.1, bf16[8,1024,128]{2,1,0:T(8,128)(2,1)S(1)} %collective-permute-done.13.refs_1_, f32[128,128]{1,0:T(8,128)S(1)} %bitcast_convert_fusion.refs_2_, f32[2,128,128]{2,1,0:T(8,128)S(1)} %get-tuple-element.15.refs_2_.refs_1_.refs_3_, ...), custom_call_target="tpu_custom_call" | custom-call | flops 536870912 | bytes 8388608 | tf_op jit(solution)/shard_map/turn_next/pallas_call | solution.py:59
  55.7 3.5 %collective-permute-done.11.refs_5_.refs_6_ = bf16[128,1024]{1,0:T(8,128)(2,1)S(1)} collective-permute-done((bf16[128,1024]{1,0:T(8,128)(2,1)S(1)}, bf16[128,1024]{1,0:T(8,128)(2,1)S(1)}, u32[]{:S(2)}, u32[]{:S(2)}) %collective-permute-start.11) | collective-permute-done | bytes 262176 | tf_op jit(solution)/shard_map/ppermute | solution.py:524
  59.4 2.4 %collective-permute-start.14 = (bf16[128,1024]{1,0:T(8,128)(2,1)S(1)}, bf16[128,1024]{1,0:T(8,128)(2,1)S(1)}, u32[]{:S(2)}, u32[]{:S(2)}) collective-permute-start(bf16[128,1024]{1,0:T(8,128)(2,1)S(1)} %regrid.1.refs_2_), channel_id=1, source_target_pairs={{0,4},{1,5},{2,6},{3,7},{4,0},{5,1},{6,2},{7,3},{8,12},{9,13},{10,... | collective-permute-start | bytes 786440 | tf_op jit(solution)/shard_map/ppermute | solution.py:524
  62.5 3.7 %collective-permute-done.14.refs_3_ = bf16[128,1024]{1,0:T(8,128)(2,1)S(1)} collective-permute-done((bf16[128,1024]{1,0:T(8,128)(2,1)S(1)}, bf16[128,1024]{1,0:T(8,128)(2,1)S(1)}, u32[]{:S(2)}, u32[]{:S(2)}) %collective-permute-start.14) | collective-permute-done | bytes 262176 | tf_op jit(solution)/shard_map/ppermute | solution.py:524
  66.8 5.8 %collective-permute-start.17 = (bf16[128,1024]{1,0:T(8,128)(2,1)S(1)}, bf16[128,1024]{1,0:T(8,128)(2,1)S(1)}, u32[]{:S(2)}, u32[]{:S(2)}) collective-permute-start(bf16[128,1024]{1,0:T(8,128)(2,1)S(1)} %collective-permute-done.16.refs_0_), channel_id=1, source_target_pairs={{0,4},{1,5},{2,6},{3,7},{4,0},{5,1},{6,2},{7,3},{8,12},{9,13},{10,... | collective-permute-start | bytes 786440 | tf_op jit(solution)/shard_map/ppermute | solution.py:524
  72.6 4.3 %collective-permute-start.20 = (bf16[128,1024]{1,0:T(8,128)(2,1)S(1)}, bf16[128,1024]{1,0:T(8,128)(2,1)S(1)}, u32[]{:S(2)}, u32[]{:S(2)}) collective-permute-start(bf16[128,1024]{1,0:T(8,128)(2,1)S(1)} %collective-permute-done.19.refs_0_), channel_id=1, source_target_pairs={{0,4},{1,5},{2,6},{3,7},{4,0},{5,1},{6,2},{7,3},{8,12},{9,13},{10,... | collective-permute-start | bytes 786440 | tf_op jit(solution)/shard_map/ppermute | solution.py:524
  77.1 1.1 %hidden.1.refs_2_ = bf16[128,1024]{1,0:T(8,128)(2,1)} custom-call(bf16[128,1024]{1,0:T(8,128)(2,1)S(1)} %copy-done.6, f32[2,1024]{1,0:T(2,128)S(1)} %get-tuple-element.24.refs_1_, bf16[128,128]{1,0:T(8,128)(2,1)S(1)} %copy-done.3, bf16[2,128,1024]{2,1,0:T(8,128)(2,1)S(1)} %get-tuple-element.21.refs_2_.refs_0_.refs_3_, ...), custom_call_target="tpu_custom_call" | custom-call | flops 67108864 | bytes 1572864 | tf_op jit(solution)/shard_map/hidden/pallas_call | solution.py:59
  78.3 1.0 %collective-permute-done.17.refs_1_ = bf16[128,1024]{1,0:T(8,128)(2,1)S(1)} collective-permute-done((bf16[128,1024]{1,0:T(8,128)(2,1)S(1)}, bf16[128,1024]{1,0:T(8,128)(2,1)S(1)}, u32[]{:S(2)}, u32[]{:S(2)}) %collective-permute-start.17) | collective-permute-done | bytes 262176 | tf_op jit(solution)/shard_map/ppermute | solution.py:524
  79.3 0.9 copy-done.7
  80.2 1.1 %collective-permute-start.21 = (bf16[128,1024]{1,0:T(8,128)(2,1)S(1)}, bf16[128,1024]{1,0:T(8,128)(2,1)S(1)}, u32[]{:S(2)}, u32[]{:S(2)}) collective-permute-start(bf16[128,1024]{1,0:T(8,128)(2,1)S(1)} %choose.2.refs_5_.refs_3_), channel_id=1, source_target_pairs={{0,2},{1,3},{2,0},{3,1},{4,6},{5,7},{6,4},{7,5},{8,10},{9,11},{10,... | collective-permute-start | bytes 786440 | tf_op jit(solution)/shard_map/ppermute | solution.py:524
  82.8 4.6 %collective-permute-done.18.refs_4_ = bf16[128,1024]{1,0:T(8,128)(2,1)S(1)} collective-permute-done((bf16[128,1024]{1,0:T(8,128)(2,1)S(1)}, bf16[128,1024]{1,0:T(8,128)(2,1)S(1)}, u32[]{:S(2)}, u32[]{:S(2)}) %collective-permute-start.18) | collective-permute-done | bytes 262176 | tf_op jit(solution)/shard_map/ppermute | solution.py:524
  87.8 4.2 %collective-permute-done.21.refs_4_ = bf16[128,1024]{1,0:T(8,128)(2,1)S(1)} collective-permute-done((bf16[128,1024]{1,0:T(8,128)(2,1)S(1)}, bf16[128,1024]{1,0:T(8,128)(2,1)S(1)}, u32[]{:S(2)}, u32[]{:S(2)}) %collective-permute-start.21) | collective-permute-done | bytes 262176 | tf_op jit(solution)/shard_map/ppermute | solution.py:524
  92.3 2.5 %collective-permute-done.22.refs_3_ = bf16[128,1024]{1,0:T(8,128)(2,1)S(1)} collective-permute-done((bf16[128,1024]{1,0:T(8,128)(2,1)S(1)}, bf16[128,1024]{1,0:T(8,128)(2,1)S(1)}, u32[]{:S(2)}, u32[]{:S(2)}) %collective-permute-start.22) | collective-permute-done | bytes 262176 | tf_op jit(solution)/shard_map/ppermute | solution.py:524
  95.1 1.3 %collective-permute-done.23.refs_1_ = f32[128,256]{1,0:T(8,128)S(1)} collective-permute-done((f32[128,256]{1,0:T(8,128)S(1)}, f32[128,256]{1,0:T(8,128)S(1)}, u32[]{:S(2)}, u32[]{:S(2)}) %collective-permute-start.23) | collective-permute-done | bytes 131104 | tf_op jit(solution)/shard_map/ppermute | solution.py:524
  (68 shorter events, 14.0 us)
Async XLA Ops:
  0.6 2.2 %copy-start = (bf16[128,16384]{1,0:T(8,128)(2,1)S(1)}, bf16[128,16384]{1,0:T(8,128)(2,1)}, u32[]{:S(2)}) copy-start(bf16[128,16384]{1,0:T(8,128)(2,1)} %refs_1_.9) | copy-start | bytes 12582916
  3.6 1.6 %copy-start.4 = (bf16[1,8192,128]{2,1,0:T(8,128)(2,1)S(1)}, bf16[1,8192,128]{2,1,0:T(8,128)(2,1)}, u32[]{:S(2)}) copy-start(bf16[1,8192,128]{2,1,0:T(8,128)(2,1)} %refs_1_.5) | copy-start | bytes 6291460
  5.2 1.6 %copy-start.5 = (bf16[1,8192,128]{2,1,0:T(8,128)(2,1)S(1)}, bf16[1,8192,128]{2,1,0:T(8,128)(2,1)}, u32[]{:S(2)}) copy-start(bf16[1,8192,128]{2,1,0:T(8,128)(2,1)} %refs_2_.3) | copy-start | bytes 6291460
  13.6 1.7 %collective-permute-start = (bf16[1,128,1024]{2,1,0:T(8,128)(2,1)S(1)}, bf16[1,128,1024]{2,1,0:T(8,128)(2,1)S(1)}, u32[]{:S(2)}, u32[]{:S(2)}) collective-permute-start(bf16[1,128,1024]{2,1,0:T(8,128)(2,1)S(1)} %get-tuple-element.17), channel_id=1, source_target_pairs={{0,1},{1,0},{2,3},{3,2},{4,5},{5,4},{6,7},{7,6},{8,9},{9,8},{10,11... | collective-permute-start | bytes 786440 | tf_op jit(solution)/shard_map/ppermute | solution.py:524
  16.6 4.4 %collective-permute-start.1 = (bf16[3,128,1024]{2,1,0:T(8,128)(2,1)S(1)}, bf16[3,128,1024]{2,1,0:T(8,128)(2,1)S(1)}, u32[]{:S(2)}, u32[]{:S(2)}) collective-permute-start(bf16[3,128,1024]{2,1,0:T(8,128)(2,1)S(1)} %get-tuple-element.19), channel_id=1, source_target_pairs={{0,1},{1,0},{2,3},{3,2},{4,5},{5,4},{6,7},{7,6},{8,9},{9,8},{10,11... | collective-permute-start | bytes 2359304 | tf_op jit(solution)/shard_map/ppermute | solution.py:524
  18.0 10.7 %collective-permute-start.6 = (bf16[2,128,1024]{2,1,0:T(8,128)(2,1)S(1)}, bf16[2,128,1024]{2,1,0:T(8,128)(2,1)S(1)}, u32[]{:S(2)}, u32[]{:S(2)}) collective-permute-start(bf16[2,128,1024]{2,1,0:T(8,128)(2,1)S(1)} %get-tuple-element.23), channel_id=1, source_target_pairs={{0,1},{1,0},{2,3},{3,2},{4,5},{5,4},{6,7},{7,6},{8,9},{9,8},{10,11... | collective-permute-start | bytes 1572872 | tf_op jit(solution)/shard_map/ppermute | solution.py:524
  18.2 9.5 %collective-permute-start.2 = (bf16[128,1024]{1,0:T(8,128)(2,1)S(1)}, bf16[128,1024]{1,0:T(8,128)(2,1)S(1)}, u32[]{:S(2)}, u32[]{:S(2)}) collective-permute-start(bf16[128,1024]{1,0:T(8,128)(2,1)S(1)} %add_up.9.refs_4_), channel_id=1, source_target_pairs={{0,2},{1,3},{2,0},{3,1},{4,6},{5,7},{6,4},{7,5},{8,10},{9,11},{10,... | collective-permute-start | bytes 786440 | tf_op jit(solution)/shard_map/ppermute | solution.py:524
  21.0 6.7 %copy-start.3 = (bf16[128,128]{1,0:T(8,128)(2,1)S(1)}, bf16[128,128]{1,0:T(8,128)(2,1)}, u32[]{:S(2)}) copy-start(bf16[128,128]{1,0:T(8,128)(2,1)} %constant.2.clone.refs_6_.refs_3_.refs_2_.refs_4_) | copy-start | bytes 98308
  27.8 2.2 %copy-start.1 = (bf16[16384,128]{1,0:T(8,128)(2,1)S(1)}, bf16[16384,128]{1,0:T(8,128)(2,1)}, u32[]{:S(2)}) copy-start(bf16[16384,128]{1,0:T(8,128)(2,1)} %refs_0_.8) | copy-start | bytes 12582916
  30.1 24.3 %collective-permute-start.13 = (bf16[8,1024,128]{2,1,0:T(8,128)(2,1)S(1)}, bf16[8,1024,128]{2,1,0:T(8,128)(2,1)S(1)}, u32[]{:S(2)}, u32[]{:S(2)}) collective-permute-start(bf16[8,1024,128]{2,1,0:T(8,128)(2,1)S(1)} %select_rows.1.refs_3_), channel_id=1, source_target_pairs={{0,1},{1,0},{2,3},{3,2},{4,5},{5,4},{6,7},{7,6},{8,9},{9,8},{10,11... | collective-permute-start | bytes 6291464 | tf_op jit(solution)/shard_map/ppermute | solution.py:524
  30.2 13.1 %collective-permute-start.3 = (bf16[2,128,1024]{2,1,0:T(8,128)(2,1)S(1)}, bf16[2,128,1024]{2,1,0:T(8,128)(2,1)S(1)}, u32[]{:S(2)}, u32[]{:S(2)}) collective-permute-start(bf16[2,128,1024]{2,1,0:T(8,128)(2,1)S(1)} %get-tuple-element.22), channel_id=1, source_target_pairs={{0,1},{1,0},{2,3},{3,2},{4,5},{5,4},{6,7},{7,6},{8,9},{9,8},{10,11... | collective-permute-start | bytes 1572872 | tf_op jit(solution)/shard_map/ppermute | solution.py:524
  30.7 8.3 %collective-permute-start.5 = (bf16[128,1024]{1,0:T(8,128)(2,1)S(1)}, bf16[128,1024]{1,0:T(8,128)(2,1)S(1)}, u32[]{:S(2)}, u32[]{:S(2)}) collective-permute-start(bf16[128,1024]{1,0:T(8,128)(2,1)S(1)} %add_up.10.refs_3_), channel_id=1, source_target_pairs={{0,2},{1,3},{2,0},{3,1},{4,6},{5,7},{6,4},{7,5},{8,10},{9,11},{10,... | collective-permute-start | bytes 786440 | tf_op jit(solution)/shard_map/ppermute | solution.py:524
  32.4 10.0 %collective-permute-start.4 = (bf16[128,1024]{1,0:T(8,128)(2,1)S(1)}, bf16[128,1024]{1,0:T(8,128)(2,1)S(1)}, u32[]{:S(2)}, u32[]{:S(2)}) collective-permute-start(bf16[128,1024]{1,0:T(8,128)(2,1)S(1)} %add_up.11.refs_4_), channel_id=1, source_target_pairs={{0,4},{1,5},{2,6},{3,7},{4,0},{5,1},{6,2},{7,3},{8,12},{9,13},{10,... | collective-permute-start | bytes 786440 | tf_op jit(solution)/shard_map/ppermute | solution.py:524
  39.0 4.9 %copy-start.6 = (bf16[128,1024]{1,0:T(8,128)(2,1)S(1)}, bf16[128,1024]{1,0:T(8,128)(2,1)}, u32[]{:S(2)}) copy-start(bf16[128,1024]{1,0:T(8,128)(2,1)} %refs_0_.9) | copy-start | bytes 786436
  39.1 7.6 %collective-permute-start.10 = (bf16[128,1024]{1,0:T(8,128)(2,1)S(1)}, bf16[128,1024]{1,0:T(8,128)(2,1)S(1)}, u32[]{:S(2)}, u32[]{:S(2)}) collective-permute-start(bf16[128,1024]{1,0:T(8,128)(2,1)S(1)} %add_up.13.refs_4_), channel_id=1, source_target_pairs={{0,4},{1,5},{2,6},{3,7},{4,0},{5,1},{6,2},{7,3},{8,12},{9,13},{10,... | collective-permute-start | bytes 786440 | tf_op jit(solution)/shard_map/ppermute | solution.py:524
  41.0 9.2 %collective-permute-start.8 = (bf16[128,1024]{1,0:T(8,128)(2,1)S(1)}, bf16[128,1024]{1,0:T(8,128)(2,1)S(1)}, u32[]{:S(2)}, u32[]{:S(2)}) collective-permute-start(bf16[128,1024]{1,0:T(8,128)(2,1)S(1)} %add_up.12.refs_1_), channel_id=1, source_target_pairs={{0,2},{1,3},{2,0},{3,1},{4,6},{5,7},{6,4},{7,5},{8,10},{9,11},{10,... | collective-permute-start | bytes 786440 | tf_op jit(solution)/shard_map/ppermute | solution.py:524
  42.6 7.6 %collective-permute-start.9 = (bf16[128,1024]{1,0:T(8,128)(2,1)S(1)}, bf16[128,1024]{1,0:T(8,128)(2,1)S(1)}, u32[]{:S(2)}, u32[]{:S(2)}) collective-permute-start(bf16[128,1024]{1,0:T(8,128)(2,1)S(1)} %add_up.14.refs_2_), channel_id=1, source_target_pairs={{0,0},{1,1},{2,2},{3,3},{4,8},{5,9},{6,10},{7,11},{8,4},{9,5},{10,... | collective-permute-start | bytes 786440 | tf_op jit(solution)/shard_map/ppermute | solution.py:524
  43.4 12.3 %collective-permute-start.7 = (bf16[128,1024]{1,0:T(8,128)(2,1)S(1)}, bf16[128,1024]{1,0:T(8,128)(2,1)S(1)}, u32[]{:S(2)}, u32[]{:S(2)}) collective-permute-start(bf16[128,1024]{1,0:T(8,128)(2,1)S(1)} %add_up.15.refs_3_), channel_id=1, source_target_pairs={{0,2},{1,3},{2,0},{3,1},{4,6},{5,7},{6,4},{7,5},{8,10},{9,11},{10,... | collective-permute-start | bytes 786440 | tf_op jit(solution)/shard_map/ppermute | solution.py:524
  46.7 7.7 %copy-start.11 = (bf16[16384]{0:T(1024)(128)(2,1)S(1)}, bf16[16384]{0:T(1024)(128)(2,1)}, u32[]{:S(2)}) copy-start(bf16[16384]{0:T(1024)(128)(2,1)} %param.17) | copy-start | bytes 98308
  46.8 12.3 %collective-permute-start.12 = (bf16[128,1024]{1,0:T(8,128)(2,1)S(1)}, bf16[128,1024]{1,0:T(8,128)(2,1)S(1)}, u32[]{:S(2)}, u32[]{:S(2)}) collective-permute-start(bf16[128,1024]{1,0:T(8,128)(2,1)S(1)} %add_up.16.refs_4_), channel_id=1, source_target_pairs={{0,0},{1,1},{2,2},{3,3},{4,8},{5,9},{6,10},{7,11},{8,4},{9,5},{10,... | collective-permute-start | bytes 786440 | tf_op jit(solution)/shard_map/ppermute | solution.py:524
  50.4 8.8 %collective-permute-start.11 = (bf16[128,1024]{1,0:T(8,128)(2,1)S(1)}, bf16[128,1024]{1,0:T(8,128)(2,1)S(1)}, u32[]{:S(2)}, u32[]{:S(2)}) collective-permute-start(bf16[128,1024]{1,0:T(8,128)(2,1)S(1)} %add_up.17.refs_5_), channel_id=1, source_target_pairs={{0,4},{1,5},{2,6},{3,7},{4,0},{5,1},{6,2},{7,3},{8,12},{9,13},{10,... | collective-permute-start | bytes 786440 | tf_op jit(solution)/shard_map/ppermute | solution.py:524
  59.4 6.7 %collective-permute-start.14 = (bf16[128,1024]{1,0:T(8,128)(2,1)S(1)}, bf16[128,1024]{1,0:T(8,128)(2,1)S(1)}, u32[]{:S(2)}, u32[]{:S(2)}) collective-permute-start(bf16[128,1024]{1,0:T(8,128)(2,1)S(1)} %regrid.1.refs_2_), channel_id=1, source_target_pairs={{0,4},{1,5},{2,6},{3,7},{4,0},{5,1},{6,2},{7,3},{8,12},{9,13},{10,... | collective-permute-start | bytes 786440 | tf_op jit(solution)/shard_map/ppermute | solution.py:524
  61.8 5.0 %collective-permute-start.16 = (bf16[128,1024]{1,0:T(8,128)(2,1)S(1)}, bf16[128,1024]{1,0:T(8,128)(2,1)S(1)}, u32[]{:S(2)}, u32[]{:S(2)}) collective-permute-start(bf16[128,1024]{1,0:T(8,128)(2,1)S(1)} %regrid.1.refs_2_), channel_id=1, source_target_pairs={{0,0},{1,1},{2,2},{3,3},{4,8},{5,9},{6,10},{7,11},{8,4},{9,5},{10,... | collective-permute-start | bytes 786440 | tf_op jit(solution)/shard_map/ppermute | solution.py:524
  66.2 6.4 %collective-permute-start.19 = (bf16[128,1024]{1,0:T(8,128)(2,1)S(1)}, bf16[128,1024]{1,0:T(8,128)(2,1)S(1)}, u32[]{:S(2)}, u32[]{:S(2)}) collective-permute-start(bf16[128,1024]{1,0:T(8,128)(2,1)S(1)} %collective-permute-done.14.refs_3_), channel_id=1, source_target_pairs={{0,0},{1,1},{2,2},{3,3},{4,8},{5,9},{6,10},{7,11},{8,4},{9,5},{10,... | collective-permute-start | bytes 786440 | tf_op jit(solution)/shard_map/ppermute | solution.py:524
  66.8 12.4 %collective-permute-start.17 = (bf16[128,1024]{1,0:T(8,128)(2,1)S(1)}, bf16[128,1024]{1,0:T(8,128)(2,1)S(1)}, u32[]{:S(2)}, u32[]{:S(2)}) collective-permute-start(bf16[128,1024]{1,0:T(8,128)(2,1)S(1)} %collective-permute-done.16.refs_0_), channel_id=1, source_target_pairs={{0,4},{1,5},{2,6},{3,7},{4,0},{5,1},{6,2},{7,3},{8,12},{9,13},{10,... | collective-permute-start | bytes 786440 | tf_op jit(solution)/shard_map/ppermute | solution.py:524
  72.6 9.2 %collective-permute-start.15 = (bf16[128,1024]{1,0:T(8,128)(2,1)S(1)}, bf16[128,1024]{1,0:T(8,128)(2,1)S(1)}, u32[]{:S(2)}, u32[]{:S(2)}) collective-permute-start(bf16[128,1024]{1,0:T(8,128)(2,1)S(1)} %regrid.1.refs_2_), channel_id=1, source_target_pairs={{0,2},{1,3},{2,0},{3,1},{4,6},{5,7},{6,4},{7,5},{8,10},{9,11},{10,... | collective-permute-start | bytes 786440 | tf_op jit(solution)/shard_map/ppermute | solution.py:524
  72.6 9.5 %collective-permute-start.20 = (bf16[128,1024]{1,0:T(8,128)(2,1)S(1)}, bf16[128,1024]{1,0:T(8,128)(2,1)S(1)}, u32[]{:S(2)}, u32[]{:S(2)}) collective-permute-start(bf16[128,1024]{1,0:T(8,128)(2,1)S(1)} %collective-permute-done.19.refs_0_), channel_id=1, source_target_pairs={{0,4},{1,5},{2,6},{3,7},{4,0},{5,1},{6,2},{7,3},{8,12},{9,13},{10,... | collective-permute-start | bytes 786440 | tf_op jit(solution)/shard_map/ppermute | solution.py:524
  76.9 10.5 %collective-permute-start.18 = (bf16[128,1024]{1,0:T(8,128)(2,1)S(1)}, bf16[128,1024]{1,0:T(8,128)(2,1)S(1)}, u32[]{:S(2)}, u32[]{:S(2)}) collective-permute-start(bf16[128,1024]{1,0:T(8,128)(2,1)S(1)} %collective-permute-done.14.refs_3_), channel_id=1, source_target_pairs={{0,2},{1,3},{2,0},{3,1},{4,6},{5,7},{6,4},{7,5},{8,10},{9,11},{10,... | collective-permute-start | bytes 786440 | tf_op jit(solution)/shard_map/ppermute | solution.py:524
  79.3 1.0 copy-start.7
  80.2 11.7 %collective-permute-start.21 = (bf16[128,1024]{1,0:T(8,128)(2,1)S(1)}, bf16[128,1024]{1,0:T(8,128)(2,1)S(1)}, u32[]{:S(2)}, u32[]{:S(2)}) collective-permute-start(bf16[128,1024]{1,0:T(8,128)(2,1)S(1)} %choose.2.refs_5_.refs_3_), channel_id=1, source_target_pairs={{0,2},{1,3},{2,0},{3,1},{4,6},{5,7},{6,4},{7,5},{8,10},{9,11},{10,... | collective-permute-start | bytes 786440 | tf_op jit(solution)/shard_map/ppermute | solution.py:524
  82.2 12.6 %collective-permute-start.22 = (bf16[128,1024]{1,0:T(8,128)(2,1)S(1)}, bf16[128,1024]{1,0:T(8,128)(2,1)S(1)}, u32[]{:S(2)}, u32[]{:S(2)}) collective-permute-start(bf16[128,1024]{1,0:T(8,128)(2,1)S(1)} %choose.3.refs_5_.refs_3_), channel_id=1, source_target_pairs={{0,2},{1,3},{2,0},{3,1},{4,6},{5,7},{6,4},{7,5},{8,10},{9,11},{10,... | collective-permute-start | bytes 786440 | tf_op jit(solution)/shard_map/ppermute | solution.py:524
  95.0 1.4 %collective-permute-start.23 = (f32[128,256]{1,0:T(8,128)S(1)}, f32[128,256]{1,0:T(8,128)S(1)}, u32[]{:S(2)}, u32[]{:S(2)}) collective-permute-start(f32[128,256]{1,0:T(8,128)S(1)} %get-tuple-element.27), channel_id=1, source_target_pairs={{0,1},{1,0},{2,3},{3,2},{4,5},{5,4},{6,7},{7,6},{8,9},{9,8},{10,11... | collective-permute-start | bytes 393224 | tf_op jit(solution)/shard_map/ppermute | solution.py:524
  (4 other events, 2.8 us)

commit v3 on v2

--- a/solution.py
+++ b/solution.py
@@ -50,7 +50,7 @@
     return jnp.logical_or(outer == 1, outer == 2)
 
 
-def kernel_call(kernel, out_shape, arrays, specs, after=(), scratch=(), flops=0, nbytes=0, exps=0, limit=24, name=None):
+def kernel_call(kernel, out_shape, arrays, specs, after=(), scratch=(), aliases=None, limit=24, name=None):
     count, extra = len(arrays), len(after)
 
     def ordered(*refs):
@@ -62,9 +62,8 @@
         in_specs=list(specs) + [anywhere()] * extra,
         out_specs=jax.tree.map(lambda _: vmem(), out_shape),
         scratch_shapes=list(scratch),
-        cost_estimate=pl.CostEstimate(
-            flops=int(flops), bytes_accessed=int(nbytes), transcendentals=int(exps)
-        ),
+        input_output_aliases=aliases or {},
+        cost_estimate=pl.CostEstimate(flops=0, bytes_accessed=0, transcendentals=0),
         compiler_params=pltpu.CompilerParams(vmem_limit_bytes=limit * MIB),
         name=name,
     )(*arrays, *after)
@@ -83,8 +82,8 @@
 
 
 def attend_kernel(
-    inner, cols, chunk, q_hbm, k_hbm, v_hbm, w_hbm, pos_ref, table_ref, h_ref,
-    ctx_ref, rows_ref, send_ref, k_ref, v_ref, w_ref, s_ref, q_ref, sems,
+    inner, cols, chunk, q_hbm, k_hbm, v_hbm, w_hbm, pos_hbm, table_hbm, h_hbm,
+    ctx_ref, rows_ref, send_ref, w_ref, h_ref, k_ref, v_ref, s_ref, q_ref, pos_ref, table_ref, sems,
 ):
     tok = q_ref.shape[0]
     slots = k_ref.shape[0]
@@ -103,25 +102,22 @@
     def shard_of(shift):
         return (dest * inner + lax.rem(mid + shift, inner)) * 2 + 1 - core
 
-    def copy_w(shift):
-        start = pl.multiple_of(shard_of(shift) * cols, 128)
-        return pltpu.make_async_copy(
-            w_hbm.at[:, pl.ds(start, cols)], w_ref.at[shift - 1], sems.at[2 * steps + shift]
-        )
-
+    copy_w = pltpu.make_async_copy(w_hbm, w_ref, sems.at[2 * steps + 1])
     copy_q = pltpu.make_async_copy(q_hbm.at[0], q_ref, sems.at[0])
+    copy_pos = pltpu.make_async_copy(pos_hbm, pos_ref, sems.at[2 * steps + 2])
+    copy_table = pltpu.make_async_copy(table_hbm, table_ref, sems.at[2 * steps + 3])
+    copy_h = pltpu.make_async_copy(h_hbm, h_ref, sems.at[2 * steps + 4])
     copy_q.start()
+    copy_pos.start()
     for j in range(steps):
         copy_k(j).start()
+    copy_table.start()
+    copy_h.start()
     for j in range(steps):
         copy_v(j).start()
-    for shift in range(1, inner):
-        copy_w(shift).start()
-
-    table = table_ref[...].astype(F32)
-    count = table.shape[1]
-    for i in range(2):
-        rows_ref[i] = jnp.broadcast_to(table[i : i + 1], (ROT, count)).T
+    copy_w.start()
+
+    copy_pos.wait()
     positions = jnp.broadcast_to(pos_ref[...].astype(F32), (ROT, tok)).T
     ahead = positions.astype(jnp.int32) - lax.broadcasted_iota(jnp.int32, (tok, ROT), 1)
 
@@ -139,6 +135,11 @@
             part = jnp.where(ahead >= base, scores[:, i * ROT : (i + 1) * ROT], -jnp.inf)
             s_ref[:, base : base + ROT] = part
             peak = jnp.maximum(peak, part)
+    copy_table.wait()
+    table = table_ref[...].astype(F32)
+    count = table.shape[1]
+    for i in range(2):
+        rows_ref[i] = jnp.broadcast_to(table[i : i + 1], (ROT, count)).T
     largest = jnp.max(peak, axis=1, keepdims=True)
     factor = math.log2(math.e) / math.sqrt(HD)
     total = jnp.zeros((tok, ROT), F32)
@@ -159,9 +160,11 @@
     ctx_ref[...] = context
 
     per = cols // ROT
+    copy_h.wait()
+    copy_w.wait()
     for shift in range(1, inner):
-        copy_w(shift).wait()
         first = shard_of(shift) * per
+        start = pl.multiple_of(shard_of(shift) * cols, 128)
 
         def scale_row(i):
             return (65536.0 / math.sqrt(ROT)) / rows_ref[0, pl.ds(first + i, 1), :]
@@ -169,7 +172,7 @@
         def store(i, value):
             send_ref[shift - 1, :, i * ROT : (i + 1) * ROT] = value
 
-        gridded(context, h_ref, w_ref[shift - 1], scale_row, store)
+        gridded(context, h_ref, w_ref[:, pl.ds(start, cols)], scale_row, store)
 
 
 def attend(inner, cols, queries, keys, values, weight, positions, table, had):
@@ -177,26 +180,27 @@
     chunk = min(1024, slots)
     steps = slots // chunk
     blocks = table.shape[1]
+    arrays = [queries, keys, values, weight, positions[None, :], table, had]
     return kernel_call(
         functools.partial(attend_kernel, inner, cols, chunk),
         [
-            jax.ShapeDtypeStruct((tok, HD), BF16),
-            jax.ShapeDtypeStruct((2, blocks, ROT), F32),
-            jax.ShapeDtypeStruct((inner - 1, tok, cols), BF16),
+            pltpu.VMEM((tok, HD), BF16),
+            pltpu.VMEM((2, blocks, ROT), F32),
+            pltpu.VMEM((inner - 1, tok, cols), BF16),
+            pltpu.VMEM(weight.shape, BF16),
+            pltpu.VMEM(had.shape, BF16),
         ],
-        [queries, keys, values, weight, positions[None, :], table, had],
-        [pl.BlockSpec(memory_space=pltpu.HBM)] * 4 + [vmem()] * 3,
+        [pltpu.with_memory_space_constraint(array, pltpu.HBM) for array in arrays],
+        [pl.BlockSpec(memory_space=pltpu.HBM)] * len(arrays),
         scratch=[
             pltpu.VMEM((slots, HD), BF16),
             pltpu.VMEM((slots, HD), BF16),
-            pltpu.VMEM((inner - 1, weight.shape[0], cols), BF16),
             pltpu.VMEM((tok, slots), F32),
             pltpu.VMEM((tok, HD), BF16),
-            pltpu.SemaphoreType.DMA((2 * steps + inner,)),
+            pltpu.VMEM((1, tok), positions.dtype),
+            pltpu.VMEM(table.shape, table.dtype),
+            pltpu.SemaphoreType.DMA((2 * steps + 5,)),
         ],
-        flops=4 * tok * slots * HD,
-        nbytes=4 * slots * HD,
-        exps=tok * slots,
         limit=28,
         name="attend",
     )
@@ -232,8 +236,6 @@
         [context, weight, rows, had],
         [vmem()] * 4,
         after=after,
-        flops=4 * count * tok * HD * cols,
-        nbytes=2 * count * (tok + HD) * cols,
         name="partials",
     )
 
@@ -260,8 +262,6 @@
         arrays,
         [vmem()] * len(arrays),
         after=after,
-        flops=terms * shape[0] * shape[1],
-        nbytes=2 * (terms + len(outputs)) * shape[0] * shape[1],
         name="add_up",
     )
 
@@ -289,8 +289,6 @@
         [residual, rows, had],
         [vmem()] * 3,
         after=after,
-        flops=2 * residual.size * ROT,
-        nbytes=6 * residual.size,
         name="turn_residual",
     )
 
@@ -321,14 +319,13 @@
         [turned, factors, *arrays],
         [vmem()] * (2 + len(arrays)),
         after=after,
-        flops=8 * turned.size,
-        nbytes=16 * turned.size,
         name="regrid",
     )
 
 
 def hidden_kernel(inner, items, res_ref, factor_ref, h_ref, *refs):
-    *ins, out_ref = refs
+    *ins, out_ref, mark_ref = refs
+    mark_ref[...] = jnp.zeros_like(mark_ref)
     for i in range(res_ref.shape[1] // ROT):
         part = slice(i * ROT, (i + 1) * ROT)
         value = summed_at(inner, items, ins, part) * factor_ref[1:2, part]
@@ -343,12 +340,10 @@
 def hidden(inner, items, residual, factors, had, arrays, after=()):
     return kernel_call(
         functools.partial(hidden_kernel, inner, items),
-        jax.ShapeDtypeStruct(residual.shape, BF16),
+        [jax.ShapeDtypeStruct(residual.shape, BF16), jax.ShapeDtypeStruct((8, ROT), F32)],
         [residual, factors, had, *arrays],
         [vmem()] * (3 + len(arrays)),
         after=after,
-        flops=4 * residual.size * ROT,
-        nbytes=12 * residual.size,
         name="hidden",
     )
 
@@ -372,32 +367,44 @@
         [at_inner, at_end],
         [vmem()] * 2,
         after=after,
-        nbytes=4 * at_inner.size,
         name="choose",
     )
 
 
-def select_rows_kernel(inner, cols, w_ref, out_ref):
+def gate(arrays, after):
+    def kernel(*refs):
+        pass
+
+    shapes = [jax.ShapeDtypeStruct(array.shape, array.dtype) for array in arrays]
+    aliases = {i: i for i in range(len(arrays))}
+    specs = [vmem()] * len(arrays)
+    return kernel_call(kernel, shapes, arrays, specs, after=after, aliases=aliases, name="gate")
+
+
+def select_rows_kernel(inner, cols, w_ref, *out_refs):
     other = 1 - place(inner)[2]
-    for j in range(out_ref.shape[0]):
+    each = out_refs[0].shape[0]
+    for j in range(each * len(out_refs)):
         start = pl.multiple_of((2 * j + other) * cols, 128)
-        out_ref[j] = w_ref[pl.ds(start, cols), :]
+        out_refs[j // each][j % each] = w_ref[pl.ds(start, cols), :]
 
 
 def select_rows(inner, weight, cols, after=()):
-    blocks = OUTER * inner
+    parts = 2 * OUTER
+    each = OUTER * inner // parts
     return kernel_call(
         functools.partial(select_rows_kernel, inner, cols),
-        jax.ShapeDtypeStruct((blocks, cols, weight.shape[1]), weight.dtype),
+        [jax.ShapeDtypeStruct((each, cols, weight.shape[1]), weight.dtype)] * parts,
         [weight],
         [vmem()],
         after=after,
-        nbytes=4 * blocks * cols * weight.shape[1],
         name="select_rows",
     )
 
 
-def turn_next_kernel(inner, cols, own_ref, other_ref, gain_ref, rows_ref, h_ref, out_ref):
+def turn_next_kernel(inner, cols, own_ref, gain_ref, rows_ref, h_ref, *refs):
+    *other_refs, out_ref = refs
+    each = other_refs[0].shape[0]
     core = place(inner)[2]
     for j in range(out_ref.shape[0]):
         shard = j * 2 + core
@@ -407,21 +414,19 @@
             rotation = (h_ref[...].astype(F32) * gain_ref[pl.ds(block, 1), :]).astype(BF16)
             part = slice(i * ROT, (i + 1) * ROT)
             own = own_ref[pl.ds(pl.multiple_of(block * ROT, ROT), ROT), :]
-            for half, value in enumerate((own, other_ref[j, part, :])):
+            for half, value in enumerate((own, other_refs[j // each][j % each, part, :])):
                 turned = jnp.dot(rotation, value, preferred_element_type=F32)
                 out_ref[j, part, half * HD : (half + 1) * HD] = (turned * factor).astype(BF16)
 
 
-def turn_next(inner, weight, other, gain, rows, had, after=()):
-    count, cols, width = other.shape
+def turn_next(inner, weight, others, gain, rows, had, after=()):
+    _, cols, width = others[0].shape
     return kernel_call(
         functools.partial(turn_next_kernel, inner, cols),
-        jax.ShapeDtypeStruct((count, cols, 2 * width), BF16),
-        [weight, other, gain, rows, had],
-        [vmem()] * 5,
-        after=after,
-        flops=4 * count * cols * width * ROT,
-        nbytes=8 * count * cols * width,
+        jax.ShapeDtypeStruct((OUTER * inner, cols, 2 * width), BF16),
+        [weight, gain, rows, had, *others],
+        [vmem()] * (4 + len(others)),
+        after=after,
         name="turn_next",
     )
 
@@ -473,8 +478,6 @@
         [weight, rows, *accs, *arrays],
         [vmem()] * (2 + len(accs) + len(arrays)),
         after=after,
-        flops=2 * len(places) * tok * cols * width,
-        nbytes=2 * len(places) * cols * (width + tok),
         name="project",
     )
 
@@ -493,8 +496,6 @@
         jax.ShapeDtypeStruct((tok, HD), BF16),
         [own, other],
         [vmem()] * 2,
-        flops=4 * tok * HD,
-        nbytes=16 * tok * HD,
         name="finish",
     )
 
@@ -536,85 +537,116 @@
         return permute(value, lambda a, b, c: ((0, 2, 1, 3)[a], b, c))
 
     everything = range(inner)
-    context, rows, send1 = attend(
+    context, rows, send1, out_weight, had = attend(
         inner, cols, queries, cache_keys, cache_values, out_weight, query_positions, scale_table, had
     )
     other1 = swap_core(send1)
     away1 = tuple((0, s) for s in shifts)
-    (keep1,) = partials(inner, cols, ((True, away1),), context, out_weight, rows, had)
-    pay1 = add_up(inner, [keep1, other1], [((0, s - 1, False), (1, s - 1, False)) for s in shifts])
-    come1 = [shift_mid(pay, s) for s, pay in zip(shifts, pay1)]
-
-    def both(blocks, after):
-        work = ((False, blocks), (True, blocks))
-        return partials(inner, cols, work, context, out_weight, rows, had, after=after)
-
     def phase_blocks(phase):
         return tuple((phase, s) for s in everything)
 
-    send2, keep2 = both(((0, 0),) + phase_blocks(1), pay1[:1])
-    other2 = swap_core(send2)
-    send3, keep3 = both(phase_blocks(2), [keep2])
+    def grid_blocks(work, after=()):
+        return partials(inner, cols, work, context, out_weight, rows, had, after=after)
+
+    blocks2 = ((0, 0),) + phase_blocks(1)
+    keep1, keep2, keep3, keep4, *send2 = grid_blocks(
+        (
+            (True, away1),
+            (True, blocks2),
+            (True, phase_blocks(2)),
+            (True, phase_blocks(3)),
+            *((False, (block,)) for block in blocks2),
+        )
+    )
+    other2 = [swap_core(send) for send in send2]
+    items1 = [((0, s - 1, False), (1, s - 1, False)) for s in shifts]
+    pay1 = add_up(inner, [keep1, other1], items1, after=[keep2])
+    come1 = [shift_mid(pay, s) for s, pay in zip(shifts, pay1)]
+    (send3,) = grid_blocks(((False, phase_blocks(2)),), pay1[:1])
     other3 = swap_core(send3)
-
-    def pay_out(keep, other, first, after):
-        items = [((0, first + s, False), (1, first + s, False)) for s in shifts]
-        return add_up(inner, [keep, other], items, after=after)
-
-    pay2 = pay_out(keep2, other2, 1, [keep3])
-    come2 = [shift_mid(pay, s) for s, pay in zip(shifts, pay2)]
-
-    n = len(come1)
-    sum1 = [(0, 0, False), (1, 0, False)] + [(2 + i, None, False) for i in range(n)]
-    sum2 = [(0, 1, False), (1, 1, False)] + [(2 + i, None, False) for i in range(n)]
-    relay = [(2 + n, None, True)]
-    (end1,) = add_up(inner, [keep2, other2, *come1], [sum1], after=pay2[:1])
-    from_end1 = swap_pairs(end1)
-    send4, keep4 = both(phase_blocks(3), [end1])
+    (send4,) = grid_blocks(((False, phase_blocks(3)),), [send3])
     other4 = swap_core(send4)
-    pay3 = pay_out(keep3, other3, 0, [keep4])
-    come3 = [shift_mid(pay, s) for s, pay in zip(shifts, pay3)]
-    picked = select_rows(inner, next_query_weight, cols, after=pay3[:1])
-    next_other = swap_core(picked)
-    (end2,) = add_up(inner, [keep2, other2, *come2], [sum2], after=[picked])
-    from_end2 = swap_pairs(end2)
-    (mid2,) = add_up(inner, [keep2, other2, *come1, from_end1], [sum1 + relay], after=[end2])
-    from_mid2 = swap_middle(mid2)
-    pay4 = pay_out(keep4, other4, 0, [mid2])
+
+    def sums(arrays, outputs, after=()):
+        names = list(arrays)
+        items = [[(names.index(name), at, only) for name, at, only in output] for output in outputs]
+        return add_up(inner, list(arrays.values()), items, after=after)
+
+    def came(step, blocks):
+        return {f"came{step}_{s}": block for s, block in zip(shifts, blocks)}
+
+    def added(names):
+        return [(name, None, False) for name in names]
+
+    own2 = {"keep2": keep2} | {f"other2_{i}": other for i, other in enumerate(other2)}
+    own3 = {"keep3": keep3, "other3": other3}
+    own4 = {"keep4": keep4, "other4": other4}
+
+    def part2(i):
+        return [("keep2", i, False), (f"other2_{i}", 0, False)]
+
+    def part(step, s):
+        return [(f"keep{step}", s, False), (f"other{step}", s, False)]
+
+    came1 = came(1, come1)
+    near1 = part2(0) + added(came1)
+    *pay2, end1 = sums(own2 | came1, [*(part2(1 + s) for s in shifts), near1], after=[send4])
+    came2 = came(2, [shift_mid(pay, s) for s, pay in zip(shifts, pay2)])
+    from_end1 = {"end1": swap_pairs(end1)}
+    turned_residual, factors = turn_residual(inner, residual, rows, had, after=[end1])
+    picked = select_rows(inner, next_query_weight, cols, after=[factors])
+    next_other = [swap_core(part) for part in picked]
+
+    near2 = part2(1) + added(came2)
+    *pay3, end2, mid2 = sums(
+        own2 | own3 | came1 | came2 | from_end1,
+        [*(part(3, s) for s in shifts), near2, near1 + [("end1", None, True)]],
+        after=picked[:1],
+    )
+    came3 = came(3, [shift_mid(pay, s) for s, pay in zip(shifts, pay3)])
+    from_end2 = {"end2": swap_pairs(end2)}
+    from_mid2 = {"mid2": swap_middle(mid2)}
+
+    *pay4, mid3, near3 = sums(
+        own2 | own3 | own4 | came2 | came3 | from_end2 | from_mid2,
+        [
+            *(part(4, s) for s in shifts),
+            near2 + [("end2", None, True)],
+            part(3, 0) + added(came3) + [("mid2", None, True)],
+        ],
+        after=next_other,
+    )
     come4 = [shift_mid(pay, s) for s, pay in zip(shifts, pay4)]
-    turned_residual, factors = turn_residual(inner, residual, rows, had, after=pay4[:1])
+    from_mid3 = swap_middle(mid3)
+    from_near3 = swap_pairs(near3)
+
     gain = norm_gain.astype(F32).reshape(-1, ROT)
-    (mid3,) = add_up(
-        inner, [keep2, other2, *come2, from_end2], [sum2 + relay], after=[turned_residual]
-    )
-    from_mid3 = swap_middle(mid3)
-    (near3,) = add_up(inner, [keep3, other3, *come3, from_mid2], [sum1 + relay], after=[mid3])
-    from_near3 = swap_pairs(near3)
     turned_next = turn_next(inner, next_query_weight, next_other, gain, rows, had, after=[near3])
 
     last = [keep4, other4, *come4, from_near3, from_mid3]
-    items = [(0, False)] * 2 + [(None, False)] * (n + 1) + [(None, True)]
+    items = [(0, False)] * 2 + [(None, False)] * (len(come4) + 1) + [(None, True)]
     grid = regrid(inner, items, turned_residual, factors, last, after=[turned_next])
 
     x1 = [shift_mid(grid, s) for s in shifts]
     near = swap_pairs(grid)
     mid1 = swap_middle(grid)
+    acc = project(inner, turned_next, rows, None, [(0, 0, grid)])
+    hidden_out, mark = hidden(inner, items, residual, factors, had, last, after=[acc])
+    near, mid1 = gate([near, mid1], after=[*x1, mark])
     x2 = [shift_mid(near, s) for s in shifts]
     ends2 = swap_pairs(mid1)
     mids2 = swap_middle(near)
-    acc = project(inner, turned_next, rows, None, [(0, 0, grid)])
-    hidden_out = hidden(inner, items, residual, factors, had, last, after=[acc])
-    third = choose(inner, mid1, ends2, after=[hidden_out])
+    acc = project(
+        inner, turned_next, rows, acc, [(1, 0, near)] + [(0, s, x1[s - 1]) for s in shifts]
+    )
+    third = choose(inner, mid1, ends2, after=[*x2, acc])
     x3 = [shift_mid(third, s) for s in shifts]
     ends3 = swap_pairs(mids2)
     acc = project(
-        inner, turned_next, rows, acc, [(1, 0, near)] + [(0, s, x1[s - 1]) for s in shifts], after=[third]
-    )
-    fourth = choose(inner, mids2, ends3, after=[acc])
+        inner, turned_next, rows, acc, [(2, 0, third)] + [(1, s, x2[s - 1]) for s in shifts]
+    )
+    fourth = choose(inner, mids2, ends3, after=[*x3, acc])
     x4 = [shift_mid(fourth, s) for s in shifts]
-    acc = project(
-        inner, turned_next, rows, acc, [(2, 0, third)] + [(1, s, x2[s - 1]) for s in shifts], after=[fourth]
-    )
     acc = project(
         inner, turned_next, rows, acc, [(3, 0, fourth)] + [(2, s, x3[s - 1]) for s in shifts]
     )

time: 97.7 us -> 91.2 us (0.933)
  local copies, waits for them, and re-layouts: 10.3 us -> 0.02 us
  waiting for transfers between devices: 38.7 us -> 44.1 us
  starting transfers between devices: 32.7 us -> 31.2 us
    unnamed x24 -> x6, local copies, waits for them, and re-layouts: 10.3 us -> 0.02 us
    ppermute x24 -> x33, waiting for transfers between devices: 38.7 us -> 44.1 us  [permute(): return lax.ppermute(value, 'tp', moves)]
    ppermute x24 -> x33, starting transfers between devices: 32.7 us -> 31.2 us  [permute(): return lax.ppermute(value, 'tp', moves)]
    pallas_call x27 -> x22, Pallas kernels: 14.5 us -> 14.8 us  [kernel_call(): pl.pallas_call(ordered, out_shape=out_shape, in_specs=list(specs) + [anyw...]
  transfers between devices with their start and end apart: 24 -> 33, of which waited for: 13 -> 16; matrix products, arithmetic and copies ran while one was open for 0% -> 0% of each run, Pallas kernels for 7% -> 9%
where the time goes in v3:
time: 91.2 us; the launch traced here: 91 us
  waiting for transfers between devices  44.1 us (48%)
  starting transfers between devices  31.2 us (34%)
  Pallas kernels  14.8 us (16%)
    ppermute x33, waiting for transfers between devices, permute(): return lax.ppermute(value, 'tp', moves)  44.1 us
    ppermute x33, starting transfers between devices, permute(): return lax.ppermute(value, 'tp', moves)  31.2 us
    pallas_call x22, Pallas kernels, kernel_call(): pl.pallas_call(ordered, out_shape=out_shape, in_specs=list(specs) + [anyw...  14.8 us
  transfers between devices with their start and end apart: 33, of which 16 were waited for; matrix products, arithmetic and copies ran while one was open for 0% of the time, Pallas kernels for 9%

profile of v3, /device:TPU:0, one launch (start us, length us, event | category | flops | bytes accessed | tf_op | source)
XLA Modules:
  0.0 91.0 jit_solution(2088929116053360295)
XLA Ops:
  0.6 5.4 %attend.1 = (bf16[128,128]{1,0:T(8,128)(2,1)S(1)}, f32[2,128,128]{2,1,0:T(8,128)S(1)}, bf16[1,128,1024]{2,1,0:T(8,128)(2,1)S(1)}, bf16[128,16384]{1,0:T(8,128)(2,1)S(1)}, bf16[128,128]{1,0:T(8,128)(2,1)S(1)}) custom-call(bf16[1,128,128]{2,1,0:T(8,128)(2,1)} %refs_0_.5, bf16[1,8192,128]{2,1,0:T(8,128)(2,1)} %refs_1_.1, bf16[1,8192,128]{2,1,0:T(8,128)(2,1)} %refs_2_.1, ...), custom_call_target="tpu_custom_call" | custom-call | tf_op jit(solution)/shard_map/attend/pallas_call | solution.py:59
  6.5 1.9 %partials.3 = (bf16[1,128,1024]{2,1,0:T(8,128)(2,1)S(1)}, bf16[3,128,1024]{2,1,0:T(8,128)(2,1)S(1)}, bf16[2,128,1024]{2,1,0:T(8,128)(2,1)S(1)}, bf16[2,128,1024]...) custom-call(bf16[128,128]{1,0:T(8,128)(2,1)S(1)} %get-tuple-element., ...), custom_call_target="tpu_custom_call" | custom-call | tf_op jit(solution)/shard_map/partials/pallas_call | solution.py:59
  9.1 3.0 %collective-permute-start.4 = (bf16[128,1024]{1,0:T(8,128)(2,1)S(1)}, bf16[128,1024]{1,0:T(8,128)(2,1)S(1)}, u32[]{:S(2)}, u32[]{:S(2)}) collective-permute-start(bf16[128,1024]{1,0:T(8,128)(2,1)S(1)} %add_up.4.refs_4_), channel_id=1, source_target_pairs={{0,2},{1,3},{2,0},{3,1},{4,6},{5,7},{6,4},{7,5},{8,10},{9,11},{10,... | collective-permute-start | bytes 786440 | tf_op jit(solution)/shard_map/ppermute | solution.py:525
  13.6 5.1 %collective-permute-done.4.refs_4_.refs_6_ = bf16[128,1024]{1,0:T(8,128)(2,1)S(1)} collective-permute-done((bf16[128,1024]{1,0:T(8,128)(2,1)S(1)}, bf16[128,1024]{1,0:T(8,128)(2,1)S(1)}, u32[]{:S(2)}, u32[]{:S(2)}) %collective-permute-start.4) | collective-permute-done | bytes 262176 | tf_op jit(solution)/shard_map/ppermute | solution.py:525
  18.8 1.8 %collective-permute-start.7 = (bf16[128,1024]{1,0:T(8,128)(2,1)S(1)}, bf16[128,1024]{1,0:T(8,128)(2,1)S(1)}, u32[]{:S(2)}, u32[]{:S(2)}) collective-permute-start(bf16[128,1024]{1,0:T(8,128)(2,1)S(1)} %get-tuple-element.52), channel_id=1, source_target_pairs={{0,2},{1,3},{2,0},{3,1},{4,6},{5,7},{6,4},{7,5},{8,10},{9,11},{10,... | collective-permute-start | bytes 786440 | tf_op jit(solution)/shard_map/ppermute | solution.py:525
  20.6 1.6 %collective-permute-start.8 = (bf16[128,1024]{1,0:T(8,128)(2,1)S(1)}, bf16[128,1024]{1,0:T(8,128)(2,1)S(1)}, u32[]{:S(2)}, u32[]{:S(2)}) collective-permute-start(bf16[128,1024]{1,0:T(8,128)(2,1)S(1)} %get-tuple-element.48.refs_3_), channel_id=1, source_target_pairs={{0,4},{1,5},{2,6},{3,7},{4,0},{5,1},{6,2},{7,3},{8,12},{9,13},{10,... | collective-permute-start | bytes 786440 | tf_op jit(solution)/shard_map/ppermute | solution.py:525
  23.2 3.5 %collective-permute-done.7.refs_7_.refs_8_ = bf16[128,1024]{1,0:T(8,128)(2,1)S(1)} collective-permute-done((bf16[128,1024]{1,0:T(8,128)(2,1)S(1)}, bf16[128,1024]{1,0:T(8,128)(2,1)S(1)}, u32[]{:S(2)}, u32[]{:S(2)}) %collective-permute-start.7) | collective-permute-done | bytes 262176 | tf_op jit(solution)/shard_map/ppermute | solution.py:525
  26.7 1.1 %collective-permute-done.8.refs_8_ = bf16[128,1024]{1,0:T(8,128)(2,1)S(1)} collective-permute-done((bf16[128,1024]{1,0:T(8,128)(2,1)S(1)}, bf16[128,1024]{1,0:T(8,128)(2,1)S(1)}, u32[]{:S(2)}, u32[]{:S(2)}) %collective-permute-start.8) | collective-permute-done | bytes 262176 | tf_op jit(solution)/shard_map/ppermute | solution.py:525
  29.2 0.9 collective-permute-done.15.refs_15_.refs_7_
  30.5 1.6 %collective-permute-start.10 = (bf16[128,1024]{1,0:T(8,128)(2,1)S(1)}, bf16[128,1024]{1,0:T(8,128)(2,1)S(1)}, u32[]{:S(2)}, u32[]{:S(2)}) collective-permute-start(bf16[128,1024]{1,0:T(8,128)(2,1)S(1)} %get-tuple-element.55), channel_id=1, source_target_pairs={{0,4},{1,5},{2,6},{3,7},{4,0},{5,1},{6,2},{7,3},{8,12},{9,13},{10,... | collective-permute-start | bytes 786440 | tf_op jit(solution)/shard_map/ppermute | solution.py:525
  32.7 0.7 collective-permute-start.9
  33.5 5.4 %collective-permute-done.10.refs_10_ = bf16[128,1024]{1,0:T(8,128)(2,1)S(1)} collective-permute-done((bf16[128,1024]{1,0:T(8,128)(2,1)S(1)}, bf16[128,1024]{1,0:T(8,128)(2,1)S(1)}, u32[]{:S(2)}, u32[]{:S(2)}) %collective-permute-start.10) | collective-permute-done | bytes 262176 | tf_op jit(solution)/shard_map/ppermute | solution.py:525
  38.8 2.0 %collective-permute-done.9.refs_9_ = bf16[128,1024]{1,0:T(8,128)(2,1)S(1)} collective-permute-done((bf16[128,1024]{1,0:T(8,128)(2,1)S(1)}, bf16[128,1024]{1,0:T(8,128)(2,1)S(1)}, u32[]{:S(2)}, u32[]{:S(2)}) %collective-permute-start.9) | collective-permute-done | bytes 262176 | tf_op jit(solution)/shard_map/ppermute | solution.py:525
  41.2 0.7 collective-permute-start.20
  41.9 4.1 %collective-permute-start.21 = (bf16[128,1024]{1,0:T(8,128)(2,1)S(1)}, bf16[128,1024]{1,0:T(8,128)(2,1)S(1)}, u32[]{:S(2)}, u32[]{:S(2)}) collective-permute-start(bf16[128,1024]{1,0:T(8,128)(2,1)S(1)} %get-tuple-element.65.refs_12_), channel_id=1, source_target_pairs={{0,4},{1,5},{2,6},{3,7},{4,0},{5,1},{6,2},{7,3},{8,12},{9,13},{10,... | collective-permute-start | bytes 786440 | tf_op jit(solution)/shard_map/ppermute | solution.py:525
  46.8 1.3 %turn_next.1.refs_7_.refs_0_ = bf16[8,1024,256]{2,1,0:T(8,128)(2,1)S(1)} custom-call(bf16[16384,128]{1,0:T(8,128)(2,1)S(1)} %copy-done, f32[128,128]{1,0:T(8,128)S(1)} %bitcast_convert_fusion.refs_1_, f32[2,128,128]{2,1,0:T(8,128)S(1)} %get-tuple-element.38.refs_2_.refs_1_, bf16[128,128]{1,0:T(8,128)(2,1)S(1)} %get-tuple-element.39.refs_3_.refs_2_, ...), custom_call_target="tpu_custom_call" | custom-call | tf_op jit(solution)/shard_map/turn_next/pallas_call | solution.py:59
  48.5 2.4 %collective-permute-done.21.refs_5_.refs_6_ = bf16[128,1024]{1,0:T(8,128)(2,1)S(1)} collective-permute-done((bf16[128,1024]{1,0:T(8,128)(2,1)S(1)}, bf16[128,1024]{1,0:T(8,128)(2,1)S(1)}, u32[]{:S(2)}, u32[]{:S(2)}) %collective-permute-start.21) | collective-permute-done | bytes 262176 | tf_op jit(solution)/shard_map/ppermute | solution.py:525
  51.2 3.7 %collective-permute-start.23 = (bf16[128,1024]{1,0:T(8,128)(2,1)S(1)}, bf16[128,1024]{1,0:T(8,128)(2,1)S(1)}, u32[]{:S(2)}, u32[]{:S(2)}) collective-permute-start(bf16[128,1024]{1,0:T(8,128)(2,1)S(1)} %regrid.1.refs_2_), channel_id=1, source_target_pairs={{0,4},{1,5},{2,6},{3,7},{4,0},{5,1},{6,2},{7,3},{8,12},{9,13},{10,... | collective-permute-start | bytes 786440 | tf_op jit(solution)/shard_map/ppermute | solution.py:525
  55.6 1.4 %collective-permute-start.25 = (bf16[128,1024]{1,0:T(8,128)(2,1)S(1)}, bf16[128,1024]{1,0:T(8,128)(2,1)S(1)}, u32[]{:S(2)}, u32[]{:S(2)}) collective-permute-start(bf16[128,1024]{1,0:T(8,128)(2,1)S(1)} %regrid.1.refs_2_), channel_id=1, source_target_pairs={{0,2},{1,3},{2,0},{3,1},{4,6},{5,7},{6,4},{7,5},{8,10},{9,11},{10,... | collective-permute-start | bytes 786440 | tf_op jit(solution)/shard_map/ppermute | solution.py:525
  57.3 1.1 %hidden.1 = (bf16[128,1024]{1,0:T(8,128)(2,1)}, f32[8,128]{1,0:T(8,128)S(1)}) custom-call(bf16[128,1024]{1,0:T(8,128)(2,1)S(1)} %copy-done.1, f32[2,1024]{1,0:T(2,128)S(1)} %get-tuple-element.49.refs_1_, bf16[128,128]{1,0:T(8,128)(2,1)S(1)} %get-tuple-element.39.refs_3_.refs_2_, bf16[2,128,1024]{2,1,0:T(8,128)(2,1)S(1)} %get-tuple-element.50.refs_6_.refs_2_.refs_3_, ...), custom_call_target="tpu_custom_call" | custom-call | tf_op jit(solution)/shard_map/hidden/pallas_call | solution.py:59
  58.4 0.9 collective-permute-done.23.refs_0_
  59.2 2.8 %collective-permute-done.25.refs_2_.refs_4_ = bf16[128,1024]{1,0:T(8,128)(2,1)S(1)} collective-permute-done((bf16[128,1024]{1,0:T(8,128)(2,1)S(1)}, bf16[128,1024]{1,0:T(8,128)(2,1)S(1)}, u32[]{:S(2)}, u32[]{:S(2)}) %collective-permute-start.25) | collective-permute-done | bytes 262176 | tf_op jit(solution)/shard_map/ppermute | solution.py:525
  62.0 2.6 %collective-permute-start.26 = (bf16[128,1024]{1,0:T(8,128)(2,1)S(1)}, bf16[128,1024]{1,0:T(8,128)(2,1)S(1)}, u32[]{:S(2)}, u32[]{:S(2)}) collective-permute-start(bf16[128,1024]{1,0:T(8,128)(2,1)S(1)} %get-tuple-element.71.refs_0_), channel_id=1, source_target_pairs={{0,4},{1,5},{2,6},{3,7},{4,0},{5,1},{6,2},{7,3},{8,12},{9,13},{10,... | collective-permute-start | bytes 786440 | tf_op jit(solution)/shard_map/ppermute | solution.py:525
  64.6 1.4 %collective-permute-start.27 = (bf16[128,1024]{1,0:T(8,128)(2,1)S(1)}, bf16[128,1024]{1,0:T(8,128)(2,1)S(1)}, u32[]{:S(2)}, u32[]{:S(2)}) collective-permute-start(bf16[128,1024]{1,0:T(8,128)(2,1)S(1)} %get-tuple-element.70.refs_3_), channel_id=1, source_target_pairs={{0,2},{1,3},{2,0},{3,1},{4,6},{5,7},{6,4},{7,5},{8,10},{9,11},{10,... | collective-permute-start | bytes 786440 | tf_op jit(solution)/shard_map/ppermute | solution.py:525
  67.0 2.0 %collective-permute-done.26.refs_1_ = bf16[128,1024]{1,0:T(8,128)(2,1)S(1)} collective-permute-done((bf16[128,1024]{1,0:T(8,128)(2,1)S(1)}, bf16[128,1024]{1,0:T(8,128)(2,1)S(1)}, u32[]{:S(2)}, u32[]{:S(2)}) %collective-permute-start.26) | collective-permute-done | bytes 262176 | tf_op jit(solution)/shard_map/ppermute | solution.py:525
  68.9 4.8 %collective-permute-done.27.refs_2_.refs_4_ = bf16[128,1024]{1,0:T(8,128)(2,1)S(1)} collective-permute-done((bf16[128,1024]{1,0:T(8,128)(2,1)S(1)}, bf16[128,1024]{1,0:T(8,128)(2,1)S(1)}, u32[]{:S(2)}, u32[]{:S(2)}) %collective-permute-start.27) | collective-permute-done | bytes 262176 | tf_op jit(solution)/shard_map/ppermute | solution.py:525
  73.7 1.4 %collective-permute-start.30 = (bf16[128,1024]{1,0:T(8,128)(2,1)S(1)}, bf16[128,1024]{1,0:T(8,128)(2,1)S(1)}, u32[]{:S(2)}, u32[]{:S(2)}) collective-permute-start(bf16[128,1024]{1,0:T(8,128)(2,1)S(1)} %choose.2.refs_3_), channel_id=1, source_target_pairs={{0,2},{1,3},{2,0},{3,1},{4,6},{5,7},{6,4},{7,5},{8,10},{9,11},{10,... | collective-permute-start | bytes 786440 | tf_op jit(solution)/shard_map/ppermute | solution.py:525
  75.5 6.6 %collective-permute-done.30.refs_2_.refs_4_ = bf16[128,1024]{1,0:T(8,128)(2,1)S(1)} collective-permute-done((bf16[128,1024]{1,0:T(8,128)(2,1)S(1)}, bf16[128,1024]{1,0:T(8,128)(2,1)S(1)}, u32[]{:S(2)}, u32[]{:S(2)}) %collective-permute-start.30) | collective-permute-done | bytes 262176 | tf_op jit(solution)/shard_map/ppermute | solution.py:525
  82.1 1.4 %collective-permute-start.31 = (bf16[128,1024]{1,0:T(8,128)(2,1)S(1)}, bf16[128,1024]{1,0:T(8,128)(2,1)S(1)}, u32[]{:S(2)}, u32[]{:S(2)}) collective-permute-start(bf16[128,1024]{1,0:T(8,128)(2,1)S(1)} %choose.3.refs_3_), channel_id=1, source_target_pairs={{0,2},{1,3},{2,0},{3,1},{4,6},{5,7},{6,4},{7,5},{8,10},{9,11},{10,... | collective-permute-start | bytes 786440 | tf_op jit(solution)/shard_map/ppermute | solution.py:525
  83.9 4.7 %collective-permute-done.31.refs_3_ = bf16[128,1024]{1,0:T(8,128)(2,1)S(1)} collective-permute-done((bf16[128,1024]{1,0:T(8,128)(2,1)S(1)}, bf16[128,1024]{1,0:T(8,128)(2,1)S(1)}, u32[]{:S(2)}, u32[]{:S(2)}) %collective-permute-start.31) | collective-permute-done | bytes 262176 | tf_op jit(solution)/shard_map/ppermute | solution.py:525
  88.9 1.3 %collective-permute-done.32.refs_1_ = f32[128,256]{1,0:T(8,128)S(1)} collective-permute-done((f32[128,256]{1,0:T(8,128)S(1)}, f32[128,256]{1,0:T(8,128)S(1)}, u32[]{:S(2)}, u32[]{:S(2)}) %collective-permute-start.32) | collective-permute-done | bytes 131104 | tf_op jit(solution)/shard_map/ppermute | solution.py:525
  90.3 0.7 finish.1
  (63 shorter events, 11.0 us)
Async XLA Ops:
  6.0 3.1 %collective-permute-start.3 = (bf16[1,128,1024]{2,1,0:T(8,128)(2,1)S(1)}, bf16[1,128,1024]{2,1,0:T(8,128)(2,1)S(1)}, u32[]{:S(2)}, u32[]{:S(2)}) collective-permute-start(bf16[1,128,1024]{2,1,0:T(8,128)(2,1)S(1)} %get-tuple-element.47), channel_id=1, source_target_pairs={{0,1},{1,0},{2,3},{3,2},{4,5},{5,4},{6,7},{7,6},{8,9},{9,8},{10,11... | collective-permute-start | bytes 786440 | tf_op jit(solution)/shard_map/ppermute | solution.py:525
  8.4 5.2 %collective-permute-start = (bf16[1,128,1024]{2,1,0:T(8,128)(2,1)S(1)}, bf16[1,128,1024]{2,1,0:T(8,128)(2,1)S(1)}, u32[]{:S(2)}, u32[]{:S(2)}) collective-permute-start(bf16[1,128,1024]{2,1,0:T(8,128)(2,1)S(1)} %get-tuple-element.43), channel_id=1, source_target_pairs={{0,1},{1,0},{2,3},{3,2},{4,5},{5,4},{6,7},{7,6},{8,9},{9,8},{10,11... | collective-permute-start | bytes 786440 | tf_op jit(solution)/shard_map/ppermute | solution.py:525
  8.5 5.0 %collective-permute-start.1 = (bf16[1,128,1024]{2,1,0:T(8,128)(2,1)S(1)}, bf16[1,128,1024]{2,1,0:T(8,128)(2,1)S(1)}, u32[]{:S(2)}, u32[]{:S(2)}) collective-permute-start(bf16[1,128,1024]{2,1,0:T(8,128)(2,1)S(1)} %get-tuple-element.44), channel_id=1, source_target_pairs={{0,1},{1,0},{2,3},{3,2},{4,5},{5,4},{6,7},{7,6},{8,9},{9,8},{10,11... | collective-permute-start | bytes 786440 | tf_op jit(solution)/shard_map/ppermute | solution.py:525
  9.0 4.6 %collective-permute-start.2 = (bf16[1,128,1024]{2,1,0:T(8,128)(2,1)S(1)}, bf16[1,128,1024]{2,1,0:T(8,128)(2,1)S(1)}, u32[]{:S(2)}, u32[]{:S(2)}) collective-permute-start(bf16[1,128,1024]{2,1,0:T(8,128)(2,1)S(1)} %get-tuple-element.45), channel_id=1, source_target_pairs={{0,1},{1,0},{2,3},{3,2},{4,5},{5,4},{6,7},{7,6},{8,9},{9,8},{10,11... | collective-permute-start | bytes 786440 | tf_op jit(solution)/shard_map/ppermute | solution.py:525
  9.1 9.5 %collective-permute-start.4 = (bf16[128,1024]{1,0:T(8,128)(2,1)S(1)}, bf16[128,1024]{1,0:T(8,128)(2,1)S(1)}, u32[]{:S(2)}, u32[]{:S(2)}) collective-permute-start(bf16[128,1024]{1,0:T(8,128)(2,1)S(1)} %add_up.4.refs_4_), channel_id=1, source_target_pairs={{0,2},{1,3},{2,0},{3,1},{4,6},{5,7},{6,4},{7,5},{8,10},{9,11},{10,... | collective-permute-start | bytes 786440 | tf_op jit(solution)/shard_map/ppermute | solution.py:525
  12.8 15.0 %collective-permute-start.6 = (bf16[2,128,1024]{2,1,0:T(8,128)(2,1)S(1)}, bf16[2,128,1024]{2,1,0:T(8,128)(2,1)S(1)}, u32[]{:S(2)}, u32[]{:S(2)}) collective-permute-start(bf16[2,128,1024]{2,1,0:T(8,128)(2,1)S(1)} %partials.4.refs_4_), channel_id=1, source_target_pairs={{0,1},{1,0},{2,3},{3,2},{4,5},{5,4},{6,7},{7,6},{8,9},{9,8},{10,11... | collective-permute-start | bytes 1572872 | tf_op jit(solution)/shard_map/ppermute | solution.py:525
  18.8 7.8 %collective-permute-start.7 = (bf16[128,1024]{1,0:T(8,128)(2,1)S(1)}, bf16[128,1024]{1,0:T(8,128)(2,1)S(1)}, u32[]{:S(2)}, u32[]{:S(2)}) collective-permute-start(bf16[128,1024]{1,0:T(8,128)(2,1)S(1)} %get-tuple-element.52), channel_id=1, source_target_pairs={{0,2},{1,3},{2,0},{3,1},{4,6},{5,7},{6,4},{7,5},{8,10},{9,11},{10,... | collective-permute-start | bytes 786440 | tf_op jit(solution)/shard_map/ppermute | solution.py:525
  20.6 7.2 %collective-permute-start.8 = (bf16[128,1024]{1,0:T(8,128)(2,1)S(1)}, bf16[128,1024]{1,0:T(8,128)(2,1)S(1)}, u32[]{:S(2)}, u32[]{:S(2)}) collective-permute-start(bf16[128,1024]{1,0:T(8,128)(2,1)S(1)} %get-tuple-element.48.refs_3_), channel_id=1, source_target_pairs={{0,4},{1,5},{2,6},{3,7},{4,0},{5,1},{6,2},{7,3},{8,12},{9,13},{10,... | collective-permute-start | bytes 786440 | tf_op jit(solution)/shard_map/ppermute | solution.py:525
  22.6 5.7 %collective-permute-start.12 = (bf16[1,1024,128]{2,1,0:T(8,128)(2,1)S(1)}, bf16[1,1024,128]{2,1,0:T(8,128)(2,1)S(1)}, u32[]{:S(2)}, u32[]{:S(2)}) collective-permute-start(bf16[1,1024,128]{2,1,0:T(8,128)(2,1)S(1)} %get-tuple-element.53.refs_9_), channel_id=1, source_target_pairs={{0,1},{1,0},{2,3},{3,2},{4,5},{5,4},{6,7},{7,6},{8,9},{9,8},{10,11... | collective-permute-start | bytes 786440 | tf_op jit(solution)/shard_map/ppermute | solution.py:525
  22.7 5.7 %collective-permute-start.13 = (bf16[1,1024,128]{2,1,0:T(8,128)(2,1)S(1)}, bf16[1,1024,128]{2,1,0:T(8,128)(2,1)S(1)}, u32[]{:S(2)}, u32[]{:S(2)}) collective-permute-start(bf16[1,1024,128]{2,1,0:T(8,128)(2,1)S(1)} %get-tuple-element.57), channel_id=1, source_target_pairs={{0,1},{1,0},{2,3},{3,2},{4,5},{5,4},{6,7},{7,6},{8,9},{9,8},{10,11... | collective-permute-start | bytes 786440 | tf_op jit(solution)/shard_map/ppermute | solution.py:525
  26.7 2.2 %collective-permute-start.14 = (bf16[1,1024,128]{2,1,0:T(8,128)(2,1)S(1)}, bf16[1,1024,128]{2,1,0:T(8,128)(2,1)S(1)}, u32[]{:S(2)}, u32[]{:S(2)}) collective-permute-start(bf16[1,1024,128]{2,1,0:T(8,128)(2,1)S(1)} %get-tuple-element.58), channel_id=1, source_target_pairs={{0,1},{1,0},{2,3},{3,2},{4,5},{5,4},{6,7},{7,6},{8,9},{9,8},{10,11... | collective-permute-start | bytes 786440 | tf_op jit(solution)/shard_map/ppermute | solution.py:525
  27.8 5.7 %collective-permute-start.5 = (bf16[2,128,1024]{2,1,0:T(8,128)(2,1)S(1)}, bf16[2,128,1024]{2,1,0:T(8,128)(2,1)S(1)}, u32[]{:S(2)}, u32[]{:S(2)}) collective-permute-start(bf16[2,128,1024]{2,1,0:T(8,128)(2,1)S(1)} %partials.5.refs_5_), channel_id=1, source_target_pairs={{0,1},{1,0},{2,3},{3,2},{4,5},{5,4},{6,7},{7,6},{8,9},{9,8},{10,11... | collective-permute-start | bytes 1572872 | tf_op jit(solution)/shard_map/ppermute | solution.py:525
  27.8 2.3 %collective-permute-start.15 = (bf16[1,1024,128]{2,1,0:T(8,128)(2,1)S(1)}, bf16[1,1024,128]{2,1,0:T(8,128)(2,1)S(1)}, u32[]{:S(2)}, u32[]{:S(2)}) collective-permute-start(bf16[1,1024,128]{2,1,0:T(8,128)(2,1)S(1)} %get-tuple-element.59), channel_id=1, source_target_pairs={{0,1},{1,0},{2,3},{3,2},{4,5},{5,4},{6,7},{7,6},{8,9},{9,8},{10,11... | collective-permute-start | bytes 786440 | tf_op jit(solution)/shard_map/ppermute | solution.py:525
  28.3 2.1 %collective-permute-start.16 = (bf16[1,1024,128]{2,1,0:T(8,128)(2,1)S(1)}, bf16[1,1024,128]{2,1,0:T(8,128)(2,1)S(1)}, u32[]{:S(2)}, u32[]{:S(2)}) collective-permute-start(bf16[1,1024,128]{2,1,0:T(8,128)(2,1)S(1)} %get-tuple-element.60), channel_id=1, source_target_pairs={{0,1},{1,0},{2,3},{3,2},{4,5},{5,4},{6,7},{7,6},{8,9},{9,8},{10,11... | collective-permute-start | bytes 786440 | tf_op jit(solution)/shard_map/ppermute | solution.py:525
  28.4 3.6 %collective-permute-start.17 = (bf16[1,1024,128]{2,1,0:T(8,128)(2,1)S(1)}, bf16[1,1024,128]{2,1,0:T(8,128)(2,1)S(1)}, u32[]{:S(2)}, u32[]{:S(2)}) collective-permute-start(bf16[1,1024,128]{2,1,0:T(8,128)(2,1)S(1)} %get-tuple-element.61), channel_id=1, source_target_pairs={{0,1},{1,0},{2,3},{3,2},{4,5},{5,4},{6,7},{7,6},{8,9},{9,8},{10,11... | collective-permute-start | bytes 786440 | tf_op jit(solution)/shard_map/ppermute | solution.py:525
  28.9 3.9 %collective-permute-start.18 = (bf16[1,1024,128]{2,1,0:T(8,128)(2,1)S(1)}, bf16[1,1024,128]{2,1,0:T(8,128)(2,1)S(1)}, u32[]{:S(2)}, u32[]{:S(2)}) collective-permute-start(bf16[1,1024,128]{2,1,0:T(8,128)(2,1)S(1)} %get-tuple-element.62), channel_id=1, source_target_pairs={{0,1},{1,0},{2,3},{3,2},{4,5},{5,4},{6,7},{7,6},{8,9},{9,8},{10,11... | collective-permute-start | bytes 786440 | tf_op jit(solution)/shard_map/ppermute | solution.py:525
  30.1 3.4 %collective-permute-start.19 = (bf16[1,1024,128]{2,1,0:T(8,128)(2,1)S(1)}, bf16[1,1024,128]{2,1,0:T(8,128)(2,1)S(1)}, u32[]{:S(2)}, u32[]{:S(2)}) collective-permute-start(bf16[1,1024,128]{2,1,0:T(8,128)(2,1)S(1)} %get-tuple-element.63), channel_id=1, source_target_pairs={{0,1},{1,0},{2,3},{3,2},{4,5},{5,4},{6,7},{7,6},{8,9},{9,8},{10,11... | collective-permute-start | bytes 786440 | tf_op jit(solution)/shard_map/ppermute | solution.py:525
  30.5 8.4 %collective-permute-start.10 = (bf16[128,1024]{1,0:T(8,128)(2,1)S(1)}, bf16[128,1024]{1,0:T(8,128)(2,1)S(1)}, u32[]{:S(2)}, u32[]{:S(2)}) collective-permute-start(bf16[128,1024]{1,0:T(8,128)(2,1)S(1)} %get-tuple-element.55), channel_id=1, source_target_pairs={{0,4},{1,5},{2,6},{3,7},{4,0},{5,1},{6,2},{7,3},{8,12},{9,13},{10,... | collective-permute-start | bytes 786440 | tf_op jit(solution)/shard_map/ppermute | solution.py:525
  32.1 6.8 %collective-permute-start.11 = (bf16[128,1024]{1,0:T(8,128)(2,1)S(1)}, bf16[128,1024]{1,0:T(8,128)(2,1)S(1)}, u32[]{:S(2)}, u32[]{:S(2)}) collective-permute-start(bf16[128,1024]{1,0:T(8,128)(2,1)S(1)} %get-tuple-element.56), channel_id=1, source_target_pairs={{0,0},{1,1},{2,2},{3,3},{4,8},{5,9},{6,10},{7,11},{8,4},{9,5},{10,... | collective-permute-start | bytes 786440 | tf_op jit(solution)/shard_map/ppermute | solution.py:525
  32.7 8.1 %collective-permute-start.9 = (bf16[128,1024]{1,0:T(8,128)(2,1)S(1)}, bf16[128,1024]{1,0:T(8,128)(2,1)S(1)}, u32[]{:S(2)}, u32[]{:S(2)}) collective-permute-start(bf16[128,1024]{1,0:T(8,128)(2,1)S(1)} %get-tuple-element.54), channel_id=1, source_target_pairs={{0,2},{1,3},{2,0},{3,1},{4,6},{5,7},{6,4},{7,5},{8,10},{9,11},{10,... | collective-permute-start | bytes 786440 | tf_op jit(solution)/shard_map/ppermute | solution.py:525
  41.2 7.3 %collective-permute-start.20 = (bf16[128,1024]{1,0:T(8,128)(2,1)S(1)}, bf16[128,1024]{1,0:T(8,128)(2,1)S(1)}, u32[]{:S(2)}, u32[]{:S(2)}) collective-permute-start(bf16[128,1024]{1,0:T(8,128)(2,1)S(1)} %get-tuple-element.64), channel_id=1, source_target_pairs={{0,2},{1,3},{2,0},{3,1},{4,6},{5,7},{6,4},{7,5},{8,10},{9,11},{10,... | collective-permute-start | bytes 786440 | tf_op jit(solution)/shard_map/ppermute | solution.py:525
  41.9 9.0 %collective-permute-start.21 = (bf16[128,1024]{1,0:T(8,128)(2,1)S(1)}, bf16[128,1024]{1,0:T(8,128)(2,1)S(1)}, u32[]{:S(2)}, u32[]{:S(2)}) collective-permute-start(bf16[128,1024]{1,0:T(8,128)(2,1)S(1)} %get-tuple-element.65.refs_12_), channel_id=1, source_target_pairs={{0,4},{1,5},{2,6},{3,7},{4,0},{5,1},{6,2},{7,3},{8,12},{9,13},{10,... | collective-permute-start | bytes 786440 | tf_op jit(solution)/shard_map/ppermute | solution.py:525
  46.1 4.9 %collective-permute-start.22 = (bf16[128,1024]{1,0:T(8,128)(2,1)S(1)}, bf16[128,1024]{1,0:T(8,128)(2,1)S(1)}, u32[]{:S(2)}, u32[]{:S(2)}) collective-permute-start(bf16[128,1024]{1,0:T(8,128)(2,1)S(1)} %get-tuple-element.66), channel_id=1, source_target_pairs={{0,0},{1,1},{2,2},{3,3},{4,8},{5,9},{6,10},{7,11},{8,4},{9,5},{10,... | collective-permute-start | bytes 786440 | tf_op jit(solution)/shard_map/ppermute | solution.py:525
  51.2 8.0 %collective-permute-start.23 = (bf16[128,1024]{1,0:T(8,128)(2,1)S(1)}, bf16[128,1024]{1,0:T(8,128)(2,1)S(1)}, u32[]{:S(2)}, u32[]{:S(2)}) collective-permute-start(bf16[128,1024]{1,0:T(8,128)(2,1)S(1)} %regrid.1.refs_2_), channel_id=1, source_target_pairs={{0,4},{1,5},{2,6},{3,7},{4,0},{5,1},{6,2},{7,3},{8,12},{9,13},{10,... | collective-permute-start | bytes 786440 | tf_op jit(solution)/shard_map/ppermute | solution.py:525
  54.9 4.4 %collective-permute-start.24 = (bf16[128,1024]{1,0:T(8,128)(2,1)S(1)}, bf16[128,1024]{1,0:T(8,128)(2,1)S(1)}, u32[]{:S(2)}, u32[]{:S(2)}) collective-permute-start(bf16[128,1024]{1,0:T(8,128)(2,1)S(1)} %regrid.1.refs_2_), channel_id=1, source_target_pairs={{0,0},{1,1},{2,2},{3,3},{4,8},{5,9},{6,10},{7,11},{8,4},{9,5},{10,... | collective-permute-start | bytes 786440 | tf_op jit(solution)/shard_map/ppermute | solution.py:525
  55.6 6.4 %collective-permute-start.25 = (bf16[128,1024]{1,0:T(8,128)(2,1)S(1)}, bf16[128,1024]{1,0:T(8,128)(2,1)S(1)}, u32[]{:S(2)}, u32[]{:S(2)}) collective-permute-start(bf16[128,1024]{1,0:T(8,128)(2,1)S(1)} %regrid.1.refs_2_), channel_id=1, source_target_pairs={{0,2},{1,3},{2,0},{3,1},{4,6},{5,7},{6,4},{7,5},{8,10},{9,11},{10,... | collective-permute-start | bytes 786440 | tf_op jit(solution)/shard_map/ppermute | solution.py:525
  62.0 6.9 %collective-permute-start.26 = (bf16[128,1024]{1,0:T(8,128)(2,1)S(1)}, bf16[128,1024]{1,0:T(8,128)(2,1)S(1)}, u32[]{:S(2)}, u32[]{:S(2)}) collective-permute-start(bf16[128,1024]{1,0:T(8,128)(2,1)S(1)} %get-tuple-element.71.refs_0_), channel_id=1, source_target_pairs={{0,4},{1,5},{2,6},{3,7},{4,0},{5,1},{6,2},{7,3},{8,12},{9,13},{10,... | collective-permute-start | bytes 786440 | tf_op jit(solution)/shard_map/ppermute | solution.py:525
  64.6 9.1 %collective-permute-start.27 = (bf16[128,1024]{1,0:T(8,128)(2,1)S(1)}, bf16[128,1024]{1,0:T(8,128)(2,1)S(1)}, u32[]{:S(2)}, u32[]{:S(2)}) collective-permute-start(bf16[128,1024]{1,0:T(8,128)(2,1)S(1)} %get-tuple-element.70.refs_3_), channel_id=1, source_target_pairs={{0,2},{1,3},{2,0},{3,1},{4,6},{5,7},{6,4},{7,5},{8,10},{9,11},{10,... | collective-permute-start | bytes 786440 | tf_op jit(solution)/shard_map/ppermute | solution.py:525
  65.9 9.2 %collective-permute-start.28 = (bf16[128,1024]{1,0:T(8,128)(2,1)S(1)}, bf16[128,1024]{1,0:T(8,128)(2,1)S(1)}, u32[]{:S(2)}, u32[]{:S(2)}) collective-permute-start(bf16[128,1024]{1,0:T(8,128)(2,1)S(1)} %get-tuple-element.70.refs_3_), channel_id=1, source_target_pairs={{0,0},{1,1},{2,2},{3,3},{4,8},{5,9},{6,10},{7,11},{8,4},{9,5},{10,... | collective-permute-start | bytes 786440 | tf_op jit(solution)/shard_map/ppermute | solution.py:525
  73.7 8.4 %collective-permute-start.30 = (bf16[128,1024]{1,0:T(8,128)(2,1)S(1)}, bf16[128,1024]{1,0:T(8,128)(2,1)S(1)}, u32[]{:S(2)}, u32[]{:S(2)}) collective-permute-start(bf16[128,1024]{1,0:T(8,128)(2,1)S(1)} %choose.2.refs_3_), channel_id=1, source_target_pairs={{0,2},{1,3},{2,0},{3,1},{4,6},{5,7},{6,4},{7,5},{8,10},{9,11},{10,... | collective-permute-start | bytes 786440 | tf_op jit(solution)/shard_map/ppermute | solution.py:525
  75.2 7.0 %collective-permute-start.29 = (bf16[128,1024]{1,0:T(8,128)(2,1)S(1)}, bf16[128,1024]{1,0:T(8,128)(2,1)S(1)}, u32[]{:S(2)}, u32[]{:S(2)}) collective-permute-start(bf16[128,1024]{1,0:T(8,128)(2,1)S(1)} %collective-permute-done.28.refs_0_), channel_id=1, source_target_pairs={{0,4},{1,5},{2,6},{3,7},{4,0},{5,1},{6,2},{7,3},{8,12},{9,13},{10,... | collective-permute-start | bytes 786440 | tf_op jit(solution)/shard_map/ppermute | solution.py:525
  82.1 6.4 %collective-permute-start.31 = (bf16[128,1024]{1,0:T(8,128)(2,1)S(1)}, bf16[128,1024]{1,0:T(8,128)(2,1)S(1)}, u32[]{:S(2)}, u32[]{:S(2)}) collective-permute-start(bf16[128,1024]{1,0:T(8,128)(2,1)S(1)} %choose.3.refs_3_), channel_id=1, source_target_pairs={{0,2},{1,3},{2,0},{3,1},{4,6},{5,7},{6,4},{7,5},{8,10},{9,11},{10,... | collective-permute-start | bytes 786440 | tf_op jit(solution)/shard_map/ppermute | solution.py:525
  (4 other events, 38.0 us)

commit v4 on v3

--- a/solution.py
+++ b/solution.py
@@ -51,22 +51,22 @@
 
 
 def kernel_call(kernel, out_shape, arrays, specs, after=(), scratch=(), aliases=None, limit=24, name=None):
-    count, extra = len(arrays), len(after)
+    extra = len(after)
 
     def ordered(*refs):
-        kernel(*refs[:count], *refs[count + extra :])
+        kernel(*refs[extra:])
 
     return pl.pallas_call(
         ordered,
         out_shape=out_shape,
-        in_specs=list(specs) + [anywhere()] * extra,
+        in_specs=[anywhere()] * extra + list(specs),
         out_specs=jax.tree.map(lambda _: vmem(), out_shape),
         scratch_shapes=list(scratch),
         input_output_aliases=aliases or {},
         cost_estimate=pl.CostEstimate(flops=0, bytes_accessed=0, transcendentals=0),
         compiler_params=pltpu.CompilerParams(vmem_limit_bytes=limit * MIB),
         name=name,
-    )(*arrays, *after)
+    )(*after, *arrays)
 
 
 def gridded(context, h_ref, weight, scale_row, store):
@@ -304,8 +304,8 @@
     return total
 
 
-def regrid_kernel(inner, items, turned_ref, factor_ref, *refs):
-    *ins, grid_ref = refs
+def regrid_kernel(inner, items, *refs):
+    *ins, turned_ref, factor_ref, grid_ref = refs
     for i in range(turned_ref.shape[1] // ROT):
         part = slice(i * ROT, (i + 1) * ROT)
         value = turned_ref[:, part] + summed_at(inner, items, ins, part) * factor_ref[0:1, part]
@@ -316,7 +316,7 @@
     return kernel_call(
         functools.partial(regrid_kernel, inner, items),
         jax.ShapeDtypeStruct(turned.shape, BF16),
-        [turned, factors, *arrays],
+        [*arrays, turned, factors],
         [vmem()] * (2 + len(arrays)),
         after=after,
         name="regrid",
@@ -376,7 +376,7 @@
         pass
 
     shapes = [jax.ShapeDtypeStruct(array.shape, array.dtype) for array in arrays]
-    aliases = {i: i for i in range(len(arrays))}
+    aliases = {len(after) + i: i for i in range(len(arrays))}
     specs = [vmem()] * len(arrays)
     return kernel_call(kernel, shapes, arrays, specs, after=after, aliases=aliases, name="gate")
 
@@ -390,7 +390,7 @@
 
 
 def select_rows(inner, weight, cols, after=()):
-    parts = 2 * OUTER
+    parts = 2
     each = OUTER * inner // parts
     return kernel_call(
         functools.partial(select_rows_kernel, inner, cols),
@@ -590,7 +590,7 @@
 
     came1 = came(1, come1)
     near1 = part2(0) + added(came1)
-    *pay2, end1 = sums(own2 | came1, [*(part2(1 + s) for s in shifts), near1], after=[send4])
+    *pay2, end1 = sums(came1 | own2, [*(part2(1 + s) for s in shifts), near1], after=[send4])
     came2 = came(2, [shift_mid(pay, s) for s, pay in zip(shifts, pay2)])
     from_end1 = {"end1": swap_pairs(end1)}
     turned_residual, factors = turn_residual(inner, residual, rows, had, after=[end1])
@@ -599,7 +599,7 @@
 
     near2 = part2(1) + added(came2)
     *pay3, end2, mid2 = sums(
-        own2 | own3 | came1 | came2 | from_end1,
+        came2 | from_end1 | own2 | own3 | came1,
         [*(part(3, s) for s in shifts), near2, near1 + [("end1", None, True)]],
         after=picked[:1],
     )
@@ -608,47 +608,45 @@
     from_mid2 = {"mid2": swap_middle(mid2)}
 
     *pay4, mid3, near3 = sums(
-        own2 | own3 | own4 | came2 | came3 | from_end2 | from_mid2,
+        came3 | from_end2 | from_mid2 | own2 | own3 | own4 | came2,
         [
             *(part(4, s) for s in shifts),
             near2 + [("end2", None, True)],
             part(3, 0) + added(came3) + [("mid2", None, True)],
         ],
-        after=next_other,
+
     )
     come4 = [shift_mid(pay, s) for s, pay in zip(shifts, pay4)]
     from_mid3 = swap_middle(mid3)
     from_near3 = swap_pairs(near3)
 
     gain = norm_gain.astype(F32).reshape(-1, ROT)
-    turned_next = turn_next(inner, next_query_weight, next_other, gain, rows, had, after=[near3])
-
-    last = [keep4, other4, *come4, from_near3, from_mid3]
-    items = [(0, False)] * 2 + [(None, False)] * (len(come4) + 1) + [(None, True)]
-    grid = regrid(inner, items, turned_residual, factors, last, after=[turned_next])
+
+    last = [*come4, from_near3, from_mid3, keep4, other4]
+    items = [(None, False)] * (len(come4) + 1) + [(None, True)] + [(0, False)] * 2
+    grid = regrid(inner, items, turned_residual, factors, last)
 
     x1 = [shift_mid(grid, s) for s in shifts]
     near = swap_pairs(grid)
     mid1 = swap_middle(grid)
-    acc = project(inner, turned_next, rows, None, [(0, 0, grid)])
-    hidden_out, mark = hidden(inner, items, residual, factors, had, last, after=[acc])
+    hidden_out, mark = hidden(inner, items, residual, factors, had, last, after=[grid])
     near, mid1 = gate([near, mid1], after=[*x1, mark])
     x2 = [shift_mid(near, s) for s in shifts]
     ends2 = swap_pairs(mid1)
     mids2 = swap_middle(near)
-    acc = project(
-        inner, turned_next, rows, acc, [(1, 0, near)] + [(0, s, x1[s - 1]) for s in shifts]
-    )
-    third = choose(inner, mid1, ends2, after=[*x2, acc])
+    third = choose(inner, mid1, ends2, after=x2)
     x3 = [shift_mid(third, s) for s in shifts]
     ends3 = swap_pairs(mids2)
-    acc = project(
-        inner, turned_next, rows, acc, [(2, 0, third)] + [(1, s, x2[s - 1]) for s in shifts]
-    )
-    fourth = choose(inner, mids2, ends3, after=[*x3, acc])
+    turned_next = turn_next(inner, next_query_weight, next_other, gain, rows, had, after=[third])
+    fourth = choose(inner, mids2, ends3, after=[*x3, turned_next])
     x4 = [shift_mid(fourth, s) for s in shifts]
     acc = project(
-        inner, turned_next, rows, acc, [(3, 0, fourth)] + [(2, s, x3[s - 1]) for s in shifts]
+        inner,
+        turned_next,
+        rows,
+        None,
+        [(0, 0, grid), (1, 0, near), (2, 0, third), (3, 0, fourth)]
+        + [(phase, s, x[s - 1]) for phase, x in enumerate((x1, x2, x3)) for s in shifts],
     )
     own, other = project(
         inner, turned_next, rows, acc, [(3, s, x4[s - 1]) for s in shifts], split=True

time: 91.2 us -> 85.6 us (0.939)
  waiting for transfers between devices: 44.1 us -> 36.6 us
  starting transfers between devices: 31.2 us -> 33.6 us
    ppermute x33 -> x27, waiting for transfers between devices: 44.1 us -> 36.6 us  [permute(): return lax.ppermute(value, 'tp', moves)]
    ppermute x33 -> x27, starting transfers between devices: 31.2 us -> 33.6 us  [permute(): return lax.ppermute(value, 'tp', moves)]
    pallas_call x22 -> x19, Pallas kernels: 14.8 us -> 14.3 us  [kernel_call(): pl.pallas_call(ordered, out_shape=out_shape, in_specs=[anywhere()] * extr...]
  transfers between devices with their start and end apart: 33 -> 27, of which waited for: 16 -> 14; matrix products, arithmetic and copies ran while one was open for 0% -> 0% of each run, Pallas kernels for 9% -> 9%
where the time goes in v4:
time: 85.6 us; the launch traced here: 85.3 us
  waiting for transfers between devices  36.6 us (43%)
  starting transfers between devices  33.6 us (39%)
  Pallas kernels  14.3 us (17%)
  between operations  0.89 us (1%)
    ppermute x27, waiting for transfers between devices, permute(): return lax.ppermute(value, 'tp', moves)  36.6 us
    ppermute x27, starting transfers between devices, permute(): return lax.ppermute(value, 'tp', moves)  33.6 us
    pallas_call x19, Pallas kernels, kernel_call(): pl.pallas_call(ordered, out_shape=out_shape, in_specs=[anywhere()] * extr...  14.3 us
  transfers between devices with their start and end apart: 27, of which 14 were waited for; matrix products, arithmetic and copies ran while one was open for 0% of the time, Pallas kernels for 9%

profile of v4, /device:TPU:0, one launch (start us, length us, event | category | flops | bytes accessed | tf_op | source)
XLA Modules:
  0.0 85.3 jit_solution(10688754253203522928)
XLA Ops:
  0.6 5.4 %attend.1 = (bf16[128,128]{1,0:T(8,128)(2,1)S(1)}, f32[2,128,128]{2,1,0:T(8,128)S(1)}, bf16[1,128,1024]{2,1,0:T(8,128)(2,1)S(1)}, bf16[128,16384]{1,0:T(8,128)(2,1)S(1)}, bf16[128,128]{1,0:T(8,128)(2,1)S(1)}) custom-call(bf16[1,128,128]{2,1,0:T(8,128)(2,1)} %refs_0_.1, bf16[1,8192,128]{2,1,0:T(8,128)(2,1)} %refs_1_.5, bf16[1,8192,128]{2,1,0:T(8,128)(2,1)} %refs_2_.1, ...), custom_call_target="tpu_custom_call" | custom-call | tf_op jit(solution)/shard_map/attend/pallas_call | solution.py:59
  6.5 1.9 %partials.3 = (bf16[1,128,1024]{2,1,0:T(8,128)(2,1)S(1)}, bf16[3,128,1024]{2,1,0:T(8,128)(2,1)S(1)}, bf16[2,128,1024]{2,1,0:T(8,128)(2,1)S(1)}, bf16[2,128,1024]...) custom-call(bf16[128,128]{1,0:T(8,128)(2,1)S(1)} %get-tuple-element., ...), custom_call_target="tpu_custom_call" | custom-call | tf_op jit(solution)/shard_map/partials/pallas_call | solution.py:59
  9.1 3.0 %collective-permute-start.1 = (bf16[128,1024]{1,0:T(8,128)(2,1)S(1)}, bf16[128,1024]{1,0:T(8,128)(2,1)S(1)}, u32[]{:S(2)}, u32[]{:S(2)}) collective-permute-start(bf16[128,1024]{1,0:T(8,128)(2,1)S(1)} %add_up.4.refs_0_), channel_id=1, source_target_pairs={{0,2},{1,3},{2,0},{3,1},{4,6},{5,7},{6,4},{7,5},{8,10},{9,11},{10,... | collective-permute-start | bytes 786440 | tf_op jit(solution)/shard_map/ppermute | solution.py:525
  12.9 0.7 partials.5.refs_0_
  13.6 5.1 %collective-permute-done.1.refs_1_.refs_9_ = bf16[128,1024]{1,0:T(8,128)(2,1)S(1)} collective-permute-done((bf16[128,1024]{1,0:T(8,128)(2,1)S(1)}, bf16[128,1024]{1,0:T(8,128)(2,1)S(1)}, u32[]{:S(2)}, u32[]{:S(2)}) %collective-permute-start.1) | collective-permute-done | bytes 262176 | tf_op jit(solution)/shard_map/ppermute | solution.py:525
  18.8 1.8 %collective-permute-start.5 = (bf16[128,1024]{1,0:T(8,128)(2,1)S(1)}, bf16[128,1024]{1,0:T(8,128)(2,1)S(1)}, u32[]{:S(2)}, u32[]{:S(2)}) collective-permute-start(bf16[128,1024]{1,0:T(8,128)(2,1)S(1)} %get-tuple-element.45), channel_id=1, source_target_pairs={{0,2},{1,3},{2,0},{3,1},{4,6},{5,7},{6,4},{7,5},{8,10},{9,11},{10,... | collective-permute-start | bytes 786440 | tf_op jit(solution)/shard_map/ppermute | solution.py:525
  20.6 1.6 %collective-permute-start.6 = (bf16[128,1024]{1,0:T(8,128)(2,1)S(1)}, bf16[128,1024]{1,0:T(8,128)(2,1)S(1)}, u32[]{:S(2)}, u32[]{:S(2)}) collective-permute-start(bf16[128,1024]{1,0:T(8,128)(2,1)S(1)} %get-tuple-element.42.refs_0_), channel_id=1, source_target_pairs={{0,4},{1,5},{2,6},{3,7},{4,0},{5,1},{6,2},{7,3},{8,12},{9,13},{10,... | collective-permute-start | bytes 786440 | tf_op jit(solution)/shard_map/ppermute | solution.py:525
  22.6 4.1 %collective-permute-done.5.refs_1_.refs_11_ = bf16[128,1024]{1,0:T(8,128)(2,1)S(1)} collective-permute-done((bf16[128,1024]{1,0:T(8,128)(2,1)S(1)}, bf16[128,1024]{1,0:T(8,128)(2,1)S(1)}, u32[]{:S(2)}, u32[]{:S(2)}) %collective-permute-start.5) | collective-permute-done | bytes 262176 | tf_op jit(solution)/shard_map/ppermute | solution.py:525
  26.7 1.1 %collective-permute-done.6.refs_2_ = bf16[128,1024]{1,0:T(8,128)(2,1)S(1)} collective-permute-done((bf16[128,1024]{1,0:T(8,128)(2,1)S(1)}, bf16[128,1024]{1,0:T(8,128)(2,1)S(1)}, u32[]{:S(2)}, u32[]{:S(2)}) %collective-permute-start.6) | collective-permute-done | bytes 262176 | tf_op jit(solution)/shard_map/ppermute | solution.py:525
  28.1 0.7 collective-permute-start.10
  29.5 4.3 %collective-permute-start.9 = (bf16[128,1024]{1,0:T(8,128)(2,1)S(1)}, bf16[128,1024]{1,0:T(8,128)(2,1)S(1)}, u32[]{:S(2)}, u32[]{:S(2)}) collective-permute-start(bf16[128,1024]{1,0:T(8,128)(2,1)S(1)} %get-tuple-element.48), channel_id=1, source_target_pairs={{0,4},{1,5},{2,6},{3,7},{4,0},{5,1},{6,2},{7,3},{8,12},{9,13},{10,... | collective-permute-start | bytes 786440 | tf_op jit(solution)/shard_map/ppermute | solution.py:525
  33.8 1.4 %collective-permute-done.8.refs_0_ = bf16[128,1024]{1,0:T(8,128)(2,1)S(1)} collective-permute-done((bf16[128,1024]{1,0:T(8,128)(2,1)S(1)}, bf16[128,1024]{1,0:T(8,128)(2,1)S(1)}, u32[]{:S(2)}, u32[]{:S(2)}) %collective-permute-start.8) | collective-permute-done | bytes 262176 | tf_op jit(solution)/shard_map/ppermute | solution.py:525
  35.2 2.9 %collective-permute-done.9.refs_1_ = bf16[128,1024]{1,0:T(8,128)(2,1)S(1)} collective-permute-done((bf16[128,1024]{1,0:T(8,128)(2,1)S(1)}, bf16[128,1024]{1,0:T(8,128)(2,1)S(1)}, u32[]{:S(2)}, u32[]{:S(2)}) %collective-permute-start.9) | collective-permute-done | bytes 262176 | tf_op jit(solution)/shard_map/ppermute | solution.py:525
  38.5 1.6 %collective-permute-start.12 = (bf16[128,1024]{1,0:T(8,128)(2,1)S(1)}, bf16[128,1024]{1,0:T(8,128)(2,1)S(1)}, u32[]{:S(2)}, u32[]{:S(2)}) collective-permute-start(bf16[128,1024]{1,0:T(8,128)(2,1)S(1)} %get-tuple-element.51), channel_id=1, source_target_pairs={{0,2},{1,3},{2,0},{3,1},{4,6},{5,7},{6,4},{7,5},{8,10},{9,11},{10,... | collective-permute-start | bytes 786440 | tf_op jit(solution)/shard_map/ppermute | solution.py:525
  40.1 2.0 %collective-permute-start.13 = (bf16[128,1024]{1,0:T(8,128)(2,1)S(1)}, bf16[128,1024]{1,0:T(8,128)(2,1)S(1)}, u32[]{:S(2)}, u32[]{:S(2)}) collective-permute-start(bf16[128,1024]{1,0:T(8,128)(2,1)S(1)} %get-tuple-element.52), channel_id=1, source_target_pairs={{0,4},{1,5},{2,6},{3,7},{4,0},{5,1},{6,2},{7,3},{8,12},{9,13},{10,... | collective-permute-start | bytes 786440 | tf_op jit(solution)/shard_map/ppermute | solution.py:525
  43.3 1.6 %collective-permute-done.12.refs_0_.refs_4_ = bf16[128,1024]{1,0:T(8,128)(2,1)S(1)} collective-permute-done((bf16[128,1024]{1,0:T(8,128)(2,1)S(1)}, bf16[128,1024]{1,0:T(8,128)(2,1)S(1)}, u32[]{:S(2)}, u32[]{:S(2)}) %collective-permute-start.12) | collective-permute-done | bytes 262176 | tf_op jit(solution)/shard_map/ppermute | solution.py:525
  44.9 1.5 %collective-permute-done.13.refs_1_.refs_5_ = bf16[128,1024]{1,0:T(8,128)(2,1)S(1)} collective-permute-done((bf16[128,1024]{1,0:T(8,128)(2,1)S(1)}, bf16[128,1024]{1,0:T(8,128)(2,1)S(1)}, u32[]{:S(2)}, u32[]{:S(2)}) %collective-permute-start.13) | collective-permute-done | bytes 262176 | tf_op jit(solution)/shard_map/ppermute | solution.py:525
  47.3 3.9 %collective-permute-start.16 = (bf16[128,1024]{1,0:T(8,128)(2,1)S(1)}, bf16[128,1024]{1,0:T(8,128)(2,1)S(1)}, u32[]{:S(2)}, u32[]{:S(2)}) collective-permute-start(bf16[128,1024]{1,0:T(8,128)(2,1)S(1)} %regrid.1.refs_0_.refs_2_), channel_id=1, source_target_pairs={{0,4},{1,5},{2,6},{3,7},{4,0},{5,1},{6,2},{7,3},{8,12},{9,13},{10,... | collective-permute-start | bytes 786440 | tf_op jit(solution)/shard_map/ppermute | solution.py:525
  51.9 1.1 %hidden.1 = (bf16[128,1024]{1,0:T(8,128)(2,1)}, f32[8,128]{1,0:T(8,128)S(1)}) custom-call(bf16[128,1024]{1,0:T(8,128)(2,1)S(1)} %regrid.1.refs_0_.refs_2_, bf16[128,1024]{1,0:T(8,128)(2,1)S(1)} %copy-done.1, f32[2,1024]{1,0:T(2,128)S(1)} %get-tuple-element.43.refs_0_.refs_6_.refs_2_, bf16[128,128]{1,0:T(8,128)(2,1)S(1)} %get-tuple-element.35.refs_3_.refs_4_, ...), custom_call_target="tpu_custom_call" | custom-call | tf_op jit(solution)/shard_map/hidden/pallas_call | solution.py:59
  53.7 1.9 %collective-permute-done.16.refs_2_ = bf16[128,1024]{1,0:T(8,128)(2,1)S(1)} collective-permute-done((bf16[128,1024]{1,0:T(8,128)(2,1)S(1)}, bf16[128,1024]{1,0:T(8,128)(2,1)S(1)}, u32[]{:S(2)}, u32[]{:S(2)}) %collective-permute-start.16) | collective-permute-done | bytes 262176 | tf_op jit(solution)/shard_map/ppermute | solution.py:525
  55.6 2.3 %collective-permute-start.18 = (bf16[128,1024]{1,0:T(8,128)(2,1)S(1)}, bf16[128,1024]{1,0:T(8,128)(2,1)S(1)}, u32[]{:S(2)}, u32[]{:S(2)}) collective-permute-start(bf16[128,1024]{1,0:T(8,128)(2,1)S(1)} %get-tuple-element.57.refs_3_), channel_id=1, source_target_pairs={{0,2},{1,3},{2,0},{3,1},{4,6},{5,7},{6,4},{7,5},{8,10},{9,11},{10,... | collective-permute-start | bytes 786440 | tf_op jit(solution)/shard_map/ppermute | solution.py:525
  57.9 4.2 %collective-permute-start.19 = (bf16[128,1024]{1,0:T(8,128)(2,1)S(1)}, bf16[128,1024]{1,0:T(8,128)(2,1)S(1)}, u32[]{:S(2)}, u32[]{:S(2)}) collective-permute-start(bf16[128,1024]{1,0:T(8,128)(2,1)S(1)} %get-tuple-element.58.refs_1_), channel_id=1, source_target_pairs={{0,4},{1,5},{2,6},{3,7},{4,0},{5,1},{6,2},{7,3},{8,12},{9,13},{10,... | collective-permute-start | bytes 786440 | tf_op jit(solution)/shard_map/ppermute | solution.py:525
  62.7 0.9 %collective-permute-done.18.refs_0_.refs_7_ = bf16[128,1024]{1,0:T(8,128)(2,1)S(1)} collective-permute-done((bf16[128,1024]{1,0:T(8,128)(2,1)S(1)}, bf16[128,1024]{1,0:T(8,128)(2,1)S(1)}, u32[]{:S(2)}, u32[]{:S(2)}) %collective-permute-start.18) | collective-permute-done | bytes 262176 | tf_op jit(solution)/shard_map/ppermute | solution.py:525
  63.7 5.0 %collective-permute-done.19.refs_2_ = bf16[128,1024]{1,0:T(8,128)(2,1)S(1)} collective-permute-done((bf16[128,1024]{1,0:T(8,128)(2,1)S(1)}, bf16[128,1024]{1,0:T(8,128)(2,1)S(1)}, u32[]{:S(2)}, u32[]{:S(2)}) %collective-permute-start.19) | collective-permute-done | bytes 262176 | tf_op jit(solution)/shard_map/ppermute | solution.py:525
  68.7 2.1 %collective-permute-start.24 = (bf16[128,1024]{1,0:T(8,128)(2,1)S(1)}, bf16[128,1024]{1,0:T(8,128)(2,1)S(1)}, u32[]{:S(2)}, u32[]{:S(2)}) collective-permute-start(bf16[128,1024]{1,0:T(8,128)(2,1)S(1)} %collective-permute-done.23.refs_2_), channel_id=1, source_target_pairs={{0,4},{1,5},{2,6},{3,7},{4,0},{5,1},{6,2},{7,3},{8,12},{9,13},{10,... | collective-permute-start | bytes 786440 | tf_op jit(solution)/shard_map/ppermute | solution.py:525
  70.9 1.3 %turn_next.1.refs_1_.refs_0_ = bf16[8,1024,256]{2,1,0:T(8,128)(2,1)S(1)} custom-call(bf16[128,1024]{1,0:T(8,128)(2,1)S(1)} %choose.2.refs_0_.refs_4_, bf16[16384,128]{1,0:T(8,128)(2,1)S(1)} %copy-done, f32[128,128]{1,0:T(8,128)S(1)} %bitcast_convert_fusion.refs_2_, f32[2,128,128]{2,1,0:T(8,128)S(1)} %get-tuple-element.34.refs_2_.refs_3_.refs_1_, ...), custom_call_target="tpu_custom_call" | custom-call | tf_op jit(solution)/shard_map/turn_next/pallas_call | solution.py:59
  72.1 4.4 %collective-permute-done.22.refs_0_.refs_8_ = bf16[128,1024]{1,0:T(8,128)(2,1)S(1)} collective-permute-done((bf16[128,1024]{1,0:T(8,128)(2,1)S(1)}, bf16[128,1024]{1,0:T(8,128)(2,1)S(1)}, u32[]{:S(2)}, u32[]{:S(2)}) %collective-permute-start.22) | collective-permute-done | bytes 262176 | tf_op jit(solution)/shard_map/ppermute | solution.py:525
  76.5 0.9 %collective-permute-start.25 = (bf16[128,1024]{1,0:T(8,128)(2,1)S(1)}, bf16[128,1024]{1,0:T(8,128)(2,1)S(1)}, u32[]{:S(2)}, u32[]{:S(2)}) collective-permute-start(bf16[128,1024]{1,0:T(8,128)(2,1)S(1)} %choose.3.refs_5_), channel_id=1, source_target_pairs={{0,2},{1,3},{2,0},{3,1},{4,6},{5,7},{6,4},{7,5},{8,10},{9,11},{10,... | collective-permute-start | bytes 786440 | tf_op jit(solution)/shard_map/ppermute | solution.py:525
  77.4 0.8 project.2.refs_2_
  78.2 4.8 %collective-permute-done.25.refs_3_ = bf16[128,1024]{1,0:T(8,128)(2,1)S(1)} collective-permute-done((bf16[128,1024]{1,0:T(8,128)(2,1)S(1)}, bf16[128,1024]{1,0:T(8,128)(2,1)S(1)}, u32[]{:S(2)}, u32[]{:S(2)}) %collective-permute-start.25) | collective-permute-done | bytes 262176 | tf_op jit(solution)/shard_map/ppermute | solution.py:525
  83.3 1.3 %collective-permute-done.26.refs_1_ = f32[128,256]{1,0:T(8,128)S(1)} collective-permute-done((f32[128,256]{1,0:T(8,128)S(1)}, f32[128,256]{1,0:T(8,128)S(1)}, u32[]{:S(2)}, u32[]{:S(2)}) %collective-permute-start.26) | collective-permute-done | bytes 131104 | tf_op jit(solution)/shard_map/ppermute | solution.py:525
  84.6 0.7 finish.1
  (48 shorter events, 8.4 us)
Async XLA Ops:
  6.0 3.1 %collective-permute-start = (bf16[1,128,1024]{2,1,0:T(8,128)(2,1)S(1)}, bf16[1,128,1024]{2,1,0:T(8,128)(2,1)S(1)}, u32[]{:S(2)}, u32[]{:S(2)}) collective-permute-start(bf16[1,128,1024]{2,1,0:T(8,128)(2,1)S(1)} %get-tuple-element.38), channel_id=1, source_target_pairs={{0,1},{1,0},{2,3},{3,2},{4,5},{5,4},{6,7},{7,6},{8,9},{9,8},{10,11... | collective-permute-start | bytes 786440 | tf_op jit(solution)/shard_map/ppermute | solution.py:525
  8.4 5.2 %collective-permute-start.2 = (bf16[1,128,1024]{2,1,0:T(8,128)(2,1)S(1)}, bf16[1,128,1024]{2,1,0:T(8,128)(2,1)S(1)}, u32[]{:S(2)}, u32[]{:S(2)}) collective-permute-start(bf16[1,128,1024]{2,1,0:T(8,128)(2,1)S(1)} %get-tuple-element.39), channel_id=1, source_target_pairs={{0,1},{1,0},{2,3},{3,2},{4,5},{5,4},{6,7},{7,6},{8,9},{9,8},{10,11... | collective-permute-start | bytes 786440 | tf_op jit(solution)/shard_map/ppermute | solution.py:525
  8.5 5.0 %collective-permute-start.3 = (bf16[1,128,1024]{2,1,0:T(8,128)(2,1)S(1)}, bf16[1,128,1024]{2,1,0:T(8,128)(2,1)S(1)}, u32[]{:S(2)}, u32[]{:S(2)}) collective-permute-start(bf16[1,128,1024]{2,1,0:T(8,128)(2,1)S(1)} %get-tuple-element.40), channel_id=1, source_target_pairs={{0,1},{1,0},{2,3},{3,2},{4,5},{5,4},{6,7},{7,6},{8,9},{9,8},{10,11... | collective-permute-start | bytes 786440 | tf_op jit(solution)/shard_map/ppermute | solution.py:525
  9.0 4.6 %collective-permute-start.4 = (bf16[1,128,1024]{2,1,0:T(8,128)(2,1)S(1)}, bf16[1,128,1024]{2,1,0:T(8,128)(2,1)S(1)}, u32[]{:S(2)}, u32[]{:S(2)}) collective-permute-start(bf16[1,128,1024]{2,1,0:T(8,128)(2,1)S(1)} %get-tuple-element.41), channel_id=1, source_target_pairs={{0,1},{1,0},{2,3},{3,2},{4,5},{5,4},{6,7},{7,6},{8,9},{9,8},{10,11... | collective-permute-start | bytes 786440 | tf_op jit(solution)/shard_map/ppermute | solution.py:525
  9.1 9.5 %collective-permute-start.1 = (bf16[128,1024]{1,0:T(8,128)(2,1)S(1)}, bf16[128,1024]{1,0:T(8,128)(2,1)S(1)}, u32[]{:S(2)}, u32[]{:S(2)}) collective-permute-start(bf16[128,1024]{1,0:T(8,128)(2,1)S(1)} %add_up.4.refs_0_), channel_id=1, source_target_pairs={{0,2},{1,3},{2,0},{3,1},{4,6},{5,7},{6,4},{7,5},{8,10},{9,11},{10,... | collective-permute-start | bytes 786440 | tf_op jit(solution)/shard_map/ppermute | solution.py:525
  12.8 9.4 %copy-start.1 = (bf16[128,1024]{1,0:T(8,128)(2,1)S(1)}, bf16[128,1024]{1,0:T(8,128)(2,1)}, u32[]{:S(2)}) copy-start(bf16[128,1024]{1,0:T(8,128)(2,1)} %refs_1_.8) | copy-start | bytes 786436
  12.8 9.6 %copy-start = (bf16[16384,128]{1,0:T(8,128)(2,1)S(1)}, bf16[16384,128]{1,0:T(8,128)(2,1)}, u32[]{:S(2)}) copy-start(bf16[16384,128]{1,0:T(8,128)(2,1)} %refs_1_.9) | copy-start | bytes 12582916
  12.8 15.0 %collective-permute-start.7 = (bf16[2,128,1024]{2,1,0:T(8,128)(2,1)S(1)}, bf16[2,128,1024]{2,1,0:T(8,128)(2,1)S(1)}, u32[]{:S(2)}, u32[]{:S(2)}) collective-permute-start(bf16[2,128,1024]{2,1,0:T(8,128)(2,1)S(1)} %partials.4.refs_0_), channel_id=1, source_target_pairs={{0,1},{1,0},{2,3},{3,2},{4,5},{5,4},{6,7},{7,6},{8,9},{9,8},{10,11... | collective-permute-start | bytes 1572872 | tf_op jit(solution)/shard_map/ppermute | solution.py:525
  18.8 7.8 %collective-permute-start.5 = (bf16[128,1024]{1,0:T(8,128)(2,1)S(1)}, bf16[128,1024]{1,0:T(8,128)(2,1)S(1)}, u32[]{:S(2)}, u32[]{:S(2)}) collective-permute-start(bf16[128,1024]{1,0:T(8,128)(2,1)S(1)} %get-tuple-element.45), channel_id=1, source_target_pairs={{0,2},{1,3},{2,0},{3,1},{4,6},{5,7},{6,4},{7,5},{8,10},{9,11},{10,... | collective-permute-start | bytes 786440 | tf_op jit(solution)/shard_map/ppermute | solution.py:525
  20.6 7.2 %collective-permute-start.6 = (bf16[128,1024]{1,0:T(8,128)(2,1)S(1)}, bf16[128,1024]{1,0:T(8,128)(2,1)S(1)}, u32[]{:S(2)}, u32[]{:S(2)}) collective-permute-start(bf16[128,1024]{1,0:T(8,128)(2,1)S(1)} %get-tuple-element.42.refs_0_), channel_id=1, source_target_pairs={{0,4},{1,5},{2,6},{3,7},{4,0},{5,1},{6,2},{7,3},{8,12},{9,13},{10,... | collective-permute-start | bytes 786440 | tf_op jit(solution)/shard_map/ppermute | solution.py:525
  22.2 11.6 %collective-permute-start.11 = (bf16[2,128,1024]{2,1,0:T(8,128)(2,1)S(1)}, bf16[2,128,1024]{2,1,0:T(8,128)(2,1)S(1)}, u32[]{:S(2)}, u32[]{:S(2)}) collective-permute-start(bf16[2,128,1024]{2,1,0:T(8,128)(2,1)S(1)} %partials.5.refs_0_), channel_id=1, source_target_pairs={{0,1},{1,0},{2,3},{3,2},{4,5},{5,4},{6,7},{7,6},{8,9},{9,8},{10,11... | collective-permute-start | bytes 1572872 | tf_op jit(solution)/shard_map/ppermute | solution.py:525
  28.1 5.7 %collective-permute-start.10 = (bf16[128,1024]{1,0:T(8,128)(2,1)S(1)}, bf16[128,1024]{1,0:T(8,128)(2,1)S(1)}, u32[]{:S(2)}, u32[]{:S(2)}) collective-permute-start(bf16[128,1024]{1,0:T(8,128)(2,1)S(1)} %get-tuple-element.49), channel_id=1, source_target_pairs={{0,0},{1,1},{2,2},{3,3},{4,8},{5,9},{6,10},{7,11},{8,4},{9,5},{10,... | collective-permute-start | bytes 786440 | tf_op jit(solution)/shard_map/ppermute | solution.py:525
  28.8 6.4 %collective-permute-start.8 = (bf16[128,1024]{1,0:T(8,128)(2,1)S(1)}, bf16[128,1024]{1,0:T(8,128)(2,1)S(1)}, u32[]{:S(2)}, u32[]{:S(2)}) collective-permute-start(bf16[128,1024]{1,0:T(8,128)(2,1)S(1)} %get-tuple-element.47), channel_id=1, source_target_pairs={{0,2},{1,3},{2,0},{3,1},{4,6},{5,7},{6,4},{7,5},{8,10},{9,11},{10,... | collective-permute-start | bytes 786440 | tf_op jit(solution)/shard_map/ppermute | solution.py:525
  29.5 8.7 %collective-permute-start.9 = (bf16[128,1024]{1,0:T(8,128)(2,1)S(1)}, bf16[128,1024]{1,0:T(8,128)(2,1)S(1)}, u32[]{:S(2)}, u32[]{:S(2)}) collective-permute-start(bf16[128,1024]{1,0:T(8,128)(2,1)S(1)} %get-tuple-element.48), channel_id=1, source_target_pairs={{0,4},{1,5},{2,6},{3,7},{4,0},{5,1},{6,2},{7,3},{8,12},{9,13},{10,... | collective-permute-start | bytes 786440 | tf_op jit(solution)/shard_map/ppermute | solution.py:525
  38.5 32.4 %copy-start.2 = (bf16[16384]{0:T(1024)(128)(2,1)S(1)}, bf16[16384]{0:T(1024)(128)(2,1)}, u32[]{:S(2)}) copy-start(bf16[16384]{0:T(1024)(128)(2,1)} %param.17) | copy-start | bytes 98308
  38.5 6.4 %collective-permute-start.12 = (bf16[128,1024]{1,0:T(8,128)(2,1)S(1)}, bf16[128,1024]{1,0:T(8,128)(2,1)S(1)}, u32[]{:S(2)}, u32[]{:S(2)}) collective-permute-start(bf16[128,1024]{1,0:T(8,128)(2,1)S(1)} %get-tuple-element.51), channel_id=1, source_target_pairs={{0,2},{1,3},{2,0},{3,1},{4,6},{5,7},{6,4},{7,5},{8,10},{9,11},{10,... | collective-permute-start | bytes 786440 | tf_op jit(solution)/shard_map/ppermute | solution.py:525
  40.1 6.4 %collective-permute-start.13 = (bf16[128,1024]{1,0:T(8,128)(2,1)S(1)}, bf16[128,1024]{1,0:T(8,128)(2,1)S(1)}, u32[]{:S(2)}, u32[]{:S(2)}) collective-permute-start(bf16[128,1024]{1,0:T(8,128)(2,1)S(1)} %get-tuple-element.52), channel_id=1, source_target_pairs={{0,4},{1,5},{2,6},{3,7},{4,0},{5,1},{6,2},{7,3},{8,12},{9,13},{10,... | collective-permute-start | bytes 786440 | tf_op jit(solution)/shard_map/ppermute | solution.py:525
  42.1 4.4 %collective-permute-start.14 = (bf16[128,1024]{1,0:T(8,128)(2,1)S(1)}, bf16[128,1024]{1,0:T(8,128)(2,1)S(1)}, u32[]{:S(2)}, u32[]{:S(2)}) collective-permute-start(bf16[128,1024]{1,0:T(8,128)(2,1)S(1)} %get-tuple-element.53), channel_id=1, source_target_pairs={{0,0},{1,1},{2,2},{3,3},{4,8},{5,9},{6,10},{7,11},{8,4},{9,5},{10,... | collective-permute-start | bytes 786440 | tf_op jit(solution)/shard_map/ppermute | solution.py:525
  42.8 28.1 %collective-permute-start.20 = (bf16[4,1024,128]{2,1,0:T(8,128)(2,1)S(1)}, bf16[4,1024,128]{2,1,0:T(8,128)(2,1)S(1)}, u32[]{:S(2)}, u32[]{:S(2)}) collective-permute-start(bf16[4,1024,128]{2,1,0:T(8,128)(2,1)S(1)} %get-tuple-element.44.refs_0_), channel_id=1, source_target_pairs={{0,1},{1,0},{2,3},{3,2},{4,5},{5,4},{6,7},{7,6},{8,9},{9,8},{10,11... | collective-permute-start | bytes 3145736 | tf_op jit(solution)/shard_map/ppermute | solution.py:525
  42.8 28.0 %collective-permute-start.21 = (bf16[4,1024,128]{2,1,0:T(8,128)(2,1)S(1)}, bf16[4,1024,128]{2,1,0:T(8,128)(2,1)S(1)}, u32[]{:S(2)}, u32[]{:S(2)}) collective-permute-start(bf16[4,1024,128]{2,1,0:T(8,128)(2,1)S(1)} %get-tuple-element.59), channel_id=1, source_target_pairs={{0,1},{1,0},{2,3},{3,2},{4,5},{5,4},{6,7},{7,6},{8,9},{9,8},{10,11... | collective-permute-start | bytes 3145736 | tf_op jit(solution)/shard_map/ppermute | solution.py:525
  46.7 7.0 %collective-permute-start.15 = (bf16[128,1024]{1,0:T(8,128)(2,1)S(1)}, bf16[128,1024]{1,0:T(8,128)(2,1)S(1)}, u32[]{:S(2)}, u32[]{:S(2)}) collective-permute-start(bf16[128,1024]{1,0:T(8,128)(2,1)S(1)} %regrid.1.refs_0_.refs_2_), channel_id=1, source_target_pairs={{0,2},{1,3},{2,0},{3,1},{4,6},{5,7},{6,4},{7,5},{8,10},{9,11},{10,... | collective-permute-start | bytes 786440 | tf_op jit(solution)/shard_map/ppermute | solution.py:525
  47.3 8.3 %collective-permute-start.16 = (bf16[128,1024]{1,0:T(8,128)(2,1)S(1)}, bf16[128,1024]{1,0:T(8,128)(2,1)S(1)}, u32[]{:S(2)}, u32[]{:S(2)}) collective-permute-start(bf16[128,1024]{1,0:T(8,128)(2,1)S(1)} %regrid.1.refs_0_.refs_2_), channel_id=1, source_target_pairs={{0,4},{1,5},{2,6},{3,7},{4,0},{5,1},{6,2},{7,3},{8,12},{9,13},{10,... | collective-permute-start | bytes 786440 | tf_op jit(solution)/shard_map/ppermute | solution.py:525
  51.2 4.4 %collective-permute-start.17 = (bf16[128,1024]{1,0:T(8,128)(2,1)S(1)}, bf16[128,1024]{1,0:T(8,128)(2,1)S(1)}, u32[]{:S(2)}, u32[]{:S(2)}) collective-permute-start(bf16[128,1024]{1,0:T(8,128)(2,1)S(1)} %regrid.1.refs_0_.refs_2_), channel_id=1, source_target_pairs={{0,0},{1,1},{2,2},{3,3},{4,8},{5,9},{6,10},{7,11},{8,4},{9,5},{10,... | collective-permute-start | bytes 786440 | tf_op jit(solution)/shard_map/ppermute | solution.py:525
  55.6 8.1 %collective-permute-start.18 = (bf16[128,1024]{1,0:T(8,128)(2,1)S(1)}, bf16[128,1024]{1,0:T(8,128)(2,1)S(1)}, u32[]{:S(2)}, u32[]{:S(2)}) collective-permute-start(bf16[128,1024]{1,0:T(8,128)(2,1)S(1)} %get-tuple-element.57.refs_3_), channel_id=1, source_target_pairs={{0,2},{1,3},{2,0},{3,1},{4,6},{5,7},{6,4},{7,5},{8,10},{9,11},{10,... | collective-permute-start | bytes 786440 | tf_op jit(solution)/shard_map/ppermute | solution.py:525
  57.9 10.7 %collective-permute-start.19 = (bf16[128,1024]{1,0:T(8,128)(2,1)S(1)}, bf16[128,1024]{1,0:T(8,128)(2,1)S(1)}, u32[]{:S(2)}, u32[]{:S(2)}) collective-permute-start(bf16[128,1024]{1,0:T(8,128)(2,1)S(1)} %get-tuple-element.58.refs_1_), channel_id=1, source_target_pairs={{0,4},{1,5},{2,6},{3,7},{4,0},{5,1},{6,2},{7,3},{8,12},{9,13},{10,... | collective-permute-start | bytes 786440 | tf_op jit(solution)/shard_map/ppermute | solution.py:525
  62.1 6.7 %collective-permute-start.23 = (bf16[128,1024]{1,0:T(8,128)(2,1)S(1)}, bf16[128,1024]{1,0:T(8,128)(2,1)S(1)}, u32[]{:S(2)}, u32[]{:S(2)}) collective-permute-start(bf16[128,1024]{1,0:T(8,128)(2,1)S(1)} %get-tuple-element.57.refs_3_), channel_id=1, source_target_pairs={{0,0},{1,1},{2,2},{3,3},{4,8},{5,9},{6,10},{7,11},{8,4},{9,5},{10,... | collective-permute-start | bytes 786440 | tf_op jit(solution)/shard_map/ppermute | solution.py:525
  68.6 7.8 %collective-permute-start.22 = (bf16[128,1024]{1,0:T(8,128)(2,1)S(1)}, bf16[128,1024]{1,0:T(8,128)(2,1)S(1)}, u32[]{:S(2)}, u32[]{:S(2)}) collective-permute-start(bf16[128,1024]{1,0:T(8,128)(2,1)S(1)} %choose.2.refs_0_.refs_4_), channel_id=1, source_target_pairs={{0,2},{1,3},{2,0},{3,1},{4,6},{5,7},{6,4},{7,5},{8,10},{9,11},{10,... | collective-permute-start | bytes 786440 | tf_op jit(solution)/shard_map/ppermute | solution.py:525
  68.7 7.8 %collective-permute-start.24 = (bf16[128,1024]{1,0:T(8,128)(2,1)S(1)}, bf16[128,1024]{1,0:T(8,128)(2,1)S(1)}, u32[]{:S(2)}, u32[]{:S(2)}) collective-permute-start(bf16[128,1024]{1,0:T(8,128)(2,1)S(1)} %collective-permute-done.23.refs_2_), channel_id=1, source_target_pairs={{0,4},{1,5},{2,6},{3,7},{4,0},{5,1},{6,2},{7,3},{8,12},{9,13},{10,... | collective-permute-start | bytes 786440 | tf_op jit(solution)/shard_map/ppermute | solution.py:525
  76.5 6.4 %collective-permute-start.25 = (bf16[128,1024]{1,0:T(8,128)(2,1)S(1)}, bf16[128,1024]{1,0:T(8,128)(2,1)S(1)}, u32[]{:S(2)}, u32[]{:S(2)}) collective-permute-start(bf16[128,1024]{1,0:T(8,128)(2,1)S(1)} %choose.3.refs_5_), channel_id=1, source_target_pairs={{0,2},{1,3},{2,0},{3,1},{4,6},{5,7},{6,4},{7,5},{8,10},{9,11},{10,... | collective-permute-start | bytes 786440 | tf_op jit(solution)/shard_map/ppermute | solution.py:525
  83.2 1.4 %collective-permute-start.26 = (f32[128,256]{1,0:T(8,128)S(1)}, f32[128,256]{1,0:T(8,128)S(1)}, u32[]{:S(2)}, u32[]{:S(2)}) collective-permute-start(f32[128,256]{1,0:T(8,128)S(1)} %get-tuple-element.61), channel_id=1, source_target_pairs={{0,1},{1,0},{2,3},{3,2},{4,5},{5,4},{6,7},{7,6},{8,9},{9,8},{10,11... | collective-permute-start | bytes 393224 | tf_op jit(solution)/shard_map/ppermute | solution.py:525

commit v5 on v4

--- a/solution.py
+++ b/solution.py
@@ -534,7 +534,7 @@
         return permute(value, lambda a, b, c: (a ^ 1, b, c))
 
     def swap_middle(value):
-        return permute(value, lambda a, b, c: ((0, 2, 1, 3)[a], b, c))
+        return permute(value, lambda a, b, c: (a, b, 1 - c) if a in (0, 3) else (3 - a, b, c))
 
     everything = range(inner)
     context, rows, send1, out_weight, had = attend(

time: 85.6 us -> 82.1 us (0.959)
  the two profiles are of different devices: /device:TPU:0 before, /device:TPU:17 now
where the time goes in v5:
time: 82.1 us; the launch traced here: 81.9 us
  waiting for transfers between devices  38.7 us (47%)
  starting transfers between devices  28.2 us (34%)
  Pallas kernels  14.2 us (17%)
  between operations  0.83 us (1%)
    ppermute x27, waiting for transfers between devices, permute(): return lax.ppermute(value, 'tp', moves)  38.7 us
    ppermute x27, starting transfers between devices, permute(): return lax.ppermute(value, 'tp', moves)  28.2 us
    pallas_call x19, Pallas kernels, kernel_call(): pl.pallas_call(ordered, out_shape=out_shape, in_specs=[anywhere()] * extr...  14.2 us
  transfers between devices with their start and end apart: 27, of which 18 were waited for; matrix products, arithmetic and copies ran while one was open for 0% of the time, Pallas kernels for 9%

profile of v5, /device:TPU:17, one launch (start us, length us, event | category | flops | bytes accessed | tf_op | source)
XLA Modules:
  0.0 81.9 jit_solution(10190535650924561469)
XLA Ops:
  0.6 5.4 %attend.1 = (bf16[128,128]{1,0:T(8,128)(2,1)S(1)}, f32[2,128,128]{2,1,0:T(8,128)S(1)}, bf16[1,128,1024]{2,1,0:T(8,128)(2,1)S(1)}, bf16[128,16384]{1,0:T(8,128)(2,1)S(1)}, bf16[128,128]{1,0:T(8,128)(2,1)S(1)}) custom-call(bf16[1,128,128]{2,1,0:T(8,128)(2,1)} %refs_0_.1, bf16[1,8192,128]{2,1,0:T(8,128)(2,1)} %refs_1_.5, bf16[1,8192,128]{2,1,0:T(8,128)(2,1)} %refs_2_.1, ...), custom_call_target="tpu_custom_call" | custom-call | tf_op jit(solution)/shard_map/attend/pallas_call | solution.py:59
  6.8 1.9 %partials.3 = (bf16[1,128,1024]{2,1,0:T(8,128)(2,1)S(1)}, bf16[3,128,1024]{2,1,0:T(8,128)(2,1)S(1)}, bf16[2,128,1024]{2,1,0:T(8,128)(2,1)S(1)}, bf16[2,128,1024]...) custom-call(bf16[128,128]{1,0:T(8,128)(2,1)S(1)} %get-tuple-element., ...), custom_call_target="tpu_custom_call" | custom-call | tf_op jit(solution)/shard_map/partials/pallas_call | solution.py:59
  9.4 1.3 %collective-permute-start.1 = (bf16[128,1024]{1,0:T(8,128)(2,1)S(1)}, bf16[128,1024]{1,0:T(8,128)(2,1)S(1)}, u32[]{:S(2)}, u32[]{:S(2)}) collective-permute-start(bf16[128,1024]{1,0:T(8,128)(2,1)S(1)} %add_up.4.refs_0_), channel_id=1, source_target_pairs={{0,2},{1,3},{2,0},{3,1},{4,6},{5,7},{6,4},{7,5},{8,10},{9,11},{10,... | collective-permute-start | bytes 786440 | tf_op jit(solution)/shard_map/ppermute | solution.py:525
  11.3 0.8 collective-permute-start.7
  12.8 4.1 %collective-permute-done.1.refs_1_.refs_9_ = bf16[128,1024]{1,0:T(8,128)(2,1)S(1)} collective-permute-done((bf16[128,1024]{1,0:T(8,128)(2,1)S(1)}, bf16[128,1024]{1,0:T(8,128)(2,1)S(1)}, u32[]{:S(2)}, u32[]{:S(2)}) %collective-permute-start.1) | collective-permute-done | bytes 262176 | tf_op jit(solution)/shard_map/ppermute | solution.py:525
  17.0 1.3 %collective-permute-start.5 = (bf16[128,1024]{1,0:T(8,128)(2,1)S(1)}, bf16[128,1024]{1,0:T(8,128)(2,1)S(1)}, u32[]{:S(2)}, u32[]{:S(2)}) collective-permute-start(bf16[128,1024]{1,0:T(8,128)(2,1)S(1)} %get-tuple-element.45), channel_id=1, source_target_pairs={{0,2},{1,3},{2,0},{3,1},{4,6},{5,7},{6,4},{7,5},{8,10},{9,11},{10,... | collective-permute-start | bytes 786440 | tf_op jit(solution)/shard_map/ppermute | solution.py:525
  18.3 1.3 %collective-permute-start.6 = (bf16[128,1024]{1,0:T(8,128)(2,1)S(1)}, bf16[128,1024]{1,0:T(8,128)(2,1)S(1)}, u32[]{:S(2)}, u32[]{:S(2)}) collective-permute-start(bf16[128,1024]{1,0:T(8,128)(2,1)S(1)} %get-tuple-element.42.refs_0_), channel_id=1, source_target_pairs={{0,4},{1,5},{2,6},{3,7},{4,0},{5,1},{6,2},{7,3},{8,12},{9,13},{10,... | collective-permute-start | bytes 786440 | tf_op jit(solution)/shard_map/ppermute | solution.py:525
  19.6 1.8 %collective-permute-start.11 = (bf16[2,128,1024]{2,1,0:T(8,128)(2,1)S(1)}, bf16[2,128,1024]{2,1,0:T(8,128)(2,1)S(1)}, u32[]{:S(2)}, u32[]{:S(2)}) collective-permute-start(bf16[2,128,1024]{2,1,0:T(8,128)(2,1)S(1)} %partials.5.refs_0_), channel_id=1, source_target_pairs={{0,1},{1,0},{2,3},{3,2},{4,5},{5,4},{6,7},{7,6},{8,9},{9,8},{10,11... | collective-permute-start | bytes 1572872 | tf_op jit(solution)/shard_map/ppermute | solution.py:525
  21.8 1.8 %collective-permute-done.5.refs_1_.refs_11_ = bf16[128,1024]{1,0:T(8,128)(2,1)S(1)} collective-permute-done((bf16[128,1024]{1,0:T(8,128)(2,1)S(1)}, bf16[128,1024]{1,0:T(8,128)(2,1)S(1)}, u32[]{:S(2)}, u32[]{:S(2)}) %collective-permute-start.5) | collective-permute-done | bytes 262176 | tf_op jit(solution)/shard_map/ppermute | solution.py:525
  23.6 0.9 %collective-permute-done.6.refs_2_ = bf16[128,1024]{1,0:T(8,128)(2,1)S(1)} collective-permute-done((bf16[128,1024]{1,0:T(8,128)(2,1)S(1)}, bf16[128,1024]{1,0:T(8,128)(2,1)S(1)}, u32[]{:S(2)}, u32[]{:S(2)}) %collective-permute-start.6) | collective-permute-done | bytes 262176 | tf_op jit(solution)/shard_map/ppermute | solution.py:525
  25.4 3.6 %collective-permute-start.9 = (bf16[128,1024]{1,0:T(8,128)(2,1)S(1)}, bf16[128,1024]{1,0:T(8,128)(2,1)S(1)}, u32[]{:S(2)}, u32[]{:S(2)}) collective-permute-start(bf16[128,1024]{1,0:T(8,128)(2,1)S(1)} %get-tuple-element.48), channel_id=1, source_target_pairs={{0,4},{1,5},{2,6},{3,7},{4,0},{5,1},{6,2},{7,3},{8,12},{9,13},{10,... | collective-permute-start | bytes 786440 | tf_op jit(solution)/shard_map/ppermute | solution.py:525
  29.0 1.2 %collective-permute-done.10.refs_2_ = bf16[128,1024]{1,0:T(8,128)(2,1)S(1)} collective-permute-done((bf16[128,1024]{1,0:T(8,128)(2,1)S(1)}, bf16[128,1024]{1,0:T(8,128)(2,1)S(1)}, u32[]{:S(2)}, u32[]{:S(2)}) %collective-permute-start.10) | collective-permute-done | bytes 262176 | tf_op jit(solution)/shard_map/ppermute | solution.py:525
  30.6 3.8 %collective-permute-done.9.refs_1_ = bf16[128,1024]{1,0:T(8,128)(2,1)S(1)} collective-permute-done((bf16[128,1024]{1,0:T(8,128)(2,1)S(1)}, bf16[128,1024]{1,0:T(8,128)(2,1)S(1)}, u32[]{:S(2)}, u32[]{:S(2)}) %collective-permute-start.9) | collective-permute-done | bytes 262176 | tf_op jit(solution)/shard_map/ppermute | solution.py:525
  34.8 1.3 %collective-permute-start.12 = (bf16[128,1024]{1,0:T(8,128)(2,1)S(1)}, bf16[128,1024]{1,0:T(8,128)(2,1)S(1)}, u32[]{:S(2)}, u32[]{:S(2)}) collective-permute-start(bf16[128,1024]{1,0:T(8,128)(2,1)S(1)} %get-tuple-element.51), channel_id=1, source_target_pairs={{0,2},{1,3},{2,0},{3,1},{4,6},{5,7},{6,4},{7,5},{8,10},{9,11},{10,... | collective-permute-start | bytes 786440 | tf_op jit(solution)/shard_map/ppermute | solution.py:525
  36.1 2.1 %collective-permute-start.13 = (bf16[128,1024]{1,0:T(8,128)(2,1)S(1)}, bf16[128,1024]{1,0:T(8,128)(2,1)S(1)}, u32[]{:S(2)}, u32[]{:S(2)}) collective-permute-start(bf16[128,1024]{1,0:T(8,128)(2,1)S(1)} %get-tuple-element.52), channel_id=1, source_target_pairs={{0,4},{1,5},{2,6},{3,7},{4,0},{5,1},{6,2},{7,3},{8,12},{9,13},{10,... | collective-permute-start | bytes 786440 | tf_op jit(solution)/shard_map/ppermute | solution.py:525
  38.2 1.7 %collective-permute-start.20 = (bf16[4,1024,128]{2,1,0:T(8,128)(2,1)S(1)}, bf16[4,1024,128]{2,1,0:T(8,128)(2,1)S(1)}, u32[]{:S(2)}, u32[]{:S(2)}) collective-permute-start(bf16[4,1024,128]{2,1,0:T(8,128)(2,1)S(1)} %get-tuple-element.44.refs_0_), channel_id=1, source_target_pairs={{0,1},{1,0},{2,3},{3,2},{4,5},{5,4},{6,7},{7,6},{8,9},{9,8},{10,11... | collective-permute-start | bytes 3145736 | tf_op jit(solution)/shard_map/ppermute | solution.py:525
  39.9 1.0 %collective-permute-done.12.refs_0_.refs_4_ = bf16[128,1024]{1,0:T(8,128)(2,1)S(1)} collective-permute-done((bf16[128,1024]{1,0:T(8,128)(2,1)S(1)}, bf16[128,1024]{1,0:T(8,128)(2,1)S(1)}, u32[]{:S(2)}, u32[]{:S(2)}) %collective-permute-start.12) | collective-permute-done | bytes 262176 | tf_op jit(solution)/shard_map/ppermute | solution.py:525
  40.9 2.1 %collective-permute-done.13.refs_1_.refs_5_ = bf16[128,1024]{1,0:T(8,128)(2,1)S(1)} collective-permute-done((bf16[128,1024]{1,0:T(8,128)(2,1)S(1)}, bf16[128,1024]{1,0:T(8,128)(2,1)S(1)}, u32[]{:S(2)}, u32[]{:S(2)}) %collective-permute-start.13) | collective-permute-done | bytes 262176 | tf_op jit(solution)/shard_map/ppermute | solution.py:525
  43.1 1.2 %collective-permute-done.14.refs_2_.refs_6_ = bf16[128,1024]{1,0:T(8,128)(2,1)S(1)} collective-permute-done((bf16[128,1024]{1,0:T(8,128)(2,1)S(1)}, bf16[128,1024]{1,0:T(8,128)(2,1)S(1)}, u32[]{:S(2)}, u32[]{:S(2)}) %collective-permute-start.14) | collective-permute-done | bytes 262176 | tf_op jit(solution)/shard_map/ppermute | solution.py:525
  45.3 1.1 %hidden.1 = (bf16[128,1024]{1,0:T(8,128)(2,1)}, f32[8,128]{1,0:T(8,128)S(1)}) custom-call(bf16[128,1024]{1,0:T(8,128)(2,1)S(1)} %regrid.1.refs_0_.refs_2_, bf16[128,1024]{1,0:T(8,128)(2,1)S(1)} %copy-done.1, f32[2,1024]{1,0:T(2,128)S(1)} %get-tuple-element.43.refs_0_.refs_6_.refs_2_, bf16[128,128]{1,0:T(8,128)(2,1)S(1)} %get-tuple-element.35.refs_3_.refs_4_, ...), custom_call_target="tpu_custom_call" | custom-call | tf_op jit(solution)/shard_map/hidden/pallas_call | solution.py:59
  46.4 3.4 %collective-permute-done.15.refs_0_.refs_6_ = bf16[128,1024]{1,0:T(8,128)(2,1)S(1)} collective-permute-done((bf16[128,1024]{1,0:T(8,128)(2,1)S(1)}, bf16[128,1024]{1,0:T(8,128)(2,1)S(1)}, u32[]{:S(2)}, u32[]{:S(2)}) %collective-permute-start.15) | collective-permute-done | bytes 262176 | tf_op jit(solution)/shard_map/ppermute | solution.py:525
  50.8 1.1 %collective-permute-start.18 = (bf16[128,1024]{1,0:T(8,128)(2,1)S(1)}, bf16[128,1024]{1,0:T(8,128)(2,1)S(1)}, u32[]{:S(2)}, u32[]{:S(2)}) collective-permute-start(bf16[128,1024]{1,0:T(8,128)(2,1)S(1)} %get-tuple-element.57.refs_3_), channel_id=1, source_target_pairs={{0,2},{1,3},{2,0},{3,1},{4,6},{5,7},{6,4},{7,5},{8,10},{9,11},{10,... | collective-permute-start | bytes 786440 | tf_op jit(solution)/shard_map/ppermute | solution.py:525
  52.0 4.0 %collective-permute-done.18.refs_0_.refs_7_ = bf16[128,1024]{1,0:T(8,128)(2,1)S(1)} collective-permute-done((bf16[128,1024]{1,0:T(8,128)(2,1)S(1)}, bf16[128,1024]{1,0:T(8,128)(2,1)S(1)}, u32[]{:S(2)}, u32[]{:S(2)}) %collective-permute-start.18) | collective-permute-done | bytes 262176 | tf_op jit(solution)/shard_map/ppermute | solution.py:525
  56.0 1.1 %collective-permute-done.19.refs_2_ = bf16[128,1024]{1,0:T(8,128)(2,1)S(1)} collective-permute-done((bf16[128,1024]{1,0:T(8,128)(2,1)S(1)}, bf16[128,1024]{1,0:T(8,128)(2,1)S(1)}, u32[]{:S(2)}, u32[]{:S(2)}) %collective-permute-start.19) | collective-permute-done | bytes 262176 | tf_op jit(solution)/shard_map/ppermute | solution.py:525
  57.6 1.4 %collective-permute-start.24 = (bf16[128,1024]{1,0:T(8,128)(2,1)S(1)}, bf16[128,1024]{1,0:T(8,128)(2,1)S(1)}, u32[]{:S(2)}, u32[]{:S(2)}) collective-permute-start(bf16[128,1024]{1,0:T(8,128)(2,1)S(1)} %collective-permute-done.23.refs_2_), channel_id=1, source_target_pairs={{0,4},{1,5},{2,6},{3,7},{4,0},{5,1},{6,2},{7,3},{8,12},{9,13},{10,... | collective-permute-start | bytes 786440 | tf_op jit(solution)/shard_map/ppermute | solution.py:525
  59.1 1.3 %turn_next.1.refs_1_.refs_0_ = bf16[8,1024,256]{2,1,0:T(8,128)(2,1)S(1)} custom-call(bf16[128,1024]{1,0:T(8,128)(2,1)S(1)} %choose.2.refs_0_.refs_4_, bf16[16384,128]{1,0:T(8,128)(2,1)S(1)} %copy-done, f32[128,128]{1,0:T(8,128)S(1)} %bitcast_convert_fusion.refs_2_, f32[2,128,128]{2,1,0:T(8,128)S(1)} %get-tuple-element.34.refs_2_.refs_3_.refs_1_, ...), custom_call_target="tpu_custom_call" | custom-call | tf_op jit(solution)/shard_map/turn_next/pallas_call | solution.py:59
  60.3 3.0 %collective-permute-done.22.refs_0_.refs_8_ = bf16[128,1024]{1,0:T(8,128)(2,1)S(1)} collective-permute-done((bf16[128,1024]{1,0:T(8,128)(2,1)S(1)}, bf16[128,1024]{1,0:T(8,128)(2,1)S(1)}, u32[]{:S(2)}, u32[]{:S(2)}) %collective-permute-start.22) | collective-permute-done | bytes 262176 | tf_op jit(solution)/shard_map/ppermute | solution.py:525
  63.3 1.3 %collective-permute-done.24.refs_3_ = bf16[128,1024]{1,0:T(8,128)(2,1)S(1)} collective-permute-done((bf16[128,1024]{1,0:T(8,128)(2,1)S(1)}, bf16[128,1024]{1,0:T(8,128)(2,1)S(1)}, u32[]{:S(2)}, u32[]{:S(2)}) %collective-permute-start.24) | collective-permute-done | bytes 262176 | tf_op jit(solution)/shard_map/ppermute | solution.py:525
  64.8 0.8 project.2.refs_2_
  65.6 7.3 %collective-permute-done.25.refs_3_ = bf16[128,1024]{1,0:T(8,128)(2,1)S(1)} collective-permute-done((bf16[128,1024]{1,0:T(8,128)(2,1)S(1)}, bf16[128,1024]{1,0:T(8,128)(2,1)S(1)}, u32[]{:S(2)}, u32[]{:S(2)}) %collective-permute-start.25) | collective-permute-done | bytes 262176 | tf_op jit(solution)/shard_map/ppermute | solution.py:525
  73.1 7.1 %collective-permute-start.26 = (f32[128,256]{1,0:T(8,128)S(1)}, f32[128,256]{1,0:T(8,128)S(1)}, u32[]{:S(2)}, u32[]{:S(2)}) collective-permute-start(f32[128,256]{1,0:T(8,128)S(1)} %get-tuple-element.61), channel_id=1, source_target_pairs={{0,1},{1,0},{2,3},{3,2},{4,5},{5,4},{6,7},{7,6},{8,9},{9,8},{10,11... | collective-permute-start | bytes 393224 | tf_op jit(solution)/shard_map/ppermute | solution.py:525
  80.2 1.0 %collective-permute-done.26.refs_1_ = f32[128,256]{1,0:T(8,128)S(1)} collective-permute-done((f32[128,256]{1,0:T(8,128)S(1)}, f32[128,256]{1,0:T(8,128)S(1)}, u32[]{:S(2)}, u32[]{:S(2)}) %collective-permute-start.26) | collective-permute-done | bytes 131104 | tf_op jit(solution)/shard_map/ppermute | solution.py:525
  (48 shorter events, 8.8 us)
Async XLA Ops:
  6.0 3.3 %collective-permute-start = (bf16[1,128,1024]{2,1,0:T(8,128)(2,1)S(1)}, bf16[1,128,1024]{2,1,0:T(8,128)(2,1)S(1)}, u32[]{:S(2)}, u32[]{:S(2)}) collective-permute-start(bf16[1,128,1024]{2,1,0:T(8,128)(2,1)S(1)} %get-tuple-element.38), channel_id=1, source_target_pairs={{0,1},{1,0},{2,3},{3,2},{4,5},{5,4},{6,7},{7,6},{8,9},{9,8},{10,11... | collective-permute-start | bytes 786440 | tf_op jit(solution)/shard_map/ppermute | solution.py:525
  8.7 4.1 %collective-permute-start.2 = (bf16[1,128,1024]{2,1,0:T(8,128)(2,1)S(1)}, bf16[1,128,1024]{2,1,0:T(8,128)(2,1)S(1)}, u32[]{:S(2)}, u32[]{:S(2)}) collective-permute-start(bf16[1,128,1024]{2,1,0:T(8,128)(2,1)S(1)} %get-tuple-element.39), channel_id=1, source_target_pairs={{0,1},{1,0},{2,3},{3,2},{4,5},{5,4},{6,7},{7,6},{8,9},{9,8},{10,11... | collective-permute-start | bytes 786440 | tf_op jit(solution)/shard_map/ppermute | solution.py:525
  8.8 4.0 %collective-permute-start.3 = (bf16[1,128,1024]{2,1,0:T(8,128)(2,1)S(1)}, bf16[1,128,1024]{2,1,0:T(8,128)(2,1)S(1)}, u32[]{:S(2)}, u32[]{:S(2)}) collective-permute-start(bf16[1,128,1024]{2,1,0:T(8,128)(2,1)S(1)} %get-tuple-element.40), channel_id=1, source_target_pairs={{0,1},{1,0},{2,3},{3,2},{4,5},{5,4},{6,7},{7,6},{8,9},{9,8},{10,11... | collective-permute-start | bytes 786440 | tf_op jit(solution)/shard_map/ppermute | solution.py:525
  9.2 3.6 %collective-permute-start.4 = (bf16[1,128,1024]{2,1,0:T(8,128)(2,1)S(1)}, bf16[1,128,1024]{2,1,0:T(8,128)(2,1)S(1)}, u32[]{:S(2)}, u32[]{:S(2)}) collective-permute-start(bf16[1,128,1024]{2,1,0:T(8,128)(2,1)S(1)} %get-tuple-element.41), channel_id=1, source_target_pairs={{0,1},{1,0},{2,3},{3,2},{4,5},{5,4},{6,7},{7,6},{8,9},{9,8},{10,11... | collective-permute-start | bytes 786440 | tf_op jit(solution)/shard_map/ppermute | solution.py:525
  9.4 7.5 %collective-permute-start.1 = (bf16[128,1024]{1,0:T(8,128)(2,1)S(1)}, bf16[128,1024]{1,0:T(8,128)(2,1)S(1)}, u32[]{:S(2)}, u32[]{:S(2)}) collective-permute-start(bf16[128,1024]{1,0:T(8,128)(2,1)S(1)} %add_up.4.refs_0_), channel_id=1, source_target_pairs={{0,2},{1,3},{2,0},{3,1},{4,6},{5,7},{6,4},{7,5},{8,10},{9,11},{10,... | collective-permute-start | bytes 786440 | tf_op jit(solution)/shard_map/ppermute | solution.py:525
  11.3 10.1 %copy-start.1 = (bf16[128,1024]{1,0:T(8,128)(2,1)S(1)}, bf16[128,1024]{1,0:T(8,128)(2,1)}, u32[]{:S(2)}) copy-start(bf16[128,1024]{1,0:T(8,128)(2,1)} %refs_1_.8) | copy-start | bytes 786436
  11.3 10.4 %copy-start = (bf16[16384,128]{1,0:T(8,128)(2,1)S(1)}, bf16[16384,128]{1,0:T(8,128)(2,1)}, u32[]{:S(2)}) copy-start(bf16[16384,128]{1,0:T(8,128)(2,1)} %refs_1_.9) | copy-start | bytes 12582916
  11.3 13.2 %collective-permute-start.7 = (bf16[2,128,1024]{2,1,0:T(8,128)(2,1)S(1)}, bf16[2,128,1024]{2,1,0:T(8,128)(2,1)S(1)}, u32[]{:S(2)}, u32[]{:S(2)}) collective-permute-start(bf16[2,128,1024]{2,1,0:T(8,128)(2,1)S(1)} %partials.4.refs_0_), channel_id=1, source_target_pairs={{0,1},{1,0},{2,3},{3,2},{4,5},{5,4},{6,7},{7,6},{8,9},{9,8},{10,11... | collective-permute-start | bytes 1572872 | tf_op jit(solution)/shard_map/ppermute | solution.py:525
  17.0 6.6 %collective-permute-start.5 = (bf16[128,1024]{1,0:T(8,128)(2,1)S(1)}, bf16[128,1024]{1,0:T(8,128)(2,1)S(1)}, u32[]{:S(2)}, u32[]{:S(2)}) collective-permute-start(bf16[128,1024]{1,0:T(8,128)(2,1)S(1)} %get-tuple-element.45), channel_id=1, source_target_pairs={{0,2},{1,3},{2,0},{3,1},{4,6},{5,7},{6,4},{7,5},{8,10},{9,11},{10,... | collective-permute-start | bytes 786440 | tf_op jit(solution)/shard_map/ppermute | solution.py:525
  18.3 6.2 %collective-permute-start.6 = (bf16[128,1024]{1,0:T(8,128)(2,1)S(1)}, bf16[128,1024]{1,0:T(8,128)(2,1)S(1)}, u32[]{:S(2)}, u32[]{:S(2)}) collective-permute-start(bf16[128,1024]{1,0:T(8,128)(2,1)S(1)} %get-tuple-element.42.refs_0_), channel_id=1, source_target_pairs={{0,4},{1,5},{2,6},{3,7},{4,0},{5,1},{6,2},{7,3},{8,12},{9,13},{10,... | collective-permute-start | bytes 786440 | tf_op jit(solution)/shard_map/ppermute | solution.py:525
  19.6 9.4 %collective-permute-start.11 = (bf16[2,128,1024]{2,1,0:T(8,128)(2,1)S(1)}, bf16[2,128,1024]{2,1,0:T(8,128)(2,1)S(1)}, u32[]{:S(2)}, u32[]{:S(2)}) collective-permute-start(bf16[2,128,1024]{2,1,0:T(8,128)(2,1)S(1)} %partials.5.refs_0_), channel_id=1, source_target_pairs={{0,1},{1,0},{2,3},{3,2},{4,5},{5,4},{6,7},{7,6},{8,9},{9,8},{10,11... | collective-permute-start | bytes 1572872 | tf_op jit(solution)/shard_map/ppermute | solution.py:525
  24.9 5.3 %collective-permute-start.10 = (bf16[128,1024]{1,0:T(8,128)(2,1)S(1)}, bf16[128,1024]{1,0:T(8,128)(2,1)S(1)}, u32[]{:S(2)}, u32[]{:S(2)}) collective-permute-start(bf16[128,1024]{1,0:T(8,128)(2,1)S(1)} %get-tuple-element.49), channel_id=1, source_target_pairs={{0,1},{1,0},{2,3},{3,2},{4,8},{5,9},{6,10},{7,11},{8,4},{9,5},{10,... | collective-permute-start | bytes 786440 | tf_op jit(solution)/shard_map/ppermute | solution.py:525
  25.1 5.5 %collective-permute-start.8 = (bf16[128,1024]{1,0:T(8,128)(2,1)S(1)}, bf16[128,1024]{1,0:T(8,128)(2,1)S(1)}, u32[]{:S(2)}, u32[]{:S(2)}) collective-permute-start(bf16[128,1024]{1,0:T(8,128)(2,1)S(1)} %get-tuple-element.47), channel_id=1, source_target_pairs={{0,2},{1,3},{2,0},{3,1},{4,6},{5,7},{6,4},{7,5},{8,10},{9,11},{10,... | collective-permute-start | bytes 786440 | tf_op jit(solution)/shard_map/ppermute | solution.py:525
  25.4 9.1 %collective-permute-start.9 = (bf16[128,1024]{1,0:T(8,128)(2,1)S(1)}, bf16[128,1024]{1,0:T(8,128)(2,1)S(1)}, u32[]{:S(2)}, u32[]{:S(2)}) collective-permute-start(bf16[128,1024]{1,0:T(8,128)(2,1)S(1)} %get-tuple-element.48), channel_id=1, source_target_pairs={{0,4},{1,5},{2,6},{3,7},{4,0},{5,1},{6,2},{7,3},{8,12},{9,13},{10,... | collective-permute-start | bytes 786440 | tf_op jit(solution)/shard_map/ppermute | solution.py:525
  34.8 24.2 %copy-start.2 = (bf16[16384]{0:T(1024)(128)(2,1)S(1)}, bf16[16384]{0:T(1024)(128)(2,1)}, u32[]{:S(2)}) copy-start(bf16[16384]{0:T(1024)(128)(2,1)} %param.17) | copy-start | bytes 98308
  34.8 6.1 %collective-permute-start.12 = (bf16[128,1024]{1,0:T(8,128)(2,1)S(1)}, bf16[128,1024]{1,0:T(8,128)(2,1)S(1)}, u32[]{:S(2)}, u32[]{:S(2)}) collective-permute-start(bf16[128,1024]{1,0:T(8,128)(2,1)S(1)} %get-tuple-element.51), channel_id=1, source_target_pairs={{0,2},{1,3},{2,0},{3,1},{4,6},{5,7},{6,4},{7,5},{8,10},{9,11},{10,... | collective-permute-start | bytes 786440 | tf_op jit(solution)/shard_map/ppermute | solution.py:525
  36.1 7.0 %collective-permute-start.13 = (bf16[128,1024]{1,0:T(8,128)(2,1)S(1)}, bf16[128,1024]{1,0:T(8,128)(2,1)S(1)}, u32[]{:S(2)}, u32[]{:S(2)}) collective-permute-start(bf16[128,1024]{1,0:T(8,128)(2,1)S(1)} %get-tuple-element.52), channel_id=1, source_target_pairs={{0,4},{1,5},{2,6},{3,7},{4,0},{5,1},{6,2},{7,3},{8,12},{9,13},{10,... | collective-permute-start | bytes 786440 | tf_op jit(solution)/shard_map/ppermute | solution.py:525
  38.2 6.1 %collective-permute-start.14 = (bf16[128,1024]{1,0:T(8,128)(2,1)S(1)}, bf16[128,1024]{1,0:T(8,128)(2,1)S(1)}, u32[]{:S(2)}, u32[]{:S(2)}) collective-permute-start(bf16[128,1024]{1,0:T(8,128)(2,1)S(1)} %get-tuple-element.53), channel_id=1, source_target_pairs={{0,1},{1,0},{2,3},{3,2},{4,8},{5,9},{6,10},{7,11},{8,4},{9,5},{10,... | collective-permute-start | bytes 786440 | tf_op jit(solution)/shard_map/ppermute | solution.py:525
  38.2 20.9 %collective-permute-start.20 = (bf16[4,1024,128]{2,1,0:T(8,128)(2,1)S(1)}, bf16[4,1024,128]{2,1,0:T(8,128)(2,1)S(1)}, u32[]{:S(2)}, u32[]{:S(2)}) collective-permute-start(bf16[4,1024,128]{2,1,0:T(8,128)(2,1)S(1)} %get-tuple-element.44.refs_0_), channel_id=1, source_target_pairs={{0,1},{1,0},{2,3},{3,2},{4,5},{5,4},{6,7},{7,6},{8,9},{9,8},{10,11... | collective-permute-start | bytes 3145736 | tf_op jit(solution)/shard_map/ppermute | solution.py:525
  39.9 19.1 %collective-permute-start.21 = (bf16[4,1024,128]{2,1,0:T(8,128)(2,1)S(1)}, bf16[4,1024,128]{2,1,0:T(8,128)(2,1)S(1)}, u32[]{:S(2)}, u32[]{:S(2)}) collective-permute-start(bf16[4,1024,128]{2,1,0:T(8,128)(2,1)S(1)} %get-tuple-element.59), channel_id=1, source_target_pairs={{0,1},{1,0},{2,3},{3,2},{4,5},{5,4},{6,7},{7,6},{8,9},{9,8},{10,11... | collective-permute-start | bytes 3145736 | tf_op jit(solution)/shard_map/ppermute | solution.py:525
  44.5 5.3 %collective-permute-start.15 = (bf16[128,1024]{1,0:T(8,128)(2,1)S(1)}, bf16[128,1024]{1,0:T(8,128)(2,1)S(1)}, u32[]{:S(2)}, u32[]{:S(2)}) collective-permute-start(bf16[128,1024]{1,0:T(8,128)(2,1)S(1)} %regrid.1.refs_0_.refs_2_), channel_id=1, source_target_pairs={{0,2},{1,3},{2,0},{3,1},{4,6},{5,7},{6,4},{7,5},{8,10},{9,11},{10,... | collective-permute-start | bytes 786440 | tf_op jit(solution)/shard_map/ppermute | solution.py:525
  45.0 5.5 %collective-permute-start.16 = (bf16[128,1024]{1,0:T(8,128)(2,1)S(1)}, bf16[128,1024]{1,0:T(8,128)(2,1)S(1)}, u32[]{:S(2)}, u32[]{:S(2)}) collective-permute-start(bf16[128,1024]{1,0:T(8,128)(2,1)S(1)} %regrid.1.refs_0_.refs_2_), channel_id=1, source_target_pairs={{0,4},{1,5},{2,6},{3,7},{4,0},{5,1},{6,2},{7,3},{8,12},{9,13},{10,... | collective-permute-start | bytes 786440 | tf_op jit(solution)/shard_map/ppermute | solution.py:525
  45.3 5.5 %collective-permute-start.17 = (bf16[128,1024]{1,0:T(8,128)(2,1)S(1)}, bf16[128,1024]{1,0:T(8,128)(2,1)S(1)}, u32[]{:S(2)}, u32[]{:S(2)}) collective-permute-start(bf16[128,1024]{1,0:T(8,128)(2,1)S(1)} %regrid.1.refs_0_.refs_2_), channel_id=1, source_target_pairs={{0,1},{1,0},{2,3},{3,2},{4,8},{5,9},{6,10},{7,11},{8,4},{9,5},{10,... | collective-permute-start | bytes 786440 | tf_op jit(solution)/shard_map/ppermute | solution.py:525
  50.8 5.2 %collective-permute-start.18 = (bf16[128,1024]{1,0:T(8,128)(2,1)S(1)}, bf16[128,1024]{1,0:T(8,128)(2,1)S(1)}, u32[]{:S(2)}, u32[]{:S(2)}) collective-permute-start(bf16[128,1024]{1,0:T(8,128)(2,1)S(1)} %get-tuple-element.57.refs_3_), channel_id=1, source_target_pairs={{0,2},{1,3},{2,0},{3,1},{4,6},{5,7},{6,4},{7,5},{8,10},{9,11},{10,... | collective-permute-start | bytes 786440 | tf_op jit(solution)/shard_map/ppermute | solution.py:525
  51.9 5.2 %collective-permute-start.19 = (bf16[128,1024]{1,0:T(8,128)(2,1)S(1)}, bf16[128,1024]{1,0:T(8,128)(2,1)S(1)}, u32[]{:S(2)}, u32[]{:S(2)}) collective-permute-start(bf16[128,1024]{1,0:T(8,128)(2,1)S(1)} %get-tuple-element.58.refs_1_), channel_id=1, source_target_pairs={{0,4},{1,5},{2,6},{3,7},{4,0},{5,1},{6,2},{7,3},{8,12},{9,13},{10,... | collective-permute-start | bytes 786440 | tf_op jit(solution)/shard_map/ppermute | solution.py:525
  52.0 5.6 %collective-permute-start.23 = (bf16[128,1024]{1,0:T(8,128)(2,1)S(1)}, bf16[128,1024]{1,0:T(8,128)(2,1)S(1)}, u32[]{:S(2)}, u32[]{:S(2)}) collective-permute-start(bf16[128,1024]{1,0:T(8,128)(2,1)S(1)} %get-tuple-element.57.refs_3_), channel_id=1, source_target_pairs={{0,1},{1,0},{2,3},{3,2},{4,8},{5,9},{6,10},{7,11},{8,4},{9,5},{10,... | collective-permute-start | bytes 786440 | tf_op jit(solution)/shard_map/ppermute | solution.py:525
  57.1 6.2 %collective-permute-start.22 = (bf16[128,1024]{1,0:T(8,128)(2,1)S(1)}, bf16[128,1024]{1,0:T(8,128)(2,1)S(1)}, u32[]{:S(2)}, u32[]{:S(2)}) collective-permute-start(bf16[128,1024]{1,0:T(8,128)(2,1)S(1)} %choose.2.refs_0_.refs_4_), channel_id=1, source_target_pairs={{0,2},{1,3},{2,0},{3,1},{4,6},{5,7},{6,4},{7,5},{8,10},{9,11},{10,... | collective-permute-start | bytes 786440 | tf_op jit(solution)/shard_map/ppermute | solution.py:525
  57.6 7.0 %collective-permute-start.24 = (bf16[128,1024]{1,0:T(8,128)(2,1)S(1)}, bf16[128,1024]{1,0:T(8,128)(2,1)S(1)}, u32[]{:S(2)}, u32[]{:S(2)}) collective-permute-start(bf16[128,1024]{1,0:T(8,128)(2,1)S(1)} %collective-permute-done.23.refs_2_), channel_id=1, source_target_pairs={{0,4},{1,5},{2,6},{3,7},{4,0},{5,1},{6,2},{7,3},{8,12},{9,13},{10,... | collective-permute-start | bytes 786440 | tf_op jit(solution)/shard_map/ppermute | solution.py:525
  64.6 8.2 %collective-permute-start.25 = (bf16[128,1024]{1,0:T(8,128)(2,1)S(1)}, bf16[128,1024]{1,0:T(8,128)(2,1)S(1)}, u32[]{:S(2)}, u32[]{:S(2)}) collective-permute-start(bf16[128,1024]{1,0:T(8,128)(2,1)S(1)} %choose.3.refs_5_), channel_id=1, source_target_pairs={{0,2},{1,3},{2,0},{3,1},{4,6},{5,7},{6,4},{7,5},{8,10},{9,11},{10,... | collective-permute-start | bytes 786440 | tf_op jit(solution)/shard_map/ppermute | solution.py:525
  73.1 8.1 %collective-permute-start.26 = (f32[128,256]{1,0:T(8,128)S(1)}, f32[128,256]{1,0:T(8,128)S(1)}, u32[]{:S(2)}, u32[]{:S(2)}) collective-permute-start(f32[128,256]{1,0:T(8,128)S(1)} %get-tuple-element.61), channel_id=1, source_target_pairs={{0,1},{1,0},{2,3},{3,2},{4,5},{5,4},{6,7},{7,6},{8,9},{9,8},{10,11... | collective-permute-start | bytes 393224 | tf_op jit(solution)/shard_map/ppermute | solution.py:525

commit v6 on v5

--- a/solution.py
+++ b/solution.py
@@ -91,12 +91,16 @@
     outer, mid, core = place(inner)
     dest = targets(outer)[0]
 
+    copies = min(4, steps)
+    per_copy = steps // copies
+    size = slots // copies
+
     def copy_k(j):
-        part = pl.ds(j * chunk, chunk)
+        part = pl.ds(j * size, size)
         return pltpu.make_async_copy(k_hbm.at[0, part], k_ref.at[part], sems.at[1 + j])
 
     def copy_v(j):
-        part = pl.ds(j * chunk, chunk)
+        part = pl.ds(j * size, size)
         return pltpu.make_async_copy(v_hbm.at[0, part], v_ref.at[part], sems.at[1 + steps + j])
 
     def shard_of(shift):
@@ -109,11 +113,11 @@
     copy_h = pltpu.make_async_copy(h_hbm, h_ref, sems.at[2 * steps + 4])
     copy_q.start()
     copy_pos.start()
-    for j in range(steps):
+    for j in range(copies):
         copy_k(j).start()
     copy_table.start()
     copy_h.start()
-    for j in range(steps):
+    for j in range(copies):
         copy_v(j).start()
     copy_w.start()
 
@@ -125,7 +129,8 @@
     queries = q_ref[...]
     peak = jnp.full((tok, ROT), -jnp.inf, F32)
     for j in range(steps):
-        copy_k(j).wait()
+        if j % per_copy == 0:
+            copy_k(j // per_copy).wait()
         scores = lax.dot_general(
             queries, k_ref[j * chunk : (j + 1) * chunk], (((1,), (1,)), ((), ())),
             preferred_element_type=F32,
@@ -144,8 +149,9 @@
     factor = math.log2(math.e) / math.sqrt(HD)
     total = jnp.zeros((tok, ROT), F32)
     acc = jnp.zeros((tok, HD), F32)
+    for j in range(copies):
+        copy_v(j).wait()
     for j in range(steps):
-        copy_v(j).wait()
         pieces = []
         for i in range(chunk // ROT):
             base = j * chunk + i * ROT
@@ -348,22 +354,36 @@
     )
 
 
-def choose_kernel(inner, inner_ref, end_ref, out_ref):
+HALVES = 2
+
+
+def halves(shape):
+    rows = shape[0] // HALVES
+    return [jax.ShapeDtypeStruct((rows, *shape[1:]), BF16)] * HALVES
+
+
+def split_rows(value_ref, out_refs):
+    rows = out_refs[0].shape[0]
+    for i, out_ref in enumerate(out_refs):
+        out_ref[...] = value_ref[i * rows : (i + 1) * rows]
+
+
+def choose_kernel(inner, inner_ref, end_ref, *out_refs):
     inside = is_inner(place(inner)[0])
 
     @pl.when(inside)
     def _():
-        out_ref[...] = inner_ref[...]
+        split_rows(inner_ref, out_refs)
 
     @pl.when(jnp.logical_not(inside))
     def _():
-        out_ref[...] = end_ref[...]
+        split_rows(end_ref, out_refs)
 
 
 def choose(inner, at_inner, at_end, after=()):
     return kernel_call(
         functools.partial(choose_kernel, inner),
-        jax.ShapeDtypeStruct(at_inner.shape, at_inner.dtype),
+        halves(at_inner.shape),
         [at_inner, at_end],
         [vmem()] * 2,
         after=after,
@@ -437,14 +457,16 @@
     order = (own, near, third, far)
     acc_in = refs[0] if has_acc else None
     refs = refs[1:] if has_acc else refs
-    values_in = refs[: len(places)]
-    outs = refs[len(places) :]
+    count = sum(parts for _, _, parts in places)
+    values_in = list(refs[:count])
+    outs = refs[count:]
     cols, width = w_ref.shape[1:]
     acc = acc_in[:, :width] if has_acc else 0.0
     squares = acc_in[:, width:] if has_acc else 0.0
-    for ref, (phase, shift) in zip(values_in, places):
+    for phase, shift, parts in places:
         block = order[phase] * inner + lax.rem(mid + inner - shift, inner)
-        values = ref[...]
+        values = [values_in.pop(0)[...] for _ in range(parts)]
+        values = values[0] if parts == 1 else jnp.concatenate(values, axis=0)
         acc = acc + jnp.dot(values, w_ref[block], preferred_element_type=F32)
         for i in range(cols // ROT):
             row = (block * 2 + core) * (cols // ROT) + i
@@ -464,9 +486,9 @@
 
 def project(inner, weight, rows, acc, pieces, split=False, after=()):
     _, cols, width = weight.shape
-    arrays = [array for _, _, array in pieces]
-    tok = arrays[0].shape[0]
-    places = tuple((phase, shift) for phase, shift, _ in pieces)
+    arrays = [part for _, _, parts in pieces for part in parts]
+    tok = sum(part.shape[0] for part in pieces[0][2])
+    places = tuple((phase, shift, len(parts)) for phase, shift, parts in pieces)
     accs = [] if acc is None else [acc]
     if split:
         out = [jax.ShapeDtypeStruct((tok, HD + ROT), F32)] * 2
@@ -548,23 +570,26 @@
     def grid_blocks(work, after=()):
         return partials(inner, cols, work, context, out_weight, rows, had, after=after)
 
-    blocks2 = ((0, 0),) + phase_blocks(1)
-    keep1, keep2, keep3, keep4, *send2 = grid_blocks(
-        (
-            (True, away1),
-            (True, blocks2),
-            (True, phase_blocks(2)),
-            (True, phase_blocks(3)),
-            *((False, (block,)) for block in blocks2),
-        )
+    blocks2 = ((0, 0),) + tuple((1, s) for s in shifts)
+    keep1, keep2, *send2 = grid_blocks(
+        ((True, away1), (True, blocks2), *((False, (block,)) for block in blocks2))
     )
     other2 = [swap_core(send) for send in send2]
     items1 = [((0, s - 1, False), (1, s - 1, False)) for s in shifts]
     pay1 = add_up(inner, [keep1, other1], items1, after=[keep2])
     come1 = [shift_mid(pay, s) for s, pay in zip(shifts, pay1)]
-    (send3,) = grid_blocks(((False, phase_blocks(2)),), pay1[:1])
-    other3 = swap_core(send3)
-    (send4,) = grid_blocks(((False, phase_blocks(3)),), [send3])
+    near_block = ((1, 0),)
+    send2n, send3 = grid_blocks(((False, near_block), (False, phase_blocks(2))), pay1[:1])
+    other2n, other3 = swap_core(send2n), swap_core(send3)
+    send4, keep2n, keep3, keep4 = grid_blocks(
+        (
+            (False, phase_blocks(3)),
+            (True, near_block),
+            (True, phase_blocks(2)),
+            (True, phase_blocks(3)),
+        ),
+        [send3],
+    )
     other4 = swap_core(send4)
 
     def sums(arrays, outputs, after=()):
@@ -579,6 +604,7 @@
         return [(name, None, False) for name in names]
 
     own2 = {"keep2": keep2} | {f"other2_{i}": other for i, other in enumerate(other2)}
+    own2n = {"keep2n": keep2n, "other2n": other2n}
     own3 = {"keep3": keep3, "other3": other3}
     own4 = {"keep4": keep4, "other4": other4}
 
@@ -590,16 +616,16 @@
 
     came1 = came(1, come1)
     near1 = part2(0) + added(came1)
-    *pay2, end1 = sums(came1 | own2, [*(part2(1 + s) for s in shifts), near1], after=[send4])
+    *pay2, end1 = sums(came1 | own2, [*(part2(s) for s in shifts), near1], after=[send4])
     came2 = came(2, [shift_mid(pay, s) for s, pay in zip(shifts, pay2)])
     from_end1 = {"end1": swap_pairs(end1)}
     turned_residual, factors = turn_residual(inner, residual, rows, had, after=[end1])
     picked = select_rows(inner, next_query_weight, cols, after=[factors])
     next_other = [swap_core(part) for part in picked]
 
-    near2 = part2(1) + added(came2)
+    near2 = part("2n", 0) + added(came2)
     *pay3, end2, mid2 = sums(
-        came2 | from_end1 | own2 | own3 | came1,
+        came2 | from_end1 | own2 | own2n | own3 | came1,
         [*(part(3, s) for s in shifts), near2, near1 + [("end1", None, True)]],
         after=picked[:1],
     )
@@ -608,7 +634,7 @@
     from_mid2 = {"mid2": swap_middle(mid2)}
 
     *pay4, mid3, near3 = sums(
-        came3 | from_end2 | from_mid2 | own2 | own3 | own4 | came2,
+        came3 | from_end2 | from_mid2 | own2n | own3 | own4 | came2,
         [
             *(part(4, s) for s in shifts),
             near2 + [("end2", None, True)],
@@ -631,22 +657,29 @@
     mid1 = swap_middle(grid)
     hidden_out, mark = hidden(inner, items, residual, factors, had, last, after=[grid])
     near, mid1 = gate([near, mid1], after=[*x1, mark])
+
+    def shift_parts(parts, shift):
+        return [shift_mid(part, shift) for part in parts]
+
     x2 = [shift_mid(near, s) for s in shifts]
     ends2 = swap_pairs(mid1)
     mids2 = swap_middle(near)
     third = choose(inner, mid1, ends2, after=x2)
-    x3 = [shift_mid(third, s) for s in shifts]
+    x3 = [shift_parts(third, s) for s in shifts]
     ends3 = swap_pairs(mids2)
-    turned_next = turn_next(inner, next_query_weight, next_other, gain, rows, had, after=[third])
-    fourth = choose(inner, mids2, ends3, after=[*x3, turned_next])
-    x4 = [shift_mid(fourth, s) for s in shifts]
+    turned_next = turn_next(
+        inner, next_query_weight, next_other, gain, rows, had, after=third[:1]
+    )
+    fourth = choose(inner, mids2, ends3, after=[*sum(x3, []), turned_next])
+    x4 = [shift_parts(fourth, s) for s in shifts]
     acc = project(
         inner,
         turned_next,
         rows,
         None,
-        [(0, 0, grid), (1, 0, near), (2, 0, third), (3, 0, fourth)]
-        + [(phase, s, x[s - 1]) for phase, x in enumerate((x1, x2, x3)) for s in shifts],
+        [(0, 0, [grid]), (1, 0, [near]), (2, 0, third), (3, 0, fourth)]
+        + [(phase, s, [x[s - 1]]) for phase, x in enumerate((x1, x2)) for s in shifts]
+        + [(2, s, x3[s - 1]) for s in shifts],
     )
     own, other = project(
         inner, turned_next, rows, acc, [(3, s, x4[s - 1]) for s in shifts], split=True

time: 82.1 us -> 83.3 us (1.015)
  the two profiles are of different devices: /device:TPU:17 before, /device:TPU:0 now
where the time goes in v6:
time: 83.3 us; the launch traced here: 83.2 us
  waiting for transfers between devices  37.2 us (45%)
  starting transfers between devices  32.1 us (39%)
  Pallas kernels  13 us (16%)
  between operations  0.84 us (1%)
    ppermute x29, waiting for transfers between devices, permute(): return lax.ppermute(value, 'tp', moves)  37.2 us
    ppermute x29, starting transfers between devices, permute(): return lax.ppermute(value, 'tp', moves)  32.1 us
    pallas_call x19, Pallas kernels, kernel_call(): pl.pallas_call(ordered, out_shape=out_shape, in_specs=[anywhere()] * extr...  13 us
  transfers between devices with their start and end apart: 29, of which 15 were waited for; matrix products, arithmetic and copies ran while one was open for 0% of the time, Pallas kernels for 9%

profile of v6, /device:TPU:0, one launch (start us, length us, event | category | flops | bytes accessed | tf_op | source)
XLA Modules:
  0.0 83.2 jit_solution(8832797380955602974)
XLA Ops:
  0.6 4.1 %attend.1 = (bf16[128,128]{1,0:T(8,128)(2,1)S(1)}, f32[2,128,128]{2,1,0:T(8,128)S(1)}, bf16[1,128,1024]{2,1,0:T(8,128)(2,1)S(1)}, bf16[128,16384]{1,0:T(8,128)(2,1)S(1)}, bf16[128,128]{1,0:T(8,128)(2,1)S(1)}) custom-call(bf16[1,128,128]{2,1,0:T(8,128)(2,1)} %refs_0_.1, bf16[1,8192,128]{2,1,0:T(8,128)(2,1)} %refs_1_.5, bf16[1,8192,128]{2,1,0:T(8,128)(2,1)} %refs_2_.1, ...), custom_call_target="tpu_custom_call" | custom-call | tf_op jit(solution)/shard_map/attend/pallas_call | solution.py:59
  5.3 1.1 %partials.3 = (bf16[1,128,1024]{2,1,0:T(8,128)(2,1)S(1)}, bf16[2,128,1024]{2,1,0:T(8,128)(2,1)S(1)}, bf16[1,128,1024]{2,1,0:T(8,128)(2,1)S(1)}, bf16[1,128,1024]{2,1,0:T(8,128)(2,1)S(1)}) custom-call(bf16[128,128]{1,0:T(8,128)(2,1)S(1)} %get-tuple-element.39.refs_0_.refs_1_, bf16[128,16384]{1,0:T(8,128)(2,1)S(1)} %get-tuple-element.40.refs_1_.refs_2_, ...), custom_call_target="tpu_custom_call" | custom-call | tf_op jit(solution)/shard_map/partials/pallas_call | solution.py:59
  7.0 2.6 %collective-permute-start.1 = (bf16[128,1024]{1,0:T(8,128)(2,1)S(1)}, bf16[128,1024]{1,0:T(8,128)(2,1)S(1)}, u32[]{:S(2)}, u32[]{:S(2)}) collective-permute-start(bf16[128,1024]{1,0:T(8,128)(2,1)S(1)} %add_up.4.refs_0_), channel_id=1, source_target_pairs={{0,2},{1,3},{2,0},{3,1},{4,6},{5,7},{6,4},{7,5},{8,10},{9,11},{10,... | collective-permute-start | bytes 786440 | tf_op jit(solution)/shard_map/ppermute | solution.py:547
  9.6 0.8 partials.4
  10.7 1.3 %partials.5 = (bf16[2,128,1024]{2,1,0:T(8,128)(2,1)S(1)}, bf16[1,128,1024]{2,1,0:T(8,128)(2,1)S(1)}, bf16[2,128,1024]{2,1,0:T(8,128)(2,1)S(1)}, bf16[2,128,1024]{2,1,0:T(8,128)(2,1)S(1)}) custom-call(bf16[2,128,1024]{2,1,0:T(8,128)(2,1)S(1)} %get-tuple-element.46.refs_0_, bf16[128,128]{1,0:T(8,128)(2,1)S(1)} %get-tuple-element.39.refs_0_.refs_1_, ...), custom_call_target="tpu_custom_call" | custom-call | tf_op jit(solution)/shard_map/partials/pallas_call | solution.py:59
  12.5 4.1 %collective-permute-done.1.refs_1_.refs_10_ = bf16[128,1024]{1,0:T(8,128)(2,1)S(1)} collective-permute-done((bf16[128,1024]{1,0:T(8,128)(2,1)S(1)}, bf16[128,1024]{1,0:T(8,128)(2,1)S(1)}, u32[]{:S(2)}, u32[]{:S(2)}) %collective-permute-start.1) | collective-permute-done | bytes 262176 | tf_op jit(solution)/shard_map/ppermute | solution.py:547
  16.7 1.8 %collective-permute-start.4 = (bf16[128,1024]{1,0:T(8,128)(2,1)S(1)}, bf16[128,1024]{1,0:T(8,128)(2,1)S(1)}, u32[]{:S(2)}, u32[]{:S(2)}) collective-permute-start(bf16[128,1024]{1,0:T(8,128)(2,1)S(1)} %get-tuple-element.53), channel_id=1, source_target_pairs={{0,2},{1,3},{2,0},{3,1},{4,6},{5,7},{6,4},{7,5},{8,10},{9,11},{10,... | collective-permute-start | bytes 786440 | tf_op jit(solution)/shard_map/ppermute | solution.py:547
  18.5 1.6 %collective-permute-start.5 = (bf16[128,1024]{1,0:T(8,128)(2,1)S(1)}, bf16[128,1024]{1,0:T(8,128)(2,1)S(1)}, u32[]{:S(2)}, u32[]{:S(2)}) collective-permute-start(bf16[128,1024]{1,0:T(8,128)(2,1)S(1)} %get-tuple-element.50.refs_0_), channel_id=1, source_target_pairs={{0,4},{1,5},{2,6},{3,7},{4,0},{5,1},{6,2},{7,3},{8,12},{9,13},{10,... | collective-permute-start | bytes 786440 | tf_op jit(solution)/shard_map/ppermute | solution.py:547
  20.5 4.3 %collective-permute-done.4.refs_1_.refs_9_ = bf16[128,1024]{1,0:T(8,128)(2,1)S(1)} collective-permute-done((bf16[128,1024]{1,0:T(8,128)(2,1)S(1)}, bf16[128,1024]{1,0:T(8,128)(2,1)S(1)}, u32[]{:S(2)}, u32[]{:S(2)}) %collective-permute-start.4) | collective-permute-done | bytes 262176 | tf_op jit(solution)/shard_map/ppermute | solution.py:547
  24.8 1.3 %collective-permute-done.5.refs_2_ = bf16[128,1024]{1,0:T(8,128)(2,1)S(1)} collective-permute-done((bf16[128,1024]{1,0:T(8,128)(2,1)S(1)}, bf16[128,1024]{1,0:T(8,128)(2,1)S(1)}, u32[]{:S(2)}, u32[]{:S(2)}) %collective-permute-start.5) | collective-permute-done | bytes 262176 | tf_op jit(solution)/shard_map/ppermute | solution.py:547
  27.0 3.1 %collective-permute-start.9 = (bf16[128,1024]{1,0:T(8,128)(2,1)S(1)}, bf16[128,1024]{1,0:T(8,128)(2,1)S(1)}, u32[]{:S(2)}, u32[]{:S(2)}) collective-permute-start(bf16[128,1024]{1,0:T(8,128)(2,1)S(1)} %get-tuple-element.58), channel_id=1, source_target_pairs={{0,4},{1,5},{2,6},{3,7},{4,0},{5,1},{6,2},{7,3},{8,12},{9,13},{10,... | collective-permute-start | bytes 786440 | tf_op jit(solution)/shard_map/ppermute | solution.py:547
  30.2 5.0 %collective-permute-done.8.refs_0_ = bf16[128,1024]{1,0:T(8,128)(2,1)S(1)} collective-permute-done((bf16[128,1024]{1,0:T(8,128)(2,1)S(1)}, bf16[128,1024]{1,0:T(8,128)(2,1)S(1)}, u32[]{:S(2)}, u32[]{:S(2)}) %collective-permute-start.8) | collective-permute-done | bytes 262176 | tf_op jit(solution)/shard_map/ppermute | solution.py:547
  35.8 1.6 %collective-permute-start.12 = (bf16[128,1024]{1,0:T(8,128)(2,1)S(1)}, bf16[128,1024]{1,0:T(8,128)(2,1)S(1)}, u32[]{:S(2)}, u32[]{:S(2)}) collective-permute-start(bf16[128,1024]{1,0:T(8,128)(2,1)S(1)} %get-tuple-element.61), channel_id=1, source_target_pairs={{0,2},{1,3},{2,0},{3,1},{4,6},{5,7},{6,4},{7,5},{8,10},{9,11},{10,... | collective-permute-start | bytes 786440 | tf_op jit(solution)/shard_map/ppermute | solution.py:547
  37.4 1.1 %collective-permute-start.13 = (bf16[128,1024]{1,0:T(8,128)(2,1)S(1)}, bf16[128,1024]{1,0:T(8,128)(2,1)S(1)}, u32[]{:S(2)}, u32[]{:S(2)}) collective-permute-start(bf16[128,1024]{1,0:T(8,128)(2,1)S(1)} %get-tuple-element.62), channel_id=1, source_target_pairs={{0,4},{1,5},{2,6},{3,7},{4,0},{5,1},{6,2},{7,3},{8,12},{9,13},{10,... | collective-permute-start | bytes 786440 | tf_op jit(solution)/shard_map/ppermute | solution.py:547
  39.0 4.5 %collective-permute-done.12.refs_0_.refs_4_ = bf16[128,1024]{1,0:T(8,128)(2,1)S(1)} collective-permute-done((bf16[128,1024]{1,0:T(8,128)(2,1)S(1)}, bf16[128,1024]{1,0:T(8,128)(2,1)S(1)}, u32[]{:S(2)}, u32[]{:S(2)}) %collective-permute-start.12) | collective-permute-done | bytes 262176 | tf_op jit(solution)/shard_map/ppermute | solution.py:547
  44.1 1.6 %collective-permute-start.15 = (bf16[128,1024]{1,0:T(8,128)(2,1)S(1)}, bf16[128,1024]{1,0:T(8,128)(2,1)S(1)}, u32[]{:S(2)}, u32[]{:S(2)}) collective-permute-start(bf16[128,1024]{1,0:T(8,128)(2,1)S(1)} %regrid.1.refs_0_.refs_2_), channel_id=1, source_target_pairs={{0,2},{1,3},{2,0},{3,1},{4,6},{5,7},{6,4},{7,5},{8,10},{9,11},{10,... | collective-permute-start | bytes 786440 | tf_op jit(solution)/shard_map/ppermute | solution.py:547
  45.6 2.7 %collective-permute-start.16 = (bf16[128,1024]{1,0:T(8,128)(2,1)S(1)}, bf16[128,1024]{1,0:T(8,128)(2,1)S(1)}, u32[]{:S(2)}, u32[]{:S(2)}) collective-permute-start(bf16[128,1024]{1,0:T(8,128)(2,1)S(1)} %regrid.1.refs_0_.refs_2_), channel_id=1, source_target_pairs={{0,4},{1,5},{2,6},{3,7},{4,0},{5,1},{6,2},{7,3},{8,12},{9,13},{10,... | collective-permute-start | bytes 786440 | tf_op jit(solution)/shard_map/ppermute | solution.py:547
  48.3 1.1 %hidden.1 = (bf16[128,1024]{1,0:T(8,128)(2,1)}, f32[8,128]{1,0:T(8,128)S(1)}) custom-call(bf16[128,1024]{1,0:T(8,128)(2,1)S(1)} %regrid.1.refs_0_.refs_2_, bf16[128,1024]{1,0:T(8,128)(2,1)S(1)} %copy-done.1, f32[2,1024]{1,0:T(2,128)S(1)} %get-tuple-element.51.refs_0_.refs_6_.refs_2_, bf16[128,128]{1,0:T(8,128)(2,1)S(1)} %get-tuple-element.42.refs_3_.refs_4_, ...), custom_call_target="tpu_custom_call" | custom-call | tf_op jit(solution)/shard_map/hidden/pallas_call | solution.py:59
  49.5 1.2 %collective-permute-done.15.refs_0_.refs_8_ = bf16[128,1024]{1,0:T(8,128)(2,1)S(1)} collective-permute-done((bf16[128,1024]{1,0:T(8,128)(2,1)S(1)}, bf16[128,1024]{1,0:T(8,128)(2,1)S(1)}, u32[]{:S(2)}, u32[]{:S(2)}) %collective-permute-start.15) | collective-permute-done | bytes 262176 | tf_op jit(solution)/shard_map/ppermute | solution.py:547
  50.7 2.1 %collective-permute-done.16.refs_2_ = bf16[128,1024]{1,0:T(8,128)(2,1)S(1)} collective-permute-done((bf16[128,1024]{1,0:T(8,128)(2,1)S(1)}, bf16[128,1024]{1,0:T(8,128)(2,1)S(1)}, u32[]{:S(2)}, u32[]{:S(2)}) %collective-permute-start.16) | collective-permute-done | bytes 262176 | tf_op jit(solution)/shard_map/ppermute | solution.py:547
  52.7 1.4 %collective-permute-start.18 = (bf16[128,1024]{1,0:T(8,128)(2,1)S(1)}, bf16[128,1024]{1,0:T(8,128)(2,1)S(1)}, u32[]{:S(2)}, u32[]{:S(2)}) collective-permute-start(bf16[128,1024]{1,0:T(8,128)(2,1)S(1)} %get-tuple-element.67.refs_3_), channel_id=1, source_target_pairs={{0,2},{1,3},{2,0},{3,1},{4,6},{5,7},{6,4},{7,5},{8,10},{9,11},{10,... | collective-permute-start | bytes 786440 | tf_op jit(solution)/shard_map/ppermute | solution.py:547
  54.2 4.6 %collective-permute-start.19 = (bf16[128,1024]{1,0:T(8,128)(2,1)S(1)}, bf16[128,1024]{1,0:T(8,128)(2,1)S(1)}, u32[]{:S(2)}, u32[]{:S(2)}) collective-permute-start(bf16[128,1024]{1,0:T(8,128)(2,1)S(1)} %get-tuple-element.68.refs_1_), channel_id=1, source_target_pairs={{0,4},{1,5},{2,6},{3,7},{4,0},{5,1},{6,2},{7,3},{8,12},{9,13},{10,... | collective-permute-start | bytes 786440 | tf_op jit(solution)/shard_map/ppermute | solution.py:547
  58.8 2.9 %collective-permute-start.25 = (bf16[128,1024]{1,0:T(8,128)(2,1)S(1)}, bf16[128,1024]{1,0:T(8,128)(2,1)S(1)}, u32[]{:S(2)}, u32[]{:S(2)}) collective-permute-start(bf16[128,1024]{1,0:T(8,128)(2,1)S(1)} %collective-permute-done.24.refs_3_), channel_id=1, source_target_pairs={{0,4},{1,5},{2,6},{3,7},{4,0},{5,1},{6,2},{7,3},{8,12},{9,13},{10,... | collective-permute-start | bytes 786440 | tf_op jit(solution)/shard_map/ppermute | solution.py:547
  61.6 3.7 %collective-permute-done.19.refs_2_ = bf16[128,1024]{1,0:T(8,128)(2,1)S(1)} collective-permute-done((bf16[128,1024]{1,0:T(8,128)(2,1)S(1)}, bf16[128,1024]{1,0:T(8,128)(2,1)S(1)}, u32[]{:S(2)}, u32[]{:S(2)}) %collective-permute-start.19) | collective-permute-done | bytes 262176 | tf_op jit(solution)/shard_map/ppermute | solution.py:547
  66.1 1.4 %collective-permute-start.23 = (bf16[64,1024]{1,0:T(8,128)(2,1)S(1)}, bf16[64,1024]{1,0:T(8,128)(2,1)S(1)}, u32[]{:S(2)}, u32[]{:S(2)}) collective-permute-start(bf16[64,1024]{1,0:T(8,128)(2,1)S(1)} %get-tuple-element.71.refs_5_), channel_id=1, source_target_pairs={{0,2},{1,3},{2,0},{3,1},{4,6},{5,7},{6,4},{7,5},{8,10},{9,11},{10,... | collective-permute-start | bytes 393224 | tf_op jit(solution)/shard_map/ppermute | solution.py:547
  67.5 1.3 %turn_next.1.refs_2_.refs_0_ = bf16[8,1024,256]{2,1,0:T(8,128)(2,1)S(1)} custom-call(bf16[64,1024]{1,0:T(8,128)(2,1)S(1)} %get-tuple-element.69.refs_0_.refs_4_, bf16[16384,128]{1,0:T(8,128)(2,1)S(1)} %copy-done, f32[128,128]{1,0:T(8,128)S(1)} %bitcast_convert_fusion.refs_2_, f32[2,128,128]{2,1,0:T(8,128)S(1)} %get-tuple-element.41.refs_2_.refs_3_.refs_1_, ...), custom_call_target="tpu_custom_call" | custom-call | tf_op jit(solution)/shard_map/turn_next/pallas_call | solution.py:59
  68.8 2.7 %collective-permute-done.22.refs_0_.refs_10_ = bf16[64,1024]{1,0:T(8,128)(2,1)S(1)} collective-permute-done((bf16[64,1024]{1,0:T(8,128)(2,1)S(1)}, bf16[64,1024]{1,0:T(8,128)(2,1)S(1)}, u32[]{:S(2)}, u32[]{:S(2)}) %collective-permute-start.22) | collective-permute-done | bytes 131104 | tf_op jit(solution)/shard_map/ppermute | solution.py:547
  71.5 2.8 %collective-permute-done.23.refs_1_.refs_11_ = bf16[64,1024]{1,0:T(8,128)(2,1)S(1)} collective-permute-done((bf16[64,1024]{1,0:T(8,128)(2,1)S(1)}, bf16[64,1024]{1,0:T(8,128)(2,1)S(1)}, u32[]{:S(2)}, u32[]{:S(2)}) %collective-permute-start.23) | collective-permute-done | bytes 131104 | tf_op jit(solution)/shard_map/ppermute | solution.py:547
  74.4 2.0 %collective-permute-start.27 = (bf16[64,1024]{1,0:T(8,128)(2,1)S(1)}, bf16[64,1024]{1,0:T(8,128)(2,1)S(1)}, u32[]{:S(2)}, u32[]{:S(2)}) collective-permute-start(bf16[64,1024]{1,0:T(8,128)(2,1)S(1)} %get-tuple-element.73.refs_7_), channel_id=1, source_target_pairs={{0,2},{1,3},{2,0},{3,1},{4,6},{5,7},{6,4},{7,5},{8,10},{9,11},{10,... | collective-permute-start | bytes 393224 | tf_op jit(solution)/shard_map/ppermute | solution.py:547
  77.2 2.2 %collective-permute-done.26.refs_3_ = bf16[64,1024]{1,0:T(8,128)(2,1)S(1)} collective-permute-done((bf16[64,1024]{1,0:T(8,128)(2,1)S(1)}, bf16[64,1024]{1,0:T(8,128)(2,1)S(1)}, u32[]{:S(2)}, u32[]{:S(2)}) %collective-permute-start.26) | collective-permute-done | bytes 131104 | tf_op jit(solution)/shard_map/ppermute | solution.py:547
  79.4 1.4 %collective-permute-done.27.refs_4_ = bf16[64,1024]{1,0:T(8,128)(2,1)S(1)} collective-permute-done((bf16[64,1024]{1,0:T(8,128)(2,1)S(1)}, bf16[64,1024]{1,0:T(8,128)(2,1)S(1)}, u32[]{:S(2)}, u32[]{:S(2)}) %collective-permute-start.27) | collective-permute-done | bytes 131104 | tf_op jit(solution)/shard_map/ppermute | solution.py:547
  81.1 1.3 %collective-permute-done.28.refs_1_ = f32[128,256]{1,0:T(8,128)S(1)} collective-permute-done((f32[128,256]{1,0:T(8,128)S(1)}, f32[128,256]{1,0:T(8,128)S(1)}, u32[]{:S(2)}, u32[]{:S(2)}) %collective-permute-start.28) | collective-permute-done | bytes 131104 | tf_op jit(solution)/shard_map/ppermute | solution.py:547
  (52 shorter events, 7.5 us)
Async XLA Ops:
  4.8 2.2 %collective-permute-start = (bf16[1,128,1024]{2,1,0:T(8,128)(2,1)S(1)}, bf16[1,128,1024]{2,1,0:T(8,128)(2,1)S(1)}, u32[]{:S(2)}, u32[]{:S(2)}) collective-permute-start(bf16[1,128,1024]{2,1,0:T(8,128)(2,1)S(1)} %get-tuple-element.45), channel_id=1, source_target_pairs={{0,1},{1,0},{2,3},{3,2},{4,5},{5,4},{6,7},{7,6},{8,9},{9,8},{10,11... | collective-permute-start | bytes 786440 | tf_op jit(solution)/shard_map/ppermute | solution.py:547
  6.4 6.1 %collective-permute-start.2 = (bf16[1,128,1024]{2,1,0:T(8,128)(2,1)S(1)}, bf16[1,128,1024]{2,1,0:T(8,128)(2,1)S(1)}, u32[]{:S(2)}, u32[]{:S(2)}) collective-permute-start(bf16[1,128,1024]{2,1,0:T(8,128)(2,1)S(1)} %get-tuple-element.48), channel_id=1, source_target_pairs={{0,1},{1,0},{2,3},{3,2},{4,5},{5,4},{6,7},{7,6},{8,9},{9,8},{10,11... | collective-permute-start | bytes 786440 | tf_op jit(solution)/shard_map/ppermute | solution.py:547
  6.5 6.0 %collective-permute-start.3 = (bf16[1,128,1024]{2,1,0:T(8,128)(2,1)S(1)}, bf16[1,128,1024]{2,1,0:T(8,128)(2,1)S(1)}, u32[]{:S(2)}, u32[]{:S(2)}) collective-permute-start(bf16[1,128,1024]{2,1,0:T(8,128)(2,1)S(1)} %get-tuple-element.49), channel_id=1, source_target_pairs={{0,1},{1,0},{2,3},{3,2},{4,5},{5,4},{6,7},{7,6},{8,9},{9,8},{10,11... | collective-permute-start | bytes 786440 | tf_op jit(solution)/shard_map/ppermute | solution.py:547
  7.0 9.5 %collective-permute-start.1 = (bf16[128,1024]{1,0:T(8,128)(2,1)S(1)}, bf16[128,1024]{1,0:T(8,128)(2,1)S(1)}, u32[]{:S(2)}, u32[]{:S(2)}) collective-permute-start(bf16[128,1024]{1,0:T(8,128)(2,1)S(1)} %add_up.4.refs_0_), channel_id=1, source_target_pairs={{0,2},{1,3},{2,0},{3,1},{4,6},{5,7},{6,4},{7,5},{8,10},{9,11},{10,... | collective-permute-start | bytes 786440 | tf_op jit(solution)/shard_map/ppermute | solution.py:547
  10.4 9.7 %copy-start.1 = (bf16[128,1024]{1,0:T(8,128)(2,1)S(1)}, bf16[128,1024]{1,0:T(8,128)(2,1)}, u32[]{:S(2)}) copy-start(bf16[128,1024]{1,0:T(8,128)(2,1)} %refs_1_.8) | copy-start | bytes 786436
  10.5 9.9 %copy-start = (bf16[16384,128]{1,0:T(8,128)(2,1)S(1)}, bf16[16384,128]{1,0:T(8,128)(2,1)}, u32[]{:S(2)}) copy-start(bf16[16384,128]{1,0:T(8,128)(2,1)} %refs_1_.9) | copy-start | bytes 12582916
  10.5 15.6 %collective-permute-start.7 = (bf16[2,128,1024]{2,1,0:T(8,128)(2,1)S(1)}, bf16[2,128,1024]{2,1,0:T(8,128)(2,1)S(1)}, u32[]{:S(2)}, u32[]{:S(2)}) collective-permute-start(bf16[2,128,1024]{2,1,0:T(8,128)(2,1)S(1)} %get-tuple-element.46.refs_0_), channel_id=1, source_target_pairs={{0,1},{1,0},{2,3},{3,2},{4,5},{5,4},{6,7},{7,6},{8,9},{9,8},{10,11... | collective-permute-start | bytes 1572872 | tf_op jit(solution)/shard_map/ppermute | solution.py:547
  12.0 8.4 %collective-permute-start.6 = (bf16[1,128,1024]{2,1,0:T(8,128)(2,1)S(1)}, bf16[1,128,1024]{2,1,0:T(8,128)(2,1)S(1)}, u32[]{:S(2)}, u32[]{:S(2)}) collective-permute-start(bf16[1,128,1024]{2,1,0:T(8,128)(2,1)S(1)} %get-tuple-element.55), channel_id=1, source_target_pairs={{0,1},{1,0},{2,3},{3,2},{4,5},{5,4},{6,7},{7,6},{8,9},{9,8},{10,11... | collective-permute-start | bytes 786440 | tf_op jit(solution)/shard_map/ppermute | solution.py:547
  16.7 8.1 %collective-permute-start.4 = (bf16[128,1024]{1,0:T(8,128)(2,1)S(1)}, bf16[128,1024]{1,0:T(8,128)(2,1)S(1)}, u32[]{:S(2)}, u32[]{:S(2)}) collective-permute-start(bf16[128,1024]{1,0:T(8,128)(2,1)S(1)} %get-tuple-element.53), channel_id=1, source_target_pairs={{0,2},{1,3},{2,0},{3,1},{4,6},{5,7},{6,4},{7,5},{8,10},{9,11},{10,... | collective-permute-start | bytes 786440 | tf_op jit(solution)/shard_map/ppermute | solution.py:547
  18.5 7.6 %collective-permute-start.5 = (bf16[128,1024]{1,0:T(8,128)(2,1)S(1)}, bf16[128,1024]{1,0:T(8,128)(2,1)S(1)}, u32[]{:S(2)}, u32[]{:S(2)}) collective-permute-start(bf16[128,1024]{1,0:T(8,128)(2,1)S(1)} %get-tuple-element.50.refs_0_), channel_id=1, source_target_pairs={{0,4},{1,5},{2,6},{3,7},{4,0},{5,1},{6,2},{7,3},{8,12},{9,13},{10,... | collective-permute-start | bytes 786440 | tf_op jit(solution)/shard_map/ppermute | solution.py:547
  20.1 10.1 %collective-permute-start.11 = (bf16[2,128,1024]{2,1,0:T(8,128)(2,1)S(1)}, bf16[2,128,1024]{2,1,0:T(8,128)(2,1)S(1)}, u32[]{:S(2)}, u32[]{:S(2)}) collective-permute-start(bf16[2,128,1024]{2,1,0:T(8,128)(2,1)S(1)} %get-tuple-element.47.refs_0_), channel_id=1, source_target_pairs={{0,1},{1,0},{2,3},{3,2},{4,5},{5,4},{6,7},{7,6},{8,9},{9,8},{10,11... | collective-permute-start | bytes 1572872 | tf_op jit(solution)/shard_map/ppermute | solution.py:547
  26.4 3.8 %collective-permute-start.10 = (bf16[128,1024]{1,0:T(8,128)(2,1)S(1)}, bf16[128,1024]{1,0:T(8,128)(2,1)S(1)}, u32[]{:S(2)}, u32[]{:S(2)}) collective-permute-start(bf16[128,1024]{1,0:T(8,128)(2,1)S(1)} %get-tuple-element.59), channel_id=1, source_target_pairs={{0,1},{1,0},{2,3},{3,2},{4,8},{5,9},{6,10},{7,11},{8,4},{9,5},{10,... | collective-permute-start | bytes 786440 | tf_op jit(solution)/shard_map/ppermute | solution.py:547
  26.5 8.7 %collective-permute-start.8 = (bf16[128,1024]{1,0:T(8,128)(2,1)S(1)}, bf16[128,1024]{1,0:T(8,128)(2,1)S(1)}, u32[]{:S(2)}, u32[]{:S(2)}) collective-permute-start(bf16[128,1024]{1,0:T(8,128)(2,1)S(1)} %get-tuple-element.57), channel_id=1, source_target_pairs={{0,2},{1,3},{2,0},{3,1},{4,6},{5,7},{6,4},{7,5},{8,10},{9,11},{10,... | collective-permute-start | bytes 786440 | tf_op jit(solution)/shard_map/ppermute | solution.py:547
  27.0 8.4 %collective-permute-start.9 = (bf16[128,1024]{1,0:T(8,128)(2,1)S(1)}, bf16[128,1024]{1,0:T(8,128)(2,1)S(1)}, u32[]{:S(2)}, u32[]{:S(2)}) collective-permute-start(bf16[128,1024]{1,0:T(8,128)(2,1)S(1)} %get-tuple-element.58), channel_id=1, source_target_pairs={{0,4},{1,5},{2,6},{3,7},{4,0},{5,1},{6,2},{7,3},{8,12},{9,13},{10,... | collective-permute-start | bytes 786440 | tf_op jit(solution)/shard_map/ppermute | solution.py:547
  35.8 31.7 %copy-start.2 = (bf16[16384]{0:T(1024)(128)(2,1)S(1)}, bf16[16384]{0:T(1024)(128)(2,1)}, u32[]{:S(2)}) copy-start(bf16[16384]{0:T(1024)(128)(2,1)} %param.17) | copy-start | bytes 98308
  35.8 7.8 %collective-permute-start.12 = (bf16[128,1024]{1,0:T(8,128)(2,1)S(1)}, bf16[128,1024]{1,0:T(8,128)(2,1)S(1)}, u32[]{:S(2)}, u32[]{:S(2)}) collective-permute-start(bf16[128,1024]{1,0:T(8,128)(2,1)S(1)} %get-tuple-element.61), channel_id=1, source_target_pairs={{0,2},{1,3},{2,0},{3,1},{4,6},{5,7},{6,4},{7,5},{8,10},{9,11},{10,... | collective-permute-start | bytes 786440 | tf_op jit(solution)/shard_map/ppermute | solution.py:547
  37.4 6.4 %collective-permute-start.13 = (bf16[128,1024]{1,0:T(8,128)(2,1)S(1)}, bf16[128,1024]{1,0:T(8,128)(2,1)S(1)}, u32[]{:S(2)}, u32[]{:S(2)}) collective-permute-start(bf16[128,1024]{1,0:T(8,128)(2,1)S(1)} %get-tuple-element.62), channel_id=1, source_target_pairs={{0,4},{1,5},{2,6},{3,7},{4,0},{5,1},{6,2},{7,3},{8,12},{9,13},{10,... | collective-permute-start | bytes 786440 | tf_op jit(solution)/shard_map/ppermute | solution.py:547
  38.5 5.3 %collective-permute-start.14 = (bf16[128,1024]{1,0:T(8,128)(2,1)S(1)}, bf16[128,1024]{1,0:T(8,128)(2,1)S(1)}, u32[]{:S(2)}, u32[]{:S(2)}) collective-permute-start(bf16[128,1024]{1,0:T(8,128)(2,1)S(1)} %get-tuple-element.63), channel_id=1, source_target_pairs={{0,1},{1,0},{2,3},{3,2},{4,8},{5,9},{6,10},{7,11},{8,4},{9,5},{10,... | collective-permute-start | bytes 786440 | tf_op jit(solution)/shard_map/ppermute | solution.py:547
  38.5 29.0 %collective-permute-start.20 = (bf16[4,1024,128]{2,1,0:T(8,128)(2,1)S(1)}, bf16[4,1024,128]{2,1,0:T(8,128)(2,1)S(1)}, u32[]{:S(2)}, u32[]{:S(2)}) collective-permute-start(bf16[4,1024,128]{2,1,0:T(8,128)(2,1)S(1)} %get-tuple-element.52.refs_0_), channel_id=1, source_target_pairs={{0,1},{1,0},{2,3},{3,2},{4,5},{5,4},{6,7},{7,6},{8,9},{9,8},{10,11... | collective-permute-start | bytes 3145736 | tf_op jit(solution)/shard_map/ppermute | solution.py:547
  39.0 28.5 %collective-permute-start.21 = (bf16[4,1024,128]{2,1,0:T(8,128)(2,1)S(1)}, bf16[4,1024,128]{2,1,0:T(8,128)(2,1)S(1)}, u32[]{:S(2)}, u32[]{:S(2)}) collective-permute-start(bf16[4,1024,128]{2,1,0:T(8,128)(2,1)S(1)} %get-tuple-element.70), channel_id=1, source_target_pairs={{0,1},{1,0},{2,3},{3,2},{4,5},{5,4},{6,7},{7,6},{8,9},{9,8},{10,11... | collective-permute-start | bytes 3145736 | tf_op jit(solution)/shard_map/ppermute | solution.py:547
  44.1 6.6 %collective-permute-start.15 = (bf16[128,1024]{1,0:T(8,128)(2,1)S(1)}, bf16[128,1024]{1,0:T(8,128)(2,1)S(1)}, u32[]{:S(2)}, u32[]{:S(2)}) collective-permute-start(bf16[128,1024]{1,0:T(8,128)(2,1)S(1)} %regrid.1.refs_0_.refs_2_), channel_id=1, source_target_pairs={{0,2},{1,3},{2,0},{3,1},{4,6},{5,7},{6,4},{7,5},{8,10},{9,11},{10,... | collective-permute-start | bytes 786440 | tf_op jit(solution)/shard_map/ppermute | solution.py:547
  45.6 7.1 %collective-permute-start.16 = (bf16[128,1024]{1,0:T(8,128)(2,1)S(1)}, bf16[128,1024]{1,0:T(8,128)(2,1)S(1)}, u32[]{:S(2)}, u32[]{:S(2)}) collective-permute-start(bf16[128,1024]{1,0:T(8,128)(2,1)S(1)} %regrid.1.refs_0_.refs_2_), channel_id=1, source_target_pairs={{0,4},{1,5},{2,6},{3,7},{4,0},{5,1},{6,2},{7,3},{8,12},{9,13},{10,... | collective-permute-start | bytes 786440 | tf_op jit(solution)/shard_map/ppermute | solution.py:547
  48.3 4.4 %collective-permute-start.17 = (bf16[128,1024]{1,0:T(8,128)(2,1)S(1)}, bf16[128,1024]{1,0:T(8,128)(2,1)S(1)}, u32[]{:S(2)}, u32[]{:S(2)}) collective-permute-start(bf16[128,1024]{1,0:T(8,128)(2,1)S(1)} %regrid.1.refs_0_.refs_2_), channel_id=1, source_target_pairs={{0,1},{1,0},{2,3},{3,2},{4,8},{5,9},{6,10},{7,11},{8,4},{9,5},{10,... | collective-permute-start | bytes 786440 | tf_op jit(solution)/shard_map/ppermute | solution.py:547
  52.7 6.0 %collective-permute-start.24 = (bf16[128,1024]{1,0:T(8,128)(2,1)S(1)}, bf16[128,1024]{1,0:T(8,128)(2,1)S(1)}, u32[]{:S(2)}, u32[]{:S(2)}) collective-permute-start(bf16[128,1024]{1,0:T(8,128)(2,1)S(1)} %get-tuple-element.67.refs_3_), channel_id=1, source_target_pairs={{0,1},{1,0},{2,3},{3,2},{4,8},{5,9},{6,10},{7,11},{8,4},{9,5},{10,... | collective-permute-start | bytes 786440 | tf_op jit(solution)/shard_map/ppermute | solution.py:547
  52.7 8.9 %collective-permute-start.18 = (bf16[128,1024]{1,0:T(8,128)(2,1)S(1)}, bf16[128,1024]{1,0:T(8,128)(2,1)S(1)}, u32[]{:S(2)}, u32[]{:S(2)}) collective-permute-start(bf16[128,1024]{1,0:T(8,128)(2,1)S(1)} %get-tuple-element.67.refs_3_), channel_id=1, source_target_pairs={{0,2},{1,3},{2,0},{3,1},{4,6},{5,7},{6,4},{7,5},{8,10},{9,11},{10,... | collective-permute-start | bytes 786440 | tf_op jit(solution)/shard_map/ppermute | solution.py:547
  54.2 11.2 %collective-permute-start.19 = (bf16[128,1024]{1,0:T(8,128)(2,1)S(1)}, bf16[128,1024]{1,0:T(8,128)(2,1)S(1)}, u32[]{:S(2)}, u32[]{:S(2)}) collective-permute-start(bf16[128,1024]{1,0:T(8,128)(2,1)S(1)} %get-tuple-element.68.refs_1_), channel_id=1, source_target_pairs={{0,4},{1,5},{2,6},{3,7},{4,0},{5,1},{6,2},{7,3},{8,12},{9,13},{10,... | collective-permute-start | bytes 786440 | tf_op jit(solution)/shard_map/ppermute | solution.py:547
  58.8 15.5 %collective-permute-start.25 = (bf16[128,1024]{1,0:T(8,128)(2,1)S(1)}, bf16[128,1024]{1,0:T(8,128)(2,1)S(1)}, u32[]{:S(2)}, u32[]{:S(2)}) collective-permute-start(bf16[128,1024]{1,0:T(8,128)(2,1)S(1)} %collective-permute-done.24.refs_3_), channel_id=1, source_target_pairs={{0,4},{1,5},{2,6},{3,7},{4,0},{5,1},{6,2},{7,3},{8,12},{9,13},{10,... | collective-permute-start | bytes 786440 | tf_op jit(solution)/shard_map/ppermute | solution.py:547
  65.4 6.1 %collective-permute-start.22 = (bf16[64,1024]{1,0:T(8,128)(2,1)S(1)}, bf16[64,1024]{1,0:T(8,128)(2,1)S(1)}, u32[]{:S(2)}, u32[]{:S(2)}) collective-permute-start(bf16[64,1024]{1,0:T(8,128)(2,1)S(1)} %get-tuple-element.69.refs_0_.refs_4_), channel_id=1, source_target_pairs={{0,2},{1,3},{2,0},{3,1},{4,6},{5,7},{6,4},{7,5},{8,10},{9,11},{10,... | collective-permute-start | bytes 393224 | tf_op jit(solution)/shard_map/ppermute | solution.py:547
  66.1 8.2 %collective-permute-start.23 = (bf16[64,1024]{1,0:T(8,128)(2,1)S(1)}, bf16[64,1024]{1,0:T(8,128)(2,1)S(1)}, u32[]{:S(2)}, u32[]{:S(2)}) collective-permute-start(bf16[64,1024]{1,0:T(8,128)(2,1)S(1)} %get-tuple-element.71.refs_5_), channel_id=1, source_target_pairs={{0,2},{1,3},{2,0},{3,1},{4,6},{5,7},{6,4},{7,5},{8,10},{9,11},{10,... | collective-permute-start | bytes 393224 | tf_op jit(solution)/shard_map/ppermute | solution.py:547
  74.3 5.0 %collective-permute-start.26 = (bf16[64,1024]{1,0:T(8,128)(2,1)S(1)}, bf16[64,1024]{1,0:T(8,128)(2,1)S(1)}, u32[]{:S(2)}, u32[]{:S(2)}) collective-permute-start(bf16[64,1024]{1,0:T(8,128)(2,1)S(1)} %get-tuple-element.72.refs_6_), channel_id=1, source_target_pairs={{0,2},{1,3},{2,0},{3,1},{4,6},{5,7},{6,4},{7,5},{8,10},{9,11},{10,... | collective-permute-start | bytes 393224 | tf_op jit(solution)/shard_map/ppermute | solution.py:547
  74.4 6.4 %collective-permute-start.27 = (bf16[64,1024]{1,0:T(8,128)(2,1)S(1)}, bf16[64,1024]{1,0:T(8,128)(2,1)S(1)}, u32[]{:S(2)}, u32[]{:S(2)}) collective-permute-start(bf16[64,1024]{1,0:T(8,128)(2,1)S(1)} %get-tuple-element.73.refs_7_), channel_id=1, source_target_pairs={{0,2},{1,3},{2,0},{3,1},{4,6},{5,7},{6,4},{7,5},{8,10},{9,11},{10,... | collective-permute-start | bytes 393224 | tf_op jit(solution)/shard_map/ppermute | solution.py:547
  81.0 1.4 %collective-permute-start.28 = (f32[128,256]{1,0:T(8,128)S(1)}, f32[128,256]{1,0:T(8,128)S(1)}, u32[]{:S(2)}, u32[]{:S(2)}) collective-permute-start(f32[128,256]{1,0:T(8,128)S(1)} %get-tuple-element.75), channel_id=1, source_target_pairs={{0,1},{1,0},{2,3},{3,2},{4,5},{5,4},{6,7},{7,6},{8,9},{9,8},{10,11... | collective-permute-start | bytes 393224 | tf_op jit(solution)/shard_map/ppermute | solution.py:547

commit v7 on v6

--- a/solution.py
+++ b/solution.py
@@ -354,51 +354,60 @@
     )
 
 
-HALVES = 2
-
-
-def halves(shape):
-    rows = shape[0] // HALVES
-    return [jax.ShapeDtypeStruct((rows, *shape[1:]), BF16)] * HALVES
-
-
-def split_rows(value_ref, out_refs):
-    rows = out_refs[0].shape[0]
-    for i, out_ref in enumerate(out_refs):
-        out_ref[...] = value_ref[i * rows : (i + 1) * rows]
-
-
-def choose_kernel(inner, inner_ref, end_ref, *out_refs):
+def choose_kernel(inner, count, inner_ref, end_ref, *refs):
     inside = is_inner(place(inner)[0])
+    others, out_ref, outs = refs[:count], refs[count], refs[count + 1 :]
+    lower, upper = outs[:count], outs[count:]
+
+    def put(ref):
+        out_ref[...] = ref[...]
+        for half in upper:
+            half[...] = ref[: half.shape[0]]
 
     @pl.when(inside)
     def _():
-        split_rows(inner_ref, out_refs)
+        put(inner_ref)
 
     @pl.when(jnp.logical_not(inside))
     def _():
-        split_rows(end_ref, out_refs)
-
-
-def choose(inner, at_inner, at_end, after=()):
-    return kernel_call(
-        functools.partial(choose_kernel, inner),
-        halves(at_inner.shape),
-        [at_inner, at_end],
-        [vmem()] * 2,
+        put(end_ref)
+
+    for ref, half in zip(others, lower):
+        half[...] = ref[half.shape[0] :]
+
+
+def choose(inner, at_inner, at_end, others=(), halved=False, after=()):
+    rows, cols = at_inner.shape
+    half = jax.ShapeDtypeStruct((rows // 2, cols), BF16)
+    return kernel_call(
+        functools.partial(choose_kernel, inner, len(others)),
+        [jax.ShapeDtypeStruct((rows, cols), BF16)] + [half] * (len(others) + halved),
+        [at_inner, at_end, *others],
+        [vmem()] * (2 + len(others)),
         after=after,
         name="choose",
     )
 
 
-def gate(arrays, after):
-    def kernel(*refs):
-        pass
-
-    shapes = [jax.ShapeDtypeStruct(array.shape, array.dtype) for array in arrays]
-    aliases = {len(after) + i: i for i in range(len(arrays))}
-    specs = [vmem()] * len(arrays)
-    return kernel_call(kernel, shapes, arrays, specs, after=after, aliases=aliases, name="gate")
+def gate_kernel(count, *refs):
+    for ref, half in zip(refs[:count], refs[-count:]):
+        half[...] = ref[half.shape[0] :]
+
+
+def gate(arrays, others, after):
+    rows, cols = arrays[0].shape
+    shapes = [jax.ShapeDtypeStruct((rows, cols), BF16)] * len(arrays)
+    half = jax.ShapeDtypeStruct((rows // 2, cols), BF16)
+    aliases = {len(after) + len(others) + i: i for i in range(len(arrays))}
+    return kernel_call(
+        functools.partial(gate_kernel, len(others)),
+        shapes + [half] * len(others),
+        [*others, *arrays],
+        [vmem()] * (len(others) + len(arrays)),
+        after=after,
+        aliases=aliases,
+        name="gate",
+    )
 
 
 def select_rows_kernel(inner, cols, w_ref, *out_refs):
@@ -453,8 +462,7 @@
 
 def project_kernel(inner, places, has_acc, split, w_ref, rows_ref, *refs):
     outer, mid, core = place(inner)
-    far, third, near, own = targets(outer)
-    order = (own, near, third, far)
+    order = (outer, targets(outer)[2], lax.rem(outer + 2, OUTER), OUTER - 1 - outer)
     acc_in = refs[0] if has_acc else None
     refs = refs[1:] if has_acc else refs
     count = sum(parts for _, _, parts in places)
@@ -465,8 +473,11 @@
     squares = acc_in[:, width:] if has_acc else 0.0
     for phase, shift, parts in places:
         block = order[phase] * inner + lax.rem(mid + inner - shift, inner)
-        values = [values_in.pop(0)[...] for _ in range(parts)]
-        values = values[0] if parts == 1 else jnp.concatenate(values, axis=0)
+        values = values_in.pop(0)[...]
+        if parts == 3:
+            at_inner, at_end = values_in.pop(0)[...], values_in.pop(0)[...]
+            lower = jnp.where(is_inner(outer), at_inner, at_end)
+            values = jnp.concatenate([values, lower], axis=0)
         acc = acc + jnp.dot(values, w_ref[block], preferred_element_type=F32)
         for i in range(cols // ROT):
             row = (block * 2 + core) * (cols // ROT) + i
@@ -487,7 +498,8 @@
 def project(inner, weight, rows, acc, pieces, split=False, after=()):
     _, cols, width = weight.shape
     arrays = [part for _, _, parts in pieces for part in parts]
-    tok = sum(part.shape[0] for part in pieces[0][2])
+    first = pieces[0][2]
+    tok = first[0].shape[0] * (1 if len(first) == 1 else 2)
     places = tuple((phase, shift, len(parts)) for phase, shift, parts in pieces)
     accs = [] if acc is None else [acc]
     if split:
@@ -656,33 +668,33 @@
     near = swap_pairs(grid)
     mid1 = swap_middle(grid)
     hidden_out, mark = hidden(inner, items, residual, factors, had, last, after=[grid])
-    near, mid1 = gate([near, mid1], after=[*x1, mark])
-
-    def shift_parts(parts, shift):
-        return [shift_mid(part, shift) for part in parts]
-
+    near, mid1, *low1 = gate([near, mid1], x1, after=[mark])
     x2 = [shift_mid(near, s) for s in shifts]
     ends2 = swap_pairs(mid1)
     mids2 = swap_middle(near)
-    third = choose(inner, mid1, ends2, after=x2)
-    x3 = [shift_parts(third, s) for s in shifts]
+    (third,) = choose(inner, mids2, ends2, after=x2)
+    x3 = [shift_mid(third, s) for s in shifts]
     ends3 = swap_pairs(mids2)
-    turned_next = turn_next(
-        inner, next_query_weight, next_other, gain, rows, had, after=third[:1]
-    )
-    fourth = choose(inner, mids2, ends3, after=[*sum(x3, []), turned_next])
-    x4 = [shift_parts(fourth, s) for s in shifts]
+    side_middle = [swap_middle(low) for low in low1]
+    turned_next = turn_next(inner, next_query_weight, next_other, gain, rows, had, after=[third])
+    fourth, *low3, up4 = choose(inner, mid1, ends3, x3, True, after=[turned_next])
+    x4 = [shift_mid(up4, s) for s in shifts]
+    side_pairs = [swap_pairs(low) for low in low3]
     acc = project(
         inner,
         turned_next,
         rows,
         None,
-        [(0, 0, [grid]), (1, 0, [near]), (2, 0, third), (3, 0, fourth)]
-        + [(phase, s, [x[s - 1]]) for phase, x in enumerate((x1, x2)) for s in shifts]
-        + [(2, s, x3[s - 1]) for s in shifts],
+        [(0, 0, [grid]), (1, 0, [near]), (2, 0, [third]), (3, 0, [fourth])]
+        + [(phase, s, [x[s - 1]]) for phase, x in enumerate((x1, x2, x3)) for s in shifts],
     )
     own, other = project(
-        inner, turned_next, rows, acc, [(3, s, x4[s - 1]) for s in shifts], split=True
+        inner,
+        turned_next,
+        rows,
+        acc,
+        [(3, s, [x4[s - 1], side_middle[s - 1], side_pairs[s - 1]]) for s in shifts],
+        split=True,
     )
     query_next = finish(own, swap_core(other), norm_gain.shape[0])
     return (hidden_out, query_next)

time: 83.3 us -> 78.6 us (0.944)
  waiting for transfers between devices: 37.2 us -> 33.3 us
    ppermute x29, waiting for transfers between devices: 37.2 us -> 33.3 us  [permute(): return lax.ppermute(value, 'tp', moves)]
  transfers between devices with their start and end apart: 29 -> 29, of which waited for: 15 -> 15; matrix products, arithmetic and copies ran while one was open for 0% -> 0% of each run, Pallas kernels for 9% -> 10%
where the time goes in v7:
time: 78.6 us; the launch traced here: 78.5 us
  waiting for transfers between devices  33.3 us (42%)
  starting transfers between devices  31.3 us (40%)
  Pallas kernels  13 us (17%)
  between operations  0.85 us (1%)
    ppermute x29, waiting for transfers between devices, permute(): return lax.ppermute(value, 'tp', moves)  33.3 us
    ppermute x29, starting transfers between devices, permute(): return lax.ppermute(value, 'tp', moves)  31.3 us
    pallas_call x19, Pallas kernels, kernel_call(): pl.pallas_call(ordered, out_shape=out_shape, in_specs=[anywhere()] * extr...  13 us
  transfers between devices with their start and end apart: 29, of which 15 were waited for; matrix products, arithmetic and copies ran while one was open for 0% of the time, Pallas kernels for 10%

profile of v7, /device:TPU:0, one launch (start us, length us, event | category | flops | bytes accessed | tf_op | source)
XLA Modules:
  0.0 78.5 jit_solution(12831194368861553451)
XLA Ops:
  0.6 4.1 %attend.1 = (bf16[128,128]{1,0:T(8,128)(2,1)S(1)}, f32[2,128,128]{2,1,0:T(8,128)S(1)}, bf16[1,128,1024]{2,1,0:T(8,128)(2,1)S(1)}, bf16[128,16384]{1,0:T(8,128)(2,1)S(1)}, bf16[128,128]{1,0:T(8,128)(2,1)S(1)}) custom-call(bf16[1,128,128]{2,1,0:T(8,128)(2,1)} %refs_0_.1, bf16[1,8192,128]{2,1,0:T(8,128)(2,1)} %refs_1_.5, bf16[1,8192,128]{2,1,0:T(8,128)(2,1)} %refs_2_.1, ...), custom_call_target="tpu_custom_call" | custom-call | tf_op jit(solution)/shard_map/attend/pallas_call | solution.py:59
  5.3 1.1 %partials.3 = (bf16[1,128,1024]{2,1,0:T(8,128)(2,1)S(1)}, bf16[2,128,1024]{2,1,0:T(8,128)(2,1)S(1)}, bf16[1,128,1024]{2,1,0:T(8,128)(2,1)S(1)}, bf16[1,128,1024]{2,1,0:T(8,128)(2,1)S(1)}) custom-call(bf16[128,128]{1,0:T(8,128)(2,1)S(1)} %get-tuple-element.39.refs_0_.refs_1_, bf16[128,16384]{1,0:T(8,128)(2,1)S(1)} %get-tuple-element.40.refs_1_.refs_2_, ...), custom_call_target="tpu_custom_call" | custom-call | tf_op jit(solution)/shard_map/partials/pallas_call | solution.py:59
  7.0 2.6 %collective-permute-start.1 = (bf16[128,1024]{1,0:T(8,128)(2,1)S(1)}, bf16[128,1024]{1,0:T(8,128)(2,1)S(1)}, u32[]{:S(2)}, u32[]{:S(2)}) collective-permute-start(bf16[128,1024]{1,0:T(8,128)(2,1)S(1)} %add_up.4.refs_0_), channel_id=1, source_target_pairs={{0,2},{1,3},{2,0},{3,1},{4,6},{5,7},{6,4},{7,5},{8,10},{9,11},{10,... | collective-permute-start | bytes 786440 | tf_op jit(solution)/shard_map/ppermute | solution.py:559
  9.6 0.8 %partials.4 = (bf16[1,128,1024]{2,1,0:T(8,128)(2,1)S(1)}, bf16[2,128,1024]{2,1,0:T(8,128)(2,1)S(1)}) custom-call(bf16[128,1024]{1,0:T(8,128)(2,1)S(1)} %add_up.4.refs_0_, bf16[128,128]{1,0:T(8,128)(2,1)S(1)} %get-tuple-element.39.refs_0_.refs_1_, bf16[128,16384]{1,0:T(8,128)(2,1)S(1)} %get-tuple-element.40.refs_1_.refs_2_, ...), custom_call_target="tpu_custom_call" | custom-call | tf_op jit(solution)/shard_map/partials/pallas_call | solution.py:59
  10.7 1.3 %partials.5 = (bf16[2,128,1024]{2,1,0:T(8,128)(2,1)S(1)}, bf16[1,128,1024]{2,1,0:T(8,128)(2,1)S(1)}, bf16[2,128,1024]{2,1,0:T(8,128)(2,1)S(1)}, bf16[2,128,1024]{2,1,0:T(8,128)(2,1)S(1)}) custom-call(bf16[2,128,1024]{2,1,0:T(8,128)(2,1)S(1)} %get-tuple-element.46.refs_0_, bf16[128,128]{1,0:T(8,128)(2,1)S(1)} %get-tuple-element.39.refs_0_.refs_1_, ...), custom_call_target="tpu_custom_call" | custom-call | tf_op jit(solution)/shard_map/partials/pallas_call | solution.py:59
  12.5 4.1 %collective-permute-done.1.refs_1_.refs_10_ = bf16[128,1024]{1,0:T(8,128)(2,1)S(1)} collective-permute-done((bf16[128,1024]{1,0:T(8,128)(2,1)S(1)}, bf16[128,1024]{1,0:T(8,128)(2,1)S(1)}, u32[]{:S(2)}, u32[]{:S(2)}) %collective-permute-start.1) | collective-permute-done | bytes 262176 | tf_op jit(solution)/shard_map/ppermute | solution.py:559
  16.7 1.8 %collective-permute-start.4 = (bf16[128,1024]{1,0:T(8,128)(2,1)S(1)}, bf16[128,1024]{1,0:T(8,128)(2,1)S(1)}, u32[]{:S(2)}, u32[]{:S(2)}) collective-permute-start(bf16[128,1024]{1,0:T(8,128)(2,1)S(1)} %get-tuple-element.53), channel_id=1, source_target_pairs={{0,2},{1,3},{2,0},{3,1},{4,6},{5,7},{6,4},{7,5},{8,10},{9,11},{10,... | collective-permute-start | bytes 786440 | tf_op jit(solution)/shard_map/ppermute | solution.py:559
  18.5 1.6 %collective-permute-start.5 = (bf16[128,1024]{1,0:T(8,128)(2,1)S(1)}, bf16[128,1024]{1,0:T(8,128)(2,1)S(1)}, u32[]{:S(2)}, u32[]{:S(2)}) collective-permute-start(bf16[128,1024]{1,0:T(8,128)(2,1)S(1)} %get-tuple-element.50.refs_0_), channel_id=1, source_target_pairs={{0,4},{1,5},{2,6},{3,7},{4,0},{5,1},{6,2},{7,3},{8,12},{9,13},{10,... | collective-permute-start | bytes 786440 | tf_op jit(solution)/shard_map/ppermute | solution.py:559
  20.5 4.3 %collective-permute-done.4.refs_1_.refs_9_ = bf16[128,1024]{1,0:T(8,128)(2,1)S(1)} collective-permute-done((bf16[128,1024]{1,0:T(8,128)(2,1)S(1)}, bf16[128,1024]{1,0:T(8,128)(2,1)S(1)}, u32[]{:S(2)}, u32[]{:S(2)}) %collective-permute-start.4) | collective-permute-done | bytes 262176 | tf_op jit(solution)/shard_map/ppermute | solution.py:559
  24.8 1.3 %collective-permute-done.5.refs_2_ = bf16[128,1024]{1,0:T(8,128)(2,1)S(1)} collective-permute-done((bf16[128,1024]{1,0:T(8,128)(2,1)S(1)}, bf16[128,1024]{1,0:T(8,128)(2,1)S(1)}, u32[]{:S(2)}, u32[]{:S(2)}) %collective-permute-start.5) | collective-permute-done | bytes 262176 | tf_op jit(solution)/shard_map/ppermute | solution.py:559
  26.9 1.6 %collective-permute-start.9 = (bf16[128,1024]{1,0:T(8,128)(2,1)S(1)}, bf16[128,1024]{1,0:T(8,128)(2,1)S(1)}, u32[]{:S(2)}, u32[]{:S(2)}) collective-permute-start(bf16[128,1024]{1,0:T(8,128)(2,1)S(1)} %get-tuple-element.58), channel_id=1, source_target_pairs={{0,4},{1,5},{2,6},{3,7},{4,0},{5,1},{6,2},{7,3},{8,12},{9,13},{10,... | collective-permute-start | bytes 786440 | tf_op jit(solution)/shard_map/ppermute | solution.py:559
  28.6 4.6 %collective-permute-done.8.refs_0_ = bf16[128,1024]{1,0:T(8,128)(2,1)S(1)} collective-permute-done((bf16[128,1024]{1,0:T(8,128)(2,1)S(1)}, bf16[128,1024]{1,0:T(8,128)(2,1)S(1)}, u32[]{:S(2)}, u32[]{:S(2)}) %collective-permute-start.8) | collective-permute-done | bytes 262176 | tf_op jit(solution)/shard_map/ppermute | solution.py:559
  33.9 1.4 %collective-permute-start.12 = (bf16[128,1024]{1,0:T(8,128)(2,1)S(1)}, bf16[128,1024]{1,0:T(8,128)(2,1)S(1)}, u32[]{:S(2)}, u32[]{:S(2)}) collective-permute-start(bf16[128,1024]{1,0:T(8,128)(2,1)S(1)} %get-tuple-element.61), channel_id=1, source_target_pairs={{0,2},{1,3},{2,0},{3,1},{4,6},{5,7},{6,4},{7,5},{8,10},{9,11},{10,... | collective-permute-start | bytes 786440 | tf_op jit(solution)/shard_map/ppermute | solution.py:559
  35.3 2.7 %collective-permute-start.13 = (bf16[128,1024]{1,0:T(8,128)(2,1)S(1)}, bf16[128,1024]{1,0:T(8,128)(2,1)S(1)}, u32[]{:S(2)}, u32[]{:S(2)}) collective-permute-start(bf16[128,1024]{1,0:T(8,128)(2,1)S(1)} %get-tuple-element.62), channel_id=1, source_target_pairs={{0,4},{1,5},{2,6},{3,7},{4,0},{5,1},{6,2},{7,3},{8,12},{9,13},{10,... | collective-permute-start | bytes 786440 | tf_op jit(solution)/shard_map/ppermute | solution.py:559
  38.5 1.8 %collective-permute-done.12.refs_0_.refs_4_ = bf16[128,1024]{1,0:T(8,128)(2,1)S(1)} collective-permute-done((bf16[128,1024]{1,0:T(8,128)(2,1)S(1)}, bf16[128,1024]{1,0:T(8,128)(2,1)S(1)}, u32[]{:S(2)}, u32[]{:S(2)}) %collective-permute-start.12) | collective-permute-done | bytes 262176 | tf_op jit(solution)/shard_map/ppermute | solution.py:559
  40.3 2.1 %collective-permute-done.13.refs_1_.refs_5_ = bf16[128,1024]{1,0:T(8,128)(2,1)S(1)} collective-permute-done((bf16[128,1024]{1,0:T(8,128)(2,1)S(1)}, bf16[128,1024]{1,0:T(8,128)(2,1)S(1)}, u32[]{:S(2)}, u32[]{:S(2)}) %collective-permute-start.13) | collective-permute-done | bytes 262176 | tf_op jit(solution)/shard_map/ppermute | solution.py:559
  42.7 0.6 collective-permute-start.15
  43.3 2.0 %collective-permute-start.16 = (bf16[128,1024]{1,0:T(8,128)(2,1)S(1)}, bf16[128,1024]{1,0:T(8,128)(2,1)S(1)}, u32[]{:S(2)}, u32[]{:S(2)}) collective-permute-start(bf16[128,1024]{1,0:T(8,128)(2,1)S(1)} %regrid.1.refs_0_.refs_2_), channel_id=1, source_target_pairs={{0,4},{1,5},{2,6},{3,7},{4,0},{5,1},{6,2},{7,3},{8,12},{9,13},{10,... | collective-permute-start | bytes 786440 | tf_op jit(solution)/shard_map/ppermute | solution.py:559
  45.4 1.1 %hidden.1 = (bf16[128,1024]{1,0:T(8,128)(2,1)}, f32[8,128]{1,0:T(8,128)S(1)}) custom-call(bf16[128,1024]{1,0:T(8,128)(2,1)S(1)} %regrid.1.refs_0_.refs_2_, bf16[128,1024]{1,0:T(8,128)(2,1)S(1)} %copy-done.1, f32[2,1024]{1,0:T(2,128)S(1)} %get-tuple-element.51.refs_0_.refs_6_.refs_2_, bf16[128,128]{1,0:T(8,128)(2,1)S(1)} %get-tuple-element.42.refs_3_.refs_4_, ...), custom_call_target="tpu_custom_call" | custom-call | tf_op jit(solution)/shard_map/hidden/pallas_call | solution.py:59
  46.5 2.6 %collective-permute-done.15.refs_1_.refs_6_ = bf16[128,1024]{1,0:T(8,128)(2,1)S(1)} collective-permute-done((bf16[128,1024]{1,0:T(8,128)(2,1)S(1)}, bf16[128,1024]{1,0:T(8,128)(2,1)S(1)}, u32[]{:S(2)}, u32[]{:S(2)}) %collective-permute-start.15) | collective-permute-done | bytes 262176 | tf_op jit(solution)/shard_map/ppermute | solution.py:559
  49.8 2.0 %collective-permute-start.18 = (bf16[128,1024]{1,0:T(8,128)(2,1)S(1)}, bf16[128,1024]{1,0:T(8,128)(2,1)S(1)}, u32[]{:S(2)}, u32[]{:S(2)}) collective-permute-start(bf16[128,1024]{1,0:T(8,128)(2,1)S(1)} %get-tuple-element.67.refs_3_), channel_id=1, source_target_pairs={{0,2},{1,3},{2,0},{3,1},{4,6},{5,7},{6,4},{7,5},{8,10},{9,11},{10,... | collective-permute-start | bytes 786440 | tf_op jit(solution)/shard_map/ppermute | solution.py:559
  51.8 7.2 %collective-permute-start.20 = (bf16[128,1024]{1,0:T(8,128)(2,1)S(1)}, bf16[128,1024]{1,0:T(8,128)(2,1)S(1)}, u32[]{:S(2)}, u32[]{:S(2)}) collective-permute-start(bf16[128,1024]{1,0:T(8,128)(2,1)S(1)} %get-tuple-element.68.refs_1_), channel_id=1, source_target_pairs={{0,4},{1,5},{2,6},{3,7},{4,0},{5,1},{6,2},{7,3},{8,12},{9,13},{10,... | collective-permute-start | bytes 786440 | tf_op jit(solution)/shard_map/ppermute | solution.py:559
  59.0 2.2 %collective-permute-start.23 = (bf16[128,1024]{1,0:T(8,128)(2,1)S(1)}, bf16[128,1024]{1,0:T(8,128)(2,1)S(1)}, u32[]{:S(2)}, u32[]{:S(2)}) collective-permute-start(bf16[128,1024]{1,0:T(8,128)(2,1)S(1)} %collective-permute-done.19.refs_1_), channel_id=1, source_target_pairs={{0,4},{1,5},{2,6},{3,7},{4,0},{5,1},{6,2},{7,3},{8,12},{9,13},{10,... | collective-permute-start | bytes 786440 | tf_op jit(solution)/shard_map/ppermute | solution.py:559
  61.2 2.1 %collective-permute-done.20.refs_2_ = bf16[128,1024]{1,0:T(8,128)(2,1)S(1)} collective-permute-done((bf16[128,1024]{1,0:T(8,128)(2,1)S(1)}, bf16[128,1024]{1,0:T(8,128)(2,1)S(1)}, u32[]{:S(2)}, u32[]{:S(2)}) %collective-permute-start.20) | collective-permute-done | bytes 262176 | tf_op jit(solution)/shard_map/ppermute | solution.py:559
  64.0 1.3 %turn_next.1.refs_0_ = bf16[8,1024,256]{2,1,0:T(8,128)(2,1)S(1)} custom-call(bf16[128,1024]{1,0:T(8,128)(2,1)S(1)} %choose.2.refs_0_.refs_4_, bf16[16384,128]{1,0:T(8,128)(2,1)S(1)} %copy-done, f32[128,128]{1,0:T(8,128)S(1)} %bitcast_convert_fusion.refs_2_, f32[2,128,128]{2,1,0:T(8,128)S(1)} %get-tuple-element.41.refs_2_.refs_3_.refs_1_, ...), custom_call_target="tpu_custom_call" | custom-call | tf_op jit(solution)/shard_map/turn_next/pallas_call | solution.py:59
  65.3 0.8 %collective-permute-done.23.refs_2_ = bf16[128,1024]{1,0:T(8,128)(2,1)S(1)} collective-permute-done((bf16[128,1024]{1,0:T(8,128)(2,1)S(1)}, bf16[128,1024]{1,0:T(8,128)(2,1)S(1)}, u32[]{:S(2)}, u32[]{:S(2)}) %collective-permute-start.23) | collective-permute-done | bytes 262176 | tf_op jit(solution)/shard_map/ppermute | solution.py:559
  66.1 4.8 %collective-permute-done.24.refs_3_.refs_8_ = bf16[128,1024]{1,0:T(8,128)(2,1)S(1)} collective-permute-done((bf16[128,1024]{1,0:T(8,128)(2,1)S(1)}, bf16[128,1024]{1,0:T(8,128)(2,1)S(1)}, u32[]{:S(2)}, u32[]{:S(2)}) %collective-permute-start.24) | collective-permute-done | bytes 262176 | tf_op jit(solution)/shard_map/ppermute | solution.py:559
  71.1 1.8 %collective-permute-start.27 = (bf16[64,1024]{1,0:T(8,128)(2,1)S(1)}, bf16[64,1024]{1,0:T(8,128)(2,1)S(1)}, u32[]{:S(2)}, u32[]{:S(2)}) collective-permute-start(bf16[64,1024]{1,0:T(8,128)(2,1)S(1)} %get-tuple-element.73), channel_id=1, source_target_pairs={{0,4},{1,5},{2,6},{3,7},{4,0},{5,1},{6,2},{7,3},{8,12},{9,13},{10,... | collective-permute-start | bytes 393224 | tf_op jit(solution)/shard_map/ppermute | solution.py:559
  72.9 0.8 project.2.refs_2_
  73.7 2.3 %collective-permute-done.25.refs_3_ = bf16[64,1024]{1,0:T(8,128)(2,1)S(1)} collective-permute-done((bf16[64,1024]{1,0:T(8,128)(2,1)S(1)}, bf16[64,1024]{1,0:T(8,128)(2,1)S(1)}, u32[]{:S(2)}, u32[]{:S(2)}) %collective-permute-start.25) | collective-permute-done | bytes 131104 | tf_op jit(solution)/shard_map/ppermute | solution.py:559
  76.5 1.3 %collective-permute-done.28.refs_1_ = f32[128,256]{1,0:T(8,128)S(1)} collective-permute-done((f32[128,256]{1,0:T(8,128)S(1)}, f32[128,256]{1,0:T(8,128)S(1)}, u32[]{:S(2)}, u32[]{:S(2)}) %collective-permute-start.28) | collective-permute-done | bytes 131104 | tf_op jit(solution)/shard_map/ppermute | solution.py:559
  77.8 0.7 finish.1
  (52 shorter events, 6.6 us)
Async XLA Ops:
  4.8 2.2 %collective-permute-start = (bf16[1,128,1024]{2,1,0:T(8,128)(2,1)S(1)}, bf16[1,128,1024]{2,1,0:T(8,128)(2,1)S(1)}, u32[]{:S(2)}, u32[]{:S(2)}) collective-permute-start(bf16[1,128,1024]{2,1,0:T(8,128)(2,1)S(1)} %get-tuple-element.45), channel_id=1, source_target_pairs={{0,1},{1,0},{2,3},{3,2},{4,5},{5,4},{6,7},{7,6},{8,9},{9,8},{10,11... | collective-permute-start | bytes 786440 | tf_op jit(solution)/shard_map/ppermute | solution.py:559
  6.4 6.1 %collective-permute-start.2 = (bf16[1,128,1024]{2,1,0:T(8,128)(2,1)S(1)}, bf16[1,128,1024]{2,1,0:T(8,128)(2,1)S(1)}, u32[]{:S(2)}, u32[]{:S(2)}) collective-permute-start(bf16[1,128,1024]{2,1,0:T(8,128)(2,1)S(1)} %get-tuple-element.48), channel_id=1, source_target_pairs={{0,1},{1,0},{2,3},{3,2},{4,5},{5,4},{6,7},{7,6},{8,9},{9,8},{10,11... | collective-permute-start | bytes 786440 | tf_op jit(solution)/shard_map/ppermute | solution.py:559
  6.5 6.0 %collective-permute-start.3 = (bf16[1,128,1024]{2,1,0:T(8,128)(2,1)S(1)}, bf16[1,128,1024]{2,1,0:T(8,128)(2,1)S(1)}, u32[]{:S(2)}, u32[]{:S(2)}) collective-permute-start(bf16[1,128,1024]{2,1,0:T(8,128)(2,1)S(1)} %get-tuple-element.49), channel_id=1, source_target_pairs={{0,1},{1,0},{2,3},{3,2},{4,5},{5,4},{6,7},{7,6},{8,9},{9,8},{10,11... | collective-permute-start | bytes 786440 | tf_op jit(solution)/shard_map/ppermute | solution.py:559
  7.0 9.5 %collective-permute-start.1 = (bf16[128,1024]{1,0:T(8,128)(2,1)S(1)}, bf16[128,1024]{1,0:T(8,128)(2,1)S(1)}, u32[]{:S(2)}, u32[]{:S(2)}) collective-permute-start(bf16[128,1024]{1,0:T(8,128)(2,1)S(1)} %add_up.4.refs_0_), channel_id=1, source_target_pairs={{0,2},{1,3},{2,0},{3,1},{4,6},{5,7},{6,4},{7,5},{8,10},{9,11},{10,... | collective-permute-start | bytes 786440 | tf_op jit(solution)/shard_map/ppermute | solution.py:559
  10.4 9.7 %copy-start.1 = (bf16[128,1024]{1,0:T(8,128)(2,1)S(1)}, bf16[128,1024]{1,0:T(8,128)(2,1)}, u32[]{:S(2)}) copy-start(bf16[128,1024]{1,0:T(8,128)(2,1)} %refs_1_.8) | copy-start | bytes 786436
  10.5 9.9 %copy-start = (bf16[16384,128]{1,0:T(8,128)(2,1)S(1)}, bf16[16384,128]{1,0:T(8,128)(2,1)}, u32[]{:S(2)}) copy-start(bf16[16384,128]{1,0:T(8,128)(2,1)} %refs_1_.9) | copy-start | bytes 12582916
  10.5 15.6 %collective-permute-start.7 = (bf16[2,128,1024]{2,1,0:T(8,128)(2,1)S(1)}, bf16[2,128,1024]{2,1,0:T(8,128)(2,1)S(1)}, u32[]{:S(2)}, u32[]{:S(2)}) collective-permute-start(bf16[2,128,1024]{2,1,0:T(8,128)(2,1)S(1)} %get-tuple-element.46.refs_0_), channel_id=1, source_target_pairs={{0,1},{1,0},{2,3},{3,2},{4,5},{5,4},{6,7},{7,6},{8,9},{9,8},{10,11... | collective-permute-start | bytes 1572872 | tf_op jit(solution)/shard_map/ppermute | solution.py:559
  12.0 8.4 %collective-permute-start.6 = (bf16[1,128,1024]{2,1,0:T(8,128)(2,1)S(1)}, bf16[1,128,1024]{2,1,0:T(8,128)(2,1)S(1)}, u32[]{:S(2)}, u32[]{:S(2)}) collective-permute-start(bf16[1,128,1024]{2,1,0:T(8,128)(2,1)S(1)} %get-tuple-element.55), channel_id=1, source_target_pairs={{0,1},{1,0},{2,3},{3,2},{4,5},{5,4},{6,7},{7,6},{8,9},{9,8},{10,11... | collective-permute-start | bytes 786440 | tf_op jit(solution)/shard_map/ppermute | solution.py:559
  16.7 8.1 %collective-permute-start.4 = (bf16[128,1024]{1,0:T(8,128)(2,1)S(1)}, bf16[128,1024]{1,0:T(8,128)(2,1)S(1)}, u32[]{:S(2)}, u32[]{:S(2)}) collective-permute-start(bf16[128,1024]{1,0:T(8,128)(2,1)S(1)} %get-tuple-element.53), channel_id=1, source_target_pairs={{0,2},{1,3},{2,0},{3,1},{4,6},{5,7},{6,4},{7,5},{8,10},{9,11},{10,... | collective-permute-start | bytes 786440 | tf_op jit(solution)/shard_map/ppermute | solution.py:559
  18.5 7.6 %collective-permute-start.5 = (bf16[128,1024]{1,0:T(8,128)(2,1)S(1)}, bf16[128,1024]{1,0:T(8,128)(2,1)S(1)}, u32[]{:S(2)}, u32[]{:S(2)}) collective-permute-start(bf16[128,1024]{1,0:T(8,128)(2,1)S(1)} %get-tuple-element.50.refs_0_), channel_id=1, source_target_pairs={{0,4},{1,5},{2,6},{3,7},{4,0},{5,1},{6,2},{7,3},{8,12},{9,13},{10,... | collective-permute-start | bytes 786440 | tf_op jit(solution)/shard_map/ppermute | solution.py:559
  20.1 8.5 %collective-permute-start.11 = (bf16[2,128,1024]{2,1,0:T(8,128)(2,1)S(1)}, bf16[2,128,1024]{2,1,0:T(8,128)(2,1)S(1)}, u32[]{:S(2)}, u32[]{:S(2)}) collective-permute-start(bf16[2,128,1024]{2,1,0:T(8,128)(2,1)S(1)} %get-tuple-element.47.refs_0_), channel_id=1, source_target_pairs={{0,1},{1,0},{2,3},{3,2},{4,5},{5,4},{6,7},{7,6},{8,9},{9,8},{10,11... | collective-permute-start | bytes 1572872 | tf_op jit(solution)/shard_map/ppermute | solution.py:559
  26.4 6.7 %collective-permute-start.8 = (bf16[128,1024]{1,0:T(8,128)(2,1)S(1)}, bf16[128,1024]{1,0:T(8,128)(2,1)S(1)}, u32[]{:S(2)}, u32[]{:S(2)}) collective-permute-start(bf16[128,1024]{1,0:T(8,128)(2,1)S(1)} %get-tuple-element.57), channel_id=1, source_target_pairs={{0,2},{1,3},{2,0},{3,1},{4,6},{5,7},{6,4},{7,5},{8,10},{9,11},{10,... | collective-permute-start | bytes 786440 | tf_op jit(solution)/shard_map/ppermute | solution.py:559
  26.9 6.6 %collective-permute-start.9 = (bf16[128,1024]{1,0:T(8,128)(2,1)S(1)}, bf16[128,1024]{1,0:T(8,128)(2,1)S(1)}, u32[]{:S(2)}, u32[]{:S(2)}) collective-permute-start(bf16[128,1024]{1,0:T(8,128)(2,1)S(1)} %get-tuple-element.58), channel_id=1, source_target_pairs={{0,4},{1,5},{2,6},{3,7},{4,0},{5,1},{6,2},{7,3},{8,12},{9,13},{10,... | collective-permute-start | bytes 786440 | tf_op jit(solution)/shard_map/ppermute | solution.py:559
  28.6 5.0 %collective-permute-start.10 = (bf16[128,1024]{1,0:T(8,128)(2,1)S(1)}, bf16[128,1024]{1,0:T(8,128)(2,1)S(1)}, u32[]{:S(2)}, u32[]{:S(2)}) collective-permute-start(bf16[128,1024]{1,0:T(8,128)(2,1)S(1)} %get-tuple-element.59), channel_id=1, source_target_pairs={{0,1},{1,0},{2,3},{3,2},{4,8},{5,9},{6,10},{7,11},{8,4},{9,5},{10,... | collective-permute-start | bytes 786440 | tf_op jit(solution)/shard_map/ppermute | solution.py:559
  33.9 30.0 %copy-start.2 = (bf16[16384]{0:T(1024)(128)(2,1)S(1)}, bf16[16384]{0:T(1024)(128)(2,1)}, u32[]{:S(2)}) copy-start(bf16[16384]{0:T(1024)(128)(2,1)} %param.17) | copy-start | bytes 98308
  33.9 6.4 %collective-permute-start.12 = (bf16[128,1024]{1,0:T(8,128)(2,1)S(1)}, bf16[128,1024]{1,0:T(8,128)(2,1)S(1)}, u32[]{:S(2)}, u32[]{:S(2)}) collective-permute-start(bf16[128,1024]{1,0:T(8,128)(2,1)S(1)} %get-tuple-element.61), channel_id=1, source_target_pairs={{0,2},{1,3},{2,0},{3,1},{4,6},{5,7},{6,4},{7,5},{8,10},{9,11},{10,... | collective-permute-start | bytes 786440 | tf_op jit(solution)/shard_map/ppermute | solution.py:559
  35.3 7.1 %collective-permute-start.13 = (bf16[128,1024]{1,0:T(8,128)(2,1)S(1)}, bf16[128,1024]{1,0:T(8,128)(2,1)S(1)}, u32[]{:S(2)}, u32[]{:S(2)}) collective-permute-start(bf16[128,1024]{1,0:T(8,128)(2,1)S(1)} %get-tuple-element.62), channel_id=1, source_target_pairs={{0,4},{1,5},{2,6},{3,7},{4,0},{5,1},{6,2},{7,3},{8,12},{9,13},{10,... | collective-permute-start | bytes 786440 | tf_op jit(solution)/shard_map/ppermute | solution.py:559
  38.0 4.4 %collective-permute-start.14 = (bf16[128,1024]{1,0:T(8,128)(2,1)S(1)}, bf16[128,1024]{1,0:T(8,128)(2,1)S(1)}, u32[]{:S(2)}, u32[]{:S(2)}) collective-permute-start(bf16[128,1024]{1,0:T(8,128)(2,1)S(1)} %get-tuple-element.63), channel_id=1, source_target_pairs={{0,1},{1,0},{2,3},{3,2},{4,8},{5,9},{6,10},{7,11},{8,4},{9,5},{10,... | collective-permute-start | bytes 786440 | tf_op jit(solution)/shard_map/ppermute | solution.py:559
  38.0 26.0 %collective-permute-start.21 = (bf16[4,1024,128]{2,1,0:T(8,128)(2,1)S(1)}, bf16[4,1024,128]{2,1,0:T(8,128)(2,1)S(1)}, u32[]{:S(2)}, u32[]{:S(2)}) collective-permute-start(bf16[4,1024,128]{2,1,0:T(8,128)(2,1)S(1)} %get-tuple-element.52.refs_0_), channel_id=1, source_target_pairs={{0,1},{1,0},{2,3},{3,2},{4,5},{5,4},{6,7},{7,6},{8,9},{9,8},{10,11... | collective-permute-start | bytes 3145736 | tf_op jit(solution)/shard_map/ppermute | solution.py:559
  38.5 25.5 %collective-permute-start.22 = (bf16[4,1024,128]{2,1,0:T(8,128)(2,1)S(1)}, bf16[4,1024,128]{2,1,0:T(8,128)(2,1)S(1)}, u32[]{:S(2)}, u32[]{:S(2)}) collective-permute-start(bf16[4,1024,128]{2,1,0:T(8,128)(2,1)S(1)} %get-tuple-element.69), channel_id=1, source_target_pairs={{0,1},{1,0},{2,3},{3,2},{4,5},{5,4},{6,7},{7,6},{8,9},{9,8},{10,11... | collective-permute-start | bytes 3145736 | tf_op jit(solution)/shard_map/ppermute | solution.py:559
  42.7 6.4 %collective-permute-start.15 = (bf16[128,1024]{1,0:T(8,128)(2,1)S(1)}, bf16[128,1024]{1,0:T(8,128)(2,1)S(1)}, u32[]{:S(2)}, u32[]{:S(2)}) collective-permute-start(bf16[128,1024]{1,0:T(8,128)(2,1)S(1)} %regrid.1.refs_0_.refs_2_), channel_id=1, source_target_pairs={{0,2},{1,3},{2,0},{3,1},{4,6},{5,7},{6,4},{7,5},{8,10},{9,11},{10,... | collective-permute-start | bytes 786440 | tf_op jit(solution)/shard_map/ppermute | solution.py:559
  43.3 6.4 %collective-permute-start.16 = (bf16[128,1024]{1,0:T(8,128)(2,1)S(1)}, bf16[128,1024]{1,0:T(8,128)(2,1)S(1)}, u32[]{:S(2)}, u32[]{:S(2)}) collective-permute-start(bf16[128,1024]{1,0:T(8,128)(2,1)S(1)} %regrid.1.refs_0_.refs_2_), channel_id=1, source_target_pairs={{0,4},{1,5},{2,6},{3,7},{4,0},{5,1},{6,2},{7,3},{8,12},{9,13},{10,... | collective-permute-start | bytes 786440 | tf_op jit(solution)/shard_map/ppermute | solution.py:559
  45.4 4.4 %collective-permute-start.17 = (bf16[128,1024]{1,0:T(8,128)(2,1)S(1)}, bf16[128,1024]{1,0:T(8,128)(2,1)S(1)}, u32[]{:S(2)}, u32[]{:S(2)}) collective-permute-start(bf16[128,1024]{1,0:T(8,128)(2,1)S(1)} %regrid.1.refs_0_.refs_2_), channel_id=1, source_target_pairs={{0,1},{1,0},{2,3},{3,2},{4,8},{5,9},{6,10},{7,11},{8,4},{9,5},{10,... | collective-permute-start | bytes 786440 | tf_op jit(solution)/shard_map/ppermute | solution.py:559
  49.7 9.2 %collective-permute-start.19 = (bf16[128,1024]{1,0:T(8,128)(2,1)S(1)}, bf16[128,1024]{1,0:T(8,128)(2,1)S(1)}, u32[]{:S(2)}, u32[]{:S(2)}) collective-permute-start(bf16[128,1024]{1,0:T(8,128)(2,1)S(1)} %get-tuple-element.67.refs_3_), channel_id=1, source_target_pairs={{0,1},{1,0},{2,3},{3,2},{4,8},{5,9},{6,10},{7,11},{8,4},{9,5},{10,... | collective-permute-start | bytes 786440 | tf_op jit(solution)/shard_map/ppermute | solution.py:559
  49.8 11.4 %collective-permute-start.18 = (bf16[128,1024]{1,0:T(8,128)(2,1)S(1)}, bf16[128,1024]{1,0:T(8,128)(2,1)S(1)}, u32[]{:S(2)}, u32[]{:S(2)}) collective-permute-start(bf16[128,1024]{1,0:T(8,128)(2,1)S(1)} %get-tuple-element.67.refs_3_), channel_id=1, source_target_pairs={{0,2},{1,3},{2,0},{3,1},{4,6},{5,7},{6,4},{7,5},{8,10},{9,11},{10,... | collective-permute-start | bytes 786440 | tf_op jit(solution)/shard_map/ppermute | solution.py:559
  51.8 11.5 %collective-permute-start.20 = (bf16[128,1024]{1,0:T(8,128)(2,1)S(1)}, bf16[128,1024]{1,0:T(8,128)(2,1)S(1)}, u32[]{:S(2)}, u32[]{:S(2)}) collective-permute-start(bf16[128,1024]{1,0:T(8,128)(2,1)S(1)} %get-tuple-element.68.refs_1_), channel_id=1, source_target_pairs={{0,4},{1,5},{2,6},{3,7},{4,0},{5,1},{6,2},{7,3},{8,12},{9,13},{10,... | collective-permute-start | bytes 786440 | tf_op jit(solution)/shard_map/ppermute | solution.py:559
  59.0 7.2 %collective-permute-start.23 = (bf16[128,1024]{1,0:T(8,128)(2,1)S(1)}, bf16[128,1024]{1,0:T(8,128)(2,1)S(1)}, u32[]{:S(2)}, u32[]{:S(2)}) collective-permute-start(bf16[128,1024]{1,0:T(8,128)(2,1)S(1)} %collective-permute-done.19.refs_1_), channel_id=1, source_target_pairs={{0,4},{1,5},{2,6},{3,7},{4,0},{5,1},{6,2},{7,3},{8,12},{9,13},{10,... | collective-permute-start | bytes 786440 | tf_op jit(solution)/shard_map/ppermute | solution.py:559
  63.3 7.6 %collective-permute-start.24 = (bf16[128,1024]{1,0:T(8,128)(2,1)S(1)}, bf16[128,1024]{1,0:T(8,128)(2,1)S(1)}, u32[]{:S(2)}, u32[]{:S(2)}) collective-permute-start(bf16[128,1024]{1,0:T(8,128)(2,1)S(1)} %choose.2.refs_0_.refs_4_), channel_id=1, source_target_pairs={{0,2},{1,3},{2,0},{3,1},{4,6},{5,7},{6,4},{7,5},{8,10},{9,11},{10,... | collective-permute-start | bytes 786440 | tf_op jit(solution)/shard_map/ppermute | solution.py:559
  63.9 9.8 %collective-permute-start.26 = (bf16[64,1024]{1,0:T(8,128)(2,1)S(1)}, bf16[64,1024]{1,0:T(8,128)(2,1)S(1)}, u32[]{:S(2)}, u32[]{:S(2)}) collective-permute-start(bf16[64,1024]{1,0:T(8,128)(2,1)S(1)} %get-tuple-element.72), channel_id=1, source_target_pairs={{0,1},{1,0},{2,3},{3,2},{4,8},{5,9},{6,10},{7,11},{8,4},{9,5},{10,... | collective-permute-start | bytes 393224 | tf_op jit(solution)/shard_map/ppermute | solution.py:559
  71.0 5.0 %collective-permute-start.25 = (bf16[64,1024]{1,0:T(8,128)(2,1)S(1)}, bf16[64,1024]{1,0:T(8,128)(2,1)S(1)}, u32[]{:S(2)}, u32[]{:S(2)}) collective-permute-start(bf16[64,1024]{1,0:T(8,128)(2,1)S(1)} %get-tuple-element.71), channel_id=1, source_target_pairs={{0,2},{1,3},{2,0},{3,1},{4,6},{5,7},{6,4},{7,5},{8,10},{9,11},{10,... | collective-permute-start | bytes 393224 | tf_op jit(solution)/shard_map/ppermute | solution.py:559
  71.1 5.0 %collective-permute-start.27 = (bf16[64,1024]{1,0:T(8,128)(2,1)S(1)}, bf16[64,1024]{1,0:T(8,128)(2,1)S(1)}, u32[]{:S(2)}, u32[]{:S(2)}) collective-permute-start(bf16[64,1024]{1,0:T(8,128)(2,1)S(1)} %get-tuple-element.73), channel_id=1, source_target_pairs={{0,4},{1,5},{2,6},{3,7},{4,0},{5,1},{6,2},{7,3},{8,12},{9,13},{10,... | collective-permute-start | bytes 393224 | tf_op jit(solution)/shard_map/ppermute | solution.py:559
  76.4 1.4 %collective-permute-start.28 = (f32[128,256]{1,0:T(8,128)S(1)}, f32[128,256]{1,0:T(8,128)S(1)}, u32[]{:S(2)}, u32[]{:S(2)}) collective-permute-start(f32[128,256]{1,0:T(8,128)S(1)} %get-tuple-element.75), channel_id=1, source_target_pairs={{0,1},{1,0},{2,3},{3,2},{4,5},{5,4},{6,7},{7,6},{8,9},{9,8},{10,11... | collective-permute-start | bytes 393224 | tf_op jit(solution)/shard_map/ppermute | solution.py:559

commit v8 on v7

--- a/solution.py
+++ b/solution.py
@@ -41,9 +41,8 @@
 
 
 def targets(outer):
-    low = outer < 2
     near = outer + 1 - 2 * lax.rem(outer, 2)
-    return jnp.where(low, 3, 0), jnp.where(low, 2, 1), near, outer
+    return OUTER - 1 - outer, lax.rem(outer + 2, OUTER), near, outer
 
 
 def is_inner(outer):
@@ -246,25 +245,39 @@
     )
 
 
+UPPER, LOWER = 0, 1
+
+
 def add_kernel(inner, inputs, outputs, *refs):
     ins, outs = refs[:inputs], refs[inputs:]
     outer = place(inner)[0]
-    for out_ref, items in zip(outs, outputs):
-        total = None
-        for which, at, inner_only in items:
-            value = (ins[which][...] if at is None else ins[which][at]).astype(F32)
-            if inner_only:
-                value = jnp.where(is_inner(outer), value, 0.0)
-            total = value if total is None else total + value
-        out_ref[...] = total.astype(BF16)
+    rows = ins[0].shape[-2] // 2
+    for out_ref, (items, which_half) in zip(outs, outputs):
+        for half in (UPPER, LOWER) if which_half is None else (which_half,):
+            part = slice(half * rows, (half + 1) * rows)
+            total = None
+            for which, at, inner_only, item_half in items:
+                if item_half is not None and item_half != half:
+                    continue
+                ref = ins[which] if at is None else ins[which].at[at]
+                value = (ref[part] if item_half is None else ref[...]).astype(F32)
+                if inner_only:
+                    value = jnp.where(is_inner(outer), value, 0.0)
+                total = value if total is None else total + value
+            if which_half is None:
+                out_ref[part] = total.astype(BF16)
+            else:
+                out_ref[...] = total.astype(BF16)
 
 
 def add_up(inner, arrays, outputs, after=()):
-    shape = arrays[0].shape[-2:]
-    terms = sum(len(items) for items in outputs)
+    rows, cols = arrays[0].shape[-2:]
+    shapes = [
+        jax.ShapeDtypeStruct((rows if half is None else rows // 2, cols), BF16) for _, half in outputs
+    ]
     return kernel_call(
         functools.partial(add_kernel, inner, len(arrays), outputs),
-        [jax.ShapeDtypeStruct(shape, BF16)] * len(outputs),
+        shapes,
         arrays,
         [vmem()] * len(arrays),
         after=after,
@@ -462,7 +475,7 @@
 
 def project_kernel(inner, places, has_acc, split, w_ref, rows_ref, *refs):
     outer, mid, core = place(inner)
-    order = (outer, targets(outer)[2], lax.rem(outer + 2, OUTER), OUTER - 1 - outer)
+    order = targets(outer)[::-1]
     acc_in = refs[0] if has_acc else None
     refs = refs[1:] if has_acc else refs
     count = sum(parts for _, _, parts in places)
@@ -587,9 +600,17 @@
         ((True, away1), (True, blocks2), *((False, (block,)) for block in blocks2))
     )
     other2 = [swap_core(send) for send in send2]
-    items1 = [((0, s - 1, False), (1, s - 1, False)) for s in shifts]
-    pay1 = add_up(inner, [keep1, other1], items1, after=[keep2])
+    items1 = [[(0, s - 1, False, None), (1, s - 1, False, None)] for s in shifts]
+    first = add_up(
+        inner,
+        [keep1, other1],
+        [(items, UPPER) for items in items1] + [(items, LOWER) for items in items1],
+        after=[keep2],
+    )
+    pay1, low1 = first[: len(shifts)], first[len(shifts) :]
     come1 = [shift_mid(pay, s) for s, pay in zip(shifts, pay1)]
+    low_pairs = [swap_pairs(low) for low in low1]
+    low_middle = [swap_middle(low) for low in low1]
     near_block = ((1, 0),)
     send2n, send3 = grid_blocks(((False, near_block), (False, phase_blocks(2))), pay1[:1])
     other2n, other3 = swap_core(send2n), swap_core(send3)
@@ -606,14 +627,16 @@
 
     def sums(arrays, outputs, after=()):
         names = list(arrays)
-        items = [[(names.index(name), at, only) for name, at, only in output] for output in outputs]
+        items = [
+            ([(names.index(name), *rest) for name, *rest in output], None) for output in outputs
+        ]
         return add_up(inner, list(arrays.values()), items, after=after)
 
-    def came(step, blocks):
-        return {f"came{step}_{s}": block for s, block in zip(shifts, blocks)}
-
-    def added(names):
-        return [(name, None, False) for name in names]
+    def named(name, blocks):
+        return {f"{name}_{s}": block for s, block in zip(shifts, blocks)}
+
+    def added(names, half=None):
+        return [(name, None, False, half) for name in names]
 
     own2 = {"keep2": keep2} | {f"other2_{i}": other for i, other in enumerate(other2)}
     own2n = {"keep2n": keep2n, "other2n": other2n}
@@ -621,38 +644,48 @@
     own4 = {"keep4": keep4, "other4": other4}
 
     def part2(i):
-        return [("keep2", i, False), (f"other2_{i}", 0, False)]
+        return [("keep2", i, False, None), (f"other2_{i}", 0, False, None)]
 
     def part(step, s):
-        return [(f"keep{step}", s, False), (f"other{step}", s, False)]
-
-    came1 = came(1, come1)
-    near1 = part2(0) + added(came1)
-    *pay2, end1 = sums(came1 | own2, [*(part2(s) for s in shifts), near1], after=[send4])
-    came2 = came(2, [shift_mid(pay, s) for s, pay in zip(shifts, pay2)])
+        return [(f"keep{step}", s, False, None), (f"other{step}", s, False, None)]
+
+    def passed(name, s):
+        return [(f"{name}_{s}", None, True, LOWER)]
+
+    def relayed(name):
+        return [(name, None, True, None)]
+
+    came1, from_pairs = named("came1", come1), named("pairs", low_pairs)
+    from_middle = named("middle", low_middle)
+    near1 = part2(0) + added(came1, UPPER)
+    *pay2, end1 = sums(
+        own2 | came1 | from_pairs,
+        [*(part2(s) + passed("pairs", s) for s in shifts), near1],
+        after=[*come1, send4],
+    )
+    came2 = named("came2", [shift_mid(pay, s) for s, pay in zip(shifts, pay2)])
     from_end1 = {"end1": swap_pairs(end1)}
     turned_residual, factors = turn_residual(inner, residual, rows, had, after=[end1])
     picked = select_rows(inner, next_query_weight, cols, after=[factors])
     next_other = [swap_core(part) for part in picked]
 
     near2 = part("2n", 0) + added(came2)
-    *pay3, end2, mid2 = sums(
-        came2 | from_end1 | own2 | own2n | own3 | came1,
-        [*(part(3, s) for s in shifts), near2, near1 + [("end1", None, True)]],
+    *pay3, sum2 = sums(
+        came2 | from_end1 | own2n | own3,
+        [*(part(3, s) for s in shifts), near2 + relayed("end1")],
         after=picked[:1],
     )
-    came3 = came(3, [shift_mid(pay, s) for s, pay in zip(shifts, pay3)])
-    from_end2 = {"end2": swap_pairs(end2)}
-    from_mid2 = {"mid2": swap_middle(mid2)}
-
-    *pay4, mid3, near3 = sums(
-        came3 | from_end2 | from_mid2 | own2n | own3 | own4 | came2,
+    came3 = named("came3", [shift_mid(pay, s) for s, pay in zip(shifts, pay3)])
+    from_end2 = {"end2": swap_pairs(sum2)}
+    from_mid2 = {"mid2": swap_middle(sum2)}
+
+    *pay4, near3, mid3 = sums(
+        came3 | from_end2 | from_mid2 | own2 | own3 | own4 | came1 | from_middle,
         [
-            *(part(4, s) for s in shifts),
-            near2 + [("end2", None, True)],
-            part(3, 0) + added(came3) + [("mid2", None, True)],
+            *(part(4, s) + passed("middle", s) for s in shifts),
+            part(3, 0) + added(came3) + relayed("mid2"),
+            near1 + relayed("end2"),
         ],
-
     )
     come4 = [shift_mid(pay, s) for s, pay in zip(shifts, pay4)]
     from_mid3 = swap_middle(mid3)
@@ -668,7 +701,7 @@
     near = swap_pairs(grid)
     mid1 = swap_middle(grid)
     hidden_out, mark = hidden(inner, items, residual, factors, had, last, after=[grid])
-    near, mid1, *low1 = gate([near, mid1], x1, after=[mark])
+    near, *low1 = gate([near], x1, after=[mark])
     x2 = [shift_mid(near, s) for s in shifts]
     ends2 = swap_pairs(mid1)
     mids2 = swap_middle(near)

time: 78.6 us -> 79.8 us (1.015)
  starting transfers between devices: 31.3 us -> 37.3 us
  waiting for transfers between devices: 33.3 us -> 28.5 us
    ppermute x29 -> x31, starting transfers between devices: 31.3 us -> 37.3 us  [permute(): return lax.ppermute(value, 'tp', moves)]
    ppermute x29 -> x31, waiting for transfers between devices: 33.3 us -> 28.5 us  [permute(): return lax.ppermute(value, 'tp', moves)]
  transfers between devices with their start and end apart: 29 -> 31, of which waited for: 15 -> 16; matrix products, arithmetic and copies ran while one was open for 0% -> 0% of each run, Pallas kernels for 10% -> 9%
where the time goes in v8:
time: 79.8 us; the launch traced here: 79.6 us
  starting transfers between devices  37.3 us (47%)
  waiting for transfers between devices  28.5 us (36%)
  Pallas kernels  13 us (16%)
  between operations  0.87 us (1%)
    ppermute x31, starting transfers between devices, permute(): return lax.ppermute(value, 'tp', moves)  37.3 us
    ppermute x31, waiting for transfers between devices, permute(): return lax.ppermute(value, 'tp', moves)  28.5 us
    pallas_call x19, Pallas kernels, kernel_call(): pl.pallas_call(ordered, out_shape=out_shape, in_specs=[anywhere()] * extr...  13 us
  transfers between devices with their start and end apart: 31, of which 16 were waited for; matrix products, arithmetic and copies ran while one was open for 0% of the time, Pallas kernels for 9%

profile of v8, /device:TPU:0, one launch (start us, length us, event | category | flops | bytes accessed | tf_op | source)
XLA Modules:
  0.0 79.6 jit_solution(7923598662694339385)
XLA Ops:
  0.6 4.1 %attend.1 = (bf16[128,128]{1,0:T(8,128)(2,1)S(1)}, f32[2,128,128]{2,1,0:T(8,128)S(1)}, bf16[1,128,1024]{2,1,0:T(8,128)(2,1)S(1)}, bf16[128,16384]{1,0:T(8,128)(2,1)S(1)}, bf16[128,128]{1,0:T(8,128)(2,1)S(1)}) custom-call(bf16[1,128,128]{2,1,0:T(8,128)(2,1)} %refs_0_.1, bf16[1,8192,128]{2,1,0:T(8,128)(2,1)} %refs_1_.5, bf16[1,8192,128]{2,1,0:T(8,128)(2,1)} %refs_2_.1, ...), custom_call_target="tpu_custom_call" | custom-call | tf_op jit(solution)/shard_map/attend/pallas_call | solution.py:58
  5.3 1.1 %partials.3 = (bf16[1,128,1024]{2,1,0:T(8,128)(2,1)S(1)}, bf16[2,128,1024]{2,1,0:T(8,128)(2,1)S(1)}, bf16[1,128,1024]{2,1,0:T(8,128)(2,1)S(1)}, bf16[1,128,1024]{2,1,0:T(8,128)(2,1)S(1)}) custom-call(bf16[128,128]{1,0:T(8,128)(2,1)S(1)} %get-tuple-element.39.refs_0_.refs_1_, bf16[128,16384]{1,0:T(8,128)(2,1)S(1)} %get-tuple-element.40.refs_1_.refs_2_, ...), custom_call_target="tpu_custom_call" | custom-call | tf_op jit(solution)/shard_map/partials/pallas_call | solution.py:58
  7.0 0.8 %partials.4 = (bf16[1,128,1024]{2,1,0:T(8,128)(2,1)S(1)}, bf16[2,128,1024]{2,1,0:T(8,128)(2,1)S(1)}) custom-call(bf16[64,1024]{1,0:T(8,128)(2,1)S(1)} %get-tuple-element.46.refs_0_, bf16[128,128]{1,0:T(8,128)(2,1)S(1)} %get-tuple-element.39.refs_0_.refs_1_, bf16[128,16384]{1,0:T(8,128)(2,1)S(1)} %get-tuple-element.40.refs_1_.refs_2_, ...), custom_call_target="tpu_custom_call" | custom-call | tf_op jit(solution)/shard_map/partials/pallas_call | solution.py:58
  8.0 2.9 %collective-permute-start.1 = (bf16[64,1024]{1,0:T(8,128)(2,1)S(1)}, bf16[64,1024]{1,0:T(8,128)(2,1)S(1)}, u32[]{:S(2)}, u32[]{:S(2)}) collective-permute-start(bf16[64,1024]{1,0:T(8,128)(2,1)S(1)} %get-tuple-element.46.refs_0_), channel_id=1, source_target_pairs={{0,2},{1,3},{2,0},{3,1},{4,6},{5,7},{6,4},{7,5},{8,10},{9,11},{10,... | collective-permute-start | bytes 393224 | tf_op jit(solution)/shard_map/ppermute | solution.py:572
  10.9 1.6 %collective-permute-start.4 = (bf16[64,1024]{1,0:T(8,128)(2,1)S(1)}, bf16[64,1024]{1,0:T(8,128)(2,1)S(1)}, u32[]{:S(2)}, u32[]{:S(2)}) collective-permute-start(bf16[64,1024]{1,0:T(8,128)(2,1)S(1)} %get-tuple-element.51), channel_id=1, source_target_pairs={{0,4},{1,5},{2,6},{3,7},{4,0},{5,1},{6,2},{7,3},{8,12},{9,13},{10,... | collective-permute-start | bytes 393224 | tf_op jit(solution)/shard_map/ppermute | solution.py:572
  12.5 1.3 %partials.5 = (bf16[2,128,1024]{2,1,0:T(8,128)(2,1)S(1)}, bf16[1,128,1024]{2,1,0:T(8,128)(2,1)S(1)}, bf16[2,128,1024]{2,1,0:T(8,128)(2,1)S(1)}, bf16[2,128,1024]{2,1,0:T(8,128)(2,1)S(1)}) custom-call(bf16[2,128,1024]{2,1,0:T(8,128)(2,1)S(1)} %get-tuple-element.47.refs_0_, bf16[128,128]{1,0:T(8,128)(2,1)S(1)} %get-tuple-element.39.refs_0_.refs_1_, ...), custom_call_target="tpu_custom_call" | custom-call | tf_op jit(solution)/shard_map/partials/pallas_call | solution.py:58
  14.7 1.5 %collective-permute-done.4.refs_6_ = bf16[64,1024]{1,0:T(8,128)(2,1)S(1)} collective-permute-done((bf16[64,1024]{1,0:T(8,128)(2,1)S(1)}, bf16[64,1024]{1,0:T(8,128)(2,1)S(1)}, u32[]{:S(2)}, u32[]{:S(2)}) %collective-permute-start.4) | collective-permute-done | bytes 131104 | tf_op jit(solution)/shard_map/ppermute | solution.py:572
  16.7 1.7 %collective-permute-start.6 = (bf16[128,1024]{1,0:T(8,128)(2,1)S(1)}, bf16[128,1024]{1,0:T(8,128)(2,1)S(1)}, u32[]{:S(2)}, u32[]{:S(2)}) collective-permute-start(bf16[128,1024]{1,0:T(8,128)(2,1)S(1)} %get-tuple-element.52.refs_0_), channel_id=1, source_target_pairs={{0,4},{1,5},{2,6},{3,7},{4,0},{5,1},{6,2},{7,3},{8,12},{9,13},{10,... | collective-permute-start | bytes 786440 | tf_op jit(solution)/shard_map/ppermute | solution.py:572
  18.9 4.6 %collective-permute-done.5.refs_1_ = bf16[128,1024]{1,0:T(8,128)(2,1)S(1)} collective-permute-done((bf16[128,1024]{1,0:T(8,128)(2,1)S(1)}, bf16[128,1024]{1,0:T(8,128)(2,1)S(1)}, u32[]{:S(2)}, u32[]{:S(2)}) %collective-permute-start.5) | collective-permute-done | bytes 262176 | tf_op jit(solution)/shard_map/ppermute | solution.py:572
  24.1 1.4 %collective-permute-start.9 = (bf16[128,1024]{1,0:T(8,128)(2,1)S(1)}, bf16[128,1024]{1,0:T(8,128)(2,1)S(1)}, u32[]{:S(2)}, u32[]{:S(2)}) collective-permute-start(bf16[128,1024]{1,0:T(8,128)(2,1)S(1)} %get-tuple-element.59), channel_id=1, source_target_pairs={{0,2},{1,3},{2,0},{3,1},{4,6},{5,7},{6,4},{7,5},{8,10},{9,11},{10,... | collective-permute-start | bytes 786440 | tf_op jit(solution)/shard_map/ppermute | solution.py:572
  25.5 1.6 %collective-permute-start.10 = (bf16[128,1024]{1,0:T(8,128)(2,1)S(1)}, bf16[128,1024]{1,0:T(8,128)(2,1)S(1)}, u32[]{:S(2)}, u32[]{:S(2)}) collective-permute-start(bf16[128,1024]{1,0:T(8,128)(2,1)S(1)} %get-tuple-element.60), channel_id=1, source_target_pairs={{0,4},{1,5},{2,6},{3,7},{4,0},{5,1},{6,2},{7,3},{8,12},{9,13},{10,... | collective-permute-start | bytes 786440 | tf_op jit(solution)/shard_map/ppermute | solution.py:572
  27.6 1.2 %collective-permute-done.13.refs_11_ = bf16[64,1024]{1,0:T(8,128)(2,1)S(1)} collective-permute-done((bf16[64,1024]{1,0:T(8,128)(2,1)S(1)}, bf16[64,1024]{1,0:T(8,128)(2,1)S(1)}, u32[]{:S(2)}, u32[]{:S(2)}) %collective-permute-start.13) | collective-permute-done | bytes 131104 | tf_op jit(solution)/shard_map/ppermute | solution.py:572
  28.8 1.7 %collective-permute-done.9.refs_0_ = bf16[128,1024]{1,0:T(8,128)(2,1)S(1)} collective-permute-done((bf16[128,1024]{1,0:T(8,128)(2,1)S(1)}, bf16[128,1024]{1,0:T(8,128)(2,1)S(1)}, u32[]{:S(2)}, u32[]{:S(2)}) %collective-permute-start.9) | collective-permute-done | bytes 262176 | tf_op jit(solution)/shard_map/ppermute | solution.py:572
  30.5 1.3 %collective-permute-done.10.refs_1_ = bf16[128,1024]{1,0:T(8,128)(2,1)S(1)} collective-permute-done((bf16[128,1024]{1,0:T(8,128)(2,1)S(1)}, bf16[128,1024]{1,0:T(8,128)(2,1)S(1)}, u32[]{:S(2)}, u32[]{:S(2)}) %collective-permute-start.10) | collective-permute-done | bytes 262176 | tf_op jit(solution)/shard_map/ppermute | solution.py:572
  32.3 0.7 collective-permute-start.14
  33.0 4.8 %collective-permute-start.15 = (bf16[128,1024]{1,0:T(8,128)(2,1)S(1)}, bf16[128,1024]{1,0:T(8,128)(2,1)S(1)}, u32[]{:S(2)}, u32[]{:S(2)}) collective-permute-start(bf16[128,1024]{1,0:T(8,128)(2,1)S(1)} %get-tuple-element.63), channel_id=1, source_target_pairs={{0,4},{1,5},{2,6},{3,7},{4,0},{5,1},{6,2},{7,3},{8,12},{9,13},{10,... | collective-permute-start | bytes 786440 | tf_op jit(solution)/shard_map/ppermute | solution.py:572
  38.7 3.5 %collective-permute-done.15.refs_1_.refs_5_ = bf16[128,1024]{1,0:T(8,128)(2,1)S(1)} collective-permute-done((bf16[128,1024]{1,0:T(8,128)(2,1)S(1)}, bf16[128,1024]{1,0:T(8,128)(2,1)S(1)}, u32[]{:S(2)}, u32[]{:S(2)}) %collective-permute-start.15) | collective-permute-done | bytes 262176 | tf_op jit(solution)/shard_map/ppermute | solution.py:572
  42.4 1.7 %collective-permute-start.17 = (bf16[128,1024]{1,0:T(8,128)(2,1)S(1)}, bf16[128,1024]{1,0:T(8,128)(2,1)S(1)}, u32[]{:S(2)}, u32[]{:S(2)}) collective-permute-start(bf16[128,1024]{1,0:T(8,128)(2,1)S(1)} %regrid.1.refs_0_.refs_2_), channel_id=1, source_target_pairs={{0,2},{1,3},{2,0},{3,1},{4,6},{5,7},{6,4},{7,5},{8,10},{9,11},{10,... | collective-permute-start | bytes 786440 | tf_op jit(solution)/shard_map/ppermute | solution.py:572
  44.1 2.5 %collective-permute-start.18 = (bf16[128,1024]{1,0:T(8,128)(2,1)S(1)}, bf16[128,1024]{1,0:T(8,128)(2,1)S(1)}, u32[]{:S(2)}, u32[]{:S(2)}) collective-permute-start(bf16[128,1024]{1,0:T(8,128)(2,1)S(1)} %regrid.1.refs_0_.refs_2_), channel_id=1, source_target_pairs={{0,4},{1,5},{2,6},{3,7},{4,0},{5,1},{6,2},{7,3},{8,12},{9,13},{10,... | collective-permute-start | bytes 786440 | tf_op jit(solution)/shard_map/ppermute | solution.py:572
  46.6 1.1 %hidden.1 = (bf16[128,1024]{1,0:T(8,128)(2,1)}, f32[8,128]{1,0:T(8,128)S(1)}) custom-call(bf16[128,1024]{1,0:T(8,128)(2,1)S(1)} %regrid.1.refs_0_.refs_2_, bf16[128,1024]{1,0:T(8,128)(2,1)S(1)} %copy-done.1, f32[2,1024]{1,0:T(2,128)S(1)} %get-tuple-element.53.refs_0_.refs_6_.refs_2_, bf16[128,128]{1,0:T(8,128)(2,1)S(1)} %get-tuple-element.42.refs_3_.refs_4_, ...), custom_call_target="tpu_custom_call" | custom-call | tf_op jit(solution)/shard_map/hidden/pallas_call | solution.py:58
  47.7 1.2 %collective-permute-done.17.refs_1_.refs_6_ = bf16[128,1024]{1,0:T(8,128)(2,1)S(1)} collective-permute-done((bf16[128,1024]{1,0:T(8,128)(2,1)S(1)}, bf16[128,1024]{1,0:T(8,128)(2,1)S(1)}, u32[]{:S(2)}, u32[]{:S(2)}) %collective-permute-start.17) | collective-permute-done | bytes 262176 | tf_op jit(solution)/shard_map/ppermute | solution.py:572
  48.9 2.0 %collective-permute-done.18.refs_2_ = bf16[128,1024]{1,0:T(8,128)(2,1)S(1)} collective-permute-done((bf16[128,1024]{1,0:T(8,128)(2,1)S(1)}, bf16[128,1024]{1,0:T(8,128)(2,1)S(1)}, u32[]{:S(2)}, u32[]{:S(2)}) %collective-permute-start.18) | collective-permute-done | bytes 262176 | tf_op jit(solution)/shard_map/ppermute | solution.py:572
  51.2 6.8 %collective-permute-start.22 = (bf16[128,1024]{1,0:T(8,128)(2,1)S(1)}, bf16[128,1024]{1,0:T(8,128)(2,1)S(1)}, u32[]{:S(2)}, u32[]{:S(2)}) collective-permute-start(bf16[128,1024]{1,0:T(8,128)(2,1)S(1)} %collective-permute-done.21.refs_1_), channel_id=1, source_target_pairs={{0,4},{1,5},{2,6},{3,7},{4,0},{5,1},{6,2},{7,3},{8,12},{9,13},{10,... | collective-permute-start | bytes 786440 | tf_op jit(solution)/shard_map/ppermute | solution.py:572
  58.0 2.2 %collective-permute-start.25 = (bf16[128,1024]{1,0:T(8,128)(2,1)S(1)}, bf16[128,1024]{1,0:T(8,128)(2,1)S(1)}, u32[]{:S(2)}, u32[]{:S(2)}) collective-permute-start(bf16[128,1024]{1,0:T(8,128)(2,1)S(1)} %collective-permute-done.20.refs_1_), channel_id=1, source_target_pairs={{0,4},{1,5},{2,6},{3,7},{4,0},{5,1},{6,2},{7,3},{8,12},{9,13},{10,... | collective-permute-start | bytes 786440 | tf_op jit(solution)/shard_map/ppermute | solution.py:572
  60.2 2.3 %collective-permute-done.22.refs_2_ = bf16[128,1024]{1,0:T(8,128)(2,1)S(1)} collective-permute-done((bf16[128,1024]{1,0:T(8,128)(2,1)S(1)}, bf16[128,1024]{1,0:T(8,128)(2,1)S(1)}, u32[]{:S(2)}, u32[]{:S(2)}) %collective-permute-start.22) | collective-permute-done | bytes 262176 | tf_op jit(solution)/shard_map/ppermute | solution.py:572
  62.6 1.8 %collective-permute-start.26 = (bf16[128,1024]{1,0:T(8,128)(2,1)S(1)}, bf16[128,1024]{1,0:T(8,128)(2,1)S(1)}, u32[]{:S(2)}, u32[]{:S(2)}) collective-permute-start(bf16[128,1024]{1,0:T(8,128)(2,1)S(1)} %choose.2.refs_0_.refs_4_), channel_id=1, source_target_pairs={{0,2},{1,3},{2,0},{3,1},{4,6},{5,7},{6,4},{7,5},{8,10},{9,11},{10,... | collective-permute-start | bytes 786440 | tf_op jit(solution)/shard_map/ppermute | solution.py:572
  64.5 1.3 %turn_next.1.refs_0_ = bf16[8,1024,256]{2,1,0:T(8,128)(2,1)S(1)} custom-call(bf16[128,1024]{1,0:T(8,128)(2,1)S(1)} %choose.2.refs_0_.refs_4_, bf16[16384,128]{1,0:T(8,128)(2,1)S(1)} %copy-done, f32[128,128]{1,0:T(8,128)S(1)} %bitcast_convert_fusion.refs_2_, f32[2,128,128]{2,1,0:T(8,128)S(1)} %get-tuple-element.41.refs_2_.refs_3_.refs_1_, ...), custom_call_target="tpu_custom_call" | custom-call | tf_op jit(solution)/shard_map/turn_next/pallas_call | solution.py:58
  65.8 3.9 %collective-permute-done.26.refs_3_.refs_8_ = bf16[128,1024]{1,0:T(8,128)(2,1)S(1)} collective-permute-done((bf16[128,1024]{1,0:T(8,128)(2,1)S(1)}, bf16[128,1024]{1,0:T(8,128)(2,1)S(1)}, u32[]{:S(2)}, u32[]{:S(2)}) %collective-permute-start.26) | collective-permute-done | bytes 262176 | tf_op jit(solution)/shard_map/ppermute | solution.py:572
  69.8 2.5 %collective-permute-start.27 = (bf16[64,1024]{1,0:T(8,128)(2,1)S(1)}, bf16[64,1024]{1,0:T(8,128)(2,1)S(1)}, u32[]{:S(2)}, u32[]{:S(2)}) collective-permute-start(bf16[64,1024]{1,0:T(8,128)(2,1)S(1)} %get-tuple-element.71), channel_id=1, source_target_pairs={{0,2},{1,3},{2,0},{3,1},{4,6},{5,7},{6,4},{7,5},{8,10},{9,11},{10,... | collective-permute-start | bytes 393224 | tf_op jit(solution)/shard_map/ppermute | solution.py:572
  72.3 1.9 %collective-permute-start.29 = (bf16[64,1024]{1,0:T(8,128)(2,1)S(1)}, bf16[64,1024]{1,0:T(8,128)(2,1)S(1)}, u32[]{:S(2)}, u32[]{:S(2)}) collective-permute-start(bf16[64,1024]{1,0:T(8,128)(2,1)S(1)} %get-tuple-element.73), channel_id=1, source_target_pairs={{0,4},{1,5},{2,6},{3,7},{4,0},{5,1},{6,2},{7,3},{8,12},{9,13},{10,... | collective-permute-start | bytes 393224 | tf_op jit(solution)/shard_map/ppermute | solution.py:572
  75.2 2.0 %collective-permute-done.29.refs_5_ = bf16[64,1024]{1,0:T(8,128)(2,1)S(1)} collective-permute-done((bf16[64,1024]{1,0:T(8,128)(2,1)S(1)}, bf16[64,1024]{1,0:T(8,128)(2,1)S(1)}, u32[]{:S(2)}, u32[]{:S(2)}) %collective-permute-start.29) | collective-permute-done | bytes 131104 | tf_op jit(solution)/shard_map/ppermute | solution.py:572
  77.6 1.3 %collective-permute-done.30.refs_1_ = f32[128,256]{1,0:T(8,128)S(1)} collective-permute-done((f32[128,256]{1,0:T(8,128)S(1)}, f32[128,256]{1,0:T(8,128)S(1)}, u32[]{:S(2)}, u32[]{:S(2)}) %collective-permute-start.30) | collective-permute-done | bytes 131104 | tf_op jit(solution)/shard_map/ppermute | solution.py:572
  (56 shorter events, 8.2 us)
Async XLA Ops:
  4.8 2.2 %collective-permute-start = (bf16[1,128,1024]{2,1,0:T(8,128)(2,1)S(1)}, bf16[1,128,1024]{2,1,0:T(8,128)(2,1)S(1)}, u32[]{:S(2)}, u32[]{:S(2)}) collective-permute-start(bf16[1,128,1024]{2,1,0:T(8,128)(2,1)S(1)} %get-tuple-element.45), channel_id=1, source_target_pairs={{0,1},{1,0},{2,3},{3,2},{4,5},{5,4},{6,7},{7,6},{8,9},{9,8},{10,11... | collective-permute-start | bytes 786440 | tf_op jit(solution)/shard_map/ppermute | solution.py:572
  6.4 7.5 %collective-permute-start.2 = (bf16[1,128,1024]{2,1,0:T(8,128)(2,1)S(1)}, bf16[1,128,1024]{2,1,0:T(8,128)(2,1)S(1)}, u32[]{:S(2)}, u32[]{:S(2)}) collective-permute-start(bf16[1,128,1024]{2,1,0:T(8,128)(2,1)S(1)} %get-tuple-element.49), channel_id=1, source_target_pairs={{0,1},{1,0},{2,3},{3,2},{4,5},{5,4},{6,7},{7,6},{8,9},{9,8},{10,11... | collective-permute-start | bytes 786440 | tf_op jit(solution)/shard_map/ppermute | solution.py:572
  6.5 7.4 %collective-permute-start.3 = (bf16[1,128,1024]{2,1,0:T(8,128)(2,1)S(1)}, bf16[1,128,1024]{2,1,0:T(8,128)(2,1)S(1)}, u32[]{:S(2)}, u32[]{:S(2)}) collective-permute-start(bf16[1,128,1024]{2,1,0:T(8,128)(2,1)S(1)} %get-tuple-element.50), channel_id=1, source_target_pairs={{0,1},{1,0},{2,3},{3,2},{4,5},{5,4},{6,7},{7,6},{8,9},{9,8},{10,11... | collective-permute-start | bytes 786440 | tf_op jit(solution)/shard_map/ppermute | solution.py:572
  7.9 16.0 %collective-permute-start.8 = (bf16[2,128,1024]{2,1,0:T(8,128)(2,1)S(1)}, bf16[2,128,1024]{2,1,0:T(8,128)(2,1)S(1)}, u32[]{:S(2)}, u32[]{:S(2)}) collective-permute-start(bf16[2,128,1024]{2,1,0:T(8,128)(2,1)S(1)} %get-tuple-element.47.refs_0_), channel_id=1, source_target_pairs={{0,1},{1,0},{2,3},{3,2},{4,5},{5,4},{6,7},{7,6},{8,9},{9,8},{10,11... | collective-permute-start | bytes 1572872 | tf_op jit(solution)/shard_map/ppermute | solution.py:572
  8.0 6.7 %collective-permute-start.1 = (bf16[64,1024]{1,0:T(8,128)(2,1)S(1)}, bf16[64,1024]{1,0:T(8,128)(2,1)S(1)}, u32[]{:S(2)}, u32[]{:S(2)}) collective-permute-start(bf16[64,1024]{1,0:T(8,128)(2,1)S(1)} %get-tuple-element.46.refs_0_), channel_id=1, source_target_pairs={{0,2},{1,3},{2,0},{3,1},{4,6},{5,7},{6,4},{7,5},{8,10},{9,11},{10,... | collective-permute-start | bytes 393224 | tf_op jit(solution)/shard_map/ppermute | solution.py:572
  10.9 5.2 %collective-permute-start.4 = (bf16[64,1024]{1,0:T(8,128)(2,1)S(1)}, bf16[64,1024]{1,0:T(8,128)(2,1)S(1)}, u32[]{:S(2)}, u32[]{:S(2)}) collective-permute-start(bf16[64,1024]{1,0:T(8,128)(2,1)S(1)} %get-tuple-element.51), channel_id=1, source_target_pairs={{0,4},{1,5},{2,6},{3,7},{4,0},{5,1},{6,2},{7,3},{8,12},{9,13},{10,... | collective-permute-start | bytes 393224 | tf_op jit(solution)/shard_map/ppermute | solution.py:572
  13.8 5.0 %collective-permute-start.7 = (bf16[1,128,1024]{2,1,0:T(8,128)(2,1)S(1)}, bf16[1,128,1024]{2,1,0:T(8,128)(2,1)S(1)}, u32[]{:S(2)}, u32[]{:S(2)}) collective-permute-start(bf16[1,128,1024]{2,1,0:T(8,128)(2,1)S(1)} %get-tuple-element.57), channel_id=1, source_target_pairs={{0,1},{1,0},{2,3},{3,2},{4,5},{5,4},{6,7},{7,6},{8,9},{9,8},{10,11... | collective-permute-start | bytes 786440 | tf_op jit(solution)/shard_map/ppermute | solution.py:572
  16.3 7.2 %collective-permute-start.5 = (bf16[128,1024]{1,0:T(8,128)(2,1)S(1)}, bf16[128,1024]{1,0:T(8,128)(2,1)S(1)}, u32[]{:S(2)}, u32[]{:S(2)}) collective-permute-start(bf16[128,1024]{1,0:T(8,128)(2,1)S(1)} %get-tuple-element.55), channel_id=1, source_target_pairs={{0,2},{1,3},{2,0},{3,1},{4,6},{5,7},{6,4},{7,5},{8,10},{9,11},{10,... | collective-permute-start | bytes 786440 | tf_op jit(solution)/shard_map/ppermute | solution.py:572
  16.7 7.2 %collective-permute-start.6 = (bf16[128,1024]{1,0:T(8,128)(2,1)S(1)}, bf16[128,1024]{1,0:T(8,128)(2,1)S(1)}, u32[]{:S(2)}, u32[]{:S(2)}) collective-permute-start(bf16[128,1024]{1,0:T(8,128)(2,1)S(1)} %get-tuple-element.52.refs_0_), channel_id=1, source_target_pairs={{0,4},{1,5},{2,6},{3,7},{4,0},{5,1},{6,2},{7,3},{8,12},{9,13},{10,... | collective-permute-start | bytes 786440 | tf_op jit(solution)/shard_map/ppermute | solution.py:572
  18.5 10.4 %collective-permute-start.12 = (bf16[2,128,1024]{2,1,0:T(8,128)(2,1)S(1)}, bf16[2,128,1024]{2,1,0:T(8,128)(2,1)S(1)}, u32[]{:S(2)}, u32[]{:S(2)}) collective-permute-start(bf16[2,128,1024]{2,1,0:T(8,128)(2,1)S(1)} %get-tuple-element.48.refs_1_), channel_id=1, source_target_pairs={{0,1},{1,0},{2,3},{3,2},{4,5},{5,4},{6,7},{7,6},{8,9},{9,8},{10,11... | collective-permute-start | bytes 1572872 | tf_op jit(solution)/shard_map/ppermute | solution.py:572
  24.1 6.4 %collective-permute-start.9 = (bf16[128,1024]{1,0:T(8,128)(2,1)S(1)}, bf16[128,1024]{1,0:T(8,128)(2,1)S(1)}, u32[]{:S(2)}, u32[]{:S(2)}) collective-permute-start(bf16[128,1024]{1,0:T(8,128)(2,1)S(1)} %get-tuple-element.59), channel_id=1, source_target_pairs={{0,2},{1,3},{2,0},{3,1},{4,6},{5,7},{6,4},{7,5},{8,10},{9,11},{10,... | collective-permute-start | bytes 786440 | tf_op jit(solution)/shard_map/ppermute | solution.py:572
  25.5 6.4 %collective-permute-start.10 = (bf16[128,1024]{1,0:T(8,128)(2,1)S(1)}, bf16[128,1024]{1,0:T(8,128)(2,1)S(1)}, u32[]{:S(2)}, u32[]{:S(2)}) collective-permute-start(bf16[128,1024]{1,0:T(8,128)(2,1)S(1)} %get-tuple-element.60), channel_id=1, source_target_pairs={{0,4},{1,5},{2,6},{3,7},{4,0},{5,1},{6,2},{7,3},{8,12},{9,13},{10,... | collective-permute-start | bytes 786440 | tf_op jit(solution)/shard_map/ppermute | solution.py:572
  27.1 4.8 %collective-permute-start.11 = (bf16[128,1024]{1,0:T(8,128)(2,1)S(1)}, bf16[128,1024]{1,0:T(8,128)(2,1)S(1)}, u32[]{:S(2)}, u32[]{:S(2)}) collective-permute-start(bf16[128,1024]{1,0:T(8,128)(2,1)S(1)} %get-tuple-element.60), channel_id=1, source_target_pairs={{0,1},{1,0},{2,3},{3,2},{4,8},{5,9},{6,10},{7,11},{8,4},{9,5},{10,... | collective-permute-start | bytes 786440 | tf_op jit(solution)/shard_map/ppermute | solution.py:572
  27.1 1.7 %collective-permute-start.13 = (bf16[64,1024]{1,0:T(8,128)(2,1)S(1)}, bf16[64,1024]{1,0:T(8,128)(2,1)S(1)}, u32[]{:S(2)}, u32[]{:S(2)}) collective-permute-start(bf16[64,1024]{1,0:T(8,128)(2,1)S(1)} %get-tuple-element.51), channel_id=1, source_target_pairs={{0,1},{1,0},{2,3},{3,2},{4,8},{5,9},{6,10},{7,11},{8,4},{9,5},{10,... | collective-permute-start | bytes 393224 | tf_op jit(solution)/shard_map/ppermute | solution.py:572
  32.2 32.1 %copy-start.2 = (bf16[16384]{0:T(1024)(128)(2,1)S(1)}, bf16[16384]{0:T(1024)(128)(2,1)}, u32[]{:S(2)}) copy-start(bf16[16384]{0:T(1024)(128)(2,1)} %param.17) | copy-start | bytes 98308
  32.3 6.4 %collective-permute-start.14 = (bf16[128,1024]{1,0:T(8,128)(2,1)S(1)}, bf16[128,1024]{1,0:T(8,128)(2,1)S(1)}, u32[]{:S(2)}, u32[]{:S(2)}) collective-permute-start(bf16[128,1024]{1,0:T(8,128)(2,1)S(1)} %get-tuple-element.62), channel_id=1, source_target_pairs={{0,2},{1,3},{2,0},{3,1},{4,6},{5,7},{6,4},{7,5},{8,10},{9,11},{10,... | collective-permute-start | bytes 786440 | tf_op jit(solution)/shard_map/ppermute | solution.py:572
  33.0 9.2 %collective-permute-start.15 = (bf16[128,1024]{1,0:T(8,128)(2,1)S(1)}, bf16[128,1024]{1,0:T(8,128)(2,1)S(1)}, u32[]{:S(2)}, u32[]{:S(2)}) collective-permute-start(bf16[128,1024]{1,0:T(8,128)(2,1)S(1)} %get-tuple-element.63), channel_id=1, source_target_pairs={{0,4},{1,5},{2,6},{3,7},{4,0},{5,1},{6,2},{7,3},{8,12},{9,13},{10,... | collective-permute-start | bytes 786440 | tf_op jit(solution)/shard_map/ppermute | solution.py:572
  37.8 4.4 %collective-permute-start.16 = (bf16[128,1024]{1,0:T(8,128)(2,1)S(1)}, bf16[128,1024]{1,0:T(8,128)(2,1)S(1)}, u32[]{:S(2)}, u32[]{:S(2)}) collective-permute-start(bf16[128,1024]{1,0:T(8,128)(2,1)S(1)} %get-tuple-element.64), channel_id=1, source_target_pairs={{0,1},{1,0},{2,3},{3,2},{4,8},{5,9},{6,10},{7,11},{8,4},{9,5},{10,... | collective-permute-start | bytes 786440 | tf_op jit(solution)/shard_map/ppermute | solution.py:572
  37.8 26.7 %collective-permute-start.23 = (bf16[4,1024,128]{2,1,0:T(8,128)(2,1)S(1)}, bf16[4,1024,128]{2,1,0:T(8,128)(2,1)S(1)}, u32[]{:S(2)}, u32[]{:S(2)}) collective-permute-start(bf16[4,1024,128]{2,1,0:T(8,128)(2,1)S(1)} %get-tuple-element.54.refs_0_), channel_id=1, source_target_pairs={{0,1},{1,0},{2,3},{3,2},{4,5},{5,4},{6,7},{7,6},{8,9},{9,8},{10,11... | collective-permute-start | bytes 3145736 | tf_op jit(solution)/shard_map/ppermute | solution.py:572
  38.3 26.2 %collective-permute-start.24 = (bf16[4,1024,128]{2,1,0:T(8,128)(2,1)S(1)}, bf16[4,1024,128]{2,1,0:T(8,128)(2,1)S(1)}, u32[]{:S(2)}, u32[]{:S(2)}) collective-permute-start(bf16[4,1024,128]{2,1,0:T(8,128)(2,1)S(1)} %get-tuple-element.69), channel_id=1, source_target_pairs={{0,1},{1,0},{2,3},{3,2},{4,5},{5,4},{6,7},{7,6},{8,9},{9,8},{10,11... | collective-permute-start | bytes 3145736 | tf_op jit(solution)/shard_map/ppermute | solution.py:572
  42.4 6.4 %collective-permute-start.17 = (bf16[128,1024]{1,0:T(8,128)(2,1)S(1)}, bf16[128,1024]{1,0:T(8,128)(2,1)S(1)}, u32[]{:S(2)}, u32[]{:S(2)}) collective-permute-start(bf16[128,1024]{1,0:T(8,128)(2,1)S(1)} %regrid.1.refs_0_.refs_2_), channel_id=1, source_target_pairs={{0,2},{1,3},{2,0},{3,1},{4,6},{5,7},{6,4},{7,5},{8,10},{9,11},{10,... | collective-permute-start | bytes 786440 | tf_op jit(solution)/shard_map/ppermute | solution.py:572
  44.1 6.8 %collective-permute-start.18 = (bf16[128,1024]{1,0:T(8,128)(2,1)S(1)}, bf16[128,1024]{1,0:T(8,128)(2,1)S(1)}, u32[]{:S(2)}, u32[]{:S(2)}) collective-permute-start(bf16[128,1024]{1,0:T(8,128)(2,1)S(1)} %regrid.1.refs_0_.refs_2_), channel_id=1, source_target_pairs={{0,4},{1,5},{2,6},{3,7},{4,0},{5,1},{6,2},{7,3},{8,12},{9,13},{10,... | collective-permute-start | bytes 786440 | tf_op jit(solution)/shard_map/ppermute | solution.py:572
  46.6 4.6 %collective-permute-start.21 = (bf16[128,1024]{1,0:T(8,128)(2,1)S(1)}, bf16[128,1024]{1,0:T(8,128)(2,1)S(1)}, u32[]{:S(2)}, u32[]{:S(2)}) collective-permute-start(bf16[128,1024]{1,0:T(8,128)(2,1)S(1)} %regrid.1.refs_0_.refs_2_), channel_id=1, source_target_pairs={{0,1},{1,0},{2,3},{3,2},{4,8},{5,9},{6,10},{7,11},{8,4},{9,5},{10,... | collective-permute-start | bytes 786440 | tf_op jit(solution)/shard_map/ppermute | solution.py:572
  50.9 7.1 %collective-permute-start.20 = (bf16[128,1024]{1,0:T(8,128)(2,1)S(1)}, bf16[128,1024]{1,0:T(8,128)(2,1)S(1)}, u32[]{:S(2)}, u32[]{:S(2)}) collective-permute-start(bf16[128,1024]{1,0:T(8,128)(2,1)S(1)} %get-tuple-element.68.refs_3_), channel_id=1, source_target_pairs={{0,1},{1,0},{2,3},{3,2},{4,8},{5,9},{6,10},{7,11},{8,4},{9,5},{10,... | collective-permute-start | bytes 786440 | tf_op jit(solution)/shard_map/ppermute | solution.py:572
  51.0 9.2 %collective-permute-start.19 = (bf16[128,1024]{1,0:T(8,128)(2,1)S(1)}, bf16[128,1024]{1,0:T(8,128)(2,1)S(1)}, u32[]{:S(2)}, u32[]{:S(2)}) collective-permute-start(bf16[128,1024]{1,0:T(8,128)(2,1)S(1)} %get-tuple-element.68.refs_3_), channel_id=1, source_target_pairs={{0,2},{1,3},{2,0},{3,1},{4,6},{5,7},{6,4},{7,5},{8,10},{9,11},{10,... | collective-permute-start | bytes 786440 | tf_op jit(solution)/shard_map/ppermute | solution.py:572
  51.2 11.4 %collective-permute-start.22 = (bf16[128,1024]{1,0:T(8,128)(2,1)S(1)}, bf16[128,1024]{1,0:T(8,128)(2,1)S(1)}, u32[]{:S(2)}, u32[]{:S(2)}) collective-permute-start(bf16[128,1024]{1,0:T(8,128)(2,1)S(1)} %collective-permute-done.21.refs_1_), channel_id=1, source_target_pairs={{0,4},{1,5},{2,6},{3,7},{4,0},{5,1},{6,2},{7,3},{8,12},{9,13},{10,... | collective-permute-start | bytes 786440 | tf_op jit(solution)/shard_map/ppermute | solution.py:572
  58.0 7.8 %collective-permute-start.25 = (bf16[128,1024]{1,0:T(8,128)(2,1)S(1)}, bf16[128,1024]{1,0:T(8,128)(2,1)S(1)}, u32[]{:S(2)}, u32[]{:S(2)}) collective-permute-start(bf16[128,1024]{1,0:T(8,128)(2,1)S(1)} %collective-permute-done.20.refs_1_), channel_id=1, source_target_pairs={{0,4},{1,5},{2,6},{3,7},{4,0},{5,1},{6,2},{7,3},{8,12},{9,13},{10,... | collective-permute-start | bytes 786440 | tf_op jit(solution)/shard_map/ppermute | solution.py:572
  62.6 7.2 %collective-permute-start.26 = (bf16[128,1024]{1,0:T(8,128)(2,1)S(1)}, bf16[128,1024]{1,0:T(8,128)(2,1)S(1)}, u32[]{:S(2)}, u32[]{:S(2)}) collective-permute-start(bf16[128,1024]{1,0:T(8,128)(2,1)S(1)} %choose.2.refs_0_.refs_4_), channel_id=1, source_target_pairs={{0,2},{1,3},{2,0},{3,1},{4,6},{5,7},{6,4},{7,5},{8,10},{9,11},{10,... | collective-permute-start | bytes 786440 | tf_op jit(solution)/shard_map/ppermute | solution.py:572
  64.4 10.5 %collective-permute-start.28 = (bf16[64,1024]{1,0:T(8,128)(2,1)S(1)}, bf16[64,1024]{1,0:T(8,128)(2,1)S(1)}, u32[]{:S(2)}, u32[]{:S(2)}) collective-permute-start(bf16[64,1024]{1,0:T(8,128)(2,1)S(1)} %get-tuple-element.72), channel_id=1, source_target_pairs={{0,1},{1,0},{2,3},{3,2},{4,8},{5,9},{6,10},{7,11},{8,4},{9,5},{10,... | collective-permute-start | bytes 393224 | tf_op jit(solution)/shard_map/ppermute | solution.py:572
  69.8 5.5 %collective-permute-start.27 = (bf16[64,1024]{1,0:T(8,128)(2,1)S(1)}, bf16[64,1024]{1,0:T(8,128)(2,1)S(1)}, u32[]{:S(2)}, u32[]{:S(2)}) collective-permute-start(bf16[64,1024]{1,0:T(8,128)(2,1)S(1)} %get-tuple-element.71), channel_id=1, source_target_pairs={{0,2},{1,3},{2,0},{3,1},{4,6},{5,7},{6,4},{7,5},{8,10},{9,11},{10,... | collective-permute-start | bytes 393224 | tf_op jit(solution)/shard_map/ppermute | solution.py:572
  72.3 5.0 %collective-permute-start.29 = (bf16[64,1024]{1,0:T(8,128)(2,1)S(1)}, bf16[64,1024]{1,0:T(8,128)(2,1)S(1)}, u32[]{:S(2)}, u32[]{:S(2)}) collective-permute-start(bf16[64,1024]{1,0:T(8,128)(2,1)S(1)} %get-tuple-element.73), channel_id=1, source_target_pairs={{0,4},{1,5},{2,6},{3,7},{4,0},{5,1},{6,2},{7,3},{8,12},{9,13},{10,... | collective-permute-start | bytes 393224 | tf_op jit(solution)/shard_map/ppermute | solution.py:572
  77.5 1.4 %collective-permute-start.30 = (f32[128,256]{1,0:T(8,128)S(1)}, f32[128,256]{1,0:T(8,128)S(1)}, u32[]{:S(2)}, u32[]{:S(2)}) collective-permute-start(f32[128,256]{1,0:T(8,128)S(1)} %get-tuple-element.75), channel_id=1, source_target_pairs={{0,1},{1,0},{2,3},{3,2},{4,5},{5,4},{6,7},{7,6},{8,9},{9,8},{10,11... | collective-permute-start | bytes 393224 | tf_op jit(solution)/shard_map/ppermute | solution.py:572
  (2 other events, 21.5 us)

commit v9 on v8

--- a/solution.py
+++ b/solution.py
@@ -367,9 +367,9 @@
     )
 
 
-def choose_kernel(inner, count, inner_ref, end_ref, *refs):
+def choose_kernel(inner, count, *refs):
     inside = is_inner(place(inner)[0])
-    others, out_ref, outs = refs[:count], refs[count], refs[count + 1 :]
+    others, (inner_ref, end_ref, out_ref, *outs) = refs[:count], refs[count:]
     lower, upper = outs[:count], outs[count:]
 
     def put(ref):
@@ -395,7 +395,7 @@
     return kernel_call(
         functools.partial(choose_kernel, inner, len(others)),
         [jax.ShapeDtypeStruct((rows, cols), BF16)] + [half] * (len(others) + halved),
-        [at_inner, at_end, *others],
+        [*others, at_inner, at_end],
         [vmem()] * (2 + len(others)),
         after=after,
         name="choose",
@@ -673,7 +673,7 @@
     *pay3, sum2 = sums(
         came2 | from_end1 | own2n | own3,
         [*(part(3, s) for s in shifts), near2 + relayed("end1")],
-        after=picked[:1],
+        after=[*picked[:1], *low_middle],
     )
     came3 = named("came3", [shift_mid(pay, s) for s, pay in zip(shifts, pay3)])
     from_end2 = {"end2": swap_pairs(sum2)}
@@ -707,7 +707,7 @@
     mids2 = swap_middle(near)
     (third,) = choose(inner, mids2, ends2, after=x2)
     x3 = [shift_mid(third, s) for s in shifts]
-    ends3 = swap_pairs(mids2)
+    ends3 = swap_pairs(third)
     side_middle = [swap_middle(low) for low in low1]
     turned_next = turn_next(inner, next_query_weight, next_other, gain, rows, had, after=[third])
     fourth, *low3, up4 = choose(inner, mid1, ends3, x3, True, after=[turned_next])

time: 79.8 us -> 80.6 us (1.010)
  waiting for transfers between devices: 28.5 us -> 32.4 us
  starting transfers between devices: 37.3 us -> 34.3 us
    ppermute x31, waiting for transfers between devices: 28.5 us -> 32.4 us  [permute(): return lax.ppermute(value, 'tp', moves)]
    ppermute x31, starting transfers between devices: 37.3 us -> 34.3 us  [permute(): return lax.ppermute(value, 'tp', moves)]
  transfers between devices with their start and end apart: 31 -> 31, of which waited for: 16 -> 15; matrix products, arithmetic and copies ran while one was open for 0% -> 0% of each run, Pallas kernels for 9% -> 9%
where the time goes in v9:
time: 80.6 us; the launch traced here: 80.5 us
  starting transfers between devices  34.3 us (43%)
  waiting for transfers between devices  32.4 us (40%)
  Pallas kernels  13 us (16%)
  between operations  0.85 us (1%)
    ppermute x31, starting transfers between devices, permute(): return lax.ppermute(value, 'tp', moves)  34.3 us
    ppermute x31, waiting for transfers between devices, permute(): return lax.ppermute(value, 'tp', moves)  32.4 us
    pallas_call x19, Pallas kernels, kernel_call(): pl.pallas_call(ordered, out_shape=out_shape, in_specs=[anywhere()] * extr...  13 us
  transfers between devices with their start and end apart: 31, of which 15 were waited for; matrix products, arithmetic and copies ran while one was open for 0% of the time, Pallas kernels for 9%

profile of v9, /device:TPU:0, one launch (start us, length us, event | category | flops | bytes accessed | tf_op | source)
XLA Modules:
  0.0 80.5 jit_solution(1991577468106381863)
XLA Ops:
  0.6 4.1 %attend.1 = (bf16[128,128]{1,0:T(8,128)(2,1)S(1)}, f32[2,128,128]{2,1,0:T(8,128)S(1)}, bf16[1,128,1024]{2,1,0:T(8,128)(2,1)S(1)}, bf16[128,16384]{1,0:T(8,128)(2,1)S(1)}, bf16[128,128]{1,0:T(8,128)(2,1)S(1)}) custom-call(bf16[1,128,128]{2,1,0:T(8,128)(2,1)} %refs_0_.1, bf16[1,8192,128]{2,1,0:T(8,128)(2,1)} %refs_1_.5, bf16[1,8192,128]{2,1,0:T(8,128)(2,1)} %refs_2_.1, ...), custom_call_target="tpu_custom_call" | custom-call | tf_op jit(solution)/shard_map/attend/pallas_call | solution.py:58
  5.3 1.1 %partials.3 = (bf16[1,128,1024]{2,1,0:T(8,128)(2,1)S(1)}, bf16[2,128,1024]{2,1,0:T(8,128)(2,1)S(1)}, bf16[1,128,1024]{2,1,0:T(8,128)(2,1)S(1)}, bf16[1,128,1024]{2,1,0:T(8,128)(2,1)S(1)}) custom-call(bf16[128,128]{1,0:T(8,128)(2,1)S(1)} %get-tuple-element.39.refs_0_.refs_1_, bf16[128,16384]{1,0:T(8,128)(2,1)S(1)} %get-tuple-element.40.refs_1_.refs_2_, ...), custom_call_target="tpu_custom_call" | custom-call | tf_op jit(solution)/shard_map/partials/pallas_call | solution.py:58
  7.0 0.8 %partials.4 = (bf16[1,128,1024]{2,1,0:T(8,128)(2,1)S(1)}, bf16[2,128,1024]{2,1,0:T(8,128)(2,1)S(1)}) custom-call(bf16[64,1024]{1,0:T(8,128)(2,1)S(1)} %get-tuple-element.46.refs_0_, bf16[128,128]{1,0:T(8,128)(2,1)S(1)} %get-tuple-element.39.refs_0_.refs_1_, bf16[128,16384]{1,0:T(8,128)(2,1)S(1)} %get-tuple-element.40.refs_1_.refs_2_, ...), custom_call_target="tpu_custom_call" | custom-call | tf_op jit(solution)/shard_map/partials/pallas_call | solution.py:58
  8.0 2.9 %collective-permute-start.1 = (bf16[64,1024]{1,0:T(8,128)(2,1)S(1)}, bf16[64,1024]{1,0:T(8,128)(2,1)S(1)}, u32[]{:S(2)}, u32[]{:S(2)}) collective-permute-start(bf16[64,1024]{1,0:T(8,128)(2,1)S(1)} %get-tuple-element.46.refs_0_), channel_id=1, source_target_pairs={{0,2},{1,3},{2,0},{3,1},{4,6},{5,7},{6,4},{7,5},{8,10},{9,11},{10,... | collective-permute-start | bytes 393224 | tf_op jit(solution)/shard_map/ppermute | solution.py:572
  10.9 1.6 %collective-permute-start.4 = (bf16[64,1024]{1,0:T(8,128)(2,1)S(1)}, bf16[64,1024]{1,0:T(8,128)(2,1)S(1)}, u32[]{:S(2)}, u32[]{:S(2)}) collective-permute-start(bf16[64,1024]{1,0:T(8,128)(2,1)S(1)} %get-tuple-element.51), channel_id=1, source_target_pairs={{0,4},{1,5},{2,6},{3,7},{4,0},{5,1},{6,2},{7,3},{8,12},{9,13},{10,... | collective-permute-start | bytes 393224 | tf_op jit(solution)/shard_map/ppermute | solution.py:572
  12.5 1.3 %partials.5 = (bf16[2,128,1024]{2,1,0:T(8,128)(2,1)S(1)}, bf16[1,128,1024]{2,1,0:T(8,128)(2,1)S(1)}, bf16[2,128,1024]{2,1,0:T(8,128)(2,1)S(1)}, bf16[2,128,1024]{2,1,0:T(8,128)(2,1)S(1)}) custom-call(bf16[2,128,1024]{2,1,0:T(8,128)(2,1)S(1)} %get-tuple-element.47.refs_0_, bf16[128,128]{1,0:T(8,128)(2,1)S(1)} %get-tuple-element.39.refs_0_.refs_1_, ...), custom_call_target="tpu_custom_call" | custom-call | tf_op jit(solution)/shard_map/partials/pallas_call | solution.py:58
  14.7 1.5 %collective-permute-done.4.refs_6_ = bf16[64,1024]{1,0:T(8,128)(2,1)S(1)} collective-permute-done((bf16[64,1024]{1,0:T(8,128)(2,1)S(1)}, bf16[64,1024]{1,0:T(8,128)(2,1)S(1)}, u32[]{:S(2)}, u32[]{:S(2)}) %collective-permute-start.4) | collective-permute-done | bytes 131104 | tf_op jit(solution)/shard_map/ppermute | solution.py:572
  16.7 1.7 %collective-permute-start.7 = (bf16[128,1024]{1,0:T(8,128)(2,1)S(1)}, bf16[128,1024]{1,0:T(8,128)(2,1)S(1)}, u32[]{:S(2)}, u32[]{:S(2)}) collective-permute-start(bf16[128,1024]{1,0:T(8,128)(2,1)S(1)} %get-tuple-element.52.refs_0_), channel_id=1, source_target_pairs={{0,4},{1,5},{2,6},{3,7},{4,0},{5,1},{6,2},{7,3},{8,12},{9,13},{10,... | collective-permute-start | bytes 786440 | tf_op jit(solution)/shard_map/ppermute | solution.py:572
  18.9 4.6 %collective-permute-done.6.refs_2_ = bf16[128,1024]{1,0:T(8,128)(2,1)S(1)} collective-permute-done((bf16[128,1024]{1,0:T(8,128)(2,1)S(1)}, bf16[128,1024]{1,0:T(8,128)(2,1)S(1)}, u32[]{:S(2)}, u32[]{:S(2)}) %collective-permute-start.6) | collective-permute-done | bytes 262176 | tf_op jit(solution)/shard_map/ppermute | solution.py:572
  23.5 1.1 %collective-permute-done.7.refs_3_ = bf16[128,1024]{1,0:T(8,128)(2,1)S(1)} collective-permute-done((bf16[128,1024]{1,0:T(8,128)(2,1)S(1)}, bf16[128,1024]{1,0:T(8,128)(2,1)S(1)}, u32[]{:S(2)}, u32[]{:S(2)}) %collective-permute-start.7) | collective-permute-done | bytes 262176 | tf_op jit(solution)/shard_map/ppermute | solution.py:572
  24.8 1.6 %collective-permute-start.10 = (bf16[128,1024]{1,0:T(8,128)(2,1)S(1)}, bf16[128,1024]{1,0:T(8,128)(2,1)S(1)}, u32[]{:S(2)}, u32[]{:S(2)}) collective-permute-start(bf16[128,1024]{1,0:T(8,128)(2,1)S(1)} %get-tuple-element.59), channel_id=1, source_target_pairs={{0,2},{1,3},{2,0},{3,1},{4,6},{5,7},{6,4},{7,5},{8,10},{9,11},{10,... | collective-permute-start | bytes 786440 | tf_op jit(solution)/shard_map/ppermute | solution.py:572
  26.3 1.7 %collective-permute-start.11 = (bf16[128,1024]{1,0:T(8,128)(2,1)S(1)}, bf16[128,1024]{1,0:T(8,128)(2,1)S(1)}, u32[]{:S(2)}, u32[]{:S(2)}) collective-permute-start(bf16[128,1024]{1,0:T(8,128)(2,1)S(1)} %get-tuple-element.60), channel_id=1, source_target_pairs={{0,4},{1,5},{2,6},{3,7},{4,0},{5,1},{6,2},{7,3},{8,12},{9,13},{10,... | collective-permute-start | bytes 786440 | tf_op jit(solution)/shard_map/ppermute | solution.py:572
  28.1 3.7 %collective-permute-done.10.refs_0_ = bf16[128,1024]{1,0:T(8,128)(2,1)S(1)} collective-permute-done((bf16[128,1024]{1,0:T(8,128)(2,1)S(1)}, bf16[128,1024]{1,0:T(8,128)(2,1)S(1)}, u32[]{:S(2)}, u32[]{:S(2)}) %collective-permute-start.10) | collective-permute-done | bytes 262176 | tf_op jit(solution)/shard_map/ppermute | solution.py:572
  31.8 1.2 %collective-permute-done.11.refs_1_ = bf16[128,1024]{1,0:T(8,128)(2,1)S(1)} collective-permute-done((bf16[128,1024]{1,0:T(8,128)(2,1)S(1)}, bf16[128,1024]{1,0:T(8,128)(2,1)S(1)}, u32[]{:S(2)}, u32[]{:S(2)}) %collective-permute-start.11) | collective-permute-done | bytes 262176 | tf_op jit(solution)/shard_map/ppermute | solution.py:572
  34.0 1.7 %collective-permute-start.15 = (bf16[128,1024]{1,0:T(8,128)(2,1)S(1)}, bf16[128,1024]{1,0:T(8,128)(2,1)S(1)}, u32[]{:S(2)}, u32[]{:S(2)}) collective-permute-start(bf16[128,1024]{1,0:T(8,128)(2,1)S(1)} %get-tuple-element.63), channel_id=1, source_target_pairs={{0,4},{1,5},{2,6},{3,7},{4,0},{5,1},{6,2},{7,3},{8,12},{9,13},{10,... | collective-permute-start | bytes 786440 | tf_op jit(solution)/shard_map/ppermute | solution.py:572
  36.3 3.5 %collective-permute-done.14.refs_0_.refs_4_ = bf16[128,1024]{1,0:T(8,128)(2,1)S(1)} collective-permute-done((bf16[128,1024]{1,0:T(8,128)(2,1)S(1)}, bf16[128,1024]{1,0:T(8,128)(2,1)S(1)}, u32[]{:S(2)}, u32[]{:S(2)}) %collective-permute-start.14) | collective-permute-done | bytes 262176 | tf_op jit(solution)/shard_map/ppermute | solution.py:572
  40.7 1.5 %collective-permute-start.17 = (bf16[128,1024]{1,0:T(8,128)(2,1)S(1)}, bf16[128,1024]{1,0:T(8,128)(2,1)S(1)}, u32[]{:S(2)}, u32[]{:S(2)}) collective-permute-start(bf16[128,1024]{1,0:T(8,128)(2,1)S(1)} %regrid.1.refs_0_.refs_2_), channel_id=1, source_target_pairs={{0,2},{1,3},{2,0},{3,1},{4,6},{5,7},{6,4},{7,5},{8,10},{9,11},{10,... | collective-permute-start | bytes 786440 | tf_op jit(solution)/shard_map/ppermute | solution.py:572
  42.2 2.3 %collective-permute-start.18 = (bf16[128,1024]{1,0:T(8,128)(2,1)S(1)}, bf16[128,1024]{1,0:T(8,128)(2,1)S(1)}, u32[]{:S(2)}, u32[]{:S(2)}) collective-permute-start(bf16[128,1024]{1,0:T(8,128)(2,1)S(1)} %regrid.1.refs_0_.refs_2_), channel_id=1, source_target_pairs={{0,4},{1,5},{2,6},{3,7},{4,0},{5,1},{6,2},{7,3},{8,12},{9,13},{10,... | collective-permute-start | bytes 786440 | tf_op jit(solution)/shard_map/ppermute | solution.py:572
  44.4 1.1 %hidden.1 = (bf16[128,1024]{1,0:T(8,128)(2,1)}, f32[8,128]{1,0:T(8,128)S(1)}) custom-call(bf16[128,1024]{1,0:T(8,128)(2,1)S(1)} %regrid.1.refs_0_.refs_2_, bf16[128,1024]{1,0:T(8,128)(2,1)S(1)} %copy-done.1, f32[2,1024]{1,0:T(2,128)S(1)} %get-tuple-element.53.refs_0_.refs_6_.refs_2_, bf16[128,128]{1,0:T(8,128)(2,1)S(1)} %get-tuple-element.42.refs_3_.refs_4_, ...), custom_call_target="tpu_custom_call" | custom-call | tf_op jit(solution)/shard_map/hidden/pallas_call | solution.py:58
  45.6 1.6 %collective-permute-done.17.refs_1_.refs_6_ = bf16[128,1024]{1,0:T(8,128)(2,1)S(1)} collective-permute-done((bf16[128,1024]{1,0:T(8,128)(2,1)S(1)}, bf16[128,1024]{1,0:T(8,128)(2,1)S(1)}, u32[]{:S(2)}, u32[]{:S(2)}) %collective-permute-start.17) | collective-permute-done | bytes 262176 | tf_op jit(solution)/shard_map/ppermute | solution.py:572
  47.1 1.7 %collective-permute-done.18.refs_2_ = bf16[128,1024]{1,0:T(8,128)(2,1)S(1)} collective-permute-done((bf16[128,1024]{1,0:T(8,128)(2,1)S(1)}, bf16[128,1024]{1,0:T(8,128)(2,1)S(1)}, u32[]{:S(2)}, u32[]{:S(2)}) %collective-permute-start.18) | collective-permute-done | bytes 262176 | tf_op jit(solution)/shard_map/ppermute | solution.py:572
  49.2 7.2 %collective-permute-start.22 = (bf16[128,1024]{1,0:T(8,128)(2,1)S(1)}, bf16[128,1024]{1,0:T(8,128)(2,1)S(1)}, u32[]{:S(2)}, u32[]{:S(2)}) collective-permute-start(bf16[128,1024]{1,0:T(8,128)(2,1)S(1)} %collective-permute-done.21.refs_2_), channel_id=1, source_target_pairs={{0,4},{1,5},{2,6},{3,7},{4,0},{5,1},{6,2},{7,3},{8,12},{9,13},{10,... | collective-permute-start | bytes 786440 | tf_op jit(solution)/shard_map/ppermute | solution.py:572
  56.5 6.3 %collective-permute-done.22.refs_2_ = bf16[128,1024]{1,0:T(8,128)(2,1)S(1)} collective-permute-done((bf16[128,1024]{1,0:T(8,128)(2,1)S(1)}, bf16[128,1024]{1,0:T(8,128)(2,1)S(1)}, u32[]{:S(2)}, u32[]{:S(2)}) %collective-permute-start.22) | collective-permute-done | bytes 262176 | tf_op jit(solution)/shard_map/ppermute | solution.py:572
  63.2 2.5 %collective-permute-start.26 = (bf16[128,1024]{1,0:T(8,128)(2,1)S(1)}, bf16[128,1024]{1,0:T(8,128)(2,1)S(1)}, u32[]{:S(2)}, u32[]{:S(2)}) collective-permute-start(bf16[128,1024]{1,0:T(8,128)(2,1)S(1)} %choose.2.refs_0_.refs_4_), channel_id=1, source_target_pairs={{0,4},{1,5},{2,6},{3,7},{4,0},{5,1},{6,2},{7,3},{8,12},{9,13},{10,... | collective-permute-start | bytes 786440 | tf_op jit(solution)/shard_map/ppermute | solution.py:572
  65.8 1.3 %turn_next.1.refs_0_ = bf16[8,1024,256]{2,1,0:T(8,128)(2,1)S(1)} custom-call(bf16[128,1024]{1,0:T(8,128)(2,1)S(1)} %choose.2.refs_0_.refs_4_, bf16[16384,128]{1,0:T(8,128)(2,1)S(1)} %copy-done, f32[128,128]{1,0:T(8,128)S(1)} %bitcast_convert_fusion.refs_2_, f32[2,128,128]{2,1,0:T(8,128)S(1)} %get-tuple-element.41.refs_2_.refs_3_.refs_1_, ...), custom_call_target="tpu_custom_call" | custom-call | tf_op jit(solution)/shard_map/turn_next/pallas_call | solution.py:58
  67.1 2.1 %collective-permute-done.25.refs_1_.refs_8_ = bf16[128,1024]{1,0:T(8,128)(2,1)S(1)} collective-permute-done((bf16[128,1024]{1,0:T(8,128)(2,1)S(1)}, bf16[128,1024]{1,0:T(8,128)(2,1)S(1)}, u32[]{:S(2)}, u32[]{:S(2)}) %collective-permute-start.25) | collective-permute-done | bytes 262176 | tf_op jit(solution)/shard_map/ppermute | solution.py:572
  69.2 0.8 %collective-permute-done.26.refs_3_ = bf16[128,1024]{1,0:T(8,128)(2,1)S(1)} collective-permute-done((bf16[128,1024]{1,0:T(8,128)(2,1)S(1)}, bf16[128,1024]{1,0:T(8,128)(2,1)S(1)}, u32[]{:S(2)}, u32[]{:S(2)}) %collective-permute-start.26) | collective-permute-done | bytes 262176 | tf_op jit(solution)/shard_map/ppermute | solution.py:572
  70.1 2.6 %collective-permute-start.27 = (bf16[64,1024]{1,0:T(8,128)(2,1)S(1)}, bf16[64,1024]{1,0:T(8,128)(2,1)S(1)}, u32[]{:S(2)}, u32[]{:S(2)}) collective-permute-start(bf16[64,1024]{1,0:T(8,128)(2,1)S(1)} %get-tuple-element.71), channel_id=1, source_target_pairs={{0,2},{1,3},{2,0},{3,1},{4,6},{5,7},{6,4},{7,5},{8,10},{9,11},{10,... | collective-permute-start | bytes 393224 | tf_op jit(solution)/shard_map/ppermute | solution.py:572
  72.7 2.5 %collective-permute-start.29 = (bf16[64,1024]{1,0:T(8,128)(2,1)S(1)}, bf16[64,1024]{1,0:T(8,128)(2,1)S(1)}, u32[]{:S(2)}, u32[]{:S(2)}) collective-permute-start(bf16[64,1024]{1,0:T(8,128)(2,1)S(1)} %get-tuple-element.73), channel_id=1, source_target_pairs={{0,4},{1,5},{2,6},{3,7},{4,0},{5,1},{6,2},{7,3},{8,12},{9,13},{10,... | collective-permute-start | bytes 393224 | tf_op jit(solution)/shard_map/ppermute | solution.py:572
  75.2 0.7 project.2.refs_2_
  75.9 2.2 %collective-permute-done.29.refs_5_ = bf16[64,1024]{1,0:T(8,128)(2,1)S(1)} collective-permute-done((bf16[64,1024]{1,0:T(8,128)(2,1)S(1)}, bf16[64,1024]{1,0:T(8,128)(2,1)S(1)}, u32[]{:S(2)}, u32[]{:S(2)}) %collective-permute-start.29) | collective-permute-done | bytes 131104 | tf_op jit(solution)/shard_map/ppermute | solution.py:572
  78.4 1.3 %collective-permute-done.30.refs_1_ = f32[128,256]{1,0:T(8,128)S(1)} collective-permute-done((f32[128,256]{1,0:T(8,128)S(1)}, f32[128,256]{1,0:T(8,128)S(1)}, u32[]{:S(2)}, u32[]{:S(2)}) %collective-permute-start.30) | collective-permute-done | bytes 131104 | tf_op jit(solution)/shard_map/ppermute | solution.py:572
  (56 shorter events, 7.8 us)
Async XLA Ops:
  4.8 2.2 %collective-permute-start = (bf16[1,128,1024]{2,1,0:T(8,128)(2,1)S(1)}, bf16[1,128,1024]{2,1,0:T(8,128)(2,1)S(1)}, u32[]{:S(2)}, u32[]{:S(2)}) collective-permute-start(bf16[1,128,1024]{2,1,0:T(8,128)(2,1)S(1)} %get-tuple-element.45), channel_id=1, source_target_pairs={{0,1},{1,0},{2,3},{3,2},{4,5},{5,4},{6,7},{7,6},{8,9},{9,8},{10,11... | collective-permute-start | bytes 786440 | tf_op jit(solution)/shard_map/ppermute | solution.py:572
  6.4 6.1 %collective-permute-start.2 = (bf16[1,128,1024]{2,1,0:T(8,128)(2,1)S(1)}, bf16[1,128,1024]{2,1,0:T(8,128)(2,1)S(1)}, u32[]{:S(2)}, u32[]{:S(2)}) collective-permute-start(bf16[1,128,1024]{2,1,0:T(8,128)(2,1)S(1)} %get-tuple-element.49), channel_id=1, source_target_pairs={{0,1},{1,0},{2,3},{3,2},{4,5},{5,4},{6,7},{7,6},{8,9},{9,8},{10,11... | collective-permute-start | bytes 786440 | tf_op jit(solution)/shard_map/ppermute | solution.py:572
  6.5 7.4 %collective-permute-start.3 = (bf16[1,128,1024]{2,1,0:T(8,128)(2,1)S(1)}, bf16[1,128,1024]{2,1,0:T(8,128)(2,1)S(1)}, u32[]{:S(2)}, u32[]{:S(2)}) collective-permute-start(bf16[1,128,1024]{2,1,0:T(8,128)(2,1)S(1)} %get-tuple-element.50), channel_id=1, source_target_pairs={{0,1},{1,0},{2,3},{3,2},{4,5},{5,4},{6,7},{7,6},{8,9},{9,8},{10,11... | collective-permute-start | bytes 786440 | tf_op jit(solution)/shard_map/ppermute | solution.py:572
  7.9 16.7 %collective-permute-start.9 = (bf16[2,128,1024]{2,1,0:T(8,128)(2,1)S(1)}, bf16[2,128,1024]{2,1,0:T(8,128)(2,1)S(1)}, u32[]{:S(2)}, u32[]{:S(2)}) collective-permute-start(bf16[2,128,1024]{2,1,0:T(8,128)(2,1)S(1)} %get-tuple-element.47.refs_0_), channel_id=1, source_target_pairs={{0,1},{1,0},{2,3},{3,2},{4,5},{5,4},{6,7},{7,6},{8,9},{9,8},{10,11... | collective-permute-start | bytes 1572872 | tf_op jit(solution)/shard_map/ppermute | solution.py:572
  8.0 6.7 %collective-permute-start.1 = (bf16[64,1024]{1,0:T(8,128)(2,1)S(1)}, bf16[64,1024]{1,0:T(8,128)(2,1)S(1)}, u32[]{:S(2)}, u32[]{:S(2)}) collective-permute-start(bf16[64,1024]{1,0:T(8,128)(2,1)S(1)} %get-tuple-element.46.refs_0_), channel_id=1, source_target_pairs={{0,2},{1,3},{2,0},{3,1},{4,6},{5,7},{6,4},{7,5},{8,10},{9,11},{10,... | collective-permute-start | bytes 393224 | tf_op jit(solution)/shard_map/ppermute | solution.py:572
  10.9 5.2 %collective-permute-start.4 = (bf16[64,1024]{1,0:T(8,128)(2,1)S(1)}, bf16[64,1024]{1,0:T(8,128)(2,1)S(1)}, u32[]{:S(2)}, u32[]{:S(2)}) collective-permute-start(bf16[64,1024]{1,0:T(8,128)(2,1)S(1)} %get-tuple-element.51), channel_id=1, source_target_pairs={{0,4},{1,5},{2,6},{3,7},{4,0},{5,1},{6,2},{7,3},{8,12},{9,13},{10,... | collective-permute-start | bytes 393224 | tf_op jit(solution)/shard_map/ppermute | solution.py:572
  12.5 6.0 %collective-permute-start.5 = (bf16[64,1024]{1,0:T(8,128)(2,1)S(1)}, bf16[64,1024]{1,0:T(8,128)(2,1)S(1)}, u32[]{:S(2)}, u32[]{:S(2)}) collective-permute-start(bf16[64,1024]{1,0:T(8,128)(2,1)S(1)} %get-tuple-element.51), channel_id=1, source_target_pairs={{0,1},{1,0},{2,3},{3,2},{4,8},{5,9},{6,10},{7,11},{8,4},{9,5},{10,... | collective-permute-start | bytes 393224 | tf_op jit(solution)/shard_map/ppermute | solution.py:572
  13.9 5.0 %collective-permute-start.8 = (bf16[1,128,1024]{2,1,0:T(8,128)(2,1)S(1)}, bf16[1,128,1024]{2,1,0:T(8,128)(2,1)S(1)}, u32[]{:S(2)}, u32[]{:S(2)}) collective-permute-start(bf16[1,128,1024]{2,1,0:T(8,128)(2,1)S(1)} %get-tuple-element.57), channel_id=1, source_target_pairs={{0,1},{1,0},{2,3},{3,2},{4,5},{5,4},{6,7},{7,6},{8,9},{9,8},{10,11... | collective-permute-start | bytes 786440 | tf_op jit(solution)/shard_map/ppermute | solution.py:572
  16.3 7.2 %collective-permute-start.6 = (bf16[128,1024]{1,0:T(8,128)(2,1)S(1)}, bf16[128,1024]{1,0:T(8,128)(2,1)S(1)}, u32[]{:S(2)}, u32[]{:S(2)}) collective-permute-start(bf16[128,1024]{1,0:T(8,128)(2,1)S(1)} %get-tuple-element.55), channel_id=1, source_target_pairs={{0,2},{1,3},{2,0},{3,1},{4,6},{5,7},{6,4},{7,5},{8,10},{9,11},{10,... | collective-permute-start | bytes 786440 | tf_op jit(solution)/shard_map/ppermute | solution.py:572
  16.7 7.8 %collective-permute-start.7 = (bf16[128,1024]{1,0:T(8,128)(2,1)S(1)}, bf16[128,1024]{1,0:T(8,128)(2,1)S(1)}, u32[]{:S(2)}, u32[]{:S(2)}) collective-permute-start(bf16[128,1024]{1,0:T(8,128)(2,1)S(1)} %get-tuple-element.52.refs_0_), channel_id=1, source_target_pairs={{0,4},{1,5},{2,6},{3,7},{4,0},{5,1},{6,2},{7,3},{8,12},{9,13},{10,... | collective-permute-start | bytes 786440 | tf_op jit(solution)/shard_map/ppermute | solution.py:572
  18.5 9.6 %collective-permute-start.13 = (bf16[2,128,1024]{2,1,0:T(8,128)(2,1)S(1)}, bf16[2,128,1024]{2,1,0:T(8,128)(2,1)S(1)}, u32[]{:S(2)}, u32[]{:S(2)}) collective-permute-start(bf16[2,128,1024]{2,1,0:T(8,128)(2,1)S(1)} %get-tuple-element.48.refs_1_), channel_id=1, source_target_pairs={{0,1},{1,0},{2,3},{3,2},{4,5},{5,4},{6,7},{7,6},{8,9},{9,8},{10,11... | collective-permute-start | bytes 1572872 | tf_op jit(solution)/shard_map/ppermute | solution.py:572
  24.8 7.0 %collective-permute-start.10 = (bf16[128,1024]{1,0:T(8,128)(2,1)S(1)}, bf16[128,1024]{1,0:T(8,128)(2,1)S(1)}, u32[]{:S(2)}, u32[]{:S(2)}) collective-permute-start(bf16[128,1024]{1,0:T(8,128)(2,1)S(1)} %get-tuple-element.59), channel_id=1, source_target_pairs={{0,2},{1,3},{2,0},{3,1},{4,6},{5,7},{6,4},{7,5},{8,10},{9,11},{10,... | collective-permute-start | bytes 786440 | tf_op jit(solution)/shard_map/ppermute | solution.py:572
  26.3 6.6 %collective-permute-start.11 = (bf16[128,1024]{1,0:T(8,128)(2,1)S(1)}, bf16[128,1024]{1,0:T(8,128)(2,1)S(1)}, u32[]{:S(2)}, u32[]{:S(2)}) collective-permute-start(bf16[128,1024]{1,0:T(8,128)(2,1)S(1)} %get-tuple-element.60), channel_id=1, source_target_pairs={{0,4},{1,5},{2,6},{3,7},{4,0},{5,1},{6,2},{7,3},{8,12},{9,13},{10,... | collective-permute-start | bytes 786440 | tf_op jit(solution)/shard_map/ppermute | solution.py:572
  28.1 4.9 %collective-permute-start.12 = (bf16[128,1024]{1,0:T(8,128)(2,1)S(1)}, bf16[128,1024]{1,0:T(8,128)(2,1)S(1)}, u32[]{:S(2)}, u32[]{:S(2)}) collective-permute-start(bf16[128,1024]{1,0:T(8,128)(2,1)S(1)} %get-tuple-element.60), channel_id=1, source_target_pairs={{0,1},{1,0},{2,3},{3,2},{4,8},{5,9},{6,10},{7,11},{8,4},{9,5},{10,... | collective-permute-start | bytes 786440 | tf_op jit(solution)/shard_map/ppermute | solution.py:572
  33.3 32.4 %copy-start.2 = (bf16[16384]{0:T(1024)(128)(2,1)S(1)}, bf16[16384]{0:T(1024)(128)(2,1)}, u32[]{:S(2)}) copy-start(bf16[16384]{0:T(1024)(128)(2,1)} %param.17) | copy-start | bytes 98308
  33.3 6.4 %collective-permute-start.14 = (bf16[128,1024]{1,0:T(8,128)(2,1)S(1)}, bf16[128,1024]{1,0:T(8,128)(2,1)S(1)}, u32[]{:S(2)}, u32[]{:S(2)}) collective-permute-start(bf16[128,1024]{1,0:T(8,128)(2,1)S(1)} %get-tuple-element.62), channel_id=1, source_target_pairs={{0,2},{1,3},{2,0},{3,1},{4,6},{5,7},{6,4},{7,5},{8,10},{9,11},{10,... | collective-permute-start | bytes 786440 | tf_op jit(solution)/shard_map/ppermute | solution.py:572
  34.0 6.4 %collective-permute-start.15 = (bf16[128,1024]{1,0:T(8,128)(2,1)S(1)}, bf16[128,1024]{1,0:T(8,128)(2,1)S(1)}, u32[]{:S(2)}, u32[]{:S(2)}) collective-permute-start(bf16[128,1024]{1,0:T(8,128)(2,1)S(1)} %get-tuple-element.63), channel_id=1, source_target_pairs={{0,4},{1,5},{2,6},{3,7},{4,0},{5,1},{6,2},{7,3},{8,12},{9,13},{10,... | collective-permute-start | bytes 786440 | tf_op jit(solution)/shard_map/ppermute | solution.py:572
  35.8 4.6 %collective-permute-start.16 = (bf16[128,1024]{1,0:T(8,128)(2,1)S(1)}, bf16[128,1024]{1,0:T(8,128)(2,1)S(1)}, u32[]{:S(2)}, u32[]{:S(2)}) collective-permute-start(bf16[128,1024]{1,0:T(8,128)(2,1)S(1)} %get-tuple-element.64), channel_id=1, source_target_pairs={{0,1},{1,0},{2,3},{3,2},{4,8},{5,9},{6,10},{7,11},{8,4},{9,5},{10,... | collective-permute-start | bytes 786440 | tf_op jit(solution)/shard_map/ppermute | solution.py:572
  35.8 30.0 %collective-permute-start.23 = (bf16[4,1024,128]{2,1,0:T(8,128)(2,1)S(1)}, bf16[4,1024,128]{2,1,0:T(8,128)(2,1)S(1)}, u32[]{:S(2)}, u32[]{:S(2)}) collective-permute-start(bf16[4,1024,128]{2,1,0:T(8,128)(2,1)S(1)} %get-tuple-element.54.refs_0_), channel_id=1, source_target_pairs={{0,1},{1,0},{2,3},{3,2},{4,5},{5,4},{6,7},{7,6},{8,9},{9,8},{10,11... | collective-permute-start | bytes 3145736 | tf_op jit(solution)/shard_map/ppermute | solution.py:572
  36.3 29.5 %collective-permute-start.24 = (bf16[4,1024,128]{2,1,0:T(8,128)(2,1)S(1)}, bf16[4,1024,128]{2,1,0:T(8,128)(2,1)S(1)}, u32[]{:S(2)}, u32[]{:S(2)}) collective-permute-start(bf16[4,1024,128]{2,1,0:T(8,128)(2,1)S(1)} %get-tuple-element.69), channel_id=1, source_target_pairs={{0,1},{1,0},{2,3},{3,2},{4,5},{5,4},{6,7},{7,6},{8,9},{9,8},{10,11... | collective-permute-start | bytes 3145736 | tf_op jit(solution)/shard_map/ppermute | solution.py:572
  40.7 6.4 %collective-permute-start.17 = (bf16[128,1024]{1,0:T(8,128)(2,1)S(1)}, bf16[128,1024]{1,0:T(8,128)(2,1)S(1)}, u32[]{:S(2)}, u32[]{:S(2)}) collective-permute-start(bf16[128,1024]{1,0:T(8,128)(2,1)S(1)} %regrid.1.refs_0_.refs_2_), channel_id=1, source_target_pairs={{0,2},{1,3},{2,0},{3,1},{4,6},{5,7},{6,4},{7,5},{8,10},{9,11},{10,... | collective-permute-start | bytes 786440 | tf_op jit(solution)/shard_map/ppermute | solution.py:572
  42.2 6.6 %collective-permute-start.18 = (bf16[128,1024]{1,0:T(8,128)(2,1)S(1)}, bf16[128,1024]{1,0:T(8,128)(2,1)S(1)}, u32[]{:S(2)}, u32[]{:S(2)}) collective-permute-start(bf16[128,1024]{1,0:T(8,128)(2,1)S(1)} %regrid.1.refs_0_.refs_2_), channel_id=1, source_target_pairs={{0,4},{1,5},{2,6},{3,7},{4,0},{5,1},{6,2},{7,3},{8,12},{9,13},{10,... | collective-permute-start | bytes 786440 | tf_op jit(solution)/shard_map/ppermute | solution.py:572
  44.4 4.8 %collective-permute-start.21 = (bf16[128,1024]{1,0:T(8,128)(2,1)S(1)}, bf16[128,1024]{1,0:T(8,128)(2,1)S(1)}, u32[]{:S(2)}, u32[]{:S(2)}) collective-permute-start(bf16[128,1024]{1,0:T(8,128)(2,1)S(1)} %regrid.1.refs_0_.refs_2_), channel_id=1, source_target_pairs={{0,1},{1,0},{2,3},{3,2},{4,8},{5,9},{6,10},{7,11},{8,4},{9,5},{10,... | collective-permute-start | bytes 786440 | tf_op jit(solution)/shard_map/ppermute | solution.py:572
  48.8 7.7 %collective-permute-start.19 = (bf16[128,1024]{1,0:T(8,128)(2,1)S(1)}, bf16[128,1024]{1,0:T(8,128)(2,1)S(1)}, u32[]{:S(2)}, u32[]{:S(2)}) collective-permute-start(bf16[128,1024]{1,0:T(8,128)(2,1)S(1)} %get-tuple-element.68.refs_3_), channel_id=1, source_target_pairs={{0,2},{1,3},{2,0},{3,1},{4,6},{5,7},{6,4},{7,5},{8,10},{9,11},{10,... | collective-permute-start | bytes 786440 | tf_op jit(solution)/shard_map/ppermute | solution.py:572
  49.2 7.2 %collective-permute-start.20 = (bf16[128,1024]{1,0:T(8,128)(2,1)S(1)}, bf16[128,1024]{1,0:T(8,128)(2,1)S(1)}, u32[]{:S(2)}, u32[]{:S(2)}) collective-permute-start(bf16[128,1024]{1,0:T(8,128)(2,1)S(1)} %get-tuple-element.68.refs_3_), channel_id=1, source_target_pairs={{0,1},{1,0},{2,3},{3,2},{4,8},{5,9},{6,10},{7,11},{8,4},{9,5},{10,... | collective-permute-start | bytes 786440 | tf_op jit(solution)/shard_map/ppermute | solution.py:572
  49.2 13.5 %collective-permute-start.22 = (bf16[128,1024]{1,0:T(8,128)(2,1)S(1)}, bf16[128,1024]{1,0:T(8,128)(2,1)S(1)}, u32[]{:S(2)}, u32[]{:S(2)}) collective-permute-start(bf16[128,1024]{1,0:T(8,128)(2,1)S(1)} %collective-permute-done.21.refs_2_), channel_id=1, source_target_pairs={{0,4},{1,5},{2,6},{3,7},{4,0},{5,1},{6,2},{7,3},{8,12},{9,13},{10,... | collective-permute-start | bytes 786440 | tf_op jit(solution)/shard_map/ppermute | solution.py:572
  62.8 6.4 %collective-permute-start.25 = (bf16[128,1024]{1,0:T(8,128)(2,1)S(1)}, bf16[128,1024]{1,0:T(8,128)(2,1)S(1)}, u32[]{:S(2)}, u32[]{:S(2)}) collective-permute-start(bf16[128,1024]{1,0:T(8,128)(2,1)S(1)} %choose.2.refs_0_.refs_4_), channel_id=1, source_target_pairs={{0,2},{1,3},{2,0},{3,1},{4,6},{5,7},{6,4},{7,5},{8,10},{9,11},{10,... | collective-permute-start | bytes 786440 | tf_op jit(solution)/shard_map/ppermute | solution.py:572
  63.2 6.8 %collective-permute-start.26 = (bf16[128,1024]{1,0:T(8,128)(2,1)S(1)}, bf16[128,1024]{1,0:T(8,128)(2,1)S(1)}, u32[]{:S(2)}, u32[]{:S(2)}) collective-permute-start(bf16[128,1024]{1,0:T(8,128)(2,1)S(1)} %choose.2.refs_0_.refs_4_), channel_id=1, source_target_pairs={{0,4},{1,5},{2,6},{3,7},{4,0},{5,1},{6,2},{7,3},{8,12},{9,13},{10,... | collective-permute-start | bytes 786440 | tf_op jit(solution)/shard_map/ppermute | solution.py:572
  65.7 10.2 %collective-permute-start.28 = (bf16[64,1024]{1,0:T(8,128)(2,1)S(1)}, bf16[64,1024]{1,0:T(8,128)(2,1)S(1)}, u32[]{:S(2)}, u32[]{:S(2)}) collective-permute-start(bf16[64,1024]{1,0:T(8,128)(2,1)S(1)} %get-tuple-element.72), channel_id=1, source_target_pairs={{0,1},{1,0},{2,3},{3,2},{4,8},{5,9},{6,10},{7,11},{8,4},{9,5},{10,... | collective-permute-start | bytes 393224 | tf_op jit(solution)/shard_map/ppermute | solution.py:572
  70.1 5.8 %collective-permute-start.27 = (bf16[64,1024]{1,0:T(8,128)(2,1)S(1)}, bf16[64,1024]{1,0:T(8,128)(2,1)S(1)}, u32[]{:S(2)}, u32[]{:S(2)}) collective-permute-start(bf16[64,1024]{1,0:T(8,128)(2,1)S(1)} %get-tuple-element.71), channel_id=1, source_target_pairs={{0,2},{1,3},{2,0},{3,1},{4,6},{5,7},{6,4},{7,5},{8,10},{9,11},{10,... | collective-permute-start | bytes 393224 | tf_op jit(solution)/shard_map/ppermute | solution.py:572
  72.7 5.4 %collective-permute-start.29 = (bf16[64,1024]{1,0:T(8,128)(2,1)S(1)}, bf16[64,1024]{1,0:T(8,128)(2,1)S(1)}, u32[]{:S(2)}, u32[]{:S(2)}) collective-permute-start(bf16[64,1024]{1,0:T(8,128)(2,1)S(1)} %get-tuple-element.73), channel_id=1, source_target_pairs={{0,4},{1,5},{2,6},{3,7},{4,0},{5,1},{6,2},{7,3},{8,12},{9,13},{10,... | collective-permute-start | bytes 393224 | tf_op jit(solution)/shard_map/ppermute | solution.py:572
  78.4 1.4 %collective-permute-start.30 = (f32[128,256]{1,0:T(8,128)S(1)}, f32[128,256]{1,0:T(8,128)S(1)}, u32[]{:S(2)}, u32[]{:S(2)}) collective-permute-start(f32[128,256]{1,0:T(8,128)S(1)} %get-tuple-element.75), channel_id=1, source_target_pairs={{0,1},{1,0},{2,3},{3,2},{4,5},{5,4},{6,7},{7,6},{8,9},{9,8},{10,11... | collective-permute-start | bytes 393224 | tf_op jit(solution)/shard_map/ppermute | solution.py:572
  (2 other events, 21.5 us)

commit v10 on v9

--- a/solution.py
+++ b/solution.py
@@ -369,7 +369,8 @@
 
 def choose_kernel(inner, count, *refs):
     inside = is_inner(place(inner)[0])
-    others, (inner_ref, end_ref, out_ref, *outs) = refs[:count], refs[count:]
+    inner_ref, end_ref, *refs = refs
+    others, (out_ref, *outs) = refs[:count], refs[count:]
     lower, upper = outs[:count], outs[count:]
 
     def put(ref):
@@ -395,7 +396,7 @@
     return kernel_call(
         functools.partial(choose_kernel, inner, len(others)),
         [jax.ShapeDtypeStruct((rows, cols), BF16)] + [half] * (len(others) + halved),
-        [*others, at_inner, at_end],
+        [at_inner, at_end, *others],
         [vmem()] * (2 + len(others)),
         after=after,
         name="choose",
@@ -701,13 +702,13 @@
     near = swap_pairs(grid)
     mid1 = swap_middle(grid)
     hidden_out, mark = hidden(inner, items, residual, factors, had, last, after=[grid])
-    near, *low1 = gate([near], x1, after=[mark])
+    near, mid1, *low1 = gate([near, mid1], x1, after=[mark])
     x2 = [shift_mid(near, s) for s in shifts]
     ends2 = swap_pairs(mid1)
     mids2 = swap_middle(near)
     (third,) = choose(inner, mids2, ends2, after=x2)
     x3 = [shift_mid(third, s) for s in shifts]
-    ends3 = swap_pairs(third)
+    ends3 = swap_pairs(mids2)
     side_middle = [swap_middle(low) for low in low1]
     turned_next = turn_next(inner, next_query_weight, next_other, gain, rows, had, after=[third])
     fourth, *low3, up4 = choose(inner, mid1, ends3, x3, True, after=[turned_next])

time: 80.6 us -> 78.1 us (0.969)
  waiting for transfers between devices: 32.4 us -> 28 us
  starting transfers between devices: 34.3 us -> 36.1 us
    ppermute x31, waiting for transfers between devices: 32.4 us -> 28 us  [permute(): return lax.ppermute(value, 'tp', moves)]
    ppermute x31, starting transfers between devices: 34.3 us -> 36.1 us  [permute(): return lax.ppermute(value, 'tp', moves)]
  transfers between devices with their start and end apart: 31 -> 31, of which waited for: 15 -> 15; matrix products, arithmetic and copies ran while one was open for 0% -> 0% of each run, Pallas kernels for 9% -> 10%
where the time goes in v10:
time: 78.1 us; the launch traced here: 78 us
  starting transfers between devices  36.1 us (46%)
  waiting for transfers between devices  28 us (36%)
  Pallas kernels  13 us (17%)
  between operations  0.85 us (1%)
    ppermute x31, starting transfers between devices, permute(): return lax.ppermute(value, 'tp', moves)  36.1 us
    ppermute x31, waiting for transfers between devices, permute(): return lax.ppermute(value, 'tp', moves)  28 us
    pallas_call x19, Pallas kernels, kernel_call(): pl.pallas_call(ordered, out_shape=out_shape, in_specs=[anywhere()] * extr...  13 us
  transfers between devices with their start and end apart: 31, of which 15 were waited for; matrix products, arithmetic and copies ran while one was open for 0% of the time, Pallas kernels for 10%

profile of v10, /device:TPU:0, one launch (start us, length us, event | category | flops | bytes accessed | tf_op | source)
XLA Modules:
  0.0 78.0 jit_solution(4979173437662045329)
XLA Ops:
  0.6 4.1 %attend.1 = (bf16[128,128]{1,0:T(8,128)(2,1)S(1)}, f32[2,128,128]{2,1,0:T(8,128)S(1)}, bf16[1,128,1024]{2,1,0:T(8,128)(2,1)S(1)}, bf16[128,16384]{1,0:T(8,128)(2,1)S(1)}, bf16[128,128]{1,0:T(8,128)(2,1)S(1)}) custom-call(bf16[1,128,128]{2,1,0:T(8,128)(2,1)} %refs_0_.1, bf16[1,8192,128]{2,1,0:T(8,128)(2,1)} %refs_1_.5, bf16[1,8192,128]{2,1,0:T(8,128)(2,1)} %refs_2_.1, ...), custom_call_target="tpu_custom_call" | custom-call | tf_op jit(solution)/shard_map/attend/pallas_call | solution.py:58
  5.3 1.1 %partials.3 = (bf16[1,128,1024]{2,1,0:T(8,128)(2,1)S(1)}, bf16[2,128,1024]{2,1,0:T(8,128)(2,1)S(1)}, bf16[1,128,1024]{2,1,0:T(8,128)(2,1)S(1)}, bf16[1,128,1024]{2,1,0:T(8,128)(2,1)S(1)}) custom-call(bf16[128,128]{1,0:T(8,128)(2,1)S(1)} %get-tuple-element.40.refs_0_.refs_1_, bf16[128,16384]{1,0:T(8,128)(2,1)S(1)} %get-tuple-element.41.refs_1_.refs_2_, ...), custom_call_target="tpu_custom_call" | custom-call | tf_op jit(solution)/shard_map/partials/pallas_call | solution.py:58
  7.0 0.8 %partials.4 = (bf16[1,128,1024]{2,1,0:T(8,128)(2,1)S(1)}, bf16[2,128,1024]{2,1,0:T(8,128)(2,1)S(1)}) custom-call(bf16[64,1024]{1,0:T(8,128)(2,1)S(1)} %get-tuple-element.47.refs_0_, bf16[128,128]{1,0:T(8,128)(2,1)S(1)} %get-tuple-element.40.refs_0_.refs_1_, bf16[128,16384]{1,0:T(8,128)(2,1)S(1)} %get-tuple-element.41.refs_1_.refs_2_, ...), custom_call_target="tpu_custom_call" | custom-call | tf_op jit(solution)/shard_map/partials/pallas_call | solution.py:58
  8.0 2.9 %collective-permute-start.1 = (bf16[64,1024]{1,0:T(8,128)(2,1)S(1)}, bf16[64,1024]{1,0:T(8,128)(2,1)S(1)}, u32[]{:S(2)}, u32[]{:S(2)}) collective-permute-start(bf16[64,1024]{1,0:T(8,128)(2,1)S(1)} %get-tuple-element.47.refs_0_), channel_id=1, source_target_pairs={{0,2},{1,3},{2,0},{3,1},{4,6},{5,7},{6,4},{7,5},{8,10},{9,11},{10,... | collective-permute-start | bytes 393224 | tf_op jit(solution)/shard_map/ppermute | solution.py:573
  10.9 1.6 %collective-permute-start.4 = (bf16[64,1024]{1,0:T(8,128)(2,1)S(1)}, bf16[64,1024]{1,0:T(8,128)(2,1)S(1)}, u32[]{:S(2)}, u32[]{:S(2)}) collective-permute-start(bf16[64,1024]{1,0:T(8,128)(2,1)S(1)} %get-tuple-element.52), channel_id=1, source_target_pairs={{0,4},{1,5},{2,6},{3,7},{4,0},{5,1},{6,2},{7,3},{8,12},{9,13},{10,... | collective-permute-start | bytes 393224 | tf_op jit(solution)/shard_map/ppermute | solution.py:573
  12.5 1.3 %partials.5 = (bf16[2,128,1024]{2,1,0:T(8,128)(2,1)S(1)}, bf16[1,128,1024]{2,1,0:T(8,128)(2,1)S(1)}, bf16[2,128,1024]{2,1,0:T(8,128)(2,1)S(1)}, bf16[2,128,1024]{2,1,0:T(8,128)(2,1)S(1)}) custom-call(bf16[2,128,1024]{2,1,0:T(8,128)(2,1)S(1)} %get-tuple-element.48.refs_0_, bf16[128,128]{1,0:T(8,128)(2,1)S(1)} %get-tuple-element.40.refs_0_.refs_1_, ...), custom_call_target="tpu_custom_call" | custom-call | tf_op jit(solution)/shard_map/partials/pallas_call | solution.py:58
  14.7 1.5 %collective-permute-done.4.refs_6_ = bf16[64,1024]{1,0:T(8,128)(2,1)S(1)} collective-permute-done((bf16[64,1024]{1,0:T(8,128)(2,1)S(1)}, bf16[64,1024]{1,0:T(8,128)(2,1)S(1)}, u32[]{:S(2)}, u32[]{:S(2)}) %collective-permute-start.4) | collective-permute-done | bytes 131104 | tf_op jit(solution)/shard_map/ppermute | solution.py:573
  16.7 1.7 %collective-permute-start.7 = (bf16[128,1024]{1,0:T(8,128)(2,1)S(1)}, bf16[128,1024]{1,0:T(8,128)(2,1)S(1)}, u32[]{:S(2)}, u32[]{:S(2)}) collective-permute-start(bf16[128,1024]{1,0:T(8,128)(2,1)S(1)} %get-tuple-element.53.refs_0_), channel_id=1, source_target_pairs={{0,4},{1,5},{2,6},{3,7},{4,0},{5,1},{6,2},{7,3},{8,12},{9,13},{10,... | collective-permute-start | bytes 786440 | tf_op jit(solution)/shard_map/ppermute | solution.py:573
  18.9 4.6 %collective-permute-done.6.refs_2_ = bf16[128,1024]{1,0:T(8,128)(2,1)S(1)} collective-permute-done((bf16[128,1024]{1,0:T(8,128)(2,1)S(1)}, bf16[128,1024]{1,0:T(8,128)(2,1)S(1)}, u32[]{:S(2)}, u32[]{:S(2)}) %collective-permute-start.6) | collective-permute-done | bytes 262176 | tf_op jit(solution)/shard_map/ppermute | solution.py:573
  23.5 1.1 %collective-permute-done.7.refs_3_ = bf16[128,1024]{1,0:T(8,128)(2,1)S(1)} collective-permute-done((bf16[128,1024]{1,0:T(8,128)(2,1)S(1)}, bf16[128,1024]{1,0:T(8,128)(2,1)S(1)}, u32[]{:S(2)}, u32[]{:S(2)}) %collective-permute-start.7) | collective-permute-done | bytes 262176 | tf_op jit(solution)/shard_map/ppermute | solution.py:573
  24.8 1.6 %collective-permute-start.10 = (bf16[128,1024]{1,0:T(8,128)(2,1)S(1)}, bf16[128,1024]{1,0:T(8,128)(2,1)S(1)}, u32[]{:S(2)}, u32[]{:S(2)}) collective-permute-start(bf16[128,1024]{1,0:T(8,128)(2,1)S(1)} %get-tuple-element.60), channel_id=1, source_target_pairs={{0,2},{1,3},{2,0},{3,1},{4,6},{5,7},{6,4},{7,5},{8,10},{9,11},{10,... | collective-permute-start | bytes 786440 | tf_op jit(solution)/shard_map/ppermute | solution.py:573
  26.3 1.7 %collective-permute-start.11 = (bf16[128,1024]{1,0:T(8,128)(2,1)S(1)}, bf16[128,1024]{1,0:T(8,128)(2,1)S(1)}, u32[]{:S(2)}, u32[]{:S(2)}) collective-permute-start(bf16[128,1024]{1,0:T(8,128)(2,1)S(1)} %get-tuple-element.61), channel_id=1, source_target_pairs={{0,4},{1,5},{2,6},{3,7},{4,0},{5,1},{6,2},{7,3},{8,12},{9,13},{10,... | collective-permute-start | bytes 786440 | tf_op jit(solution)/shard_map/ppermute | solution.py:573
  28.1 3.7 %collective-permute-done.10.refs_0_ = bf16[128,1024]{1,0:T(8,128)(2,1)S(1)} collective-permute-done((bf16[128,1024]{1,0:T(8,128)(2,1)S(1)}, bf16[128,1024]{1,0:T(8,128)(2,1)S(1)}, u32[]{:S(2)}, u32[]{:S(2)}) %collective-permute-start.10) | collective-permute-done | bytes 262176 | tf_op jit(solution)/shard_map/ppermute | solution.py:573
  31.8 1.2 %collective-permute-done.11.refs_1_ = bf16[128,1024]{1,0:T(8,128)(2,1)S(1)} collective-permute-done((bf16[128,1024]{1,0:T(8,128)(2,1)S(1)}, bf16[128,1024]{1,0:T(8,128)(2,1)S(1)}, u32[]{:S(2)}, u32[]{:S(2)}) %collective-permute-start.11) | collective-permute-done | bytes 262176 | tf_op jit(solution)/shard_map/ppermute | solution.py:573
  34.0 1.7 %collective-permute-start.15 = (bf16[128,1024]{1,0:T(8,128)(2,1)S(1)}, bf16[128,1024]{1,0:T(8,128)(2,1)S(1)}, u32[]{:S(2)}, u32[]{:S(2)}) collective-permute-start(bf16[128,1024]{1,0:T(8,128)(2,1)S(1)} %get-tuple-element.64), channel_id=1, source_target_pairs={{0,4},{1,5},{2,6},{3,7},{4,0},{5,1},{6,2},{7,3},{8,12},{9,13},{10,... | collective-permute-start | bytes 786440 | tf_op jit(solution)/shard_map/ppermute | solution.py:573
  36.3 3.5 %collective-permute-done.14.refs_0_.refs_4_ = bf16[128,1024]{1,0:T(8,128)(2,1)S(1)} collective-permute-done((bf16[128,1024]{1,0:T(8,128)(2,1)S(1)}, bf16[128,1024]{1,0:T(8,128)(2,1)S(1)}, u32[]{:S(2)}, u32[]{:S(2)}) %collective-permute-start.14) | collective-permute-done | bytes 262176 | tf_op jit(solution)/shard_map/ppermute | solution.py:573
  40.7 1.5 %collective-permute-start.17 = (bf16[128,1024]{1,0:T(8,128)(2,1)S(1)}, bf16[128,1024]{1,0:T(8,128)(2,1)S(1)}, u32[]{:S(2)}, u32[]{:S(2)}) collective-permute-start(bf16[128,1024]{1,0:T(8,128)(2,1)S(1)} %regrid.1.refs_0_.refs_2_), channel_id=1, source_target_pairs={{0,2},{1,3},{2,0},{3,1},{4,6},{5,7},{6,4},{7,5},{8,10},{9,11},{10,... | collective-permute-start | bytes 786440 | tf_op jit(solution)/shard_map/ppermute | solution.py:573
  42.2 2.3 %collective-permute-start.18 = (bf16[128,1024]{1,0:T(8,128)(2,1)S(1)}, bf16[128,1024]{1,0:T(8,128)(2,1)S(1)}, u32[]{:S(2)}, u32[]{:S(2)}) collective-permute-start(bf16[128,1024]{1,0:T(8,128)(2,1)S(1)} %regrid.1.refs_0_.refs_2_), channel_id=1, source_target_pairs={{0,4},{1,5},{2,6},{3,7},{4,0},{5,1},{6,2},{7,3},{8,12},{9,13},{10,... | collective-permute-start | bytes 786440 | tf_op jit(solution)/shard_map/ppermute | solution.py:573
  44.4 1.1 %hidden.1 = (bf16[128,1024]{1,0:T(8,128)(2,1)}, f32[8,128]{1,0:T(8,128)S(1)}) custom-call(bf16[128,1024]{1,0:T(8,128)(2,1)S(1)} %regrid.1.refs_0_.refs_2_, bf16[128,1024]{1,0:T(8,128)(2,1)S(1)} %copy-done.1, f32[2,1024]{1,0:T(2,128)S(1)} %get-tuple-element.54.refs_0_.refs_6_.refs_2_, bf16[128,128]{1,0:T(8,128)(2,1)S(1)} %get-tuple-element.43.refs_3_.refs_4_, ...), custom_call_target="tpu_custom_call" | custom-call | tf_op jit(solution)/shard_map/hidden/pallas_call | solution.py:58
  45.6 1.6 %collective-permute-done.17.refs_1_.refs_6_ = bf16[128,1024]{1,0:T(8,128)(2,1)S(1)} collective-permute-done((bf16[128,1024]{1,0:T(8,128)(2,1)S(1)}, bf16[128,1024]{1,0:T(8,128)(2,1)S(1)}, u32[]{:S(2)}, u32[]{:S(2)}) %collective-permute-start.17) | collective-permute-done | bytes 262176 | tf_op jit(solution)/shard_map/ppermute | solution.py:573
  47.1 1.7 %collective-permute-done.18.refs_2_ = bf16[128,1024]{1,0:T(8,128)(2,1)S(1)} collective-permute-done((bf16[128,1024]{1,0:T(8,128)(2,1)S(1)}, bf16[128,1024]{1,0:T(8,128)(2,1)S(1)}, u32[]{:S(2)}, u32[]{:S(2)}) %collective-permute-start.18) | collective-permute-done | bytes 262176 | tf_op jit(solution)/shard_map/ppermute | solution.py:573
  49.3 7.3 %collective-permute-start.22 = (bf16[128,1024]{1,0:T(8,128)(2,1)S(1)}, bf16[128,1024]{1,0:T(8,128)(2,1)S(1)}, u32[]{:S(2)}, u32[]{:S(2)}) collective-permute-start(bf16[128,1024]{1,0:T(8,128)(2,1)S(1)} %get-tuple-element.70.refs_1_), channel_id=1, source_target_pairs={{0,4},{1,5},{2,6},{3,7},{4,0},{5,1},{6,2},{7,3},{8,12},{9,13},{10,... | collective-permute-start | bytes 786440 | tf_op jit(solution)/shard_map/ppermute | solution.py:573
  56.7 4.5 %collective-permute-start.25 = (bf16[128,1024]{1,0:T(8,128)(2,1)S(1)}, bf16[128,1024]{1,0:T(8,128)(2,1)S(1)}, u32[]{:S(2)}, u32[]{:S(2)}) collective-permute-start(bf16[128,1024]{1,0:T(8,128)(2,1)S(1)} %collective-permute-done.21.refs_1_), channel_id=1, source_target_pairs={{0,4},{1,5},{2,6},{3,7},{4,0},{5,1},{6,2},{7,3},{8,12},{9,13},{10,... | collective-permute-start | bytes 786440 | tf_op jit(solution)/shard_map/ppermute | solution.py:573
  61.1 1.7 %collective-permute-start.26 = (bf16[128,1024]{1,0:T(8,128)(2,1)S(1)}, bf16[128,1024]{1,0:T(8,128)(2,1)S(1)}, u32[]{:S(2)}, u32[]{:S(2)}) collective-permute-start(bf16[128,1024]{1,0:T(8,128)(2,1)S(1)} %choose.2.refs_0_.refs_4_), channel_id=1, source_target_pairs={{0,2},{1,3},{2,0},{3,1},{4,6},{5,7},{6,4},{7,5},{8,10},{9,11},{10,... | collective-permute-start | bytes 786440 | tf_op jit(solution)/shard_map/ppermute | solution.py:573
  62.9 1.3 %turn_next.1.refs_0_ = bf16[8,1024,256]{2,1,0:T(8,128)(2,1)S(1)} custom-call(bf16[128,1024]{1,0:T(8,128)(2,1)S(1)} %choose.2.refs_0_.refs_4_, bf16[16384,128]{1,0:T(8,128)(2,1)S(1)} %copy-done, f32[128,128]{1,0:T(8,128)S(1)} %bitcast_convert_fusion.refs_2_, f32[2,128,128]{2,1,0:T(8,128)S(1)} %get-tuple-element.42.refs_2_.refs_3_.refs_1_, ...), custom_call_target="tpu_custom_call" | custom-call | tf_op jit(solution)/shard_map/turn_next/pallas_call | solution.py:58
  64.2 1.3 %collective-permute-done.25.refs_2_ = bf16[128,1024]{1,0:T(8,128)(2,1)S(1)} collective-permute-done((bf16[128,1024]{1,0:T(8,128)(2,1)S(1)}, bf16[128,1024]{1,0:T(8,128)(2,1)S(1)}, u32[]{:S(2)}, u32[]{:S(2)}) %collective-permute-start.25) | collective-permute-done | bytes 262176 | tf_op jit(solution)/shard_map/ppermute | solution.py:573
  65.5 2.5 %collective-permute-done.26.refs_3_.refs_8_ = bf16[128,1024]{1,0:T(8,128)(2,1)S(1)} collective-permute-done((bf16[128,1024]{1,0:T(8,128)(2,1)S(1)}, bf16[128,1024]{1,0:T(8,128)(2,1)S(1)}, u32[]{:S(2)}, u32[]{:S(2)}) %collective-permute-start.26) | collective-permute-done | bytes 262176 | tf_op jit(solution)/shard_map/ppermute | solution.py:573
  68.0 2.5 %collective-permute-start.27 = (bf16[64,1024]{1,0:T(8,128)(2,1)S(1)}, bf16[64,1024]{1,0:T(8,128)(2,1)S(1)}, u32[]{:S(2)}, u32[]{:S(2)}) collective-permute-start(bf16[64,1024]{1,0:T(8,128)(2,1)S(1)} %get-tuple-element.73), channel_id=1, source_target_pairs={{0,2},{1,3},{2,0},{3,1},{4,6},{5,7},{6,4},{7,5},{8,10},{9,11},{10,... | collective-permute-start | bytes 393224 | tf_op jit(solution)/shard_map/ppermute | solution.py:573
  70.6 0.9 %collective-permute-start.29 = (bf16[64,1024]{1,0:T(8,128)(2,1)S(1)}, bf16[64,1024]{1,0:T(8,128)(2,1)S(1)}, u32[]{:S(2)}, u32[]{:S(2)}) collective-permute-start(bf16[64,1024]{1,0:T(8,128)(2,1)S(1)} %get-tuple-element.75), channel_id=1, source_target_pairs={{0,4},{1,5},{2,6},{3,7},{4,0},{5,1},{6,2},{7,3},{8,12},{9,13},{10,... | collective-permute-start | bytes 393224 | tf_op jit(solution)/shard_map/ppermute | solution.py:573
  72.3 1.2 %collective-permute-done.27.refs_3_ = bf16[64,1024]{1,0:T(8,128)(2,1)S(1)} collective-permute-done((bf16[64,1024]{1,0:T(8,128)(2,1)S(1)}, bf16[64,1024]{1,0:T(8,128)(2,1)S(1)}, u32[]{:S(2)}, u32[]{:S(2)}) %collective-permute-start.27) | collective-permute-done | bytes 131104 | tf_op jit(solution)/shard_map/ppermute | solution.py:573
  73.5 2.0 %collective-permute-done.29.refs_5_ = bf16[64,1024]{1,0:T(8,128)(2,1)S(1)} collective-permute-done((bf16[64,1024]{1,0:T(8,128)(2,1)S(1)}, bf16[64,1024]{1,0:T(8,128)(2,1)S(1)}, u32[]{:S(2)}, u32[]{:S(2)}) %collective-permute-start.29) | collective-permute-done | bytes 131104 | tf_op jit(solution)/shard_map/ppermute | solution.py:573
  75.9 1.3 %collective-permute-done.30.refs_1_ = f32[128,256]{1,0:T(8,128)S(1)} collective-permute-done((f32[128,256]{1,0:T(8,128)S(1)}, f32[128,256]{1,0:T(8,128)S(1)}, u32[]{:S(2)}, u32[]{:S(2)}) %collective-permute-start.30) | collective-permute-done | bytes 131104 | tf_op jit(solution)/shard_map/ppermute | solution.py:573
  (56 shorter events, 8.2 us)
Async XLA Ops:
  4.8 2.2 %collective-permute-start = (bf16[1,128,1024]{2,1,0:T(8,128)(2,1)S(1)}, bf16[1,128,1024]{2,1,0:T(8,128)(2,1)S(1)}, u32[]{:S(2)}, u32[]{:S(2)}) collective-permute-start(bf16[1,128,1024]{2,1,0:T(8,128)(2,1)S(1)} %get-tuple-element.46), channel_id=1, source_target_pairs={{0,1},{1,0},{2,3},{3,2},{4,5},{5,4},{6,7},{7,6},{8,9},{9,8},{10,11... | collective-permute-start | bytes 786440 | tf_op jit(solution)/shard_map/ppermute | solution.py:573
  6.4 6.1 %collective-permute-start.2 = (bf16[1,128,1024]{2,1,0:T(8,128)(2,1)S(1)}, bf16[1,128,1024]{2,1,0:T(8,128)(2,1)S(1)}, u32[]{:S(2)}, u32[]{:S(2)}) collective-permute-start(bf16[1,128,1024]{2,1,0:T(8,128)(2,1)S(1)} %get-tuple-element.50), channel_id=1, source_target_pairs={{0,1},{1,0},{2,3},{3,2},{4,5},{5,4},{6,7},{7,6},{8,9},{9,8},{10,11... | collective-permute-start | bytes 786440 | tf_op jit(solution)/shard_map/ppermute | solution.py:573
  6.5 7.4 %collective-permute-start.3 = (bf16[1,128,1024]{2,1,0:T(8,128)(2,1)S(1)}, bf16[1,128,1024]{2,1,0:T(8,128)(2,1)S(1)}, u32[]{:S(2)}, u32[]{:S(2)}) collective-permute-start(bf16[1,128,1024]{2,1,0:T(8,128)(2,1)S(1)} %get-tuple-element.51), channel_id=1, source_target_pairs={{0,1},{1,0},{2,3},{3,2},{4,5},{5,4},{6,7},{7,6},{8,9},{9,8},{10,11... | collective-permute-start | bytes 786440 | tf_op jit(solution)/shard_map/ppermute | solution.py:573
  7.9 16.7 %collective-permute-start.9 = (bf16[2,128,1024]{2,1,0:T(8,128)(2,1)S(1)}, bf16[2,128,1024]{2,1,0:T(8,128)(2,1)S(1)}, u32[]{:S(2)}, u32[]{:S(2)}) collective-permute-start(bf16[2,128,1024]{2,1,0:T(8,128)(2,1)S(1)} %get-tuple-element.48.refs_0_), channel_id=1, source_target_pairs={{0,1},{1,0},{2,3},{3,2},{4,5},{5,4},{6,7},{7,6},{8,9},{9,8},{10,11... | collective-permute-start | bytes 1572872 | tf_op jit(solution)/shard_map/ppermute | solution.py:573
  8.0 6.7 %collective-permute-start.1 = (bf16[64,1024]{1,0:T(8,128)(2,1)S(1)}, bf16[64,1024]{1,0:T(8,128)(2,1)S(1)}, u32[]{:S(2)}, u32[]{:S(2)}) collective-permute-start(bf16[64,1024]{1,0:T(8,128)(2,1)S(1)} %get-tuple-element.47.refs_0_), channel_id=1, source_target_pairs={{0,2},{1,3},{2,0},{3,1},{4,6},{5,7},{6,4},{7,5},{8,10},{9,11},{10,... | collective-permute-start | bytes 393224 | tf_op jit(solution)/shard_map/ppermute | solution.py:573
  10.9 5.2 %collective-permute-start.4 = (bf16[64,1024]{1,0:T(8,128)(2,1)S(1)}, bf16[64,1024]{1,0:T(8,128)(2,1)S(1)}, u32[]{:S(2)}, u32[]{:S(2)}) collective-permute-start(bf16[64,1024]{1,0:T(8,128)(2,1)S(1)} %get-tuple-element.52), channel_id=1, source_target_pairs={{0,4},{1,5},{2,6},{3,7},{4,0},{5,1},{6,2},{7,3},{8,12},{9,13},{10,... | collective-permute-start | bytes 393224 | tf_op jit(solution)/shard_map/ppermute | solution.py:573
  12.5 6.0 %collective-permute-start.5 = (bf16[64,1024]{1,0:T(8,128)(2,1)S(1)}, bf16[64,1024]{1,0:T(8,128)(2,1)S(1)}, u32[]{:S(2)}, u32[]{:S(2)}) collective-permute-start(bf16[64,1024]{1,0:T(8,128)(2,1)S(1)} %get-tuple-element.52), channel_id=1, source_target_pairs={{0,1},{1,0},{2,3},{3,2},{4,8},{5,9},{6,10},{7,11},{8,4},{9,5},{10,... | collective-permute-start | bytes 393224 | tf_op jit(solution)/shard_map/ppermute | solution.py:573
  13.9 5.0 %collective-permute-start.8 = (bf16[1,128,1024]{2,1,0:T(8,128)(2,1)S(1)}, bf16[1,128,1024]{2,1,0:T(8,128)(2,1)S(1)}, u32[]{:S(2)}, u32[]{:S(2)}) collective-permute-start(bf16[1,128,1024]{2,1,0:T(8,128)(2,1)S(1)} %get-tuple-element.58), channel_id=1, source_target_pairs={{0,1},{1,0},{2,3},{3,2},{4,5},{5,4},{6,7},{7,6},{8,9},{9,8},{10,11... | collective-permute-start | bytes 786440 | tf_op jit(solution)/shard_map/ppermute | solution.py:573
  16.3 7.2 %collective-permute-start.6 = (bf16[128,1024]{1,0:T(8,128)(2,1)S(1)}, bf16[128,1024]{1,0:T(8,128)(2,1)S(1)}, u32[]{:S(2)}, u32[]{:S(2)}) collective-permute-start(bf16[128,1024]{1,0:T(8,128)(2,1)S(1)} %get-tuple-element.56), channel_id=1, source_target_pairs={{0,2},{1,3},{2,0},{3,1},{4,6},{5,7},{6,4},{7,5},{8,10},{9,11},{10,... | collective-permute-start | bytes 786440 | tf_op jit(solution)/shard_map/ppermute | solution.py:573
  16.7 7.8 %collective-permute-start.7 = (bf16[128,1024]{1,0:T(8,128)(2,1)S(1)}, bf16[128,1024]{1,0:T(8,128)(2,1)S(1)}, u32[]{:S(2)}, u32[]{:S(2)}) collective-permute-start(bf16[128,1024]{1,0:T(8,128)(2,1)S(1)} %get-tuple-element.53.refs_0_), channel_id=1, source_target_pairs={{0,4},{1,5},{2,6},{3,7},{4,0},{5,1},{6,2},{7,3},{8,12},{9,13},{10,... | collective-permute-start | bytes 786440 | tf_op jit(solution)/shard_map/ppermute | solution.py:573
  18.5 9.6 %collective-permute-start.13 = (bf16[2,128,1024]{2,1,0:T(8,128)(2,1)S(1)}, bf16[2,128,1024]{2,1,0:T(8,128)(2,1)S(1)}, u32[]{:S(2)}, u32[]{:S(2)}) collective-permute-start(bf16[2,128,1024]{2,1,0:T(8,128)(2,1)S(1)} %get-tuple-element.49.refs_1_), channel_id=1, source_target_pairs={{0,1},{1,0},{2,3},{3,2},{4,5},{5,4},{6,7},{7,6},{8,9},{9,8},{10,11... | collective-permute-start | bytes 1572872 | tf_op jit(solution)/shard_map/ppermute | solution.py:573
  24.8 7.0 %collective-permute-start.10 = (bf16[128,1024]{1,0:T(8,128)(2,1)S(1)}, bf16[128,1024]{1,0:T(8,128)(2,1)S(1)}, u32[]{:S(2)}, u32[]{:S(2)}) collective-permute-start(bf16[128,1024]{1,0:T(8,128)(2,1)S(1)} %get-tuple-element.60), channel_id=1, source_target_pairs={{0,2},{1,3},{2,0},{3,1},{4,6},{5,7},{6,4},{7,5},{8,10},{9,11},{10,... | collective-permute-start | bytes 786440 | tf_op jit(solution)/shard_map/ppermute | solution.py:573
  26.3 6.6 %collective-permute-start.11 = (bf16[128,1024]{1,0:T(8,128)(2,1)S(1)}, bf16[128,1024]{1,0:T(8,128)(2,1)S(1)}, u32[]{:S(2)}, u32[]{:S(2)}) collective-permute-start(bf16[128,1024]{1,0:T(8,128)(2,1)S(1)} %get-tuple-element.61), channel_id=1, source_target_pairs={{0,4},{1,5},{2,6},{3,7},{4,0},{5,1},{6,2},{7,3},{8,12},{9,13},{10,... | collective-permute-start | bytes 786440 | tf_op jit(solution)/shard_map/ppermute | solution.py:573
  28.1 4.9 %collective-permute-start.12 = (bf16[128,1024]{1,0:T(8,128)(2,1)S(1)}, bf16[128,1024]{1,0:T(8,128)(2,1)S(1)}, u32[]{:S(2)}, u32[]{:S(2)}) collective-permute-start(bf16[128,1024]{1,0:T(8,128)(2,1)S(1)} %get-tuple-element.61), channel_id=1, source_target_pairs={{0,1},{1,0},{2,3},{3,2},{4,8},{5,9},{6,10},{7,11},{8,4},{9,5},{10,... | collective-permute-start | bytes 786440 | tf_op jit(solution)/shard_map/ppermute | solution.py:573
  33.3 29.5 %copy-start.2 = (bf16[16384]{0:T(1024)(128)(2,1)S(1)}, bf16[16384]{0:T(1024)(128)(2,1)}, u32[]{:S(2)}) copy-start(bf16[16384]{0:T(1024)(128)(2,1)} %param.17) | copy-start | bytes 98308
  33.3 6.4 %collective-permute-start.14 = (bf16[128,1024]{1,0:T(8,128)(2,1)S(1)}, bf16[128,1024]{1,0:T(8,128)(2,1)S(1)}, u32[]{:S(2)}, u32[]{:S(2)}) collective-permute-start(bf16[128,1024]{1,0:T(8,128)(2,1)S(1)} %get-tuple-element.63), channel_id=1, source_target_pairs={{0,2},{1,3},{2,0},{3,1},{4,6},{5,7},{6,4},{7,5},{8,10},{9,11},{10,... | collective-permute-start | bytes 786440 | tf_op jit(solution)/shard_map/ppermute | solution.py:573
  34.0 6.4 %collective-permute-start.15 = (bf16[128,1024]{1,0:T(8,128)(2,1)S(1)}, bf16[128,1024]{1,0:T(8,128)(2,1)S(1)}, u32[]{:S(2)}, u32[]{:S(2)}) collective-permute-start(bf16[128,1024]{1,0:T(8,128)(2,1)S(1)} %get-tuple-element.64), channel_id=1, source_target_pairs={{0,4},{1,5},{2,6},{3,7},{4,0},{5,1},{6,2},{7,3},{8,12},{9,13},{10,... | collective-permute-start | bytes 786440 | tf_op jit(solution)/shard_map/ppermute | solution.py:573
  35.8 4.6 %collective-permute-start.16 = (bf16[128,1024]{1,0:T(8,128)(2,1)S(1)}, bf16[128,1024]{1,0:T(8,128)(2,1)S(1)}, u32[]{:S(2)}, u32[]{:S(2)}) collective-permute-start(bf16[128,1024]{1,0:T(8,128)(2,1)S(1)} %get-tuple-element.65), channel_id=1, source_target_pairs={{0,1},{1,0},{2,3},{3,2},{4,8},{5,9},{6,10},{7,11},{8,4},{9,5},{10,... | collective-permute-start | bytes 786440 | tf_op jit(solution)/shard_map/ppermute | solution.py:573
  35.8 27.2 %collective-permute-start.23 = (bf16[4,1024,128]{2,1,0:T(8,128)(2,1)S(1)}, bf16[4,1024,128]{2,1,0:T(8,128)(2,1)S(1)}, u32[]{:S(2)}, u32[]{:S(2)}) collective-permute-start(bf16[4,1024,128]{2,1,0:T(8,128)(2,1)S(1)} %get-tuple-element.55.refs_0_), channel_id=1, source_target_pairs={{0,1},{1,0},{2,3},{3,2},{4,5},{5,4},{6,7},{7,6},{8,9},{9,8},{10,11... | collective-permute-start | bytes 3145736 | tf_op jit(solution)/shard_map/ppermute | solution.py:573
  36.3 26.7 %collective-permute-start.24 = (bf16[4,1024,128]{2,1,0:T(8,128)(2,1)S(1)}, bf16[4,1024,128]{2,1,0:T(8,128)(2,1)S(1)}, u32[]{:S(2)}, u32[]{:S(2)}) collective-permute-start(bf16[4,1024,128]{2,1,0:T(8,128)(2,1)S(1)} %get-tuple-element.71), channel_id=1, source_target_pairs={{0,1},{1,0},{2,3},{3,2},{4,5},{5,4},{6,7},{7,6},{8,9},{9,8},{10,11... | collective-permute-start | bytes 3145736 | tf_op jit(solution)/shard_map/ppermute | solution.py:573
  40.7 6.4 %collective-permute-start.17 = (bf16[128,1024]{1,0:T(8,128)(2,1)S(1)}, bf16[128,1024]{1,0:T(8,128)(2,1)S(1)}, u32[]{:S(2)}, u32[]{:S(2)}) collective-permute-start(bf16[128,1024]{1,0:T(8,128)(2,1)S(1)} %regrid.1.refs_0_.refs_2_), channel_id=1, source_target_pairs={{0,2},{1,3},{2,0},{3,1},{4,6},{5,7},{6,4},{7,5},{8,10},{9,11},{10,... | collective-permute-start | bytes 786440 | tf_op jit(solution)/shard_map/ppermute | solution.py:573
  42.2 6.6 %collective-permute-start.18 = (bf16[128,1024]{1,0:T(8,128)(2,1)S(1)}, bf16[128,1024]{1,0:T(8,128)(2,1)S(1)}, u32[]{:S(2)}, u32[]{:S(2)}) collective-permute-start(bf16[128,1024]{1,0:T(8,128)(2,1)S(1)} %regrid.1.refs_0_.refs_2_), channel_id=1, source_target_pairs={{0,4},{1,5},{2,6},{3,7},{4,0},{5,1},{6,2},{7,3},{8,12},{9,13},{10,... | collective-permute-start | bytes 786440 | tf_op jit(solution)/shard_map/ppermute | solution.py:573
  44.4 4.4 %collective-permute-start.19 = (bf16[128,1024]{1,0:T(8,128)(2,1)S(1)}, bf16[128,1024]{1,0:T(8,128)(2,1)S(1)}, u32[]{:S(2)}, u32[]{:S(2)}) collective-permute-start(bf16[128,1024]{1,0:T(8,128)(2,1)S(1)} %regrid.1.refs_0_.refs_2_), channel_id=1, source_target_pairs={{0,1},{1,0},{2,3},{3,2},{4,8},{5,9},{6,10},{7,11},{8,4},{9,5},{10,... | collective-permute-start | bytes 786440 | tf_op jit(solution)/shard_map/ppermute | solution.py:573
  48.8 7.9 %collective-permute-start.21 = (bf16[128,1024]{1,0:T(8,128)(2,1)S(1)}, bf16[128,1024]{1,0:T(8,128)(2,1)S(1)}, u32[]{:S(2)}, u32[]{:S(2)}) collective-permute-start(bf16[128,1024]{1,0:T(8,128)(2,1)S(1)} %get-tuple-element.69.refs_3_), channel_id=1, source_target_pairs={{0,1},{1,0},{2,3},{3,2},{4,8},{5,9},{6,10},{7,11},{8,4},{9,5},{10,... | collective-permute-start | bytes 786440 | tf_op jit(solution)/shard_map/ppermute | solution.py:573
  48.9 12.2 %collective-permute-start.20 = (bf16[128,1024]{1,0:T(8,128)(2,1)S(1)}, bf16[128,1024]{1,0:T(8,128)(2,1)S(1)}, u32[]{:S(2)}, u32[]{:S(2)}) collective-permute-start(bf16[128,1024]{1,0:T(8,128)(2,1)S(1)} %get-tuple-element.69.refs_3_), channel_id=1, source_target_pairs={{0,2},{1,3},{2,0},{3,1},{4,6},{5,7},{6,4},{7,5},{8,10},{9,11},{10,... | collective-permute-start | bytes 786440 | tf_op jit(solution)/shard_map/ppermute | solution.py:573
  49.3 11.8 %collective-permute-start.22 = (bf16[128,1024]{1,0:T(8,128)(2,1)S(1)}, bf16[128,1024]{1,0:T(8,128)(2,1)S(1)}, u32[]{:S(2)}, u32[]{:S(2)}) collective-permute-start(bf16[128,1024]{1,0:T(8,128)(2,1)S(1)} %get-tuple-element.70.refs_1_), channel_id=1, source_target_pairs={{0,4},{1,5},{2,6},{3,7},{4,0},{5,1},{6,2},{7,3},{8,12},{9,13},{10,... | collective-permute-start | bytes 786440 | tf_op jit(solution)/shard_map/ppermute | solution.py:573
  56.7 8.8 %collective-permute-start.25 = (bf16[128,1024]{1,0:T(8,128)(2,1)S(1)}, bf16[128,1024]{1,0:T(8,128)(2,1)S(1)}, u32[]{:S(2)}, u32[]{:S(2)}) collective-permute-start(bf16[128,1024]{1,0:T(8,128)(2,1)S(1)} %collective-permute-done.21.refs_1_), channel_id=1, source_target_pairs={{0,4},{1,5},{2,6},{3,7},{4,0},{5,1},{6,2},{7,3},{8,12},{9,13},{10,... | collective-permute-start | bytes 786440 | tf_op jit(solution)/shard_map/ppermute | solution.py:573
  61.1 6.9 %collective-permute-start.26 = (bf16[128,1024]{1,0:T(8,128)(2,1)S(1)}, bf16[128,1024]{1,0:T(8,128)(2,1)S(1)}, u32[]{:S(2)}, u32[]{:S(2)}) collective-permute-start(bf16[128,1024]{1,0:T(8,128)(2,1)S(1)} %choose.2.refs_0_.refs_4_), channel_id=1, source_target_pairs={{0,2},{1,3},{2,0},{3,1},{4,6},{5,7},{6,4},{7,5},{8,10},{9,11},{10,... | collective-permute-start | bytes 786440 | tf_op jit(solution)/shard_map/ppermute | solution.py:573
  62.8 9.5 %collective-permute-start.28 = (bf16[64,1024]{1,0:T(8,128)(2,1)S(1)}, bf16[64,1024]{1,0:T(8,128)(2,1)S(1)}, u32[]{:S(2)}, u32[]{:S(2)}) collective-permute-start(bf16[64,1024]{1,0:T(8,128)(2,1)S(1)} %get-tuple-element.74), channel_id=1, source_target_pairs={{0,1},{1,0},{2,3},{3,2},{4,8},{5,9},{6,10},{7,11},{8,4},{9,5},{10,... | collective-permute-start | bytes 393224 | tf_op jit(solution)/shard_map/ppermute | solution.py:573
  68.0 5.5 %collective-permute-start.27 = (bf16[64,1024]{1,0:T(8,128)(2,1)S(1)}, bf16[64,1024]{1,0:T(8,128)(2,1)S(1)}, u32[]{:S(2)}, u32[]{:S(2)}) collective-permute-start(bf16[64,1024]{1,0:T(8,128)(2,1)S(1)} %get-tuple-element.73), channel_id=1, source_target_pairs={{0,2},{1,3},{2,0},{3,1},{4,6},{5,7},{6,4},{7,5},{8,10},{9,11},{10,... | collective-permute-start | bytes 393224 | tf_op jit(solution)/shard_map/ppermute | solution.py:573
  70.6 5.0 %collective-permute-start.29 = (bf16[64,1024]{1,0:T(8,128)(2,1)S(1)}, bf16[64,1024]{1,0:T(8,128)(2,1)S(1)}, u32[]{:S(2)}, u32[]{:S(2)}) collective-permute-start(bf16[64,1024]{1,0:T(8,128)(2,1)S(1)} %get-tuple-element.75), channel_id=1, source_target_pairs={{0,4},{1,5},{2,6},{3,7},{4,0},{5,1},{6,2},{7,3},{8,12},{9,13},{10,... | collective-permute-start | bytes 393224 | tf_op jit(solution)/shard_map/ppermute | solution.py:573
  75.8 1.4 %collective-permute-start.30 = (f32[128,256]{1,0:T(8,128)S(1)}, f32[128,256]{1,0:T(8,128)S(1)}, u32[]{:S(2)}, u32[]{:S(2)}) collective-permute-start(f32[128,256]{1,0:T(8,128)S(1)} %get-tuple-element.77), channel_id=1, source_target_pairs={{0,1},{1,0},{2,3},{3,2},{4,5},{5,4},{6,7},{7,6},{8,9},{9,8},{10,11... | collective-permute-start | bytes 393224 | tf_op jit(solution)/shard_map/ppermute | solution.py:573
  (2 other events, 21.5 us)

commit v11 on v10

--- a/solution.py
+++ b/solution.py
@@ -403,8 +403,8 @@
     )
 
 
-def gate_kernel(count, *refs):
-    for ref, half in zip(refs[:count], refs[-count:]):
+def gate_kernel(skip, count, *refs):
+    for ref, half in zip(refs[skip : skip + count], refs[-count:]):
         half[...] = ref[half.shape[0] :]
 
 
@@ -412,11 +412,11 @@
     rows, cols = arrays[0].shape
     shapes = [jax.ShapeDtypeStruct((rows, cols), BF16)] * len(arrays)
     half = jax.ShapeDtypeStruct((rows // 2, cols), BF16)
-    aliases = {len(after) + len(others) + i: i for i in range(len(arrays))}
-    return kernel_call(
-        functools.partial(gate_kernel, len(others)),
+    aliases = {len(after) + i: i for i in range(len(arrays))}
+    return kernel_call(
+        functools.partial(gate_kernel, len(arrays), len(others)),
         shapes + [half] * len(others),
-        [*others, *arrays],
+        [*arrays, *others],
         [vmem()] * (len(others) + len(arrays)),
         after=after,
         aliases=aliases,

time: 78.1 us -> 79.6 us (1.019)
  waiting for transfers between devices: 28 us -> 36.2 us
  starting transfers between devices: 36.1 us -> 29.3 us
    ppermute x31, waiting for transfers between devices: 28 us -> 36.2 us  [permute(): return lax.ppermute(value, 'tp', moves)]
    ppermute x31, starting transfers between devices: 36.1 us -> 29.3 us  [permute(): return lax.ppermute(value, 'tp', moves)]
  transfers between devices with their start and end apart: 31 -> 31, of which waited for: 15 -> 16; matrix products, arithmetic and copies ran while one was open for 0% -> 0% of each run, Pallas kernels for 10% -> 9%
where the time goes in v11:
time: 79.6 us; the launch traced here: 79.4 us
  waiting for transfers between devices  36.2 us (45%)
  starting transfers between devices  29.3 us (37%)
  Pallas kernels  13 us (16%)
  between operations  0.86 us (1%)
    ppermute x31, waiting for transfers between devices, permute(): return lax.ppermute(value, 'tp', moves)  36.2 us
    ppermute x31, starting transfers between devices, permute(): return lax.ppermute(value, 'tp', moves)  29.3 us
    pallas_call x19, Pallas kernels, kernel_call(): pl.pallas_call(ordered, out_shape=out_shape, in_specs=[anywhere()] * extr...  13 us
  transfers between devices with their start and end apart: 31, of which 16 were waited for; matrix products, arithmetic and copies ran while one was open for 0% of the time, Pallas kernels for 9%

profile of v11, /device:TPU:0, one launch (start us, length us, event | category | flops | bytes accessed | tf_op | source)
XLA Modules:
  0.0 79.4 jit_solution(11999176813750634082)
XLA Ops:
  0.6 4.1 %attend.1 = (bf16[128,128]{1,0:T(8,128)(2,1)S(1)}, f32[2,128,128]{2,1,0:T(8,128)S(1)}, bf16[1,128,1024]{2,1,0:T(8,128)(2,1)S(1)}, bf16[128,16384]{1,0:T(8,128)(2,1)S(1)}, bf16[128,128]{1,0:T(8,128)(2,1)S(1)}) custom-call(bf16[1,128,128]{2,1,0:T(8,128)(2,1)} %refs_0_.1, bf16[1,8192,128]{2,1,0:T(8,128)(2,1)} %refs_1_.5, bf16[1,8192,128]{2,1,0:T(8,128)(2,1)} %refs_2_.1, ...), custom_call_target="tpu_custom_call" | custom-call | tf_op jit(solution)/shard_map/attend/pallas_call | solution.py:58
  5.3 1.1 %partials.3 = (bf16[1,128,1024]{2,1,0:T(8,128)(2,1)S(1)}, bf16[2,128,1024]{2,1,0:T(8,128)(2,1)S(1)}, bf16[1,128,1024]{2,1,0:T(8,128)(2,1)S(1)}, bf16[1,128,1024]{2,1,0:T(8,128)(2,1)S(1)}) custom-call(bf16[128,128]{1,0:T(8,128)(2,1)S(1)} %get-tuple-element.40.refs_0_.refs_1_, bf16[128,16384]{1,0:T(8,128)(2,1)S(1)} %get-tuple-element.41.refs_1_.refs_2_, ...), custom_call_target="tpu_custom_call" | custom-call | tf_op jit(solution)/shard_map/partials/pallas_call | solution.py:58
  7.0 0.8 %partials.4 = (bf16[1,128,1024]{2,1,0:T(8,128)(2,1)S(1)}, bf16[2,128,1024]{2,1,0:T(8,128)(2,1)S(1)}) custom-call(bf16[64,1024]{1,0:T(8,128)(2,1)S(1)} %get-tuple-element.47.refs_0_, bf16[128,128]{1,0:T(8,128)(2,1)S(1)} %get-tuple-element.40.refs_0_.refs_1_, bf16[128,16384]{1,0:T(8,128)(2,1)S(1)} %get-tuple-element.41.refs_1_.refs_2_, ...), custom_call_target="tpu_custom_call" | custom-call | tf_op jit(solution)/shard_map/partials/pallas_call | solution.py:58
  8.0 2.9 %collective-permute-start.1 = (bf16[64,1024]{1,0:T(8,128)(2,1)S(1)}, bf16[64,1024]{1,0:T(8,128)(2,1)S(1)}, u32[]{:S(2)}, u32[]{:S(2)}) collective-permute-start(bf16[64,1024]{1,0:T(8,128)(2,1)S(1)} %get-tuple-element.47.refs_0_), channel_id=1, source_target_pairs={{0,2},{1,3},{2,0},{3,1},{4,6},{5,7},{6,4},{7,5},{8,10},{9,11},{10,... | collective-permute-start | bytes 393224 | tf_op jit(solution)/shard_map/ppermute | solution.py:573
  10.9 1.6 %collective-permute-start.4 = (bf16[64,1024]{1,0:T(8,128)(2,1)S(1)}, bf16[64,1024]{1,0:T(8,128)(2,1)S(1)}, u32[]{:S(2)}, u32[]{:S(2)}) collective-permute-start(bf16[64,1024]{1,0:T(8,128)(2,1)S(1)} %get-tuple-element.52), channel_id=1, source_target_pairs={{0,4},{1,5},{2,6},{3,7},{4,0},{5,1},{6,2},{7,3},{8,12},{9,13},{10,... | collective-permute-start | bytes 393224 | tf_op jit(solution)/shard_map/ppermute | solution.py:573
  12.5 1.3 %partials.5 = (bf16[2,128,1024]{2,1,0:T(8,128)(2,1)S(1)}, bf16[1,128,1024]{2,1,0:T(8,128)(2,1)S(1)}, bf16[2,128,1024]{2,1,0:T(8,128)(2,1)S(1)}, bf16[2,128,1024]{2,1,0:T(8,128)(2,1)S(1)}) custom-call(bf16[2,128,1024]{2,1,0:T(8,128)(2,1)S(1)} %get-tuple-element.48.refs_0_, bf16[128,128]{1,0:T(8,128)(2,1)S(1)} %get-tuple-element.40.refs_0_.refs_1_, ...), custom_call_target="tpu_custom_call" | custom-call | tf_op jit(solution)/shard_map/partials/pallas_call | solution.py:58
  14.7 1.5 %collective-permute-done.4.refs_6_ = bf16[64,1024]{1,0:T(8,128)(2,1)S(1)} collective-permute-done((bf16[64,1024]{1,0:T(8,128)(2,1)S(1)}, bf16[64,1024]{1,0:T(8,128)(2,1)S(1)}, u32[]{:S(2)}, u32[]{:S(2)}) %collective-permute-start.4) | collective-permute-done | bytes 131104 | tf_op jit(solution)/shard_map/ppermute | solution.py:573
  16.7 1.7 %collective-permute-start.7 = (bf16[128,1024]{1,0:T(8,128)(2,1)S(1)}, bf16[128,1024]{1,0:T(8,128)(2,1)S(1)}, u32[]{:S(2)}, u32[]{:S(2)}) collective-permute-start(bf16[128,1024]{1,0:T(8,128)(2,1)S(1)} %get-tuple-element.53.refs_0_), channel_id=1, source_target_pairs={{0,4},{1,5},{2,6},{3,7},{4,0},{5,1},{6,2},{7,3},{8,12},{9,13},{10,... | collective-permute-start | bytes 786440 | tf_op jit(solution)/shard_map/ppermute | solution.py:573
  18.9 4.6 %collective-permute-done.6.refs_2_ = bf16[128,1024]{1,0:T(8,128)(2,1)S(1)} collective-permute-done((bf16[128,1024]{1,0:T(8,128)(2,1)S(1)}, bf16[128,1024]{1,0:T(8,128)(2,1)S(1)}, u32[]{:S(2)}, u32[]{:S(2)}) %collective-permute-start.6) | collective-permute-done | bytes 262176 | tf_op jit(solution)/shard_map/ppermute | solution.py:573
  23.5 1.1 %collective-permute-done.7.refs_3_ = bf16[128,1024]{1,0:T(8,128)(2,1)S(1)} collective-permute-done((bf16[128,1024]{1,0:T(8,128)(2,1)S(1)}, bf16[128,1024]{1,0:T(8,128)(2,1)S(1)}, u32[]{:S(2)}, u32[]{:S(2)}) %collective-permute-start.7) | collective-permute-done | bytes 262176 | tf_op jit(solution)/shard_map/ppermute | solution.py:573
  24.8 1.6 %collective-permute-start.10 = (bf16[128,1024]{1,0:T(8,128)(2,1)S(1)}, bf16[128,1024]{1,0:T(8,128)(2,1)S(1)}, u32[]{:S(2)}, u32[]{:S(2)}) collective-permute-start(bf16[128,1024]{1,0:T(8,128)(2,1)S(1)} %get-tuple-element.60), channel_id=1, source_target_pairs={{0,2},{1,3},{2,0},{3,1},{4,6},{5,7},{6,4},{7,5},{8,10},{9,11},{10,... | collective-permute-start | bytes 786440 | tf_op jit(solution)/shard_map/ppermute | solution.py:573
  26.3 1.7 %collective-permute-start.11 = (bf16[128,1024]{1,0:T(8,128)(2,1)S(1)}, bf16[128,1024]{1,0:T(8,128)(2,1)S(1)}, u32[]{:S(2)}, u32[]{:S(2)}) collective-permute-start(bf16[128,1024]{1,0:T(8,128)(2,1)S(1)} %get-tuple-element.61), channel_id=1, source_target_pairs={{0,4},{1,5},{2,6},{3,7},{4,0},{5,1},{6,2},{7,3},{8,12},{9,13},{10,... | collective-permute-start | bytes 786440 | tf_op jit(solution)/shard_map/ppermute | solution.py:573
  28.1 3.7 %collective-permute-done.10.refs_0_ = bf16[128,1024]{1,0:T(8,128)(2,1)S(1)} collective-permute-done((bf16[128,1024]{1,0:T(8,128)(2,1)S(1)}, bf16[128,1024]{1,0:T(8,128)(2,1)S(1)}, u32[]{:S(2)}, u32[]{:S(2)}) %collective-permute-start.10) | collective-permute-done | bytes 262176 | tf_op jit(solution)/shard_map/ppermute | solution.py:573
  31.8 1.2 %collective-permute-done.11.refs_1_ = bf16[128,1024]{1,0:T(8,128)(2,1)S(1)} collective-permute-done((bf16[128,1024]{1,0:T(8,128)(2,1)S(1)}, bf16[128,1024]{1,0:T(8,128)(2,1)S(1)}, u32[]{:S(2)}, u32[]{:S(2)}) %collective-permute-start.11) | collective-permute-done | bytes 262176 | tf_op jit(solution)/shard_map/ppermute | solution.py:573
  34.0 1.7 %collective-permute-start.15 = (bf16[128,1024]{1,0:T(8,128)(2,1)S(1)}, bf16[128,1024]{1,0:T(8,128)(2,1)S(1)}, u32[]{:S(2)}, u32[]{:S(2)}) collective-permute-start(bf16[128,1024]{1,0:T(8,128)(2,1)S(1)} %get-tuple-element.64), channel_id=1, source_target_pairs={{0,4},{1,5},{2,6},{3,7},{4,0},{5,1},{6,2},{7,3},{8,12},{9,13},{10,... | collective-permute-start | bytes 786440 | tf_op jit(solution)/shard_map/ppermute | solution.py:573
  36.3 3.5 %collective-permute-done.14.refs_0_.refs_4_ = bf16[128,1024]{1,0:T(8,128)(2,1)S(1)} collective-permute-done((bf16[128,1024]{1,0:T(8,128)(2,1)S(1)}, bf16[128,1024]{1,0:T(8,128)(2,1)S(1)}, u32[]{:S(2)}, u32[]{:S(2)}) %collective-permute-start.14) | collective-permute-done | bytes 262176 | tf_op jit(solution)/shard_map/ppermute | solution.py:573
  40.8 2.5 %collective-permute-start.17 = (bf16[128,1024]{1,0:T(8,128)(2,1)S(1)}, bf16[128,1024]{1,0:T(8,128)(2,1)S(1)}, u32[]{:S(2)}, u32[]{:S(2)}) collective-permute-start(bf16[128,1024]{1,0:T(8,128)(2,1)S(1)} %regrid.1.refs_0_.refs_2_), channel_id=1, source_target_pairs={{0,4},{1,5},{2,6},{3,7},{4,0},{5,1},{6,2},{7,3},{8,12},{9,13},{10,... | collective-permute-start | bytes 786440 | tf_op jit(solution)/shard_map/ppermute | solution.py:573
  43.3 1.2 %collective-permute-start.19 = (bf16[128,1024]{1,0:T(8,128)(2,1)S(1)}, bf16[128,1024]{1,0:T(8,128)(2,1)S(1)}, u32[]{:S(2)}, u32[]{:S(2)}) collective-permute-start(bf16[128,1024]{1,0:T(8,128)(2,1)S(1)} %regrid.1.refs_0_.refs_2_), channel_id=1, source_target_pairs={{0,2},{1,3},{2,0},{3,1},{4,6},{5,7},{6,4},{7,5},{8,10},{9,11},{10,... | collective-permute-start | bytes 786440 | tf_op jit(solution)/shard_map/ppermute | solution.py:573
  44.5 1.1 %hidden.1 = (bf16[128,1024]{1,0:T(8,128)(2,1)}, f32[8,128]{1,0:T(8,128)S(1)}) custom-call(bf16[128,1024]{1,0:T(8,128)(2,1)S(1)} %regrid.1.refs_0_.refs_2_, bf16[128,1024]{1,0:T(8,128)(2,1)S(1)} %copy-done.1, f32[2,1024]{1,0:T(2,128)S(1)} %get-tuple-element.54.refs_0_.refs_6_.refs_2_, bf16[128,128]{1,0:T(8,128)(2,1)S(1)} %get-tuple-element.43.refs_3_.refs_4_, ...), custom_call_target="tpu_custom_call" | custom-call | tf_op jit(solution)/shard_map/hidden/pallas_call | solution.py:58
  45.7 2.0 %collective-permute-done.17.refs_1_ = bf16[128,1024]{1,0:T(8,128)(2,1)S(1)} collective-permute-done((bf16[128,1024]{1,0:T(8,128)(2,1)S(1)}, bf16[128,1024]{1,0:T(8,128)(2,1)S(1)}, u32[]{:S(2)}, u32[]{:S(2)}) %collective-permute-start.17) | collective-permute-done | bytes 262176 | tf_op jit(solution)/shard_map/ppermute | solution.py:573
  47.7 4.4 %collective-permute-done.19.refs_3_.refs_6_ = bf16[128,1024]{1,0:T(8,128)(2,1)S(1)} collective-permute-done((bf16[128,1024]{1,0:T(8,128)(2,1)S(1)}, bf16[128,1024]{1,0:T(8,128)(2,1)S(1)}, u32[]{:S(2)}, u32[]{:S(2)}) %collective-permute-start.19) | collective-permute-done | bytes 262176 | tf_op jit(solution)/shard_map/ppermute | solution.py:573
  52.1 1.3 %collective-permute-start.20 = (bf16[128,1024]{1,0:T(8,128)(2,1)S(1)}, bf16[128,1024]{1,0:T(8,128)(2,1)S(1)}, u32[]{:S(2)}, u32[]{:S(2)}) collective-permute-start(bf16[128,1024]{1,0:T(8,128)(2,1)S(1)} %get-tuple-element.69.refs_3_), channel_id=1, source_target_pairs={{0,2},{1,3},{2,0},{3,1},{4,6},{5,7},{6,4},{7,5},{8,10},{9,11},{10,... | collective-permute-start | bytes 786440 | tf_op jit(solution)/shard_map/ppermute | solution.py:573
  53.4 3.4 %collective-permute-start.22 = (bf16[128,1024]{1,0:T(8,128)(2,1)S(1)}, bf16[128,1024]{1,0:T(8,128)(2,1)S(1)}, u32[]{:S(2)}, u32[]{:S(2)}) collective-permute-start(bf16[128,1024]{1,0:T(8,128)(2,1)S(1)} %get-tuple-element.70.refs_1_), channel_id=1, source_target_pairs={{0,4},{1,5},{2,6},{3,7},{4,0},{5,1},{6,2},{7,3},{8,12},{9,13},{10,... | collective-permute-start | bytes 786440 | tf_op jit(solution)/shard_map/ppermute | solution.py:573
  56.8 4.5 %collective-permute-start.25 = (bf16[128,1024]{1,0:T(8,128)(2,1)S(1)}, bf16[128,1024]{1,0:T(8,128)(2,1)S(1)}, u32[]{:S(2)}, u32[]{:S(2)}) collective-permute-start(bf16[128,1024]{1,0:T(8,128)(2,1)S(1)} %collective-permute-done.21.refs_1_), channel_id=1, source_target_pairs={{0,4},{1,5},{2,6},{3,7},{4,0},{5,1},{6,2},{7,3},{8,12},{9,13},{10,... | collective-permute-start | bytes 786440 | tf_op jit(solution)/shard_map/ppermute | solution.py:573
  61.4 2.7 %collective-permute-done.22.refs_2_ = bf16[128,1024]{1,0:T(8,128)(2,1)S(1)} collective-permute-done((bf16[128,1024]{1,0:T(8,128)(2,1)S(1)}, bf16[128,1024]{1,0:T(8,128)(2,1)S(1)}, u32[]{:S(2)}, u32[]{:S(2)}) %collective-permute-start.22) | collective-permute-done | bytes 262176 | tf_op jit(solution)/shard_map/ppermute | solution.py:573
  64.5 1.3 %turn_next.1.refs_0_ = bf16[8,1024,256]{2,1,0:T(8,128)(2,1)S(1)} custom-call(bf16[128,1024]{1,0:T(8,128)(2,1)S(1)} %choose.2.refs_0_.refs_4_, bf16[16384,128]{1,0:T(8,128)(2,1)S(1)} %copy-done, f32[128,128]{1,0:T(8,128)S(1)} %bitcast_convert_fusion.refs_2_, f32[2,128,128]{2,1,0:T(8,128)S(1)} %get-tuple-element.42.refs_2_.refs_3_.refs_1_, ...), custom_call_target="tpu_custom_call" | custom-call | tf_op jit(solution)/shard_map/turn_next/pallas_call | solution.py:58
  65.8 1.6 %collective-permute-done.25.refs_2_ = bf16[128,1024]{1,0:T(8,128)(2,1)S(1)} collective-permute-done((bf16[128,1024]{1,0:T(8,128)(2,1)S(1)}, bf16[128,1024]{1,0:T(8,128)(2,1)S(1)}, u32[]{:S(2)}, u32[]{:S(2)}) %collective-permute-start.25) | collective-permute-done | bytes 262176 | tf_op jit(solution)/shard_map/ppermute | solution.py:573
  67.4 4.5 %collective-permute-done.26.refs_3_.refs_8_ = bf16[128,1024]{1,0:T(8,128)(2,1)S(1)} collective-permute-done((bf16[128,1024]{1,0:T(8,128)(2,1)S(1)}, bf16[128,1024]{1,0:T(8,128)(2,1)S(1)}, u32[]{:S(2)}, u32[]{:S(2)}) %collective-permute-start.26) | collective-permute-done | bytes 262176 | tf_op jit(solution)/shard_map/ppermute | solution.py:573
  72.0 1.0 %collective-permute-start.29 = (bf16[64,1024]{1,0:T(8,128)(2,1)S(1)}, bf16[64,1024]{1,0:T(8,128)(2,1)S(1)}, u32[]{:S(2)}, u32[]{:S(2)}) collective-permute-start(bf16[64,1024]{1,0:T(8,128)(2,1)S(1)} %get-tuple-element.75), channel_id=1, source_target_pairs={{0,4},{1,5},{2,6},{3,7},{4,0},{5,1},{6,2},{7,3},{8,12},{9,13},{10,... | collective-permute-start | bytes 393224 | tf_op jit(solution)/shard_map/ppermute | solution.py:573
  73.0 0.8 project.2.refs_2_
  73.8 3.2 %collective-permute-done.27.refs_3_ = bf16[64,1024]{1,0:T(8,128)(2,1)S(1)} collective-permute-done((bf16[64,1024]{1,0:T(8,128)(2,1)S(1)}, bf16[64,1024]{1,0:T(8,128)(2,1)S(1)}, u32[]{:S(2)}, u32[]{:S(2)}) %collective-permute-start.27) | collective-permute-done | bytes 131104 | tf_op jit(solution)/shard_map/ppermute | solution.py:573
  77.4 1.3 %collective-permute-done.30.refs_1_ = f32[128,256]{1,0:T(8,128)S(1)} collective-permute-done((f32[128,256]{1,0:T(8,128)S(1)}, f32[128,256]{1,0:T(8,128)S(1)}, u32[]{:S(2)}, u32[]{:S(2)}) %collective-permute-start.30) | collective-permute-done | bytes 131104 | tf_op jit(solution)/shard_map/ppermute | solution.py:573
  (56 shorter events, 7.6 us)
Async XLA Ops:
  4.8 2.2 %collective-permute-start = (bf16[1,128,1024]{2,1,0:T(8,128)(2,1)S(1)}, bf16[1,128,1024]{2,1,0:T(8,128)(2,1)S(1)}, u32[]{:S(2)}, u32[]{:S(2)}) collective-permute-start(bf16[1,128,1024]{2,1,0:T(8,128)(2,1)S(1)} %get-tuple-element.46), channel_id=1, source_target_pairs={{0,1},{1,0},{2,3},{3,2},{4,5},{5,4},{6,7},{7,6},{8,9},{9,8},{10,11... | collective-permute-start | bytes 786440 | tf_op jit(solution)/shard_map/ppermute | solution.py:573
  6.4 6.1 %collective-permute-start.2 = (bf16[1,128,1024]{2,1,0:T(8,128)(2,1)S(1)}, bf16[1,128,1024]{2,1,0:T(8,128)(2,1)S(1)}, u32[]{:S(2)}, u32[]{:S(2)}) collective-permute-start(bf16[1,128,1024]{2,1,0:T(8,128)(2,1)S(1)} %get-tuple-element.50), channel_id=1, source_target_pairs={{0,1},{1,0},{2,3},{3,2},{4,5},{5,4},{6,7},{7,6},{8,9},{9,8},{10,11... | collective-permute-start | bytes 786440 | tf_op jit(solution)/shard_map/ppermute | solution.py:573
  6.5 7.4 %collective-permute-start.3 = (bf16[1,128,1024]{2,1,0:T(8,128)(2,1)S(1)}, bf16[1,128,1024]{2,1,0:T(8,128)(2,1)S(1)}, u32[]{:S(2)}, u32[]{:S(2)}) collective-permute-start(bf16[1,128,1024]{2,1,0:T(8,128)(2,1)S(1)} %get-tuple-element.51), channel_id=1, source_target_pairs={{0,1},{1,0},{2,3},{3,2},{4,5},{5,4},{6,7},{7,6},{8,9},{9,8},{10,11... | collective-permute-start | bytes 786440 | tf_op jit(solution)/shard_map/ppermute | solution.py:573
  7.9 16.7 %collective-permute-start.9 = (bf16[2,128,1024]{2,1,0:T(8,128)(2,1)S(1)}, bf16[2,128,1024]{2,1,0:T(8,128)(2,1)S(1)}, u32[]{:S(2)}, u32[]{:S(2)}) collective-permute-start(bf16[2,128,1024]{2,1,0:T(8,128)(2,1)S(1)} %get-tuple-element.48.refs_0_), channel_id=1, source_target_pairs={{0,1},{1,0},{2,3},{3,2},{4,5},{5,4},{6,7},{7,6},{8,9},{9,8},{10,11... | collective-permute-start | bytes 1572872 | tf_op jit(solution)/shard_map/ppermute | solution.py:573
  8.0 6.7 %collective-permute-start.1 = (bf16[64,1024]{1,0:T(8,128)(2,1)S(1)}, bf16[64,1024]{1,0:T(8,128)(2,1)S(1)}, u32[]{:S(2)}, u32[]{:S(2)}) collective-permute-start(bf16[64,1024]{1,0:T(8,128)(2,1)S(1)} %get-tuple-element.47.refs_0_), channel_id=1, source_target_pairs={{0,2},{1,3},{2,0},{3,1},{4,6},{5,7},{6,4},{7,5},{8,10},{9,11},{10,... | collective-permute-start | bytes 393224 | tf_op jit(solution)/shard_map/ppermute | solution.py:573
  10.9 5.2 %collective-permute-start.4 = (bf16[64,1024]{1,0:T(8,128)(2,1)S(1)}, bf16[64,1024]{1,0:T(8,128)(2,1)S(1)}, u32[]{:S(2)}, u32[]{:S(2)}) collective-permute-start(bf16[64,1024]{1,0:T(8,128)(2,1)S(1)} %get-tuple-element.52), channel_id=1, source_target_pairs={{0,4},{1,5},{2,6},{3,7},{4,0},{5,1},{6,2},{7,3},{8,12},{9,13},{10,... | collective-permute-start | bytes 393224 | tf_op jit(solution)/shard_map/ppermute | solution.py:573
  12.5 6.0 %collective-permute-start.5 = (bf16[64,1024]{1,0:T(8,128)(2,1)S(1)}, bf16[64,1024]{1,0:T(8,128)(2,1)S(1)}, u32[]{:S(2)}, u32[]{:S(2)}) collective-permute-start(bf16[64,1024]{1,0:T(8,128)(2,1)S(1)} %get-tuple-element.52), channel_id=1, source_target_pairs={{0,1},{1,0},{2,3},{3,2},{4,8},{5,9},{6,10},{7,11},{8,4},{9,5},{10,... | collective-permute-start | bytes 393224 | tf_op jit(solution)/shard_map/ppermute | solution.py:573
  13.9 5.0 %collective-permute-start.8 = (bf16[1,128,1024]{2,1,0:T(8,128)(2,1)S(1)}, bf16[1,128,1024]{2,1,0:T(8,128)(2,1)S(1)}, u32[]{:S(2)}, u32[]{:S(2)}) collective-permute-start(bf16[1,128,1024]{2,1,0:T(8,128)(2,1)S(1)} %get-tuple-element.58), channel_id=1, source_target_pairs={{0,1},{1,0},{2,3},{3,2},{4,5},{5,4},{6,7},{7,6},{8,9},{9,8},{10,11... | collective-permute-start | bytes 786440 | tf_op jit(solution)/shard_map/ppermute | solution.py:573
  16.3 7.2 %collective-permute-start.6 = (bf16[128,1024]{1,0:T(8,128)(2,1)S(1)}, bf16[128,1024]{1,0:T(8,128)(2,1)S(1)}, u32[]{:S(2)}, u32[]{:S(2)}) collective-permute-start(bf16[128,1024]{1,0:T(8,128)(2,1)S(1)} %get-tuple-element.56), channel_id=1, source_target_pairs={{0,2},{1,3},{2,0},{3,1},{4,6},{5,7},{6,4},{7,5},{8,10},{9,11},{10,... | collective-permute-start | bytes 786440 | tf_op jit(solution)/shard_map/ppermute | solution.py:573
  16.7 7.8 %collective-permute-start.7 = (bf16[128,1024]{1,0:T(8,128)(2,1)S(1)}, bf16[128,1024]{1,0:T(8,128)(2,1)S(1)}, u32[]{:S(2)}, u32[]{:S(2)}) collective-permute-start(bf16[128,1024]{1,0:T(8,128)(2,1)S(1)} %get-tuple-element.53.refs_0_), channel_id=1, source_target_pairs={{0,4},{1,5},{2,6},{3,7},{4,0},{5,1},{6,2},{7,3},{8,12},{9,13},{10,... | collective-permute-start | bytes 786440 | tf_op jit(solution)/shard_map/ppermute | solution.py:573
  18.5 9.6 %collective-permute-start.13 = (bf16[2,128,1024]{2,1,0:T(8,128)(2,1)S(1)}, bf16[2,128,1024]{2,1,0:T(8,128)(2,1)S(1)}, u32[]{:S(2)}, u32[]{:S(2)}) collective-permute-start(bf16[2,128,1024]{2,1,0:T(8,128)(2,1)S(1)} %get-tuple-element.49.refs_1_), channel_id=1, source_target_pairs={{0,1},{1,0},{2,3},{3,2},{4,5},{5,4},{6,7},{7,6},{8,9},{9,8},{10,11... | collective-permute-start | bytes 1572872 | tf_op jit(solution)/shard_map/ppermute | solution.py:573
  24.8 7.0 %collective-permute-start.10 = (bf16[128,1024]{1,0:T(8,128)(2,1)S(1)}, bf16[128,1024]{1,0:T(8,128)(2,1)S(1)}, u32[]{:S(2)}, u32[]{:S(2)}) collective-permute-start(bf16[128,1024]{1,0:T(8,128)(2,1)S(1)} %get-tuple-element.60), channel_id=1, source_target_pairs={{0,2},{1,3},{2,0},{3,1},{4,6},{5,7},{6,4},{7,5},{8,10},{9,11},{10,... | collective-permute-start | bytes 786440 | tf_op jit(solution)/shard_map/ppermute | solution.py:573
  26.3 6.6 %collective-permute-start.11 = (bf16[128,1024]{1,0:T(8,128)(2,1)S(1)}, bf16[128,1024]{1,0:T(8,128)(2,1)S(1)}, u32[]{:S(2)}, u32[]{:S(2)}) collective-permute-start(bf16[128,1024]{1,0:T(8,128)(2,1)S(1)} %get-tuple-element.61), channel_id=1, source_target_pairs={{0,4},{1,5},{2,6},{3,7},{4,0},{5,1},{6,2},{7,3},{8,12},{9,13},{10,... | collective-permute-start | bytes 786440 | tf_op jit(solution)/shard_map/ppermute | solution.py:573
  28.1 4.9 %collective-permute-start.12 = (bf16[128,1024]{1,0:T(8,128)(2,1)S(1)}, bf16[128,1024]{1,0:T(8,128)(2,1)S(1)}, u32[]{:S(2)}, u32[]{:S(2)}) collective-permute-start(bf16[128,1024]{1,0:T(8,128)(2,1)S(1)} %get-tuple-element.61), channel_id=1, source_target_pairs={{0,1},{1,0},{2,3},{3,2},{4,8},{5,9},{6,10},{7,11},{8,4},{9,5},{10,... | collective-permute-start | bytes 786440 | tf_op jit(solution)/shard_map/ppermute | solution.py:573
  33.3 31.1 %copy-start.2 = (bf16[16384]{0:T(1024)(128)(2,1)S(1)}, bf16[16384]{0:T(1024)(128)(2,1)}, u32[]{:S(2)}) copy-start(bf16[16384]{0:T(1024)(128)(2,1)} %param.17) | copy-start | bytes 98308
  33.3 6.4 %collective-permute-start.14 = (bf16[128,1024]{1,0:T(8,128)(2,1)S(1)}, bf16[128,1024]{1,0:T(8,128)(2,1)S(1)}, u32[]{:S(2)}, u32[]{:S(2)}) collective-permute-start(bf16[128,1024]{1,0:T(8,128)(2,1)S(1)} %get-tuple-element.63), channel_id=1, source_target_pairs={{0,2},{1,3},{2,0},{3,1},{4,6},{5,7},{6,4},{7,5},{8,10},{9,11},{10,... | collective-permute-start | bytes 786440 | tf_op jit(solution)/shard_map/ppermute | solution.py:573
  34.0 6.5 %collective-permute-start.15 = (bf16[128,1024]{1,0:T(8,128)(2,1)S(1)}, bf16[128,1024]{1,0:T(8,128)(2,1)S(1)}, u32[]{:S(2)}, u32[]{:S(2)}) collective-permute-start(bf16[128,1024]{1,0:T(8,128)(2,1)S(1)} %get-tuple-element.64), channel_id=1, source_target_pairs={{0,4},{1,5},{2,6},{3,7},{4,0},{5,1},{6,2},{7,3},{8,12},{9,13},{10,... | collective-permute-start | bytes 786440 | tf_op jit(solution)/shard_map/ppermute | solution.py:573
  35.8 4.7 %collective-permute-start.16 = (bf16[128,1024]{1,0:T(8,128)(2,1)S(1)}, bf16[128,1024]{1,0:T(8,128)(2,1)S(1)}, u32[]{:S(2)}, u32[]{:S(2)}) collective-permute-start(bf16[128,1024]{1,0:T(8,128)(2,1)S(1)} %get-tuple-element.65), channel_id=1, source_target_pairs={{0,1},{1,0},{2,3},{3,2},{4,8},{5,9},{6,10},{7,11},{8,4},{9,5},{10,... | collective-permute-start | bytes 786440 | tf_op jit(solution)/shard_map/ppermute | solution.py:573
  35.8 28.7 %collective-permute-start.23 = (bf16[4,1024,128]{2,1,0:T(8,128)(2,1)S(1)}, bf16[4,1024,128]{2,1,0:T(8,128)(2,1)S(1)}, u32[]{:S(2)}, u32[]{:S(2)}) collective-permute-start(bf16[4,1024,128]{2,1,0:T(8,128)(2,1)S(1)} %get-tuple-element.55.refs_0_), channel_id=1, source_target_pairs={{0,1},{1,0},{2,3},{3,2},{4,5},{5,4},{6,7},{7,6},{8,9},{9,8},{10,11... | collective-permute-start | bytes 3145736 | tf_op jit(solution)/shard_map/ppermute | solution.py:573
  36.3 28.2 %collective-permute-start.24 = (bf16[4,1024,128]{2,1,0:T(8,128)(2,1)S(1)}, bf16[4,1024,128]{2,1,0:T(8,128)(2,1)S(1)}, u32[]{:S(2)}, u32[]{:S(2)}) collective-permute-start(bf16[4,1024,128]{2,1,0:T(8,128)(2,1)S(1)} %get-tuple-element.71), channel_id=1, source_target_pairs={{0,1},{1,0},{2,3},{3,2},{4,5},{5,4},{6,7},{7,6},{8,9},{9,8},{10,11... | collective-permute-start | bytes 3145736 | tf_op jit(solution)/shard_map/ppermute | solution.py:573
  40.8 6.9 %collective-permute-start.17 = (bf16[128,1024]{1,0:T(8,128)(2,1)S(1)}, bf16[128,1024]{1,0:T(8,128)(2,1)S(1)}, u32[]{:S(2)}, u32[]{:S(2)}) collective-permute-start(bf16[128,1024]{1,0:T(8,128)(2,1)S(1)} %regrid.1.refs_0_.refs_2_), channel_id=1, source_target_pairs={{0,4},{1,5},{2,6},{3,7},{4,0},{5,1},{6,2},{7,3},{8,12},{9,13},{10,... | collective-permute-start | bytes 786440 | tf_op jit(solution)/shard_map/ppermute | solution.py:573
  43.3 4.4 %collective-permute-start.18 = (bf16[128,1024]{1,0:T(8,128)(2,1)S(1)}, bf16[128,1024]{1,0:T(8,128)(2,1)S(1)}, u32[]{:S(2)}, u32[]{:S(2)}) collective-permute-start(bf16[128,1024]{1,0:T(8,128)(2,1)S(1)} %regrid.1.refs_0_.refs_2_), channel_id=1, source_target_pairs={{0,1},{1,0},{2,3},{3,2},{4,8},{5,9},{6,10},{7,11},{8,4},{9,5},{10,... | collective-permute-start | bytes 786440 | tf_op jit(solution)/shard_map/ppermute | solution.py:573
  43.3 8.7 %collective-permute-start.19 = (bf16[128,1024]{1,0:T(8,128)(2,1)S(1)}, bf16[128,1024]{1,0:T(8,128)(2,1)S(1)}, u32[]{:S(2)}, u32[]{:S(2)}) collective-permute-start(bf16[128,1024]{1,0:T(8,128)(2,1)S(1)} %regrid.1.refs_0_.refs_2_), channel_id=1, source_target_pairs={{0,2},{1,3},{2,0},{3,1},{4,6},{5,7},{6,4},{7,5},{8,10},{9,11},{10,... | collective-permute-start | bytes 786440 | tf_op jit(solution)/shard_map/ppermute | solution.py:573
  52.1 4.8 %collective-permute-start.21 = (bf16[128,1024]{1,0:T(8,128)(2,1)S(1)}, bf16[128,1024]{1,0:T(8,128)(2,1)S(1)}, u32[]{:S(2)}, u32[]{:S(2)}) collective-permute-start(bf16[128,1024]{1,0:T(8,128)(2,1)S(1)} %get-tuple-element.69.refs_3_), channel_id=1, source_target_pairs={{0,1},{1,0},{2,3},{3,2},{4,8},{5,9},{6,10},{7,11},{8,4},{9,5},{10,... | collective-permute-start | bytes 786440 | tf_op jit(solution)/shard_map/ppermute | solution.py:573
  52.1 9.2 %collective-permute-start.20 = (bf16[128,1024]{1,0:T(8,128)(2,1)S(1)}, bf16[128,1024]{1,0:T(8,128)(2,1)S(1)}, u32[]{:S(2)}, u32[]{:S(2)}) collective-permute-start(bf16[128,1024]{1,0:T(8,128)(2,1)S(1)} %get-tuple-element.69.refs_3_), channel_id=1, source_target_pairs={{0,2},{1,3},{2,0},{3,1},{4,6},{5,7},{6,4},{7,5},{8,10},{9,11},{10,... | collective-permute-start | bytes 786440 | tf_op jit(solution)/shard_map/ppermute | solution.py:573
  53.4 10.6 %collective-permute-start.22 = (bf16[128,1024]{1,0:T(8,128)(2,1)S(1)}, bf16[128,1024]{1,0:T(8,128)(2,1)S(1)}, u32[]{:S(2)}, u32[]{:S(2)}) collective-permute-start(bf16[128,1024]{1,0:T(8,128)(2,1)S(1)} %get-tuple-element.70.refs_1_), channel_id=1, source_target_pairs={{0,4},{1,5},{2,6},{3,7},{4,0},{5,1},{6,2},{7,3},{8,12},{9,13},{10,... | collective-permute-start | bytes 786440 | tf_op jit(solution)/shard_map/ppermute | solution.py:573
  56.8 10.6 %collective-permute-start.25 = (bf16[128,1024]{1,0:T(8,128)(2,1)S(1)}, bf16[128,1024]{1,0:T(8,128)(2,1)S(1)}, u32[]{:S(2)}, u32[]{:S(2)}) collective-permute-start(bf16[128,1024]{1,0:T(8,128)(2,1)S(1)} %collective-permute-done.21.refs_1_), channel_id=1, source_target_pairs={{0,4},{1,5},{2,6},{3,7},{4,0},{5,1},{6,2},{7,3},{8,12},{9,13},{10,... | collective-permute-start | bytes 786440 | tf_op jit(solution)/shard_map/ppermute | solution.py:573
  64.1 7.8 %collective-permute-start.26 = (bf16[128,1024]{1,0:T(8,128)(2,1)S(1)}, bf16[128,1024]{1,0:T(8,128)(2,1)S(1)}, u32[]{:S(2)}, u32[]{:S(2)}) collective-permute-start(bf16[128,1024]{1,0:T(8,128)(2,1)S(1)} %choose.2.refs_0_.refs_4_), channel_id=1, source_target_pairs={{0,2},{1,3},{2,0},{3,1},{4,6},{5,7},{6,4},{7,5},{8,10},{9,11},{10,... | collective-permute-start | bytes 786440 | tf_op jit(solution)/shard_map/ppermute | solution.py:573
  64.4 9.4 %collective-permute-start.28 = (bf16[64,1024]{1,0:T(8,128)(2,1)S(1)}, bf16[64,1024]{1,0:T(8,128)(2,1)S(1)}, u32[]{:S(2)}, u32[]{:S(2)}) collective-permute-start(bf16[64,1024]{1,0:T(8,128)(2,1)S(1)} %get-tuple-element.74), channel_id=1, source_target_pairs={{0,1},{1,0},{2,3},{3,2},{4,8},{5,9},{6,10},{7,11},{8,4},{9,5},{10,... | collective-permute-start | bytes 393224 | tf_op jit(solution)/shard_map/ppermute | solution.py:573
  71.9 5.0 %collective-permute-start.27 = (bf16[64,1024]{1,0:T(8,128)(2,1)S(1)}, bf16[64,1024]{1,0:T(8,128)(2,1)S(1)}, u32[]{:S(2)}, u32[]{:S(2)}) collective-permute-start(bf16[64,1024]{1,0:T(8,128)(2,1)S(1)} %get-tuple-element.73), channel_id=1, source_target_pairs={{0,2},{1,3},{2,0},{3,1},{4,6},{5,7},{6,4},{7,5},{8,10},{9,11},{10,... | collective-permute-start | bytes 393224 | tf_op jit(solution)/shard_map/ppermute | solution.py:573
  72.0 5.0 %collective-permute-start.29 = (bf16[64,1024]{1,0:T(8,128)(2,1)S(1)}, bf16[64,1024]{1,0:T(8,128)(2,1)S(1)}, u32[]{:S(2)}, u32[]{:S(2)}) collective-permute-start(bf16[64,1024]{1,0:T(8,128)(2,1)S(1)} %get-tuple-element.75), channel_id=1, source_target_pairs={{0,4},{1,5},{2,6},{3,7},{4,0},{5,1},{6,2},{7,3},{8,12},{9,13},{10,... | collective-permute-start | bytes 393224 | tf_op jit(solution)/shard_map/ppermute | solution.py:573
  77.3 1.4 %collective-permute-start.30 = (f32[128,256]{1,0:T(8,128)S(1)}, f32[128,256]{1,0:T(8,128)S(1)}, u32[]{:S(2)}, u32[]{:S(2)}) collective-permute-start(f32[128,256]{1,0:T(8,128)S(1)} %get-tuple-element.77), channel_id=1, source_target_pairs={{0,1},{1,0},{2,3},{3,2},{4,5},{5,4},{6,7},{7,6},{8,9},{9,8},{10,11... | collective-permute-start | bytes 393224 | tf_op jit(solution)/shard_map/ppermute | solution.py:573
  (2 other events, 21.5 us)

commit v12 on v10

--- a/solution.py
+++ b/solution.py
@@ -324,7 +324,8 @@
 
 
 def regrid_kernel(inner, items, *refs):
-    *ins, turned_ref, factor_ref, grid_ref = refs
+    *ins, turned_ref, factor_ref, grid_ref, mark_ref = refs
+    mark_ref[...] = jnp.zeros_like(mark_ref)
     for i in range(turned_ref.shape[1] // ROT):
         part = slice(i * ROT, (i + 1) * ROT)
         value = turned_ref[:, part] + summed_at(inner, items, ins, part) * factor_ref[0:1, part]
@@ -334,7 +335,7 @@
 def regrid(inner, items, turned, factors, arrays, after=()):
     return kernel_call(
         functools.partial(regrid_kernel, inner, items),
-        jax.ShapeDtypeStruct(turned.shape, BF16),
+        [jax.ShapeDtypeStruct(turned.shape, BF16), jax.ShapeDtypeStruct((8, ROT), F32)],
         [*arrays, turned, factors],
         [vmem()] * (2 + len(arrays)),
         after=after,
@@ -404,7 +405,7 @@
 
 
 def gate_kernel(count, *refs):
-    for ref, half in zip(refs[:count], refs[-count:]):
+    for ref, half in zip(refs[:count], refs[len(refs) - count :]):
         half[...] = ref[half.shape[0] :]
 
 
@@ -696,7 +697,8 @@
 
     last = [*come4, from_near3, from_mid3, keep4, other4]
     items = [(None, False)] * (len(come4) + 1) + [(None, True)] + [(0, False)] * 2
-    grid = regrid(inner, items, turned_residual, factors, last)
+    grid, meet = regrid(inner, items, turned_residual, factors, last)
+    (grid,) = gate([grid], [], after=[swap_core(meet)])
 
     x1 = [shift_mid(grid, s) for s in shifts]
     near = swap_pairs(grid)

time: 78.1 us -> 79.5 us (1.018)
  waiting for transfers between devices: 28 us -> 31.2 us
  starting transfers between devices: 36.1 us -> 34.3 us
    ppermute x31 -> x32, waiting for transfers between devices: 28 us -> 31.2 us  [permute(): return lax.ppermute(value, 'tp', moves)]
    ppermute x31 -> x32, starting transfers between devices: 36.1 us -> 34.3 us  [permute(): return lax.ppermute(value, 'tp', moves)]
    pallas_call x19 -> x20, Pallas kernels: 13 us -> 13 us  [kernel_call(): pl.pallas_call(ordered, out_shape=out_shape, in_specs=[anywhere()] * extr...]
  transfers between devices with their start and end apart: 31 -> 32, of which waited for: 15 -> 17; matrix products, arithmetic and copies ran while one was open for 0% -> 0% of each run, Pallas kernels for 10% -> 9%
where the time goes in v12:
time: 79.5 us; the launch traced here: 79.4 us
  starting transfers between devices  34.3 us (43%)
  waiting for transfers between devices  31.2 us (39%)
  Pallas kernels  13 us (16%)
  between operations  0.86 us (1%)
    ppermute x32, starting transfers between devices, permute(): return lax.ppermute(value, 'tp', moves)  34.3 us
    ppermute x32, waiting for transfers between devices, permute(): return lax.ppermute(value, 'tp', moves)  31.2 us
    pallas_call x20, Pallas kernels, kernel_call(): pl.pallas_call(ordered, out_shape=out_shape, in_specs=[anywhere()] * extr...  13 us
  transfers between devices with their start and end apart: 32, of which 17 were waited for; matrix products, arithmetic and copies ran while one was open for 0% of the time, Pallas kernels for 9%

profile of v12, /device:TPU:0, one launch (start us, length us, event | category | flops | bytes accessed | tf_op | source)
XLA Modules:
  0.0 79.4 jit_solution(9975778163205238208)
XLA Ops:
  0.6 4.1 %attend.1 = (bf16[128,128]{1,0:T(8,128)(2,1)S(1)}, f32[2,128,128]{2,1,0:T(8,128)S(1)}, bf16[1,128,1024]{2,1,0:T(8,128)(2,1)S(1)}, bf16[128,16384]{1,0:T(8,128)(2,1)S(1)}, bf16[128,128]{1,0:T(8,128)(2,1)S(1)}) custom-call(bf16[1,128,128]{2,1,0:T(8,128)(2,1)} %refs_0_.1, bf16[1,8192,128]{2,1,0:T(8,128)(2,1)} %refs_1_.5, bf16[1,8192,128]{2,1,0:T(8,128)(2,1)} %refs_2_.1, ...), custom_call_target="tpu_custom_call" | custom-call | tf_op jit(solution)/shard_map/attend/pallas_call | solution.py:58
  5.3 1.1 %partials.3 = (bf16[1,128,1024]{2,1,0:T(8,128)(2,1)S(1)}, bf16[2,128,1024]{2,1,0:T(8,128)(2,1)S(1)}, bf16[1,128,1024]{2,1,0:T(8,128)(2,1)S(1)}, bf16[1,128,1024]{2,1,0:T(8,128)(2,1)S(1)}) custom-call(bf16[128,128]{1,0:T(8,128)(2,1)S(1)} %get-tuple-element.42.refs_0_.refs_1_, bf16[128,16384]{1,0:T(8,128)(2,1)S(1)} %get-tuple-element.43.refs_1_.refs_2_, ...), custom_call_target="tpu_custom_call" | custom-call | tf_op jit(solution)/shard_map/partials/pallas_call | solution.py:58
  8.0 2.9 %collective-permute-start.1 = (bf16[64,1024]{1,0:T(8,128)(2,1)S(1)}, bf16[64,1024]{1,0:T(8,128)(2,1)S(1)}, u32[]{:S(2)}, u32[]{:S(2)}) collective-permute-start(bf16[64,1024]{1,0:T(8,128)(2,1)S(1)} %get-tuple-element.49.refs_0_), channel_id=1, source_target_pairs={{0,2},{1,3},{2,0},{3,1},{4,6},{5,7},{6,4},{7,5},{8,10},{9,11},{10,... | collective-permute-start | bytes 393224 | tf_op jit(solution)/shard_map/ppermute | solution.py:574
  10.9 1.6 %collective-permute-start.4 = (bf16[64,1024]{1,0:T(8,128)(2,1)S(1)}, bf16[64,1024]{1,0:T(8,128)(2,1)S(1)}, u32[]{:S(2)}, u32[]{:S(2)}) collective-permute-start(bf16[64,1024]{1,0:T(8,128)(2,1)S(1)} %get-tuple-element.54), channel_id=1, source_target_pairs={{0,4},{1,5},{2,6},{3,7},{4,0},{5,1},{6,2},{7,3},{8,12},{9,13},{10,... | collective-permute-start | bytes 393224 | tf_op jit(solution)/shard_map/ppermute | solution.py:574
  12.5 1.3 %partials.5 = (bf16[2,128,1024]{2,1,0:T(8,128)(2,1)S(1)}, bf16[1,128,1024]{2,1,0:T(8,128)(2,1)S(1)}, bf16[2,128,1024]{2,1,0:T(8,128)(2,1)S(1)}, bf16[2,128,1024]{2,1,0:T(8,128)(2,1)S(1)}) custom-call(bf16[2,128,1024]{2,1,0:T(8,128)(2,1)S(1)} %get-tuple-element.50.refs_0_, bf16[128,128]{1,0:T(8,128)(2,1)S(1)} %get-tuple-element.42.refs_0_.refs_1_, ...), custom_call_target="tpu_custom_call" | custom-call | tf_op jit(solution)/shard_map/partials/pallas_call | solution.py:58
  14.7 1.5 %collective-permute-done.4.refs_6_ = bf16[64,1024]{1,0:T(8,128)(2,1)S(1)} collective-permute-done((bf16[64,1024]{1,0:T(8,128)(2,1)S(1)}, bf16[64,1024]{1,0:T(8,128)(2,1)S(1)}, u32[]{:S(2)}, u32[]{:S(2)}) %collective-permute-start.4) | collective-permute-done | bytes 131104 | tf_op jit(solution)/shard_map/ppermute | solution.py:574
  16.7 1.7 %collective-permute-start.7 = (bf16[128,1024]{1,0:T(8,128)(2,1)S(1)}, bf16[128,1024]{1,0:T(8,128)(2,1)S(1)}, u32[]{:S(2)}, u32[]{:S(2)}) collective-permute-start(bf16[128,1024]{1,0:T(8,128)(2,1)S(1)} %get-tuple-element.55.refs_0_), channel_id=1, source_target_pairs={{0,4},{1,5},{2,6},{3,7},{4,0},{5,1},{6,2},{7,3},{8,12},{9,13},{10,... | collective-permute-start | bytes 786440 | tf_op jit(solution)/shard_map/ppermute | solution.py:574
  18.9 4.6 %collective-permute-done.6.refs_2_ = bf16[128,1024]{1,0:T(8,128)(2,1)S(1)} collective-permute-done((bf16[128,1024]{1,0:T(8,128)(2,1)S(1)}, bf16[128,1024]{1,0:T(8,128)(2,1)S(1)}, u32[]{:S(2)}, u32[]{:S(2)}) %collective-permute-start.6) | collective-permute-done | bytes 262176 | tf_op jit(solution)/shard_map/ppermute | solution.py:574
  23.5 1.1 %collective-permute-done.7.refs_3_ = bf16[128,1024]{1,0:T(8,128)(2,1)S(1)} collective-permute-done((bf16[128,1024]{1,0:T(8,128)(2,1)S(1)}, bf16[128,1024]{1,0:T(8,128)(2,1)S(1)}, u32[]{:S(2)}, u32[]{:S(2)}) %collective-permute-start.7) | collective-permute-done | bytes 262176 | tf_op jit(solution)/shard_map/ppermute | solution.py:574
  24.8 1.6 %collective-permute-start.10 = (bf16[128,1024]{1,0:T(8,128)(2,1)S(1)}, bf16[128,1024]{1,0:T(8,128)(2,1)S(1)}, u32[]{:S(2)}, u32[]{:S(2)}) collective-permute-start(bf16[128,1024]{1,0:T(8,128)(2,1)S(1)} %get-tuple-element.62), channel_id=1, source_target_pairs={{0,2},{1,3},{2,0},{3,1},{4,6},{5,7},{6,4},{7,5},{8,10},{9,11},{10,... | collective-permute-start | bytes 786440 | tf_op jit(solution)/shard_map/ppermute | solution.py:574
  26.3 1.7 %collective-permute-start.11 = (bf16[128,1024]{1,0:T(8,128)(2,1)S(1)}, bf16[128,1024]{1,0:T(8,128)(2,1)S(1)}, u32[]{:S(2)}, u32[]{:S(2)}) collective-permute-start(bf16[128,1024]{1,0:T(8,128)(2,1)S(1)} %get-tuple-element.63), channel_id=1, source_target_pairs={{0,4},{1,5},{2,6},{3,7},{4,0},{5,1},{6,2},{7,3},{8,12},{9,13},{10,... | collective-permute-start | bytes 786440 | tf_op jit(solution)/shard_map/ppermute | solution.py:574
  28.1 3.7 %collective-permute-done.10.refs_0_ = bf16[128,1024]{1,0:T(8,128)(2,1)S(1)} collective-permute-done((bf16[128,1024]{1,0:T(8,128)(2,1)S(1)}, bf16[128,1024]{1,0:T(8,128)(2,1)S(1)}, u32[]{:S(2)}, u32[]{:S(2)}) %collective-permute-start.10) | collective-permute-done | bytes 262176 | tf_op jit(solution)/shard_map/ppermute | solution.py:574
  31.8 1.2 %collective-permute-done.11.refs_1_ = bf16[128,1024]{1,0:T(8,128)(2,1)S(1)} collective-permute-done((bf16[128,1024]{1,0:T(8,128)(2,1)S(1)}, bf16[128,1024]{1,0:T(8,128)(2,1)S(1)}, u32[]{:S(2)}, u32[]{:S(2)}) %collective-permute-start.11) | collective-permute-done | bytes 262176 | tf_op jit(solution)/shard_map/ppermute | solution.py:574
  34.0 1.7 %collective-permute-start.15 = (bf16[128,1024]{1,0:T(8,128)(2,1)S(1)}, bf16[128,1024]{1,0:T(8,128)(2,1)S(1)}, u32[]{:S(2)}, u32[]{:S(2)}) collective-permute-start(bf16[128,1024]{1,0:T(8,128)(2,1)S(1)} %get-tuple-element.66), channel_id=1, source_target_pairs={{0,4},{1,5},{2,6},{3,7},{4,0},{5,1},{6,2},{7,3},{8,12},{9,13},{10,... | collective-permute-start | bytes 786440 | tf_op jit(solution)/shard_map/ppermute | solution.py:574
  36.3 3.5 %collective-permute-done.14.refs_0_.refs_4_ = bf16[128,1024]{1,0:T(8,128)(2,1)S(1)} collective-permute-done((bf16[128,1024]{1,0:T(8,128)(2,1)S(1)}, bf16[128,1024]{1,0:T(8,128)(2,1)S(1)}, u32[]{:S(2)}, u32[]{:S(2)}) %collective-permute-start.14) | collective-permute-done | bytes 262176 | tf_op jit(solution)/shard_map/ppermute | solution.py:574
  40.8 1.2 %collective-permute-done.17.refs_0_ = f32[8,128]{1,0:T(8,128)S(1)} collective-permute-done((f32[8,128]{1,0:T(8,128)S(1)}, f32[8,128]{1,0:T(8,128)S(1)}, u32[]{:S(2)}, u32[]{:S(2)}) %collective-permute-start.17) | collective-permute-done | bytes 4128 | tf_op jit(solution)/shard_map/ppermute | solution.py:574
  41.9 1.4 %collective-permute-start.18 = (bf16[128,1024]{1,0:T(8,128)(2,1)S(1)}, bf16[128,1024]{1,0:T(8,128)(2,1)S(1)}, u32[]{:S(2)}, u32[]{:S(2)}) collective-permute-start(bf16[128,1024]{1,0:T(8,128)(2,1)S(1)} %gate.2.refs_0_.refs_2_), channel_id=1, source_target_pairs={{0,2},{1,3},{2,0},{3,1},{4,6},{5,7},{6,4},{7,5},{8,10},{9,11},{10,... | collective-permute-start | bytes 786440 | tf_op jit(solution)/shard_map/ppermute | solution.py:574
  43.3 2.0 %collective-permute-start.19 = (bf16[128,1024]{1,0:T(8,128)(2,1)S(1)}, bf16[128,1024]{1,0:T(8,128)(2,1)S(1)}, u32[]{:S(2)}, u32[]{:S(2)}) collective-permute-start(bf16[128,1024]{1,0:T(8,128)(2,1)S(1)} %gate.2.refs_0_.refs_2_), channel_id=1, source_target_pairs={{0,4},{1,5},{2,6},{3,7},{4,0},{5,1},{6,2},{7,3},{8,12},{9,13},{10,... | collective-permute-start | bytes 786440 | tf_op jit(solution)/shard_map/ppermute | solution.py:574
  45.4 1.1 %hidden.1 = (bf16[128,1024]{1,0:T(8,128)(2,1)}, f32[8,128]{1,0:T(8,128)S(1)}) custom-call(bf16[128,1024]{1,0:T(8,128)(2,1)S(1)} %gate.2.refs_0_.refs_2_, bf16[128,1024]{1,0:T(8,128)(2,1)S(1)} %copy-done.1, f32[2,1024]{1,0:T(2,128)S(1)} %get-tuple-element.56.refs_0_.refs_6_.refs_2_, bf16[128,128]{1,0:T(8,128)(2,1)S(1)} %get-tuple-element.45.refs_3_.refs_4_, ...), custom_call_target="tpu_custom_call" | custom-call | tf_op jit(solution)/shard_map/hidden/pallas_call | solution.py:58
  46.5 3.8 %collective-permute-done.18.refs_1_.refs_6_ = bf16[128,1024]{1,0:T(8,128)(2,1)S(1)} collective-permute-done((bf16[128,1024]{1,0:T(8,128)(2,1)S(1)}, bf16[128,1024]{1,0:T(8,128)(2,1)S(1)}, u32[]{:S(2)}, u32[]{:S(2)}) %collective-permute-start.18) | collective-permute-done | bytes 262176 | tf_op jit(solution)/shard_map/ppermute | solution.py:574
  50.3 1.4 %collective-permute-done.19.refs_2_ = bf16[128,1024]{1,0:T(8,128)(2,1)S(1)} collective-permute-done((bf16[128,1024]{1,0:T(8,128)(2,1)S(1)}, bf16[128,1024]{1,0:T(8,128)(2,1)S(1)}, u32[]{:S(2)}, u32[]{:S(2)}) %collective-permute-start.19) | collective-permute-done | bytes 262176 | tf_op jit(solution)/shard_map/ppermute | solution.py:574
  52.5 3.3 %collective-permute-start.23 = (bf16[128,1024]{1,0:T(8,128)(2,1)S(1)}, bf16[128,1024]{1,0:T(8,128)(2,1)S(1)}, u32[]{:S(2)}, u32[]{:S(2)}) collective-permute-start(bf16[128,1024]{1,0:T(8,128)(2,1)S(1)} %get-tuple-element.74.refs_1_), channel_id=1, source_target_pairs={{0,4},{1,5},{2,6},{3,7},{4,0},{5,1},{6,2},{7,3},{8,12},{9,13},{10,... | collective-permute-start | bytes 786440 | tf_op jit(solution)/shard_map/ppermute | solution.py:574
  55.8 5.1 %collective-permute-start.26 = (bf16[128,1024]{1,0:T(8,128)(2,1)S(1)}, bf16[128,1024]{1,0:T(8,128)(2,1)S(1)}, u32[]{:S(2)}, u32[]{:S(2)}) collective-permute-start(bf16[128,1024]{1,0:T(8,128)(2,1)S(1)} %collective-permute-done.22.refs_1_), channel_id=1, source_target_pairs={{0,4},{1,5},{2,6},{3,7},{4,0},{5,1},{6,2},{7,3},{8,12},{9,13},{10,... | collective-permute-start | bytes 786440 | tf_op jit(solution)/shard_map/ppermute | solution.py:574
  60.9 0.9 %collective-permute-done.23.refs_2_ = bf16[128,1024]{1,0:T(8,128)(2,1)S(1)} collective-permute-done((bf16[128,1024]{1,0:T(8,128)(2,1)S(1)}, bf16[128,1024]{1,0:T(8,128)(2,1)S(1)}, u32[]{:S(2)}, u32[]{:S(2)}) %collective-permute-start.23) | collective-permute-done | bytes 262176 | tf_op jit(solution)/shard_map/ppermute | solution.py:574
  61.8 2.4 %collective-permute-start.27 = (bf16[128,1024]{1,0:T(8,128)(2,1)S(1)}, bf16[128,1024]{1,0:T(8,128)(2,1)S(1)}, u32[]{:S(2)}, u32[]{:S(2)}) collective-permute-start(bf16[128,1024]{1,0:T(8,128)(2,1)S(1)} %choose.2.refs_0_.refs_4_), channel_id=1, source_target_pairs={{0,2},{1,3},{2,0},{3,1},{4,6},{5,7},{6,4},{7,5},{8,10},{9,11},{10,... | collective-permute-start | bytes 786440 | tf_op jit(solution)/shard_map/ppermute | solution.py:574
  64.3 1.3 %turn_next.1.refs_0_ = bf16[8,1024,256]{2,1,0:T(8,128)(2,1)S(1)} custom-call(bf16[128,1024]{1,0:T(8,128)(2,1)S(1)} %choose.2.refs_0_.refs_4_, bf16[16384,128]{1,0:T(8,128)(2,1)S(1)} %copy-done, f32[128,128]{1,0:T(8,128)S(1)} %bitcast_convert_fusion.refs_2_, f32[2,128,128]{2,1,0:T(8,128)S(1)} %get-tuple-element.44.refs_2_.refs_3_.refs_1_, ...), custom_call_target="tpu_custom_call" | custom-call | tf_op jit(solution)/shard_map/turn_next/pallas_call | solution.py:58
  65.5 0.9 %collective-permute-done.26.refs_2_ = bf16[128,1024]{1,0:T(8,128)(2,1)S(1)} collective-permute-done((bf16[128,1024]{1,0:T(8,128)(2,1)S(1)}, bf16[128,1024]{1,0:T(8,128)(2,1)S(1)}, u32[]{:S(2)}, u32[]{:S(2)}) %collective-permute-start.26) | collective-permute-done | bytes 262176 | tf_op jit(solution)/shard_map/ppermute | solution.py:574
  66.5 3.0 %collective-permute-done.27.refs_3_.refs_8_ = bf16[128,1024]{1,0:T(8,128)(2,1)S(1)} collective-permute-done((bf16[128,1024]{1,0:T(8,128)(2,1)S(1)}, bf16[128,1024]{1,0:T(8,128)(2,1)S(1)}, u32[]{:S(2)}, u32[]{:S(2)}) %collective-permute-start.27) | collective-permute-done | bytes 262176 | tf_op jit(solution)/shard_map/ppermute | solution.py:574
  69.5 2.5 %collective-permute-start.28 = (bf16[64,1024]{1,0:T(8,128)(2,1)S(1)}, bf16[64,1024]{1,0:T(8,128)(2,1)S(1)}, u32[]{:S(2)}, u32[]{:S(2)}) collective-permute-start(bf16[64,1024]{1,0:T(8,128)(2,1)S(1)} %get-tuple-element.77), channel_id=1, source_target_pairs={{0,2},{1,3},{2,0},{3,1},{4,6},{5,7},{6,4},{7,5},{8,10},{9,11},{10,... | collective-permute-start | bytes 393224 | tf_op jit(solution)/shard_map/ppermute | solution.py:574
  72.0 1.8 %collective-permute-start.30 = (bf16[64,1024]{1,0:T(8,128)(2,1)S(1)}, bf16[64,1024]{1,0:T(8,128)(2,1)S(1)}, u32[]{:S(2)}, u32[]{:S(2)}) collective-permute-start(bf16[64,1024]{1,0:T(8,128)(2,1)S(1)} %get-tuple-element.79), channel_id=1, source_target_pairs={{0,4},{1,5},{2,6},{3,7},{4,0},{5,1},{6,2},{7,3},{8,12},{9,13},{10,... | collective-permute-start | bytes 393224 | tf_op jit(solution)/shard_map/ppermute | solution.py:574
  75.0 2.0 %collective-permute-done.30.refs_5_ = bf16[64,1024]{1,0:T(8,128)(2,1)S(1)} collective-permute-done((bf16[64,1024]{1,0:T(8,128)(2,1)S(1)}, bf16[64,1024]{1,0:T(8,128)(2,1)S(1)}, u32[]{:S(2)}, u32[]{:S(2)}) %collective-permute-start.30) | collective-permute-done | bytes 131104 | tf_op jit(solution)/shard_map/ppermute | solution.py:574
  77.3 1.3 %collective-permute-done.31.refs_1_ = f32[128,256]{1,0:T(8,128)S(1)} collective-permute-done((f32[128,256]{1,0:T(8,128)S(1)}, f32[128,256]{1,0:T(8,128)S(1)}, u32[]{:S(2)}, u32[]{:S(2)}) %collective-permute-start.31) | collective-permute-done | bytes 131104 | tf_op jit(solution)/shard_map/ppermute | solution.py:574
  (59 shorter events, 9.7 us)
Async XLA Ops:
  4.8 2.2 %collective-permute-start = (bf16[1,128,1024]{2,1,0:T(8,128)(2,1)S(1)}, bf16[1,128,1024]{2,1,0:T(8,128)(2,1)S(1)}, u32[]{:S(2)}, u32[]{:S(2)}) collective-permute-start(bf16[1,128,1024]{2,1,0:T(8,128)(2,1)S(1)} %get-tuple-element.48), channel_id=1, source_target_pairs={{0,1},{1,0},{2,3},{3,2},{4,5},{5,4},{6,7},{7,6},{8,9},{9,8},{10,11... | collective-permute-start | bytes 786440 | tf_op jit(solution)/shard_map/ppermute | solution.py:574
  6.4 6.1 %collective-permute-start.2 = (bf16[1,128,1024]{2,1,0:T(8,128)(2,1)S(1)}, bf16[1,128,1024]{2,1,0:T(8,128)(2,1)S(1)}, u32[]{:S(2)}, u32[]{:S(2)}) collective-permute-start(bf16[1,128,1024]{2,1,0:T(8,128)(2,1)S(1)} %get-tuple-element.52), channel_id=1, source_target_pairs={{0,1},{1,0},{2,3},{3,2},{4,5},{5,4},{6,7},{7,6},{8,9},{9,8},{10,11... | collective-permute-start | bytes 786440 | tf_op jit(solution)/shard_map/ppermute | solution.py:574
  6.5 7.4 %collective-permute-start.3 = (bf16[1,128,1024]{2,1,0:T(8,128)(2,1)S(1)}, bf16[1,128,1024]{2,1,0:T(8,128)(2,1)S(1)}, u32[]{:S(2)}, u32[]{:S(2)}) collective-permute-start(bf16[1,128,1024]{2,1,0:T(8,128)(2,1)S(1)} %get-tuple-element.53), channel_id=1, source_target_pairs={{0,1},{1,0},{2,3},{3,2},{4,5},{5,4},{6,7},{7,6},{8,9},{9,8},{10,11... | collective-permute-start | bytes 786440 | tf_op jit(solution)/shard_map/ppermute | solution.py:574
  7.9 16.7 %collective-permute-start.9 = (bf16[2,128,1024]{2,1,0:T(8,128)(2,1)S(1)}, bf16[2,128,1024]{2,1,0:T(8,128)(2,1)S(1)}, u32[]{:S(2)}, u32[]{:S(2)}) collective-permute-start(bf16[2,128,1024]{2,1,0:T(8,128)(2,1)S(1)} %get-tuple-element.50.refs_0_), channel_id=1, source_target_pairs={{0,1},{1,0},{2,3},{3,2},{4,5},{5,4},{6,7},{7,6},{8,9},{9,8},{10,11... | collective-permute-start | bytes 1572872 | tf_op jit(solution)/shard_map/ppermute | solution.py:574
  8.0 6.7 %collective-permute-start.1 = (bf16[64,1024]{1,0:T(8,128)(2,1)S(1)}, bf16[64,1024]{1,0:T(8,128)(2,1)S(1)}, u32[]{:S(2)}, u32[]{:S(2)}) collective-permute-start(bf16[64,1024]{1,0:T(8,128)(2,1)S(1)} %get-tuple-element.49.refs_0_), channel_id=1, source_target_pairs={{0,2},{1,3},{2,0},{3,1},{4,6},{5,7},{6,4},{7,5},{8,10},{9,11},{10,... | collective-permute-start | bytes 393224 | tf_op jit(solution)/shard_map/ppermute | solution.py:574
  10.9 5.2 %collective-permute-start.4 = (bf16[64,1024]{1,0:T(8,128)(2,1)S(1)}, bf16[64,1024]{1,0:T(8,128)(2,1)S(1)}, u32[]{:S(2)}, u32[]{:S(2)}) collective-permute-start(bf16[64,1024]{1,0:T(8,128)(2,1)S(1)} %get-tuple-element.54), channel_id=1, source_target_pairs={{0,4},{1,5},{2,6},{3,7},{4,0},{5,1},{6,2},{7,3},{8,12},{9,13},{10,... | collective-permute-start | bytes 393224 | tf_op jit(solution)/shard_map/ppermute | solution.py:574
  12.5 6.0 %collective-permute-start.5 = (bf16[64,1024]{1,0:T(8,128)(2,1)S(1)}, bf16[64,1024]{1,0:T(8,128)(2,1)S(1)}, u32[]{:S(2)}, u32[]{:S(2)}) collective-permute-start(bf16[64,1024]{1,0:T(8,128)(2,1)S(1)} %get-tuple-element.54), channel_id=1, source_target_pairs={{0,1},{1,0},{2,3},{3,2},{4,8},{5,9},{6,10},{7,11},{8,4},{9,5},{10,... | collective-permute-start | bytes 393224 | tf_op jit(solution)/shard_map/ppermute | solution.py:574
  13.9 5.0 %collective-permute-start.8 = (bf16[1,128,1024]{2,1,0:T(8,128)(2,1)S(1)}, bf16[1,128,1024]{2,1,0:T(8,128)(2,1)S(1)}, u32[]{:S(2)}, u32[]{:S(2)}) collective-permute-start(bf16[1,128,1024]{2,1,0:T(8,128)(2,1)S(1)} %get-tuple-element.60), channel_id=1, source_target_pairs={{0,1},{1,0},{2,3},{3,2},{4,5},{5,4},{6,7},{7,6},{8,9},{9,8},{10,11... | collective-permute-start | bytes 786440 | tf_op jit(solution)/shard_map/ppermute | solution.py:574
  16.3 7.2 %collective-permute-start.6 = (bf16[128,1024]{1,0:T(8,128)(2,1)S(1)}, bf16[128,1024]{1,0:T(8,128)(2,1)S(1)}, u32[]{:S(2)}, u32[]{:S(2)}) collective-permute-start(bf16[128,1024]{1,0:T(8,128)(2,1)S(1)} %get-tuple-element.58), channel_id=1, source_target_pairs={{0,2},{1,3},{2,0},{3,1},{4,6},{5,7},{6,4},{7,5},{8,10},{9,11},{10,... | collective-permute-start | bytes 786440 | tf_op jit(solution)/shard_map/ppermute | solution.py:574
  16.7 7.8 %collective-permute-start.7 = (bf16[128,1024]{1,0:T(8,128)(2,1)S(1)}, bf16[128,1024]{1,0:T(8,128)(2,1)S(1)}, u32[]{:S(2)}, u32[]{:S(2)}) collective-permute-start(bf16[128,1024]{1,0:T(8,128)(2,1)S(1)} %get-tuple-element.55.refs_0_), channel_id=1, source_target_pairs={{0,4},{1,5},{2,6},{3,7},{4,0},{5,1},{6,2},{7,3},{8,12},{9,13},{10,... | collective-permute-start | bytes 786440 | tf_op jit(solution)/shard_map/ppermute | solution.py:574
  18.5 9.6 %collective-permute-start.13 = (bf16[2,128,1024]{2,1,0:T(8,128)(2,1)S(1)}, bf16[2,128,1024]{2,1,0:T(8,128)(2,1)S(1)}, u32[]{:S(2)}, u32[]{:S(2)}) collective-permute-start(bf16[2,128,1024]{2,1,0:T(8,128)(2,1)S(1)} %get-tuple-element.51.refs_1_), channel_id=1, source_target_pairs={{0,1},{1,0},{2,3},{3,2},{4,5},{5,4},{6,7},{7,6},{8,9},{9,8},{10,11... | collective-permute-start | bytes 1572872 | tf_op jit(solution)/shard_map/ppermute | solution.py:574
  24.8 7.0 %collective-permute-start.10 = (bf16[128,1024]{1,0:T(8,128)(2,1)S(1)}, bf16[128,1024]{1,0:T(8,128)(2,1)S(1)}, u32[]{:S(2)}, u32[]{:S(2)}) collective-permute-start(bf16[128,1024]{1,0:T(8,128)(2,1)S(1)} %get-tuple-element.62), channel_id=1, source_target_pairs={{0,2},{1,3},{2,0},{3,1},{4,6},{5,7},{6,4},{7,5},{8,10},{9,11},{10,... | collective-permute-start | bytes 786440 | tf_op jit(solution)/shard_map/ppermute | solution.py:574
  26.3 6.7 %collective-permute-start.11 = (bf16[128,1024]{1,0:T(8,128)(2,1)S(1)}, bf16[128,1024]{1,0:T(8,128)(2,1)S(1)}, u32[]{:S(2)}, u32[]{:S(2)}) collective-permute-start(bf16[128,1024]{1,0:T(8,128)(2,1)S(1)} %get-tuple-element.63), channel_id=1, source_target_pairs={{0,4},{1,5},{2,6},{3,7},{4,0},{5,1},{6,2},{7,3},{8,12},{9,13},{10,... | collective-permute-start | bytes 786440 | tf_op jit(solution)/shard_map/ppermute | solution.py:574
  28.1 4.9 %collective-permute-start.12 = (bf16[128,1024]{1,0:T(8,128)(2,1)S(1)}, bf16[128,1024]{1,0:T(8,128)(2,1)S(1)}, u32[]{:S(2)}, u32[]{:S(2)}) collective-permute-start(bf16[128,1024]{1,0:T(8,128)(2,1)S(1)} %get-tuple-element.63), channel_id=1, source_target_pairs={{0,1},{1,0},{2,3},{3,2},{4,8},{5,9},{6,10},{7,11},{8,4},{9,5},{10,... | collective-permute-start | bytes 786440 | tf_op jit(solution)/shard_map/ppermute | solution.py:574
  33.4 6.4 %collective-permute-start.14 = (bf16[128,1024]{1,0:T(8,128)(2,1)S(1)}, bf16[128,1024]{1,0:T(8,128)(2,1)S(1)}, u32[]{:S(2)}, u32[]{:S(2)}) collective-permute-start(bf16[128,1024]{1,0:T(8,128)(2,1)S(1)} %get-tuple-element.65), channel_id=1, source_target_pairs={{0,2},{1,3},{2,0},{3,1},{4,6},{5,7},{6,4},{7,5},{8,10},{9,11},{10,... | collective-permute-start | bytes 786440 | tf_op jit(solution)/shard_map/ppermute | solution.py:574
  34.0 6.4 %collective-permute-start.15 = (bf16[128,1024]{1,0:T(8,128)(2,1)S(1)}, bf16[128,1024]{1,0:T(8,128)(2,1)S(1)}, u32[]{:S(2)}, u32[]{:S(2)}) collective-permute-start(bf16[128,1024]{1,0:T(8,128)(2,1)S(1)} %get-tuple-element.66), channel_id=1, source_target_pairs={{0,4},{1,5},{2,6},{3,7},{4,0},{5,1},{6,2},{7,3},{8,12},{9,13},{10,... | collective-permute-start | bytes 786440 | tf_op jit(solution)/shard_map/ppermute | solution.py:574
  35.8 4.6 %collective-permute-start.16 = (bf16[128,1024]{1,0:T(8,128)(2,1)S(1)}, bf16[128,1024]{1,0:T(8,128)(2,1)S(1)}, u32[]{:S(2)}, u32[]{:S(2)}) collective-permute-start(bf16[128,1024]{1,0:T(8,128)(2,1)S(1)} %get-tuple-element.67), channel_id=1, source_target_pairs={{0,1},{1,0},{2,3},{3,2},{4,8},{5,9},{6,10},{7,11},{8,4},{9,5},{10,... | collective-permute-start | bytes 786440 | tf_op jit(solution)/shard_map/ppermute | solution.py:574
  35.8 28.5 %collective-permute-start.24 = (bf16[4,1024,128]{2,1,0:T(8,128)(2,1)S(1)}, bf16[4,1024,128]{2,1,0:T(8,128)(2,1)S(1)}, u32[]{:S(2)}, u32[]{:S(2)}) collective-permute-start(bf16[4,1024,128]{2,1,0:T(8,128)(2,1)S(1)} %get-tuple-element.57.refs_0_), channel_id=1, source_target_pairs={{0,1},{1,0},{2,3},{3,2},{4,5},{5,4},{6,7},{7,6},{8,9},{9,8},{10,11... | collective-permute-start | bytes 3145736 | tf_op jit(solution)/shard_map/ppermute | solution.py:574
  36.3 28.0 %collective-permute-start.25 = (bf16[4,1024,128]{2,1,0:T(8,128)(2,1)S(1)}, bf16[4,1024,128]{2,1,0:T(8,128)(2,1)S(1)}, u32[]{:S(2)}, u32[]{:S(2)}) collective-permute-start(bf16[4,1024,128]{2,1,0:T(8,128)(2,1)S(1)} %get-tuple-element.75), channel_id=1, source_target_pairs={{0,1},{1,0},{2,3},{3,2},{4,5},{5,4},{6,7},{7,6},{8,9},{9,8},{10,11... | collective-permute-start | bytes 3145736 | tf_op jit(solution)/shard_map/ppermute | solution.py:574
  40.7 1.2 %collective-permute-start.17 = (f32[8,128]{1,0:T(8,128)S(1)}, f32[8,128]{1,0:T(8,128)S(1)}, u32[]{:S(2)}, u32[]{:S(2)}) collective-permute-start(f32[8,128]{1,0:T(8,128)S(1)} %get-tuple-element.69), channel_id=1, source_target_pairs={{0,1},{1,0},{2,3},{3,2},{4,5},{5,4},{6,7},{7,6},{8,9},{9,8},{10,11... | collective-permute-start | bytes 12296 | tf_op jit(solution)/shard_map/ppermute | solution.py:574
  41.9 8.4 %collective-permute-start.18 = (bf16[128,1024]{1,0:T(8,128)(2,1)S(1)}, bf16[128,1024]{1,0:T(8,128)(2,1)S(1)}, u32[]{:S(2)}, u32[]{:S(2)}) collective-permute-start(bf16[128,1024]{1,0:T(8,128)(2,1)S(1)} %gate.2.refs_0_.refs_2_), channel_id=1, source_target_pairs={{0,2},{1,3},{2,0},{3,1},{4,6},{5,7},{6,4},{7,5},{8,10},{9,11},{10,... | collective-permute-start | bytes 786440 | tf_op jit(solution)/shard_map/ppermute | solution.py:574
  43.3 8.4 %collective-permute-start.19 = (bf16[128,1024]{1,0:T(8,128)(2,1)S(1)}, bf16[128,1024]{1,0:T(8,128)(2,1)S(1)}, u32[]{:S(2)}, u32[]{:S(2)}) collective-permute-start(bf16[128,1024]{1,0:T(8,128)(2,1)S(1)} %gate.2.refs_0_.refs_2_), channel_id=1, source_target_pairs={{0,4},{1,5},{2,6},{3,7},{4,0},{5,1},{6,2},{7,3},{8,12},{9,13},{10,... | collective-permute-start | bytes 786440 | tf_op jit(solution)/shard_map/ppermute | solution.py:574
  45.4 6.4 %collective-permute-start.20 = (bf16[128,1024]{1,0:T(8,128)(2,1)S(1)}, bf16[128,1024]{1,0:T(8,128)(2,1)S(1)}, u32[]{:S(2)}, u32[]{:S(2)}) collective-permute-start(bf16[128,1024]{1,0:T(8,128)(2,1)S(1)} %gate.2.refs_0_.refs_2_), channel_id=1, source_target_pairs={{0,1},{1,0},{2,3},{3,2},{4,8},{5,9},{6,10},{7,11},{8,4},{9,5},{10,... | collective-permute-start | bytes 786440 | tf_op jit(solution)/shard_map/ppermute | solution.py:574
  51.7 4.0 %collective-permute-start.22 = (bf16[128,1024]{1,0:T(8,128)(2,1)S(1)}, bf16[128,1024]{1,0:T(8,128)(2,1)S(1)}, u32[]{:S(2)}, u32[]{:S(2)}) collective-permute-start(bf16[128,1024]{1,0:T(8,128)(2,1)S(1)} %get-tuple-element.73.refs_3_), channel_id=1, source_target_pairs={{0,1},{1,0},{2,3},{3,2},{4,8},{5,9},{6,10},{7,11},{8,4},{9,5},{10,... | collective-permute-start | bytes 786440 | tf_op jit(solution)/shard_map/ppermute | solution.py:574
  51.8 9.1 %collective-permute-start.21 = (bf16[128,1024]{1,0:T(8,128)(2,1)S(1)}, bf16[128,1024]{1,0:T(8,128)(2,1)S(1)}, u32[]{:S(2)}, u32[]{:S(2)}) collective-permute-start(bf16[128,1024]{1,0:T(8,128)(2,1)S(1)} %get-tuple-element.73.refs_3_), channel_id=1, source_target_pairs={{0,2},{1,3},{2,0},{3,1},{4,6},{5,7},{6,4},{7,5},{8,10},{9,11},{10,... | collective-permute-start | bytes 786440 | tf_op jit(solution)/shard_map/ppermute | solution.py:574
  52.5 9.3 %collective-permute-start.23 = (bf16[128,1024]{1,0:T(8,128)(2,1)S(1)}, bf16[128,1024]{1,0:T(8,128)(2,1)S(1)}, u32[]{:S(2)}, u32[]{:S(2)}) collective-permute-start(bf16[128,1024]{1,0:T(8,128)(2,1)S(1)} %get-tuple-element.74.refs_1_), channel_id=1, source_target_pairs={{0,4},{1,5},{2,6},{3,7},{4,0},{5,1},{6,2},{7,3},{8,12},{9,13},{10,... | collective-permute-start | bytes 786440 | tf_op jit(solution)/shard_map/ppermute | solution.py:574
  55.8 10.7 %collective-permute-start.26 = (bf16[128,1024]{1,0:T(8,128)(2,1)S(1)}, bf16[128,1024]{1,0:T(8,128)(2,1)S(1)}, u32[]{:S(2)}, u32[]{:S(2)}) collective-permute-start(bf16[128,1024]{1,0:T(8,128)(2,1)S(1)} %collective-permute-done.22.refs_1_), channel_id=1, source_target_pairs={{0,4},{1,5},{2,6},{3,7},{4,0},{5,1},{6,2},{7,3},{8,12},{9,13},{10,... | collective-permute-start | bytes 786440 | tf_op jit(solution)/shard_map/ppermute | solution.py:574
  61.8 7.7 %collective-permute-start.27 = (bf16[128,1024]{1,0:T(8,128)(2,1)S(1)}, bf16[128,1024]{1,0:T(8,128)(2,1)S(1)}, u32[]{:S(2)}, u32[]{:S(2)}) collective-permute-start(bf16[128,1024]{1,0:T(8,128)(2,1)S(1)} %choose.2.refs_0_.refs_4_), channel_id=1, source_target_pairs={{0,2},{1,3},{2,0},{3,1},{4,6},{5,7},{6,4},{7,5},{8,10},{9,11},{10,... | collective-permute-start | bytes 786440 | tf_op jit(solution)/shard_map/ppermute | solution.py:574
  64.2 10.4 %collective-permute-start.29 = (bf16[64,1024]{1,0:T(8,128)(2,1)S(1)}, bf16[64,1024]{1,0:T(8,128)(2,1)S(1)}, u32[]{:S(2)}, u32[]{:S(2)}) collective-permute-start(bf16[64,1024]{1,0:T(8,128)(2,1)S(1)} %get-tuple-element.78), channel_id=1, source_target_pairs={{0,1},{1,0},{2,3},{3,2},{4,8},{5,9},{6,10},{7,11},{8,4},{9,5},{10,... | collective-permute-start | bytes 393224 | tf_op jit(solution)/shard_map/ppermute | solution.py:574
  69.5 5.5 %collective-permute-start.28 = (bf16[64,1024]{1,0:T(8,128)(2,1)S(1)}, bf16[64,1024]{1,0:T(8,128)(2,1)S(1)}, u32[]{:S(2)}, u32[]{:S(2)}) collective-permute-start(bf16[64,1024]{1,0:T(8,128)(2,1)S(1)} %get-tuple-element.77), channel_id=1, source_target_pairs={{0,2},{1,3},{2,0},{3,1},{4,6},{5,7},{6,4},{7,5},{8,10},{9,11},{10,... | collective-permute-start | bytes 393224 | tf_op jit(solution)/shard_map/ppermute | solution.py:574
  72.0 5.0 %collective-permute-start.30 = (bf16[64,1024]{1,0:T(8,128)(2,1)S(1)}, bf16[64,1024]{1,0:T(8,128)(2,1)S(1)}, u32[]{:S(2)}, u32[]{:S(2)}) collective-permute-start(bf16[64,1024]{1,0:T(8,128)(2,1)S(1)} %get-tuple-element.79), channel_id=1, source_target_pairs={{0,4},{1,5},{2,6},{3,7},{4,0},{5,1},{6,2},{7,3},{8,12},{9,13},{10,... | collective-permute-start | bytes 393224 | tf_op jit(solution)/shard_map/ppermute | solution.py:574
  77.3 1.4 %collective-permute-start.31 = (f32[128,256]{1,0:T(8,128)S(1)}, f32[128,256]{1,0:T(8,128)S(1)}, u32[]{:S(2)}, u32[]{:S(2)}) collective-permute-start(f32[128,256]{1,0:T(8,128)S(1)} %get-tuple-element.81), channel_id=1, source_target_pairs={{0,1},{1,0},{2,3},{3,2},{4,5},{5,4},{6,7},{7,6},{8,9},{9,8},{10,11... | collective-permute-start | bytes 393224 | tf_op jit(solution)/shard_map/ppermute | solution.py:574
  (3 other events, 52.3 us)

commit v13 on v10

--- a/solution.py
+++ b/solution.py
@@ -116,9 +116,6 @@
         copy_k(j).start()
     copy_table.start()
     copy_h.start()
-    for j in range(copies):
-        copy_v(j).start()
-    copy_w.start()
 
     copy_pos.wait()
     positions = jnp.broadcast_to(pos_ref[...].astype(F32), (ROT, tok)).T
@@ -130,6 +127,11 @@
     for j in range(steps):
         if j % per_copy == 0:
             copy_k(j // per_copy).wait()
+        if j == 0:
+            for i in range(copies):
+                copy_v(i).start()
+        if j == min(per_copy, steps - 1):
+            copy_w.start()
         scores = lax.dot_general(
             queries, k_ref[j * chunk : (j + 1) * chunk], (((1,), (1,)), ((), ())),
             preferred_element_type=F32,

time: 78.1 us -> 78.6 us (level)
  no operation moved by 1% of the time
where the time goes in v13:
time: 78.6 us; the launch traced here: 78.4 us
  starting transfers between devices  36 us (46%)
  waiting for transfers between devices  28.1 us (36%)
  Pallas kernels  13.5 us (17%)
  between operations  0.85 us (1%)
    ppermute x31, starting transfers between devices, permute(): return lax.ppermute(value, 'tp', moves)  36 us
    ppermute x31, waiting for transfers between devices, permute(): return lax.ppermute(value, 'tp', moves)  28.1 us
    pallas_call x19, Pallas kernels, kernel_call(): pl.pallas_call(ordered, out_shape=out_shape, in_specs=[anywhere()] * extr...  13.5 us
  transfers between devices with their start and end apart: 31, of which 15 were waited for; matrix products, arithmetic and copies ran while one was open for 0% of the time, Pallas kernels for 10%

profile of v13, /device:TPU:0, one launch (start us, length us, event | category | flops | bytes accessed | tf_op | source)
XLA Modules:
  0.0 78.4 jit_solution(5908778173195903225)
XLA Ops:
  0.6 4.6 %attend.1 = (bf16[128,128]{1,0:T(8,128)(2,1)S(1)}, f32[2,128,128]{2,1,0:T(8,128)S(1)}, bf16[1,128,1024]{2,1,0:T(8,128)(2,1)S(1)}, bf16[128,16384]{1,0:T(8,128)(2,1)S(1)}, bf16[128,128]{1,0:T(8,128)(2,1)S(1)}) custom-call(bf16[1,128,128]{2,1,0:T(8,128)(2,1)} %refs_0_.1, bf16[1,8192,128]{2,1,0:T(8,128)(2,1)} %refs_1_.5, bf16[1,8192,128]{2,1,0:T(8,128)(2,1)} %refs_2_.1, ...), custom_call_target="tpu_custom_call" | custom-call | tf_op jit(solution)/shard_map/attend/pallas_call | solution.py:58
  5.8 1.1 %partials.3 = (bf16[1,128,1024]{2,1,0:T(8,128)(2,1)S(1)}, bf16[2,128,1024]{2,1,0:T(8,128)(2,1)S(1)}, bf16[1,128,1024]{2,1,0:T(8,128)(2,1)S(1)}, bf16[1,128,1024]{2,1,0:T(8,128)(2,1)S(1)}) custom-call(bf16[128,128]{1,0:T(8,128)(2,1)S(1)} %get-tuple-element.40.refs_0_.refs_1_, bf16[128,16384]{1,0:T(8,128)(2,1)S(1)} %get-tuple-element.41.refs_1_.refs_2_, ...), custom_call_target="tpu_custom_call" | custom-call | tf_op jit(solution)/shard_map/partials/pallas_call | solution.py:58
  7.5 0.8 %partials.4 = (bf16[1,128,1024]{2,1,0:T(8,128)(2,1)S(1)}, bf16[2,128,1024]{2,1,0:T(8,128)(2,1)S(1)}) custom-call(bf16[64,1024]{1,0:T(8,128)(2,1)S(1)} %get-tuple-element.47.refs_0_, bf16[128,128]{1,0:T(8,128)(2,1)S(1)} %get-tuple-element.40.refs_0_.refs_1_, bf16[128,16384]{1,0:T(8,128)(2,1)S(1)} %get-tuple-element.41.refs_1_.refs_2_, ...), custom_call_target="tpu_custom_call" | custom-call | tf_op jit(solution)/shard_map/partials/pallas_call | solution.py:58
  8.5 2.9 %collective-permute-start.1 = (bf16[64,1024]{1,0:T(8,128)(2,1)S(1)}, bf16[64,1024]{1,0:T(8,128)(2,1)S(1)}, u32[]{:S(2)}, u32[]{:S(2)}) collective-permute-start(bf16[64,1024]{1,0:T(8,128)(2,1)S(1)} %get-tuple-element.47.refs_0_), channel_id=1, source_target_pairs={{0,2},{1,3},{2,0},{3,1},{4,6},{5,7},{6,4},{7,5},{8,10},{9,11},{10,... | collective-permute-start | bytes 393224 | tf_op jit(solution)/shard_map/ppermute | solution.py:575
  11.4 1.6 %collective-permute-start.4 = (bf16[64,1024]{1,0:T(8,128)(2,1)S(1)}, bf16[64,1024]{1,0:T(8,128)(2,1)S(1)}, u32[]{:S(2)}, u32[]{:S(2)}) collective-permute-start(bf16[64,1024]{1,0:T(8,128)(2,1)S(1)} %get-tuple-element.52), channel_id=1, source_target_pairs={{0,4},{1,5},{2,6},{3,7},{4,0},{5,1},{6,2},{7,3},{8,12},{9,13},{10,... | collective-permute-start | bytes 393224 | tf_op jit(solution)/shard_map/ppermute | solution.py:575
  13.0 1.3 %partials.5 = (bf16[2,128,1024]{2,1,0:T(8,128)(2,1)S(1)}, bf16[1,128,1024]{2,1,0:T(8,128)(2,1)S(1)}, bf16[2,128,1024]{2,1,0:T(8,128)(2,1)S(1)}, bf16[2,128,1024]{2,1,0:T(8,128)(2,1)S(1)}) custom-call(bf16[2,128,1024]{2,1,0:T(8,128)(2,1)S(1)} %get-tuple-element.48.refs_0_, bf16[128,128]{1,0:T(8,128)(2,1)S(1)} %get-tuple-element.40.refs_0_.refs_1_, ...), custom_call_target="tpu_custom_call" | custom-call | tf_op jit(solution)/shard_map/partials/pallas_call | solution.py:58
  15.1 1.5 %collective-permute-done.4.refs_6_ = bf16[64,1024]{1,0:T(8,128)(2,1)S(1)} collective-permute-done((bf16[64,1024]{1,0:T(8,128)(2,1)S(1)}, bf16[64,1024]{1,0:T(8,128)(2,1)S(1)}, u32[]{:S(2)}, u32[]{:S(2)}) %collective-permute-start.4) | collective-permute-done | bytes 131104 | tf_op jit(solution)/shard_map/ppermute | solution.py:575
  17.2 1.7 %collective-permute-start.7 = (bf16[128,1024]{1,0:T(8,128)(2,1)S(1)}, bf16[128,1024]{1,0:T(8,128)(2,1)S(1)}, u32[]{:S(2)}, u32[]{:S(2)}) collective-permute-start(bf16[128,1024]{1,0:T(8,128)(2,1)S(1)} %get-tuple-element.53.refs_0_), channel_id=1, source_target_pairs={{0,4},{1,5},{2,6},{3,7},{4,0},{5,1},{6,2},{7,3},{8,12},{9,13},{10,... | collective-permute-start | bytes 786440 | tf_op jit(solution)/shard_map/ppermute | solution.py:575
  19.3 4.6 %collective-permute-done.6.refs_2_ = bf16[128,1024]{1,0:T(8,128)(2,1)S(1)} collective-permute-done((bf16[128,1024]{1,0:T(8,128)(2,1)S(1)}, bf16[128,1024]{1,0:T(8,128)(2,1)S(1)}, u32[]{:S(2)}, u32[]{:S(2)}) %collective-permute-start.6) | collective-permute-done | bytes 262176 | tf_op jit(solution)/shard_map/ppermute | solution.py:575
  24.0 1.1 %collective-permute-done.7.refs_3_ = bf16[128,1024]{1,0:T(8,128)(2,1)S(1)} collective-permute-done((bf16[128,1024]{1,0:T(8,128)(2,1)S(1)}, bf16[128,1024]{1,0:T(8,128)(2,1)S(1)}, u32[]{:S(2)}, u32[]{:S(2)}) %collective-permute-start.7) | collective-permute-done | bytes 262176 | tf_op jit(solution)/shard_map/ppermute | solution.py:575
  25.2 1.6 %collective-permute-start.10 = (bf16[128,1024]{1,0:T(8,128)(2,1)S(1)}, bf16[128,1024]{1,0:T(8,128)(2,1)S(1)}, u32[]{:S(2)}, u32[]{:S(2)}) collective-permute-start(bf16[128,1024]{1,0:T(8,128)(2,1)S(1)} %get-tuple-element.60), channel_id=1, source_target_pairs={{0,2},{1,3},{2,0},{3,1},{4,6},{5,7},{6,4},{7,5},{8,10},{9,11},{10,... | collective-permute-start | bytes 786440 | tf_op jit(solution)/shard_map/ppermute | solution.py:575
  26.8 1.7 %collective-permute-start.11 = (bf16[128,1024]{1,0:T(8,128)(2,1)S(1)}, bf16[128,1024]{1,0:T(8,128)(2,1)S(1)}, u32[]{:S(2)}, u32[]{:S(2)}) collective-permute-start(bf16[128,1024]{1,0:T(8,128)(2,1)S(1)} %get-tuple-element.61), channel_id=1, source_target_pairs={{0,4},{1,5},{2,6},{3,7},{4,0},{5,1},{6,2},{7,3},{8,12},{9,13},{10,... | collective-permute-start | bytes 786440 | tf_op jit(solution)/shard_map/ppermute | solution.py:575
  28.6 3.7 %collective-permute-done.10.refs_0_ = bf16[128,1024]{1,0:T(8,128)(2,1)S(1)} collective-permute-done((bf16[128,1024]{1,0:T(8,128)(2,1)S(1)}, bf16[128,1024]{1,0:T(8,128)(2,1)S(1)}, u32[]{:S(2)}, u32[]{:S(2)}) %collective-permute-start.10) | collective-permute-done | bytes 262176 | tf_op jit(solution)/shard_map/ppermute | solution.py:575
  32.2 1.2 %collective-permute-done.11.refs_1_ = bf16[128,1024]{1,0:T(8,128)(2,1)S(1)} collective-permute-done((bf16[128,1024]{1,0:T(8,128)(2,1)S(1)}, bf16[128,1024]{1,0:T(8,128)(2,1)S(1)}, u32[]{:S(2)}, u32[]{:S(2)}) %collective-permute-start.11) | collective-permute-done | bytes 262176 | tf_op jit(solution)/shard_map/ppermute | solution.py:575
  34.5 1.7 %collective-permute-start.15 = (bf16[128,1024]{1,0:T(8,128)(2,1)S(1)}, bf16[128,1024]{1,0:T(8,128)(2,1)S(1)}, u32[]{:S(2)}, u32[]{:S(2)}) collective-permute-start(bf16[128,1024]{1,0:T(8,128)(2,1)S(1)} %get-tuple-element.64), channel_id=1, source_target_pairs={{0,4},{1,5},{2,6},{3,7},{4,0},{5,1},{6,2},{7,3},{8,12},{9,13},{10,... | collective-permute-start | bytes 786440 | tf_op jit(solution)/shard_map/ppermute | solution.py:575
  36.8 3.5 %collective-permute-done.14.refs_0_.refs_4_ = bf16[128,1024]{1,0:T(8,128)(2,1)S(1)} collective-permute-done((bf16[128,1024]{1,0:T(8,128)(2,1)S(1)}, bf16[128,1024]{1,0:T(8,128)(2,1)S(1)}, u32[]{:S(2)}, u32[]{:S(2)}) %collective-permute-start.14) | collective-permute-done | bytes 262176 | tf_op jit(solution)/shard_map/ppermute | solution.py:575
  41.2 1.5 %collective-permute-start.17 = (bf16[128,1024]{1,0:T(8,128)(2,1)S(1)}, bf16[128,1024]{1,0:T(8,128)(2,1)S(1)}, u32[]{:S(2)}, u32[]{:S(2)}) collective-permute-start(bf16[128,1024]{1,0:T(8,128)(2,1)S(1)} %regrid.1.refs_0_.refs_2_), channel_id=1, source_target_pairs={{0,2},{1,3},{2,0},{3,1},{4,6},{5,7},{6,4},{7,5},{8,10},{9,11},{10,... | collective-permute-start | bytes 786440 | tf_op jit(solution)/shard_map/ppermute | solution.py:575
  42.7 2.2 %collective-permute-start.18 = (bf16[128,1024]{1,0:T(8,128)(2,1)S(1)}, bf16[128,1024]{1,0:T(8,128)(2,1)S(1)}, u32[]{:S(2)}, u32[]{:S(2)}) collective-permute-start(bf16[128,1024]{1,0:T(8,128)(2,1)S(1)} %regrid.1.refs_0_.refs_2_), channel_id=1, source_target_pairs={{0,4},{1,5},{2,6},{3,7},{4,0},{5,1},{6,2},{7,3},{8,12},{9,13},{10,... | collective-permute-start | bytes 786440 | tf_op jit(solution)/shard_map/ppermute | solution.py:575
  44.9 1.1 %hidden.1 = (bf16[128,1024]{1,0:T(8,128)(2,1)}, f32[8,128]{1,0:T(8,128)S(1)}) custom-call(bf16[128,1024]{1,0:T(8,128)(2,1)S(1)} %regrid.1.refs_0_.refs_2_, bf16[128,1024]{1,0:T(8,128)(2,1)S(1)} %copy-done.1, f32[2,1024]{1,0:T(2,128)S(1)} %get-tuple-element.54.refs_0_.refs_6_.refs_2_, bf16[128,128]{1,0:T(8,128)(2,1)S(1)} %get-tuple-element.43.refs_3_.refs_4_, ...), custom_call_target="tpu_custom_call" | custom-call | tf_op jit(solution)/shard_map/hidden/pallas_call | solution.py:58
  46.0 1.6 %collective-permute-done.17.refs_1_.refs_6_ = bf16[128,1024]{1,0:T(8,128)(2,1)S(1)} collective-permute-done((bf16[128,1024]{1,0:T(8,128)(2,1)S(1)}, bf16[128,1024]{1,0:T(8,128)(2,1)S(1)}, u32[]{:S(2)}, u32[]{:S(2)}) %collective-permute-start.17) | collective-permute-done | bytes 262176 | tf_op jit(solution)/shard_map/ppermute | solution.py:575
  47.6 1.6 %collective-permute-done.18.refs_2_ = bf16[128,1024]{1,0:T(8,128)(2,1)S(1)} collective-permute-done((bf16[128,1024]{1,0:T(8,128)(2,1)S(1)}, bf16[128,1024]{1,0:T(8,128)(2,1)S(1)}, u32[]{:S(2)}, u32[]{:S(2)}) %collective-permute-start.18) | collective-permute-done | bytes 262176 | tf_op jit(solution)/shard_map/ppermute | solution.py:575
  49.8 7.3 %collective-permute-start.22 = (bf16[128,1024]{1,0:T(8,128)(2,1)S(1)}, bf16[128,1024]{1,0:T(8,128)(2,1)S(1)}, u32[]{:S(2)}, u32[]{:S(2)}) collective-permute-start(bf16[128,1024]{1,0:T(8,128)(2,1)S(1)} %get-tuple-element.70.refs_1_), channel_id=1, source_target_pairs={{0,4},{1,5},{2,6},{3,7},{4,0},{5,1},{6,2},{7,3},{8,12},{9,13},{10,... | collective-permute-start | bytes 786440 | tf_op jit(solution)/shard_map/ppermute | solution.py:575
  57.1 4.5 %collective-permute-start.25 = (bf16[128,1024]{1,0:T(8,128)(2,1)S(1)}, bf16[128,1024]{1,0:T(8,128)(2,1)S(1)}, u32[]{:S(2)}, u32[]{:S(2)}) collective-permute-start(bf16[128,1024]{1,0:T(8,128)(2,1)S(1)} %collective-permute-done.21.refs_1_), channel_id=1, source_target_pairs={{0,4},{1,5},{2,6},{3,7},{4,0},{5,1},{6,2},{7,3},{8,12},{9,13},{10,... | collective-permute-start | bytes 786440 | tf_op jit(solution)/shard_map/ppermute | solution.py:575
  61.6 1.7 %collective-permute-start.26 = (bf16[128,1024]{1,0:T(8,128)(2,1)S(1)}, bf16[128,1024]{1,0:T(8,128)(2,1)S(1)}, u32[]{:S(2)}, u32[]{:S(2)}) collective-permute-start(bf16[128,1024]{1,0:T(8,128)(2,1)S(1)} %choose.2.refs_0_.refs_4_), channel_id=1, source_target_pairs={{0,2},{1,3},{2,0},{3,1},{4,6},{5,7},{6,4},{7,5},{8,10},{9,11},{10,... | collective-permute-start | bytes 786440 | tf_op jit(solution)/shard_map/ppermute | solution.py:575
  63.4 1.3 %turn_next.1.refs_0_ = bf16[8,1024,256]{2,1,0:T(8,128)(2,1)S(1)} custom-call(bf16[128,1024]{1,0:T(8,128)(2,1)S(1)} %choose.2.refs_0_.refs_4_, bf16[16384,128]{1,0:T(8,128)(2,1)S(1)} %copy-done, f32[128,128]{1,0:T(8,128)S(1)} %bitcast_convert_fusion.refs_2_, f32[2,128,128]{2,1,0:T(8,128)S(1)} %get-tuple-element.42.refs_2_.refs_3_.refs_1_, ...), custom_call_target="tpu_custom_call" | custom-call | tf_op jit(solution)/shard_map/turn_next/pallas_call | solution.py:58
  64.7 1.3 %collective-permute-done.25.refs_2_ = bf16[128,1024]{1,0:T(8,128)(2,1)S(1)} collective-permute-done((bf16[128,1024]{1,0:T(8,128)(2,1)S(1)}, bf16[128,1024]{1,0:T(8,128)(2,1)S(1)}, u32[]{:S(2)}, u32[]{:S(2)}) %collective-permute-start.25) | collective-permute-done | bytes 262176 | tf_op jit(solution)/shard_map/ppermute | solution.py:575
  65.9 2.5 %collective-permute-done.26.refs_3_.refs_8_ = bf16[128,1024]{1,0:T(8,128)(2,1)S(1)} collective-permute-done((bf16[128,1024]{1,0:T(8,128)(2,1)S(1)}, bf16[128,1024]{1,0:T(8,128)(2,1)S(1)}, u32[]{:S(2)}, u32[]{:S(2)}) %collective-permute-start.26) | collective-permute-done | bytes 262176 | tf_op jit(solution)/shard_map/ppermute | solution.py:575
  68.5 2.5 %collective-permute-start.27 = (bf16[64,1024]{1,0:T(8,128)(2,1)S(1)}, bf16[64,1024]{1,0:T(8,128)(2,1)S(1)}, u32[]{:S(2)}, u32[]{:S(2)}) collective-permute-start(bf16[64,1024]{1,0:T(8,128)(2,1)S(1)} %get-tuple-element.73), channel_id=1, source_target_pairs={{0,2},{1,3},{2,0},{3,1},{4,6},{5,7},{6,4},{7,5},{8,10},{9,11},{10,... | collective-permute-start | bytes 393224 | tf_op jit(solution)/shard_map/ppermute | solution.py:575
  71.1 0.9 %collective-permute-start.29 = (bf16[64,1024]{1,0:T(8,128)(2,1)S(1)}, bf16[64,1024]{1,0:T(8,128)(2,1)S(1)}, u32[]{:S(2)}, u32[]{:S(2)}) collective-permute-start(bf16[64,1024]{1,0:T(8,128)(2,1)S(1)} %get-tuple-element.75), channel_id=1, source_target_pairs={{0,4},{1,5},{2,6},{3,7},{4,0},{5,1},{6,2},{7,3},{8,12},{9,13},{10,... | collective-permute-start | bytes 393224 | tf_op jit(solution)/shard_map/ppermute | solution.py:575
  72.8 1.3 %collective-permute-done.27.refs_3_ = bf16[64,1024]{1,0:T(8,128)(2,1)S(1)} collective-permute-done((bf16[64,1024]{1,0:T(8,128)(2,1)S(1)}, bf16[64,1024]{1,0:T(8,128)(2,1)S(1)}, u32[]{:S(2)}, u32[]{:S(2)}) %collective-permute-start.27) | collective-permute-done | bytes 131104 | tf_op jit(solution)/shard_map/ppermute | solution.py:575
  74.0 2.0 %collective-permute-done.29.refs_5_ = bf16[64,1024]{1,0:T(8,128)(2,1)S(1)} collective-permute-done((bf16[64,1024]{1,0:T(8,128)(2,1)S(1)}, bf16[64,1024]{1,0:T(8,128)(2,1)S(1)}, u32[]{:S(2)}, u32[]{:S(2)}) %collective-permute-start.29) | collective-permute-done | bytes 131104 | tf_op jit(solution)/shard_map/ppermute | solution.py:575
  76.4 1.3 %collective-permute-done.30.refs_1_ = f32[128,256]{1,0:T(8,128)S(1)} collective-permute-done((f32[128,256]{1,0:T(8,128)S(1)}, f32[128,256]{1,0:T(8,128)S(1)}, u32[]{:S(2)}, u32[]{:S(2)}) %collective-permute-start.30) | collective-permute-done | bytes 131104 | tf_op jit(solution)/shard_map/ppermute | solution.py:575
  (56 shorter events, 8.2 us)
Async XLA Ops:
  5.2 2.2 %collective-permute-start = (bf16[1,128,1024]{2,1,0:T(8,128)(2,1)S(1)}, bf16[1,128,1024]{2,1,0:T(8,128)(2,1)S(1)}, u32[]{:S(2)}, u32[]{:S(2)}) collective-permute-start(bf16[1,128,1024]{2,1,0:T(8,128)(2,1)S(1)} %get-tuple-element.46), channel_id=1, source_target_pairs={{0,1},{1,0},{2,3},{3,2},{4,5},{5,4},{6,7},{7,6},{8,9},{9,8},{10,11... | collective-permute-start | bytes 786440 | tf_op jit(solution)/shard_map/ppermute | solution.py:575
  6.8 6.1 %collective-permute-start.2 = (bf16[1,128,1024]{2,1,0:T(8,128)(2,1)S(1)}, bf16[1,128,1024]{2,1,0:T(8,128)(2,1)S(1)}, u32[]{:S(2)}, u32[]{:S(2)}) collective-permute-start(bf16[1,128,1024]{2,1,0:T(8,128)(2,1)S(1)} %get-tuple-element.50), channel_id=1, source_target_pairs={{0,1},{1,0},{2,3},{3,2},{4,5},{5,4},{6,7},{7,6},{8,9},{9,8},{10,11... | collective-permute-start | bytes 786440 | tf_op jit(solution)/shard_map/ppermute | solution.py:575
  7.0 7.4 %collective-permute-start.3 = (bf16[1,128,1024]{2,1,0:T(8,128)(2,1)S(1)}, bf16[1,128,1024]{2,1,0:T(8,128)(2,1)S(1)}, u32[]{:S(2)}, u32[]{:S(2)}) collective-permute-start(bf16[1,128,1024]{2,1,0:T(8,128)(2,1)S(1)} %get-tuple-element.51), channel_id=1, source_target_pairs={{0,1},{1,0},{2,3},{3,2},{4,5},{5,4},{6,7},{7,6},{8,9},{9,8},{10,11... | collective-permute-start | bytes 786440 | tf_op jit(solution)/shard_map/ppermute | solution.py:575
  8.3 16.7 %collective-permute-start.9 = (bf16[2,128,1024]{2,1,0:T(8,128)(2,1)S(1)}, bf16[2,128,1024]{2,1,0:T(8,128)(2,1)S(1)}, u32[]{:S(2)}, u32[]{:S(2)}) collective-permute-start(bf16[2,128,1024]{2,1,0:T(8,128)(2,1)S(1)} %get-tuple-element.48.refs_0_), channel_id=1, source_target_pairs={{0,1},{1,0},{2,3},{3,2},{4,5},{5,4},{6,7},{7,6},{8,9},{9,8},{10,11... | collective-permute-start | bytes 1572872 | tf_op jit(solution)/shard_map/ppermute | solution.py:575
  8.5 6.7 %collective-permute-start.1 = (bf16[64,1024]{1,0:T(8,128)(2,1)S(1)}, bf16[64,1024]{1,0:T(8,128)(2,1)S(1)}, u32[]{:S(2)}, u32[]{:S(2)}) collective-permute-start(bf16[64,1024]{1,0:T(8,128)(2,1)S(1)} %get-tuple-element.47.refs_0_), channel_id=1, source_target_pairs={{0,2},{1,3},{2,0},{3,1},{4,6},{5,7},{6,4},{7,5},{8,10},{9,11},{10,... | collective-permute-start | bytes 393224 | tf_op jit(solution)/shard_map/ppermute | solution.py:575
  11.4 5.2 %collective-permute-start.4 = (bf16[64,1024]{1,0:T(8,128)(2,1)S(1)}, bf16[64,1024]{1,0:T(8,128)(2,1)S(1)}, u32[]{:S(2)}, u32[]{:S(2)}) collective-permute-start(bf16[64,1024]{1,0:T(8,128)(2,1)S(1)} %get-tuple-element.52), channel_id=1, source_target_pairs={{0,4},{1,5},{2,6},{3,7},{4,0},{5,1},{6,2},{7,3},{8,12},{9,13},{10,... | collective-permute-start | bytes 393224 | tf_op jit(solution)/shard_map/ppermute | solution.py:575
  13.0 6.0 %collective-permute-start.5 = (bf16[64,1024]{1,0:T(8,128)(2,1)S(1)}, bf16[64,1024]{1,0:T(8,128)(2,1)S(1)}, u32[]{:S(2)}, u32[]{:S(2)}) collective-permute-start(bf16[64,1024]{1,0:T(8,128)(2,1)S(1)} %get-tuple-element.52), channel_id=1, source_target_pairs={{0,1},{1,0},{2,3},{3,2},{4,8},{5,9},{6,10},{7,11},{8,4},{9,5},{10,... | collective-permute-start | bytes 393224 | tf_op jit(solution)/shard_map/ppermute | solution.py:575
  14.3 5.0 %collective-permute-start.8 = (bf16[1,128,1024]{2,1,0:T(8,128)(2,1)S(1)}, bf16[1,128,1024]{2,1,0:T(8,128)(2,1)S(1)}, u32[]{:S(2)}, u32[]{:S(2)}) collective-permute-start(bf16[1,128,1024]{2,1,0:T(8,128)(2,1)S(1)} %get-tuple-element.58), channel_id=1, source_target_pairs={{0,1},{1,0},{2,3},{3,2},{4,5},{5,4},{6,7},{7,6},{8,9},{9,8},{10,11... | collective-permute-start | bytes 786440 | tf_op jit(solution)/shard_map/ppermute | solution.py:575
  16.8 7.2 %collective-permute-start.6 = (bf16[128,1024]{1,0:T(8,128)(2,1)S(1)}, bf16[128,1024]{1,0:T(8,128)(2,1)S(1)}, u32[]{:S(2)}, u32[]{:S(2)}) collective-permute-start(bf16[128,1024]{1,0:T(8,128)(2,1)S(1)} %get-tuple-element.56), channel_id=1, source_target_pairs={{0,2},{1,3},{2,0},{3,1},{4,6},{5,7},{6,4},{7,5},{8,10},{9,11},{10,... | collective-permute-start | bytes 786440 | tf_op jit(solution)/shard_map/ppermute | solution.py:575
  17.2 7.8 %collective-permute-start.7 = (bf16[128,1024]{1,0:T(8,128)(2,1)S(1)}, bf16[128,1024]{1,0:T(8,128)(2,1)S(1)}, u32[]{:S(2)}, u32[]{:S(2)}) collective-permute-start(bf16[128,1024]{1,0:T(8,128)(2,1)S(1)} %get-tuple-element.53.refs_0_), channel_id=1, source_target_pairs={{0,4},{1,5},{2,6},{3,7},{4,0},{5,1},{6,2},{7,3},{8,12},{9,13},{10,... | collective-permute-start | bytes 786440 | tf_op jit(solution)/shard_map/ppermute | solution.py:575
  18.9 9.6 %collective-permute-start.13 = (bf16[2,128,1024]{2,1,0:T(8,128)(2,1)S(1)}, bf16[2,128,1024]{2,1,0:T(8,128)(2,1)S(1)}, u32[]{:S(2)}, u32[]{:S(2)}) collective-permute-start(bf16[2,128,1024]{2,1,0:T(8,128)(2,1)S(1)} %get-tuple-element.49.refs_1_), channel_id=1, source_target_pairs={{0,1},{1,0},{2,3},{3,2},{4,5},{5,4},{6,7},{7,6},{8,9},{9,8},{10,11... | collective-permute-start | bytes 1572872 | tf_op jit(solution)/shard_map/ppermute | solution.py:575
  25.2 7.0 %collective-permute-start.10 = (bf16[128,1024]{1,0:T(8,128)(2,1)S(1)}, bf16[128,1024]{1,0:T(8,128)(2,1)S(1)}, u32[]{:S(2)}, u32[]{:S(2)}) collective-permute-start(bf16[128,1024]{1,0:T(8,128)(2,1)S(1)} %get-tuple-element.60), channel_id=1, source_target_pairs={{0,2},{1,3},{2,0},{3,1},{4,6},{5,7},{6,4},{7,5},{8,10},{9,11},{10,... | collective-permute-start | bytes 786440 | tf_op jit(solution)/shard_map/ppermute | solution.py:575
  26.8 6.7 %collective-permute-start.11 = (bf16[128,1024]{1,0:T(8,128)(2,1)S(1)}, bf16[128,1024]{1,0:T(8,128)(2,1)S(1)}, u32[]{:S(2)}, u32[]{:S(2)}) collective-permute-start(bf16[128,1024]{1,0:T(8,128)(2,1)S(1)} %get-tuple-element.61), channel_id=1, source_target_pairs={{0,4},{1,5},{2,6},{3,7},{4,0},{5,1},{6,2},{7,3},{8,12},{9,13},{10,... | collective-permute-start | bytes 786440 | tf_op jit(solution)/shard_map/ppermute | solution.py:575
  28.5 4.9 %collective-permute-start.12 = (bf16[128,1024]{1,0:T(8,128)(2,1)S(1)}, bf16[128,1024]{1,0:T(8,128)(2,1)S(1)}, u32[]{:S(2)}, u32[]{:S(2)}) collective-permute-start(bf16[128,1024]{1,0:T(8,128)(2,1)S(1)} %get-tuple-element.61), channel_id=1, source_target_pairs={{0,1},{1,0},{2,3},{3,2},{4,8},{5,9},{6,10},{7,11},{8,4},{9,5},{10,... | collective-permute-start | bytes 786440 | tf_op jit(solution)/shard_map/ppermute | solution.py:575
  33.8 29.5 %copy-start.2 = (bf16[16384]{0:T(1024)(128)(2,1)S(1)}, bf16[16384]{0:T(1024)(128)(2,1)}, u32[]{:S(2)}) copy-start(bf16[16384]{0:T(1024)(128)(2,1)} %param.17) | copy-start | bytes 98308
  33.8 6.4 %collective-permute-start.14 = (bf16[128,1024]{1,0:T(8,128)(2,1)S(1)}, bf16[128,1024]{1,0:T(8,128)(2,1)S(1)}, u32[]{:S(2)}, u32[]{:S(2)}) collective-permute-start(bf16[128,1024]{1,0:T(8,128)(2,1)S(1)} %get-tuple-element.63), channel_id=1, source_target_pairs={{0,2},{1,3},{2,0},{3,1},{4,6},{5,7},{6,4},{7,5},{8,10},{9,11},{10,... | collective-permute-start | bytes 786440 | tf_op jit(solution)/shard_map/ppermute | solution.py:575
  34.5 6.4 %collective-permute-start.15 = (bf16[128,1024]{1,0:T(8,128)(2,1)S(1)}, bf16[128,1024]{1,0:T(8,128)(2,1)S(1)}, u32[]{:S(2)}, u32[]{:S(2)}) collective-permute-start(bf16[128,1024]{1,0:T(8,128)(2,1)S(1)} %get-tuple-element.64), channel_id=1, source_target_pairs={{0,4},{1,5},{2,6},{3,7},{4,0},{5,1},{6,2},{7,3},{8,12},{9,13},{10,... | collective-permute-start | bytes 786440 | tf_op jit(solution)/shard_map/ppermute | solution.py:575
  36.2 4.6 %collective-permute-start.16 = (bf16[128,1024]{1,0:T(8,128)(2,1)S(1)}, bf16[128,1024]{1,0:T(8,128)(2,1)S(1)}, u32[]{:S(2)}, u32[]{:S(2)}) collective-permute-start(bf16[128,1024]{1,0:T(8,128)(2,1)S(1)} %get-tuple-element.65), channel_id=1, source_target_pairs={{0,1},{1,0},{2,3},{3,2},{4,8},{5,9},{6,10},{7,11},{8,4},{9,5},{10,... | collective-permute-start | bytes 786440 | tf_op jit(solution)/shard_map/ppermute | solution.py:575
  36.3 27.1 %collective-permute-start.23 = (bf16[4,1024,128]{2,1,0:T(8,128)(2,1)S(1)}, bf16[4,1024,128]{2,1,0:T(8,128)(2,1)S(1)}, u32[]{:S(2)}, u32[]{:S(2)}) collective-permute-start(bf16[4,1024,128]{2,1,0:T(8,128)(2,1)S(1)} %get-tuple-element.55.refs_0_), channel_id=1, source_target_pairs={{0,1},{1,0},{2,3},{3,2},{4,5},{5,4},{6,7},{7,6},{8,9},{9,8},{10,11... | collective-permute-start | bytes 3145736 | tf_op jit(solution)/shard_map/ppermute | solution.py:575
  36.8 26.6 %collective-permute-start.24 = (bf16[4,1024,128]{2,1,0:T(8,128)(2,1)S(1)}, bf16[4,1024,128]{2,1,0:T(8,128)(2,1)S(1)}, u32[]{:S(2)}, u32[]{:S(2)}) collective-permute-start(bf16[4,1024,128]{2,1,0:T(8,128)(2,1)S(1)} %get-tuple-element.71), channel_id=1, source_target_pairs={{0,1},{1,0},{2,3},{3,2},{4,5},{5,4},{6,7},{7,6},{8,9},{9,8},{10,11... | collective-permute-start | bytes 3145736 | tf_op jit(solution)/shard_map/ppermute | solution.py:575
  41.2 6.4 %collective-permute-start.17 = (bf16[128,1024]{1,0:T(8,128)(2,1)S(1)}, bf16[128,1024]{1,0:T(8,128)(2,1)S(1)}, u32[]{:S(2)}, u32[]{:S(2)}) collective-permute-start(bf16[128,1024]{1,0:T(8,128)(2,1)S(1)} %regrid.1.refs_0_.refs_2_), channel_id=1, source_target_pairs={{0,2},{1,3},{2,0},{3,1},{4,6},{5,7},{6,4},{7,5},{8,10},{9,11},{10,... | collective-permute-start | bytes 786440 | tf_op jit(solution)/shard_map/ppermute | solution.py:575
  42.7 6.6 %collective-permute-start.18 = (bf16[128,1024]{1,0:T(8,128)(2,1)S(1)}, bf16[128,1024]{1,0:T(8,128)(2,1)S(1)}, u32[]{:S(2)}, u32[]{:S(2)}) collective-permute-start(bf16[128,1024]{1,0:T(8,128)(2,1)S(1)} %regrid.1.refs_0_.refs_2_), channel_id=1, source_target_pairs={{0,4},{1,5},{2,6},{3,7},{4,0},{5,1},{6,2},{7,3},{8,12},{9,13},{10,... | collective-permute-start | bytes 786440 | tf_op jit(solution)/shard_map/ppermute | solution.py:575
  44.9 4.4 %collective-permute-start.19 = (bf16[128,1024]{1,0:T(8,128)(2,1)S(1)}, bf16[128,1024]{1,0:T(8,128)(2,1)S(1)}, u32[]{:S(2)}, u32[]{:S(2)}) collective-permute-start(bf16[128,1024]{1,0:T(8,128)(2,1)S(1)} %regrid.1.refs_0_.refs_2_), channel_id=1, source_target_pairs={{0,1},{1,0},{2,3},{3,2},{4,8},{5,9},{6,10},{7,11},{8,4},{9,5},{10,... | collective-permute-start | bytes 786440 | tf_op jit(solution)/shard_map/ppermute | solution.py:575
  49.3 7.9 %collective-permute-start.21 = (bf16[128,1024]{1,0:T(8,128)(2,1)S(1)}, bf16[128,1024]{1,0:T(8,128)(2,1)S(1)}, u32[]{:S(2)}, u32[]{:S(2)}) collective-permute-start(bf16[128,1024]{1,0:T(8,128)(2,1)S(1)} %get-tuple-element.69.refs_3_), channel_id=1, source_target_pairs={{0,1},{1,0},{2,3},{3,2},{4,8},{5,9},{6,10},{7,11},{8,4},{9,5},{10,... | collective-permute-start | bytes 786440 | tf_op jit(solution)/shard_map/ppermute | solution.py:575
  49.3 12.3 %collective-permute-start.20 = (bf16[128,1024]{1,0:T(8,128)(2,1)S(1)}, bf16[128,1024]{1,0:T(8,128)(2,1)S(1)}, u32[]{:S(2)}, u32[]{:S(2)}) collective-permute-start(bf16[128,1024]{1,0:T(8,128)(2,1)S(1)} %get-tuple-element.69.refs_3_), channel_id=1, source_target_pairs={{0,2},{1,3},{2,0},{3,1},{4,6},{5,7},{6,4},{7,5},{8,10},{9,11},{10,... | collective-permute-start | bytes 786440 | tf_op jit(solution)/shard_map/ppermute | solution.py:575
  49.8 11.8 %collective-permute-start.22 = (bf16[128,1024]{1,0:T(8,128)(2,1)S(1)}, bf16[128,1024]{1,0:T(8,128)(2,1)S(1)}, u32[]{:S(2)}, u32[]{:S(2)}) collective-permute-start(bf16[128,1024]{1,0:T(8,128)(2,1)S(1)} %get-tuple-element.70.refs_1_), channel_id=1, source_target_pairs={{0,4},{1,5},{2,6},{3,7},{4,0},{5,1},{6,2},{7,3},{8,12},{9,13},{10,... | collective-permute-start | bytes 786440 | tf_op jit(solution)/shard_map/ppermute | solution.py:575
  57.1 8.8 %collective-permute-start.25 = (bf16[128,1024]{1,0:T(8,128)(2,1)S(1)}, bf16[128,1024]{1,0:T(8,128)(2,1)S(1)}, u32[]{:S(2)}, u32[]{:S(2)}) collective-permute-start(bf16[128,1024]{1,0:T(8,128)(2,1)S(1)} %collective-permute-done.21.refs_1_), channel_id=1, source_target_pairs={{0,4},{1,5},{2,6},{3,7},{4,0},{5,1},{6,2},{7,3},{8,12},{9,13},{10,... | collective-permute-start | bytes 786440 | tf_op jit(solution)/shard_map/ppermute | solution.py:575
  61.6 6.9 %collective-permute-start.26 = (bf16[128,1024]{1,0:T(8,128)(2,1)S(1)}, bf16[128,1024]{1,0:T(8,128)(2,1)S(1)}, u32[]{:S(2)}, u32[]{:S(2)}) collective-permute-start(bf16[128,1024]{1,0:T(8,128)(2,1)S(1)} %choose.2.refs_0_.refs_4_), channel_id=1, source_target_pairs={{0,2},{1,3},{2,0},{3,1},{4,6},{5,7},{6,4},{7,5},{8,10},{9,11},{10,... | collective-permute-start | bytes 786440 | tf_op jit(solution)/shard_map/ppermute | solution.py:575
  63.3 9.4 %collective-permute-start.28 = (bf16[64,1024]{1,0:T(8,128)(2,1)S(1)}, bf16[64,1024]{1,0:T(8,128)(2,1)S(1)}, u32[]{:S(2)}, u32[]{:S(2)}) collective-permute-start(bf16[64,1024]{1,0:T(8,128)(2,1)S(1)} %get-tuple-element.74), channel_id=1, source_target_pairs={{0,1},{1,0},{2,3},{3,2},{4,8},{5,9},{6,10},{7,11},{8,4},{9,5},{10,... | collective-permute-start | bytes 393224 | tf_op jit(solution)/shard_map/ppermute | solution.py:575
  68.5 5.5 %collective-permute-start.27 = (bf16[64,1024]{1,0:T(8,128)(2,1)S(1)}, bf16[64,1024]{1,0:T(8,128)(2,1)S(1)}, u32[]{:S(2)}, u32[]{:S(2)}) collective-permute-start(bf16[64,1024]{1,0:T(8,128)(2,1)S(1)} %get-tuple-element.73), channel_id=1, source_target_pairs={{0,2},{1,3},{2,0},{3,1},{4,6},{5,7},{6,4},{7,5},{8,10},{9,11},{10,... | collective-permute-start | bytes 393224 | tf_op jit(solution)/shard_map/ppermute | solution.py:575
  71.1 5.0 %collective-permute-start.29 = (bf16[64,1024]{1,0:T(8,128)(2,1)S(1)}, bf16[64,1024]{1,0:T(8,128)(2,1)S(1)}, u32[]{:S(2)}, u32[]{:S(2)}) collective-permute-start(bf16[64,1024]{1,0:T(8,128)(2,1)S(1)} %get-tuple-element.75), channel_id=1, source_target_pairs={{0,4},{1,5},{2,6},{3,7},{4,0},{5,1},{6,2},{7,3},{8,12},{9,13},{10,... | collective-permute-start | bytes 393224 | tf_op jit(solution)/shard_map/ppermute | solution.py:575
  76.3 1.4 %collective-permute-start.30 = (f32[128,256]{1,0:T(8,128)S(1)}, f32[128,256]{1,0:T(8,128)S(1)}, u32[]{:S(2)}, u32[]{:S(2)}) collective-permute-start(f32[128,256]{1,0:T(8,128)S(1)} %get-tuple-element.77), channel_id=1, source_target_pairs={{0,1},{1,0},{2,3},{3,2},{4,5},{5,4},{6,7},{7,6},{8,9},{9,8},{10,11... | collective-permute-start | bytes 393224 | tf_op jit(solution)/shard_map/ppermute | solution.py:575
  (2 other events, 21.5 us)

commit v14 on v10

--- a/solution.py
+++ b/solution.py
@@ -90,7 +90,7 @@
     outer, mid, core = place(inner)
     dest = targets(outer)[0]
 
-    copies = min(4, steps)
+    copies = min(2, steps)
     per_copy = steps // copies
     size = slots // copies
 

time: 78.1 us -> 78.1 us (level)
  no operation moved by 1% of the time
where the time goes in v14:
time: 78.1 us; the launch traced here: 78 us
  starting transfers between devices  36 us (46%)
  waiting for transfers between devices  28.1 us (36%)
  Pallas kernels  13 us (17%)
  between operations  0.85 us (1%)
    ppermute x31, starting transfers between devices, permute(): return lax.ppermute(value, 'tp', moves)  36 us
    ppermute x31, waiting for transfers between devices, permute(): return lax.ppermute(value, 'tp', moves)  28.1 us
    pallas_call x19, Pallas kernels, kernel_call(): pl.pallas_call(ordered, out_shape=out_shape, in_specs=[anywhere()] * extr...  13 us
  transfers between devices with their start and end apart: 31, of which 15 were waited for; matrix products, arithmetic and copies ran while one was open for 0% of the time, Pallas kernels for 10%

profile of v14, /device:TPU:0, one launch (start us, length us, event | category | flops | bytes accessed | tf_op | source)
XLA Modules:
  0.0 78.0 jit_solution(18251334312945549496)
XLA Ops:
  0.6 4.1 %attend.1 = (bf16[128,128]{1,0:T(8,128)(2,1)S(1)}, f32[2,128,128]{2,1,0:T(8,128)S(1)}, bf16[1,128,1024]{2,1,0:T(8,128)(2,1)S(1)}, bf16[128,16384]{1,0:T(8,128)(2,1)S(1)}, bf16[128,128]{1,0:T(8,128)(2,1)S(1)}) custom-call(bf16[1,128,128]{2,1,0:T(8,128)(2,1)} %refs_0_.1, bf16[1,8192,128]{2,1,0:T(8,128)(2,1)} %refs_1_.5, bf16[1,8192,128]{2,1,0:T(8,128)(2,1)} %refs_2_.1, ...), custom_call_target="tpu_custom_call" | custom-call | tf_op jit(solution)/shard_map/attend/pallas_call | solution.py:58
  5.3 1.1 %partials.3 = (bf16[1,128,1024]{2,1,0:T(8,128)(2,1)S(1)}, bf16[2,128,1024]{2,1,0:T(8,128)(2,1)S(1)}, bf16[1,128,1024]{2,1,0:T(8,128)(2,1)S(1)}, bf16[1,128,1024]{2,1,0:T(8,128)(2,1)S(1)}) custom-call(bf16[128,128]{1,0:T(8,128)(2,1)S(1)} %get-tuple-element.40.refs_0_.refs_1_, bf16[128,16384]{1,0:T(8,128)(2,1)S(1)} %get-tuple-element.41.refs_1_.refs_2_, ...), custom_call_target="tpu_custom_call" | custom-call | tf_op jit(solution)/shard_map/partials/pallas_call | solution.py:58
  7.0 0.8 %partials.4 = (bf16[1,128,1024]{2,1,0:T(8,128)(2,1)S(1)}, bf16[2,128,1024]{2,1,0:T(8,128)(2,1)S(1)}) custom-call(bf16[64,1024]{1,0:T(8,128)(2,1)S(1)} %get-tuple-element.47.refs_0_, bf16[128,128]{1,0:T(8,128)(2,1)S(1)} %get-tuple-element.40.refs_0_.refs_1_, bf16[128,16384]{1,0:T(8,128)(2,1)S(1)} %get-tuple-element.41.refs_1_.refs_2_, ...), custom_call_target="tpu_custom_call" | custom-call | tf_op jit(solution)/shard_map/partials/pallas_call | solution.py:58
  8.0 2.9 %collective-permute-start.1 = (bf16[64,1024]{1,0:T(8,128)(2,1)S(1)}, bf16[64,1024]{1,0:T(8,128)(2,1)S(1)}, u32[]{:S(2)}, u32[]{:S(2)}) collective-permute-start(bf16[64,1024]{1,0:T(8,128)(2,1)S(1)} %get-tuple-element.47.refs_0_), channel_id=1, source_target_pairs={{0,2},{1,3},{2,0},{3,1},{4,6},{5,7},{6,4},{7,5},{8,10},{9,11},{10,... | collective-permute-start | bytes 393224 | tf_op jit(solution)/shard_map/ppermute | solution.py:573
  10.9 1.6 %collective-permute-start.4 = (bf16[64,1024]{1,0:T(8,128)(2,1)S(1)}, bf16[64,1024]{1,0:T(8,128)(2,1)S(1)}, u32[]{:S(2)}, u32[]{:S(2)}) collective-permute-start(bf16[64,1024]{1,0:T(8,128)(2,1)S(1)} %get-tuple-element.52), channel_id=1, source_target_pairs={{0,4},{1,5},{2,6},{3,7},{4,0},{5,1},{6,2},{7,3},{8,12},{9,13},{10,... | collective-permute-start | bytes 393224 | tf_op jit(solution)/shard_map/ppermute | solution.py:573
  12.5 1.3 %partials.5 = (bf16[2,128,1024]{2,1,0:T(8,128)(2,1)S(1)}, bf16[1,128,1024]{2,1,0:T(8,128)(2,1)S(1)}, bf16[2,128,1024]{2,1,0:T(8,128)(2,1)S(1)}, bf16[2,128,1024]{2,1,0:T(8,128)(2,1)S(1)}) custom-call(bf16[2,128,1024]{2,1,0:T(8,128)(2,1)S(1)} %get-tuple-element.48.refs_0_, bf16[128,128]{1,0:T(8,128)(2,1)S(1)} %get-tuple-element.40.refs_0_.refs_1_, ...), custom_call_target="tpu_custom_call" | custom-call | tf_op jit(solution)/shard_map/partials/pallas_call | solution.py:58
  14.6 1.5 %collective-permute-done.4.refs_6_ = bf16[64,1024]{1,0:T(8,128)(2,1)S(1)} collective-permute-done((bf16[64,1024]{1,0:T(8,128)(2,1)S(1)}, bf16[64,1024]{1,0:T(8,128)(2,1)S(1)}, u32[]{:S(2)}, u32[]{:S(2)}) %collective-permute-start.4) | collective-permute-done | bytes 131104 | tf_op jit(solution)/shard_map/ppermute | solution.py:573
  16.7 1.7 %collective-permute-start.7 = (bf16[128,1024]{1,0:T(8,128)(2,1)S(1)}, bf16[128,1024]{1,0:T(8,128)(2,1)S(1)}, u32[]{:S(2)}, u32[]{:S(2)}) collective-permute-start(bf16[128,1024]{1,0:T(8,128)(2,1)S(1)} %get-tuple-element.53.refs_0_), channel_id=1, source_target_pairs={{0,4},{1,5},{2,6},{3,7},{4,0},{5,1},{6,2},{7,3},{8,12},{9,13},{10,... | collective-permute-start | bytes 786440 | tf_op jit(solution)/shard_map/ppermute | solution.py:573
  18.9 4.6 %collective-permute-done.6.refs_2_ = bf16[128,1024]{1,0:T(8,128)(2,1)S(1)} collective-permute-done((bf16[128,1024]{1,0:T(8,128)(2,1)S(1)}, bf16[128,1024]{1,0:T(8,128)(2,1)S(1)}, u32[]{:S(2)}, u32[]{:S(2)}) %collective-permute-start.6) | collective-permute-done | bytes 262176 | tf_op jit(solution)/shard_map/ppermute | solution.py:573
  23.5 1.1 %collective-permute-done.7.refs_3_ = bf16[128,1024]{1,0:T(8,128)(2,1)S(1)} collective-permute-done((bf16[128,1024]{1,0:T(8,128)(2,1)S(1)}, bf16[128,1024]{1,0:T(8,128)(2,1)S(1)}, u32[]{:S(2)}, u32[]{:S(2)}) %collective-permute-start.7) | collective-permute-done | bytes 262176 | tf_op jit(solution)/shard_map/ppermute | solution.py:573
  24.8 1.6 %collective-permute-start.10 = (bf16[128,1024]{1,0:T(8,128)(2,1)S(1)}, bf16[128,1024]{1,0:T(8,128)(2,1)S(1)}, u32[]{:S(2)}, u32[]{:S(2)}) collective-permute-start(bf16[128,1024]{1,0:T(8,128)(2,1)S(1)} %get-tuple-element.60), channel_id=1, source_target_pairs={{0,2},{1,3},{2,0},{3,1},{4,6},{5,7},{6,4},{7,5},{8,10},{9,11},{10,... | collective-permute-start | bytes 786440 | tf_op jit(solution)/shard_map/ppermute | solution.py:573
  26.3 1.7 %collective-permute-start.11 = (bf16[128,1024]{1,0:T(8,128)(2,1)S(1)}, bf16[128,1024]{1,0:T(8,128)(2,1)S(1)}, u32[]{:S(2)}, u32[]{:S(2)}) collective-permute-start(bf16[128,1024]{1,0:T(8,128)(2,1)S(1)} %get-tuple-element.61), channel_id=1, source_target_pairs={{0,4},{1,5},{2,6},{3,7},{4,0},{5,1},{6,2},{7,3},{8,12},{9,13},{10,... | collective-permute-start | bytes 786440 | tf_op jit(solution)/shard_map/ppermute | solution.py:573
  28.1 3.7 %collective-permute-done.10.refs_0_ = bf16[128,1024]{1,0:T(8,128)(2,1)S(1)} collective-permute-done((bf16[128,1024]{1,0:T(8,128)(2,1)S(1)}, bf16[128,1024]{1,0:T(8,128)(2,1)S(1)}, u32[]{:S(2)}, u32[]{:S(2)}) %collective-permute-start.10) | collective-permute-done | bytes 262176 | tf_op jit(solution)/shard_map/ppermute | solution.py:573
  31.7 1.2 %collective-permute-done.11.refs_1_ = bf16[128,1024]{1,0:T(8,128)(2,1)S(1)} collective-permute-done((bf16[128,1024]{1,0:T(8,128)(2,1)S(1)}, bf16[128,1024]{1,0:T(8,128)(2,1)S(1)}, u32[]{:S(2)}, u32[]{:S(2)}) %collective-permute-start.11) | collective-permute-done | bytes 262176 | tf_op jit(solution)/shard_map/ppermute | solution.py:573
  34.0 1.7 %collective-permute-start.15 = (bf16[128,1024]{1,0:T(8,128)(2,1)S(1)}, bf16[128,1024]{1,0:T(8,128)(2,1)S(1)}, u32[]{:S(2)}, u32[]{:S(2)}) collective-permute-start(bf16[128,1024]{1,0:T(8,128)(2,1)S(1)} %get-tuple-element.64), channel_id=1, source_target_pairs={{0,4},{1,5},{2,6},{3,7},{4,0},{5,1},{6,2},{7,3},{8,12},{9,13},{10,... | collective-permute-start | bytes 786440 | tf_op jit(solution)/shard_map/ppermute | solution.py:573
  36.3 3.5 %collective-permute-done.14.refs_0_.refs_4_ = bf16[128,1024]{1,0:T(8,128)(2,1)S(1)} collective-permute-done((bf16[128,1024]{1,0:T(8,128)(2,1)S(1)}, bf16[128,1024]{1,0:T(8,128)(2,1)S(1)}, u32[]{:S(2)}, u32[]{:S(2)}) %collective-permute-start.14) | collective-permute-done | bytes 262176 | tf_op jit(solution)/shard_map/ppermute | solution.py:573
  40.7 1.5 %collective-permute-start.17 = (bf16[128,1024]{1,0:T(8,128)(2,1)S(1)}, bf16[128,1024]{1,0:T(8,128)(2,1)S(1)}, u32[]{:S(2)}, u32[]{:S(2)}) collective-permute-start(bf16[128,1024]{1,0:T(8,128)(2,1)S(1)} %regrid.1.refs_0_.refs_2_), channel_id=1, source_target_pairs={{0,2},{1,3},{2,0},{3,1},{4,6},{5,7},{6,4},{7,5},{8,10},{9,11},{10,... | collective-permute-start | bytes 786440 | tf_op jit(solution)/shard_map/ppermute | solution.py:573
  42.2 2.2 %collective-permute-start.18 = (bf16[128,1024]{1,0:T(8,128)(2,1)S(1)}, bf16[128,1024]{1,0:T(8,128)(2,1)S(1)}, u32[]{:S(2)}, u32[]{:S(2)}) collective-permute-start(bf16[128,1024]{1,0:T(8,128)(2,1)S(1)} %regrid.1.refs_0_.refs_2_), channel_id=1, source_target_pairs={{0,4},{1,5},{2,6},{3,7},{4,0},{5,1},{6,2},{7,3},{8,12},{9,13},{10,... | collective-permute-start | bytes 786440 | tf_op jit(solution)/shard_map/ppermute | solution.py:573
  44.4 1.1 %hidden.1 = (bf16[128,1024]{1,0:T(8,128)(2,1)}, f32[8,128]{1,0:T(8,128)S(1)}) custom-call(bf16[128,1024]{1,0:T(8,128)(2,1)S(1)} %regrid.1.refs_0_.refs_2_, bf16[128,1024]{1,0:T(8,128)(2,1)S(1)} %copy-done.1, f32[2,1024]{1,0:T(2,128)S(1)} %get-tuple-element.54.refs_0_.refs_6_.refs_2_, bf16[128,128]{1,0:T(8,128)(2,1)S(1)} %get-tuple-element.43.refs_3_.refs_4_, ...), custom_call_target="tpu_custom_call" | custom-call | tf_op jit(solution)/shard_map/hidden/pallas_call | solution.py:58
  45.5 1.6 %collective-permute-done.17.refs_1_.refs_6_ = bf16[128,1024]{1,0:T(8,128)(2,1)S(1)} collective-permute-done((bf16[128,1024]{1,0:T(8,128)(2,1)S(1)}, bf16[128,1024]{1,0:T(8,128)(2,1)S(1)}, u32[]{:S(2)}, u32[]{:S(2)}) %collective-permute-start.17) | collective-permute-done | bytes 262176 | tf_op jit(solution)/shard_map/ppermute | solution.py:573
  47.1 1.6 %collective-permute-done.18.refs_2_ = bf16[128,1024]{1,0:T(8,128)(2,1)S(1)} collective-permute-done((bf16[128,1024]{1,0:T(8,128)(2,1)S(1)}, bf16[128,1024]{1,0:T(8,128)(2,1)S(1)}, u32[]{:S(2)}, u32[]{:S(2)}) %collective-permute-start.18) | collective-permute-done | bytes 262176 | tf_op jit(solution)/shard_map/ppermute | solution.py:573
  49.3 7.3 %collective-permute-start.22 = (bf16[128,1024]{1,0:T(8,128)(2,1)S(1)}, bf16[128,1024]{1,0:T(8,128)(2,1)S(1)}, u32[]{:S(2)}, u32[]{:S(2)}) collective-permute-start(bf16[128,1024]{1,0:T(8,128)(2,1)S(1)} %get-tuple-element.70.refs_1_), channel_id=1, source_target_pairs={{0,4},{1,5},{2,6},{3,7},{4,0},{5,1},{6,2},{7,3},{8,12},{9,13},{10,... | collective-permute-start | bytes 786440 | tf_op jit(solution)/shard_map/ppermute | solution.py:573
  56.7 4.5 %collective-permute-start.25 = (bf16[128,1024]{1,0:T(8,128)(2,1)S(1)}, bf16[128,1024]{1,0:T(8,128)(2,1)S(1)}, u32[]{:S(2)}, u32[]{:S(2)}) collective-permute-start(bf16[128,1024]{1,0:T(8,128)(2,1)S(1)} %collective-permute-done.21.refs_1_), channel_id=1, source_target_pairs={{0,4},{1,5},{2,6},{3,7},{4,0},{5,1},{6,2},{7,3},{8,12},{9,13},{10,... | collective-permute-start | bytes 786440 | tf_op jit(solution)/shard_map/ppermute | solution.py:573
  61.1 1.7 %collective-permute-start.26 = (bf16[128,1024]{1,0:T(8,128)(2,1)S(1)}, bf16[128,1024]{1,0:T(8,128)(2,1)S(1)}, u32[]{:S(2)}, u32[]{:S(2)}) collective-permute-start(bf16[128,1024]{1,0:T(8,128)(2,1)S(1)} %choose.2.refs_0_.refs_4_), channel_id=1, source_target_pairs={{0,2},{1,3},{2,0},{3,1},{4,6},{5,7},{6,4},{7,5},{8,10},{9,11},{10,... | collective-permute-start | bytes 786440 | tf_op jit(solution)/shard_map/ppermute | solution.py:573
  62.9 1.3 %turn_next.1.refs_0_ = bf16[8,1024,256]{2,1,0:T(8,128)(2,1)S(1)} custom-call(bf16[128,1024]{1,0:T(8,128)(2,1)S(1)} %choose.2.refs_0_.refs_4_, bf16[16384,128]{1,0:T(8,128)(2,1)S(1)} %copy-done, f32[128,128]{1,0:T(8,128)S(1)} %bitcast_convert_fusion.refs_2_, f32[2,128,128]{2,1,0:T(8,128)S(1)} %get-tuple-element.42.refs_2_.refs_3_.refs_1_, ...), custom_call_target="tpu_custom_call" | custom-call | tf_op jit(solution)/shard_map/turn_next/pallas_call | solution.py:58
  64.2 1.3 %collective-permute-done.25.refs_2_ = bf16[128,1024]{1,0:T(8,128)(2,1)S(1)} collective-permute-done((bf16[128,1024]{1,0:T(8,128)(2,1)S(1)}, bf16[128,1024]{1,0:T(8,128)(2,1)S(1)}, u32[]{:S(2)}, u32[]{:S(2)}) %collective-permute-start.25) | collective-permute-done | bytes 262176 | tf_op jit(solution)/shard_map/ppermute | solution.py:573
  65.5 2.5 %collective-permute-done.26.refs_3_.refs_8_ = bf16[128,1024]{1,0:T(8,128)(2,1)S(1)} collective-permute-done((bf16[128,1024]{1,0:T(8,128)(2,1)S(1)}, bf16[128,1024]{1,0:T(8,128)(2,1)S(1)}, u32[]{:S(2)}, u32[]{:S(2)}) %collective-permute-start.26) | collective-permute-done | bytes 262176 | tf_op jit(solution)/shard_map/ppermute | solution.py:573
  68.0 2.5 %collective-permute-start.27 = (bf16[64,1024]{1,0:T(8,128)(2,1)S(1)}, bf16[64,1024]{1,0:T(8,128)(2,1)S(1)}, u32[]{:S(2)}, u32[]{:S(2)}) collective-permute-start(bf16[64,1024]{1,0:T(8,128)(2,1)S(1)} %get-tuple-element.73), channel_id=1, source_target_pairs={{0,2},{1,3},{2,0},{3,1},{4,6},{5,7},{6,4},{7,5},{8,10},{9,11},{10,... | collective-permute-start | bytes 393224 | tf_op jit(solution)/shard_map/ppermute | solution.py:573
  70.6 0.9 %collective-permute-start.29 = (bf16[64,1024]{1,0:T(8,128)(2,1)S(1)}, bf16[64,1024]{1,0:T(8,128)(2,1)S(1)}, u32[]{:S(2)}, u32[]{:S(2)}) collective-permute-start(bf16[64,1024]{1,0:T(8,128)(2,1)S(1)} %get-tuple-element.75), channel_id=1, source_target_pairs={{0,4},{1,5},{2,6},{3,7},{4,0},{5,1},{6,2},{7,3},{8,12},{9,13},{10,... | collective-permute-start | bytes 393224 | tf_op jit(solution)/shard_map/ppermute | solution.py:573
  72.3 1.3 %collective-permute-done.27.refs_3_ = bf16[64,1024]{1,0:T(8,128)(2,1)S(1)} collective-permute-done((bf16[64,1024]{1,0:T(8,128)(2,1)S(1)}, bf16[64,1024]{1,0:T(8,128)(2,1)S(1)}, u32[]{:S(2)}, u32[]{:S(2)}) %collective-permute-start.27) | collective-permute-done | bytes 131104 | tf_op jit(solution)/shard_map/ppermute | solution.py:573
  73.5 2.0 %collective-permute-done.29.refs_5_ = bf16[64,1024]{1,0:T(8,128)(2,1)S(1)} collective-permute-done((bf16[64,1024]{1,0:T(8,128)(2,1)S(1)}, bf16[64,1024]{1,0:T(8,128)(2,1)S(1)}, u32[]{:S(2)}, u32[]{:S(2)}) %collective-permute-start.29) | collective-permute-done | bytes 131104 | tf_op jit(solution)/shard_map/ppermute | solution.py:573
  75.9 1.3 %collective-permute-done.30.refs_1_ = f32[128,256]{1,0:T(8,128)S(1)} collective-permute-done((f32[128,256]{1,0:T(8,128)S(1)}, f32[128,256]{1,0:T(8,128)S(1)}, u32[]{:S(2)}, u32[]{:S(2)}) %collective-permute-start.30) | collective-permute-done | bytes 131104 | tf_op jit(solution)/shard_map/ppermute | solution.py:573
  (56 shorter events, 8.3 us)
Async XLA Ops:
  4.8 2.2 %collective-permute-start = (bf16[1,128,1024]{2,1,0:T(8,128)(2,1)S(1)}, bf16[1,128,1024]{2,1,0:T(8,128)(2,1)S(1)}, u32[]{:S(2)}, u32[]{:S(2)}) collective-permute-start(bf16[1,128,1024]{2,1,0:T(8,128)(2,1)S(1)} %get-tuple-element.46), channel_id=1, source_target_pairs={{0,1},{1,0},{2,3},{3,2},{4,5},{5,4},{6,7},{7,6},{8,9},{9,8},{10,11... | collective-permute-start | bytes 786440 | tf_op jit(solution)/shard_map/ppermute | solution.py:573
  6.4 6.1 %collective-permute-start.2 = (bf16[1,128,1024]{2,1,0:T(8,128)(2,1)S(1)}, bf16[1,128,1024]{2,1,0:T(8,128)(2,1)S(1)}, u32[]{:S(2)}, u32[]{:S(2)}) collective-permute-start(bf16[1,128,1024]{2,1,0:T(8,128)(2,1)S(1)} %get-tuple-element.50), channel_id=1, source_target_pairs={{0,1},{1,0},{2,3},{3,2},{4,5},{5,4},{6,7},{7,6},{8,9},{9,8},{10,11... | collective-permute-start | bytes 786440 | tf_op jit(solution)/shard_map/ppermute | solution.py:573
  6.5 7.4 %collective-permute-start.3 = (bf16[1,128,1024]{2,1,0:T(8,128)(2,1)S(1)}, bf16[1,128,1024]{2,1,0:T(8,128)(2,1)S(1)}, u32[]{:S(2)}, u32[]{:S(2)}) collective-permute-start(bf16[1,128,1024]{2,1,0:T(8,128)(2,1)S(1)} %get-tuple-element.51), channel_id=1, source_target_pairs={{0,1},{1,0},{2,3},{3,2},{4,5},{5,4},{6,7},{7,6},{8,9},{9,8},{10,11... | collective-permute-start | bytes 786440 | tf_op jit(solution)/shard_map/ppermute | solution.py:573
  7.8 16.7 %collective-permute-start.9 = (bf16[2,128,1024]{2,1,0:T(8,128)(2,1)S(1)}, bf16[2,128,1024]{2,1,0:T(8,128)(2,1)S(1)}, u32[]{:S(2)}, u32[]{:S(2)}) collective-permute-start(bf16[2,128,1024]{2,1,0:T(8,128)(2,1)S(1)} %get-tuple-element.48.refs_0_), channel_id=1, source_target_pairs={{0,1},{1,0},{2,3},{3,2},{4,5},{5,4},{6,7},{7,6},{8,9},{9,8},{10,11... | collective-permute-start | bytes 1572872 | tf_op jit(solution)/shard_map/ppermute | solution.py:573
  8.0 6.7 %collective-permute-start.1 = (bf16[64,1024]{1,0:T(8,128)(2,1)S(1)}, bf16[64,1024]{1,0:T(8,128)(2,1)S(1)}, u32[]{:S(2)}, u32[]{:S(2)}) collective-permute-start(bf16[64,1024]{1,0:T(8,128)(2,1)S(1)} %get-tuple-element.47.refs_0_), channel_id=1, source_target_pairs={{0,2},{1,3},{2,0},{3,1},{4,6},{5,7},{6,4},{7,5},{8,10},{9,11},{10,... | collective-permute-start | bytes 393224 | tf_op jit(solution)/shard_map/ppermute | solution.py:573
  10.9 5.2 %collective-permute-start.4 = (bf16[64,1024]{1,0:T(8,128)(2,1)S(1)}, bf16[64,1024]{1,0:T(8,128)(2,1)S(1)}, u32[]{:S(2)}, u32[]{:S(2)}) collective-permute-start(bf16[64,1024]{1,0:T(8,128)(2,1)S(1)} %get-tuple-element.52), channel_id=1, source_target_pairs={{0,4},{1,5},{2,6},{3,7},{4,0},{5,1},{6,2},{7,3},{8,12},{9,13},{10,... | collective-permute-start | bytes 393224 | tf_op jit(solution)/shard_map/ppermute | solution.py:573
  12.5 6.0 %collective-permute-start.5 = (bf16[64,1024]{1,0:T(8,128)(2,1)S(1)}, bf16[64,1024]{1,0:T(8,128)(2,1)S(1)}, u32[]{:S(2)}, u32[]{:S(2)}) collective-permute-start(bf16[64,1024]{1,0:T(8,128)(2,1)S(1)} %get-tuple-element.52), channel_id=1, source_target_pairs={{0,1},{1,0},{2,3},{3,2},{4,8},{5,9},{6,10},{7,11},{8,4},{9,5},{10,... | collective-permute-start | bytes 393224 | tf_op jit(solution)/shard_map/ppermute | solution.py:573
  13.9 5.0 %collective-permute-start.8 = (bf16[1,128,1024]{2,1,0:T(8,128)(2,1)S(1)}, bf16[1,128,1024]{2,1,0:T(8,128)(2,1)S(1)}, u32[]{:S(2)}, u32[]{:S(2)}) collective-permute-start(bf16[1,128,1024]{2,1,0:T(8,128)(2,1)S(1)} %get-tuple-element.58), channel_id=1, source_target_pairs={{0,1},{1,0},{2,3},{3,2},{4,5},{5,4},{6,7},{7,6},{8,9},{9,8},{10,11... | collective-permute-start | bytes 786440 | tf_op jit(solution)/shard_map/ppermute | solution.py:573
  16.3 7.2 %collective-permute-start.6 = (bf16[128,1024]{1,0:T(8,128)(2,1)S(1)}, bf16[128,1024]{1,0:T(8,128)(2,1)S(1)}, u32[]{:S(2)}, u32[]{:S(2)}) collective-permute-start(bf16[128,1024]{1,0:T(8,128)(2,1)S(1)} %get-tuple-element.56), channel_id=1, source_target_pairs={{0,2},{1,3},{2,0},{3,1},{4,6},{5,7},{6,4},{7,5},{8,10},{9,11},{10,... | collective-permute-start | bytes 786440 | tf_op jit(solution)/shard_map/ppermute | solution.py:573
  16.7 7.8 %collective-permute-start.7 = (bf16[128,1024]{1,0:T(8,128)(2,1)S(1)}, bf16[128,1024]{1,0:T(8,128)(2,1)S(1)}, u32[]{:S(2)}, u32[]{:S(2)}) collective-permute-start(bf16[128,1024]{1,0:T(8,128)(2,1)S(1)} %get-tuple-element.53.refs_0_), channel_id=1, source_target_pairs={{0,4},{1,5},{2,6},{3,7},{4,0},{5,1},{6,2},{7,3},{8,12},{9,13},{10,... | collective-permute-start | bytes 786440 | tf_op jit(solution)/shard_map/ppermute | solution.py:573
  18.5 9.6 %collective-permute-start.13 = (bf16[2,128,1024]{2,1,0:T(8,128)(2,1)S(1)}, bf16[2,128,1024]{2,1,0:T(8,128)(2,1)S(1)}, u32[]{:S(2)}, u32[]{:S(2)}) collective-permute-start(bf16[2,128,1024]{2,1,0:T(8,128)(2,1)S(1)} %get-tuple-element.49.refs_1_), channel_id=1, source_target_pairs={{0,1},{1,0},{2,3},{3,2},{4,5},{5,4},{6,7},{7,6},{8,9},{9,8},{10,11... | collective-permute-start | bytes 1572872 | tf_op jit(solution)/shard_map/ppermute | solution.py:573
  24.8 7.0 %collective-permute-start.10 = (bf16[128,1024]{1,0:T(8,128)(2,1)S(1)}, bf16[128,1024]{1,0:T(8,128)(2,1)S(1)}, u32[]{:S(2)}, u32[]{:S(2)}) collective-permute-start(bf16[128,1024]{1,0:T(8,128)(2,1)S(1)} %get-tuple-element.60), channel_id=1, source_target_pairs={{0,2},{1,3},{2,0},{3,1},{4,6},{5,7},{6,4},{7,5},{8,10},{9,11},{10,... | collective-permute-start | bytes 786440 | tf_op jit(solution)/shard_map/ppermute | solution.py:573
  26.3 6.7 %collective-permute-start.11 = (bf16[128,1024]{1,0:T(8,128)(2,1)S(1)}, bf16[128,1024]{1,0:T(8,128)(2,1)S(1)}, u32[]{:S(2)}, u32[]{:S(2)}) collective-permute-start(bf16[128,1024]{1,0:T(8,128)(2,1)S(1)} %get-tuple-element.61), channel_id=1, source_target_pairs={{0,4},{1,5},{2,6},{3,7},{4,0},{5,1},{6,2},{7,3},{8,12},{9,13},{10,... | collective-permute-start | bytes 786440 | tf_op jit(solution)/shard_map/ppermute | solution.py:573
  28.1 4.9 %collective-permute-start.12 = (bf16[128,1024]{1,0:T(8,128)(2,1)S(1)}, bf16[128,1024]{1,0:T(8,128)(2,1)S(1)}, u32[]{:S(2)}, u32[]{:S(2)}) collective-permute-start(bf16[128,1024]{1,0:T(8,128)(2,1)S(1)} %get-tuple-element.61), channel_id=1, source_target_pairs={{0,1},{1,0},{2,3},{3,2},{4,8},{5,9},{6,10},{7,11},{8,4},{9,5},{10,... | collective-permute-start | bytes 786440 | tf_op jit(solution)/shard_map/ppermute | solution.py:573
  33.3 29.5 %copy-start.2 = (bf16[16384]{0:T(1024)(128)(2,1)S(1)}, bf16[16384]{0:T(1024)(128)(2,1)}, u32[]{:S(2)}) copy-start(bf16[16384]{0:T(1024)(128)(2,1)} %param.17) | copy-start | bytes 98308
  33.4 6.4 %collective-permute-start.14 = (bf16[128,1024]{1,0:T(8,128)(2,1)S(1)}, bf16[128,1024]{1,0:T(8,128)(2,1)S(1)}, u32[]{:S(2)}, u32[]{:S(2)}) collective-permute-start(bf16[128,1024]{1,0:T(8,128)(2,1)S(1)} %get-tuple-element.63), channel_id=1, source_target_pairs={{0,2},{1,3},{2,0},{3,1},{4,6},{5,7},{6,4},{7,5},{8,10},{9,11},{10,... | collective-permute-start | bytes 786440 | tf_op jit(solution)/shard_map/ppermute | solution.py:573
  34.0 6.4 %collective-permute-start.15 = (bf16[128,1024]{1,0:T(8,128)(2,1)S(1)}, bf16[128,1024]{1,0:T(8,128)(2,1)S(1)}, u32[]{:S(2)}, u32[]{:S(2)}) collective-permute-start(bf16[128,1024]{1,0:T(8,128)(2,1)S(1)} %get-tuple-element.64), channel_id=1, source_target_pairs={{0,4},{1,5},{2,6},{3,7},{4,0},{5,1},{6,2},{7,3},{8,12},{9,13},{10,... | collective-permute-start | bytes 786440 | tf_op jit(solution)/shard_map/ppermute | solution.py:573
  35.8 4.6 %collective-permute-start.16 = (bf16[128,1024]{1,0:T(8,128)(2,1)S(1)}, bf16[128,1024]{1,0:T(8,128)(2,1)S(1)}, u32[]{:S(2)}, u32[]{:S(2)}) collective-permute-start(bf16[128,1024]{1,0:T(8,128)(2,1)S(1)} %get-tuple-element.65), channel_id=1, source_target_pairs={{0,1},{1,0},{2,3},{3,2},{4,8},{5,9},{6,10},{7,11},{8,4},{9,5},{10,... | collective-permute-start | bytes 786440 | tf_op jit(solution)/shard_map/ppermute | solution.py:573
  35.8 27.1 %collective-permute-start.23 = (bf16[4,1024,128]{2,1,0:T(8,128)(2,1)S(1)}, bf16[4,1024,128]{2,1,0:T(8,128)(2,1)S(1)}, u32[]{:S(2)}, u32[]{:S(2)}) collective-permute-start(bf16[4,1024,128]{2,1,0:T(8,128)(2,1)S(1)} %get-tuple-element.55.refs_0_), channel_id=1, source_target_pairs={{0,1},{1,0},{2,3},{3,2},{4,5},{5,4},{6,7},{7,6},{8,9},{9,8},{10,11... | collective-permute-start | bytes 3145736 | tf_op jit(solution)/shard_map/ppermute | solution.py:573
  36.3 26.6 %collective-permute-start.24 = (bf16[4,1024,128]{2,1,0:T(8,128)(2,1)S(1)}, bf16[4,1024,128]{2,1,0:T(8,128)(2,1)S(1)}, u32[]{:S(2)}, u32[]{:S(2)}) collective-permute-start(bf16[4,1024,128]{2,1,0:T(8,128)(2,1)S(1)} %get-tuple-element.71), channel_id=1, source_target_pairs={{0,1},{1,0},{2,3},{3,2},{4,5},{5,4},{6,7},{7,6},{8,9},{9,8},{10,11... | collective-permute-start | bytes 3145736 | tf_op jit(solution)/shard_map/ppermute | solution.py:573
  40.7 6.4 %collective-permute-start.17 = (bf16[128,1024]{1,0:T(8,128)(2,1)S(1)}, bf16[128,1024]{1,0:T(8,128)(2,1)S(1)}, u32[]{:S(2)}, u32[]{:S(2)}) collective-permute-start(bf16[128,1024]{1,0:T(8,128)(2,1)S(1)} %regrid.1.refs_0_.refs_2_), channel_id=1, source_target_pairs={{0,2},{1,3},{2,0},{3,1},{4,6},{5,7},{6,4},{7,5},{8,10},{9,11},{10,... | collective-permute-start | bytes 786440 | tf_op jit(solution)/shard_map/ppermute | solution.py:573
  42.2 6.6 %collective-permute-start.18 = (bf16[128,1024]{1,0:T(8,128)(2,1)S(1)}, bf16[128,1024]{1,0:T(8,128)(2,1)S(1)}, u32[]{:S(2)}, u32[]{:S(2)}) collective-permute-start(bf16[128,1024]{1,0:T(8,128)(2,1)S(1)} %regrid.1.refs_0_.refs_2_), channel_id=1, source_target_pairs={{0,4},{1,5},{2,6},{3,7},{4,0},{5,1},{6,2},{7,3},{8,12},{9,13},{10,... | collective-permute-start | bytes 786440 | tf_op jit(solution)/shard_map/ppermute | solution.py:573
  44.4 4.4 %collective-permute-start.19 = (bf16[128,1024]{1,0:T(8,128)(2,1)S(1)}, bf16[128,1024]{1,0:T(8,128)(2,1)S(1)}, u32[]{:S(2)}, u32[]{:S(2)}) collective-permute-start(bf16[128,1024]{1,0:T(8,128)(2,1)S(1)} %regrid.1.refs_0_.refs_2_), channel_id=1, source_target_pairs={{0,1},{1,0},{2,3},{3,2},{4,8},{5,9},{6,10},{7,11},{8,4},{9,5},{10,... | collective-permute-start | bytes 786440 | tf_op jit(solution)/shard_map/ppermute | solution.py:573
  48.8 7.9 %collective-permute-start.21 = (bf16[128,1024]{1,0:T(8,128)(2,1)S(1)}, bf16[128,1024]{1,0:T(8,128)(2,1)S(1)}, u32[]{:S(2)}, u32[]{:S(2)}) collective-permute-start(bf16[128,1024]{1,0:T(8,128)(2,1)S(1)} %get-tuple-element.69.refs_3_), channel_id=1, source_target_pairs={{0,1},{1,0},{2,3},{3,2},{4,8},{5,9},{6,10},{7,11},{8,4},{9,5},{10,... | collective-permute-start | bytes 786440 | tf_op jit(solution)/shard_map/ppermute | solution.py:573
  48.8 12.3 %collective-permute-start.20 = (bf16[128,1024]{1,0:T(8,128)(2,1)S(1)}, bf16[128,1024]{1,0:T(8,128)(2,1)S(1)}, u32[]{:S(2)}, u32[]{:S(2)}) collective-permute-start(bf16[128,1024]{1,0:T(8,128)(2,1)S(1)} %get-tuple-element.69.refs_3_), channel_id=1, source_target_pairs={{0,2},{1,3},{2,0},{3,1},{4,6},{5,7},{6,4},{7,5},{8,10},{9,11},{10,... | collective-permute-start | bytes 786440 | tf_op jit(solution)/shard_map/ppermute | solution.py:573
  49.3 11.8 %collective-permute-start.22 = (bf16[128,1024]{1,0:T(8,128)(2,1)S(1)}, bf16[128,1024]{1,0:T(8,128)(2,1)S(1)}, u32[]{:S(2)}, u32[]{:S(2)}) collective-permute-start(bf16[128,1024]{1,0:T(8,128)(2,1)S(1)} %get-tuple-element.70.refs_1_), channel_id=1, source_target_pairs={{0,4},{1,5},{2,6},{3,7},{4,0},{5,1},{6,2},{7,3},{8,12},{9,13},{10,... | collective-permute-start | bytes 786440 | tf_op jit(solution)/shard_map/ppermute | solution.py:573
  56.7 8.8 %collective-permute-start.25 = (bf16[128,1024]{1,0:T(8,128)(2,1)S(1)}, bf16[128,1024]{1,0:T(8,128)(2,1)S(1)}, u32[]{:S(2)}, u32[]{:S(2)}) collective-permute-start(bf16[128,1024]{1,0:T(8,128)(2,1)S(1)} %collective-permute-done.21.refs_1_), channel_id=1, source_target_pairs={{0,4},{1,5},{2,6},{3,7},{4,0},{5,1},{6,2},{7,3},{8,12},{9,13},{10,... | collective-permute-start | bytes 786440 | tf_op jit(solution)/shard_map/ppermute | solution.py:573
  61.1 6.9 %collective-permute-start.26 = (bf16[128,1024]{1,0:T(8,128)(2,1)S(1)}, bf16[128,1024]{1,0:T(8,128)(2,1)S(1)}, u32[]{:S(2)}, u32[]{:S(2)}) collective-permute-start(bf16[128,1024]{1,0:T(8,128)(2,1)S(1)} %choose.2.refs_0_.refs_4_), channel_id=1, source_target_pairs={{0,2},{1,3},{2,0},{3,1},{4,6},{5,7},{6,4},{7,5},{8,10},{9,11},{10,... | collective-permute-start | bytes 786440 | tf_op jit(solution)/shard_map/ppermute | solution.py:573
  62.8 9.4 %collective-permute-start.28 = (bf16[64,1024]{1,0:T(8,128)(2,1)S(1)}, bf16[64,1024]{1,0:T(8,128)(2,1)S(1)}, u32[]{:S(2)}, u32[]{:S(2)}) collective-permute-start(bf16[64,1024]{1,0:T(8,128)(2,1)S(1)} %get-tuple-element.74), channel_id=1, source_target_pairs={{0,1},{1,0},{2,3},{3,2},{4,8},{5,9},{6,10},{7,11},{8,4},{9,5},{10,... | collective-permute-start | bytes 393224 | tf_op jit(solution)/shard_map/ppermute | solution.py:573
  68.0 5.5 %collective-permute-start.27 = (bf16[64,1024]{1,0:T(8,128)(2,1)S(1)}, bf16[64,1024]{1,0:T(8,128)(2,1)S(1)}, u32[]{:S(2)}, u32[]{:S(2)}) collective-permute-start(bf16[64,1024]{1,0:T(8,128)(2,1)S(1)} %get-tuple-element.73), channel_id=1, source_target_pairs={{0,2},{1,3},{2,0},{3,1},{4,6},{5,7},{6,4},{7,5},{8,10},{9,11},{10,... | collective-permute-start | bytes 393224 | tf_op jit(solution)/shard_map/ppermute | solution.py:573
  70.6 5.0 %collective-permute-start.29 = (bf16[64,1024]{1,0:T(8,128)(2,1)S(1)}, bf16[64,1024]{1,0:T(8,128)(2,1)S(1)}, u32[]{:S(2)}, u32[]{:S(2)}) collective-permute-start(bf16[64,1024]{1,0:T(8,128)(2,1)S(1)} %get-tuple-element.75), channel_id=1, source_target_pairs={{0,4},{1,5},{2,6},{3,7},{4,0},{5,1},{6,2},{7,3},{8,12},{9,13},{10,... | collective-permute-start | bytes 393224 | tf_op jit(solution)/shard_map/ppermute | solution.py:573
  75.8 1.4 %collective-permute-start.30 = (f32[128,256]{1,0:T(8,128)S(1)}, f32[128,256]{1,0:T(8,128)S(1)}, u32[]{:S(2)}, u32[]{:S(2)}) collective-permute-start(f32[128,256]{1,0:T(8,128)S(1)} %get-tuple-element.77), channel_id=1, source_target_pairs={{0,1},{1,0},{2,3},{3,2},{4,5},{5,4},{6,7},{7,6},{8,9},{9,8},{10,11... | collective-permute-start | bytes 393224 | tf_op jit(solution)/shard_map/ppermute | solution.py:573
  (2 other events, 21.5 us)
